TPU v7x, 32 devices: a whole 2x2x4 slice. The times are simulated.
32 devices in a mesh: member: 4 (over x, core), lat: 8 (over z, y).
Axes of the slice: x: 2, y: 2, z: 4, core: 2. Of those that a mesh axis runs over, the one named last changes fastest.
Arguments:
- velocity: bfloat16 [8, 8, 1024, 2048], P('member', None, 'lat'), may hold values from -6 to 6
- tracer: bfloat16 [8, 8, 1024, 2048], P('member', None, 'lat'), may hold values from -6 to 6
- wave_slots: int32 [704], replicated, may hold values from 0 to 703, each once
- parents: int32 [8], replicated, may hold values from 0 to 7, as said below
- noise: bfloat16 [704, 8, 2, 8, 683], P('lat', 'member'), may hold values from -4 to 4
Outputs:
- child_spectra: bfloat16 [704, 8, 2, 8, 683], P('lat', 'member')
- child_fourier: bfloat16 [704, 8, 2, 8, 1024], P('lat', 'member')
Inputs may be any that keep to these rules, and one draw needn't show every extreme that they name: `wave_slots`: each number below 683 stands in exactly one slot; a slot holding 683 or more is empty. `parents`: the parent of child i lies within 2 of i, and some child's parent is exactly 2 above it.
All inputs are finite; a program needn't handle non-finite values.
Results may differ from a plain program's by a relative error of at most 0.008.
Values may be sent and summed in bfloat16 or wider, within the bound.
No kernel may reach another device: no remote copies, remote signals or barrier semaphores. Data moves between devices by JAX's collectives and lax.ppermute only.
A program may use at most 128 MiB of HBM per device.

v0:
```python
import math

import jax
import jax.numpy as jnp
from jax import lax
from jax.sharding import PartitionSpec as P

NLAT = 1024
NLON = 2048
TRUNC = 683
SPREAD = 2


def extended(block, sides, width):
    for axis, dim in sides:
        count = lax.axis_size(axis)
        forward = [(i, i + 1) for i in range(count - 1)]
        backward = [(target, source) for source, target in forward]
        low = lax.ppermute(
            lax.slice_in_dim(block, block.shape[dim] - width, None, axis=dim), axis, forward
        )
        high = lax.ppermute(lax.slice_in_dim(block, 0, width, axis=dim), axis, backward)
        block = jnp.concatenate([low, block, high], axis=dim)
    return block


def zonal_table(wavenumbers):
    longitude = jnp.arange(NLON, dtype=jnp.int32)
    active = (wavenumbers < TRUNC).astype(jnp.float32)
    phase = wavenumbers[:, None] * longitude[None, :] % NLON
    angle = phase.astype(jnp.float32) * (2.0 * math.pi / NLON)
    weight = active[:, None] / math.sqrt(NLON)
    table = jnp.stack([jnp.cos(angle) * weight, -jnp.sin(angle) * weight], axis=1)
    return table.astype(jnp.bfloat16)


def meridional_table(wavenumbers):
    degree = jnp.arange(TRUNC, dtype=jnp.int32)
    latitude = jnp.arange(NLAT, dtype=jnp.int32)
    phase = degree[:, None] * (2 * latitude + 1)[None, :] % (4 * NLAT)
    angle = phase.astype(jnp.float32) * (math.pi / (2 * NLAT))
    factor = math.sqrt(2.0 / NLAT)
    even_table = (jnp.cos(angle) * factor).astype(jnp.bfloat16)
    odd_table = (jnp.sin(angle) * factor).astype(jnp.bfloat16)
    active = (degree[None, :] >= wavenumbers[:, None]) & (wavenumbers[:, None] < TRUNC)
    is_odd = (wavenumbers % 2 == 1)[:, None, None]
    table = jnp.where(is_odd, odd_table[None], even_table[None])
    return jnp.where(active[:, :, None], table, jnp.zeros((), jnp.bfloat16))


def per_device(velocity, tracer, wave_slots, parents, noise):
    lat_count = lax.axis_size("lat")
    lat_index = lax.axis_index("lat")
    group_index = lax.axis_index("member")
    mem_local, field_count, lat_local, lon_count = velocity.shape
    slots_all = wave_slots.shape[0]
    slots_here = slots_all // lat_count
    product = (velocity.astype(jnp.float32) * tracer.astype(jnp.float32)).astype(jnp.bfloat16)
    table = zonal_table(wave_slots)
    fourier = jnp.einsum(
        "sck,mflk->smcfl", table, product, preferred_element_type=jnp.float32
    ).astype(jnp.bfloat16)
    outgoing = fourier.reshape(slots_all, 1, mem_local * 2 * field_count * lat_local)
    received = lax.all_to_all(outgoing, "lat", split_axis=0, concat_axis=1, tiled=True)
    received = received.reshape(slots_here, lat_count, mem_local, 2, field_count, lat_local)
    own_waves = lax.dynamic_slice_in_dim(wave_slots, lat_index * slots_here, slots_here)
    basis = meridional_table(own_waves)
    basis_split = basis.reshape(slots_here, TRUNC, lat_count, lat_local)
    first_member = group_index * mem_local

    def forward(coefficients):
        return jnp.einsum(
            "sgmcfl,sngl->smcfn", coefficients, basis_split, preferred_element_type=jnp.float32
        ).astype(jnp.bfloat16)

    spectra = forward(received)
    spectra_wide = extended(spectra, (("member", 1),), SPREAD)
    own_parents = lax.dynamic_slice_in_dim(parents, first_member, mem_local)
    offset = own_parents - first_member + SPREAD
    columns = jnp.arange(mem_local + 2 * SPREAD, dtype=jnp.int32)
    selector = (offset[:, None] == columns[None, :]).astype(jnp.bfloat16)
    chosen = jnp.einsum(
        "ip,spcfn->sicfn", selector, spectra_wide, preferred_element_type=jnp.float32
    )
    degree = jnp.arange(TRUNC, dtype=jnp.int32)
    active = ((degree[None, :] >= own_waves[:, None]) & (own_waves[:, None] < TRUNC)).astype(
        jnp.float32
    )
    children = (chosen + noise.astype(jnp.float32) * active[:, None, None, None, :]).astype(
        jnp.bfloat16
    )
    returned = jnp.einsum(
        "sicfn,snj->sicfj", children, basis, preferred_element_type=jnp.float32
    ).astype(jnp.bfloat16)
    return (children, returned)


def solution(mesh):
    in_specs = (
        P("member", None, "lat", None),
        P("member", None, "lat", None),
        P(),
        P(),
        P("lat", "member", None, None, None),
    )
    out_specs = (P("lat", "member", None, None, None), P("lat", "member", None, None, None))
    return jax.shard_map(
        per_device, mesh=mesh, in_specs=in_specs, out_specs=out_specs, check_vma=False
    )
```

profile of v0, /device:TPU:1, one launch (start us, length us, event | category | flops | bytes accessed | tf_op | source)
XLA Modules:
  0.0 424.4 jit_solution(7668368348657858996)
XLA Ops:
  0.6 0.7 compare_select_fusion
  1.3 25.1 %multiply_convert_fusion.2 = (bf16[704,1,2048]{2,0,1:T(8,128)(2,1)S(1)}, bf16[704,1,2048]{2,0,1:T(8,128)(2,1)S(1)}) fusion(f32[704]{0:T(1024)S(1)} %compare_select_fusion, s32[704]{0:T(1024)} %param.7), kind=kLoop, calls=%fused_computation.40 | loop fusion | flops 27394048 | bytes 5772800 | tf_op jit(solution)/shard_map/convert
  26.4 15.4 %convert_bitcast_fusion = bf16[704,2,2,8,128]{4,0,2,3,1:T(8,128)(2,1)S(1)} fusion(bf16[704,1,2048]{2,0,1:T(8,128)(2,1)S(1)} %get-tuple-element.11, bf16[704,1,2048]{2,0,1:T(8,128)(2,1)S(1)} %get-tuple-element.10, bf16[2,8,128,2048]{3,2,1,0:T(8,128)(2,1)} %param.6, bf16[2,8,128,2048]{3,2,1,0:T(8,128)(2,1)} %param.5), kind=kOutput, calls=%fused_computation.38 | convolution fusion | flops 11842355200 | bytes 28311552 | tf_op jit(solution)/shard_map/sck,mflk->smcfl/dot_general | solution.py:60
  41.9 6.2 %copy.18 = bf16[704,2,2,8,128]{4,3,2,1,0:T(8,128)(2,1)} copy(bf16[704,2,2,8,128]{4,0,2,3,1:T(8,128)(2,1)S(1)} %convert_bitcast_fusion) | data formatting | bytes 11534336 | tf_op jit(solution)/shard_map/convert_element_type | solution.py:62
  48.1 31.2 %reshape.300 = bf16[704,1,4096]{2,1,0:T(2,128)(2,1)} reshape(bf16[704,2,2,8,128]{4,3,2,1,0:T(8,128)(2,1)} %copy.18) | data formatting | bytes 11534336 | tf_op jit(solution)/shard_map/reshape | solution.py:63
  79.3 0.5 broadcast.348
  79.8 37.1 %reduce = bf16[704,4096]{1,0:T(8,128)(2,1)} reduce(bf16[704,1,4096]{2,1,0:T(2,128)(2,1)} %reshape.300, bf16[]{:T(256)} %broadcast.348), dimensions={1}, to_apply=%reshape.300.reduce_sub_computation | reduce | bytes 11534338 | tf_op jit(solution)/shard_map/reshape | solution.py:63
  116.9 11.2 %reshape.302 = bf16[8,2,180224]{2,1,0:T(2,128)(2,1)} reshape(bf16[704,4096]{1,0:T(8,128)(2,1)} %reduce) | data formatting | bytes 11534336
  128.1 6.4 %all-to-all-start = ((bf16[8,2,180224]{2,1,0:T(2,128)(2,1)}), bf16[8,2,180224]{2,1,0:T(2,128)(2,1)}, u32[]{:S(2)}, u32[]{:S(2)}) async-start(bf16[8,2,180224]{2,1,0:T(2,128)(2,1)} %reshape.302), calls=%async_computation | async-start | bytes 11534336 | tf_op jit(solution)/shard_map/all_to_all | solution.py:64
  134.5 0.8 broadcast_compare_fusion
  135.3 0.1 fusion.66
  135.4 11.6 %multiply_convert_fusion.6 = (bf16[683,8,128]{2,0,1:T(8,128)(2,1)S(1)}, bf16[683,8,128]{2,0,1:T(8,128)(2,1)S(1)}) fusion(s32[8,128]{1,0:T(8,128)S(1)} %multiply_add_fusion.1), kind=kLoop, calls=%fused_computation.62 | loop fusion | flops 12589056 | bytes 2801664 | tf_op jit(solution)/shard_map/convert_element_type | solution.py:44
  147.0 113.6 %all-to-all-done = bf16[8,2,180224]{2,1,0:T(2,128)(2,1)} async-done(((bf16[8,2,180224]{2,1,0:T(2,128)(2,1)}), bf16[8,2,180224]{2,1,0:T(2,128)(2,1)}, u32[]{:S(2)}, u32[]{:S(2)}) %all-to-all-start) | async-done | bytes 5767200 | tf_op jit(solution)/shard_map/all_to_all | solution.py:64
  260.6 10.4 %reshape.303 = bf16[704,1,4096]{2,1,0:T(2,128)(2,1)} reshape(bf16[8,2,180224]{2,1,0:T(2,128)(2,1)} %all-to-all-done) | data formatting | bytes 11534336
  271.0 10.8 %copy.47 = bf16[704,1,4096]{2,0,1:T(8,128)(2,1)S(1)} copy(bf16[704,1,4096]{2,1,0:T(2,128)(2,1)} %reshape.303) | data formatting | bytes 11534336
  281.8 1.8 copy.35
  283.6 0.0 copy-start.3
  283.7 37.6 %bitcast_convert_fusion = bf16[88,2,2,8,683]{4,3,2,1,0:T(8,128)(2,1)} fusion(pred[88]{0:T(512)(128)(4,1)S(1)} %fusion.60, pred[88,683]{1,0:T(8,128)(4,1)S(1)} %get-tuple-element.17, bf16[683,8,128]{2,0,1:T(8,128)(2,1)S(1)} %get-tuple-element.15, bf16[683,8,128]{2,0,1:T(8,128)(2,1)S(1)} %get-tuple-element.14, bf16[88,8,2,2,8,128]{5,4,3,2,0,1:T(8,128)(2,1)S(1)} %bitcast.64), kind=kOutput, calls=%fused_computation.24 | convolution fusion | flops 4063992064 | bytes 12471584 | tf_op jit(solution)/shard_map/sgmcfl,sngl->smcfn/dot_general | solution.py:72
  321.3 4.8 %collective-permute-start = (bf16[88,2,2,8,683]{4,3,2,1,0:T(8,128)(2,1)}, bf16[88,2,2,8,683]{4,3,2,1,0:T(8,128)(2,1)}, u32[]{:S(2)}, u32[]{:S(2)}) collective-permute-start(bf16[88,2,2,8,683]{4,3,2,1,0:T(8,128)(2,1)} %bitcast_convert_fusion), channel_id=1, source_target_pairs={{0,8},{8,16},{16,24},{1,9},{9,17},{17,25},{2,10},{10,18},{18,26},{... | collective-permute-start | bytes 11539976 | tf_op jit(solution)/shard_map/ppermute | solution.py:19
  326.1 2.2 collective-permute-start.1
  328.4 0.0 copy-done.3
  328.4 0.1 subtract_add_fusion
  328.5 12.8 %multiply_convert_fusion.4 = (bf16[683,1024]{1,0:T(8,128)(2,1)}, bf16[683,1024]{1,0:T(8,128)(2,1)}) fusion(s32[1024]{0:T(1024)S(1)} %multiply_add_fusion), kind=kLoop, calls=%fused_computation.58 | loop fusion | flops 12589056 | bytes 2801664 | tf_op jit(solution)/shard_map/convert_element_type | solution.py:44
  341.2 32.0 %collective-permute-done = bf16[88,2,2,8,683]{4,3,2,1,0:T(8,128)(2,1)} collective-permute-done((bf16[88,2,2,8,683]{4,3,2,1,0:T(8,128)(2,1)}, bf16[88,2,2,8,683]{4,3,2,1,0:T(8,128)(2,1)}, u32[]{:S(2)}, u32[]{:S(2)}) %collective-permute-start) | collective-permute-done | bytes 3846688 | tf_op jit(solution)/shard_map/ppermute | solution.py:19
  373.3 4.4 %collective-permute-done.1 = bf16[88,2,2,8,683]{4,3,2,1,0:T(8,128)(2,1)} collective-permute-done((bf16[88,2,2,8,683]{4,3,2,1,0:T(8,128)(2,1)}, bf16[88,2,2,8,683]{4,3,2,1,0:T(8,128)(2,1)}, u32[]{:S(2)}, u32[]{:S(2)}) %collective-permute-start.1) | collective-permute-done | bytes 3846688 | tf_op jit(solution)/shard_map/ppermute | solution.py:22
  377.7 7.2 %pad_maximum_fusion = bf16[88,6,2,8,683]{4,3,2,1,0:T(8,128)(2,1)S(1)} fusion(bf16[88,2,2,8,683]{4,3,2,1,0:T(8,128)(2,1)} %collective-permute-done.1, bf16[88,2,2,8,683]{4,3,2,1,0:T(8,128)(2,1)} %bitcast_convert_fusion, bf16[88,2,2,8,683]{4,3,2,1,0:T(8,128)(2,1)} %collective-permute-done), kind=kLoop, calls=%fused_computation.21 | loop fusion | flops 11539968 | bytes 23079936 | tf_op jit(solution)/shard_map/concatenate | solution.py:23
  384.9 10.7 %fusion.20 = bf16[88,2,2,8,683]{4,1,3,2,0:T(2,128)(2,1)S(1)} fusion(bf16[88,6,2,8,683]{4,3,2,1,0:T(8,128)(2,1)S(1)} %pad_maximum_fusion, bf16[88,2,2,8,683]{4,3,2,1,0:T(8,128)(2,1)} %param.9, f32[88,683]{1,0:T(8,128)S(1)} %get-tuple-element.16, s32[2]{0:T(128)S(1)} %subtract_add_fusion), kind=kOutput, calls=%fused_computation.23 | convolution fusion | flops 30773260 | bytes 19473704 | tf_op jit(solution)/shard_map/ip,spcfn->sicfn/dot_general | solution.py:82
  395.6 0.0 copy-start.1
  395.6 0.0 copy-start.2
  395.6 1.0 copy.25
  396.6 0.0 copy-start
  396.6 0.4 copy-done.1
  396.9 0.4 copy-done.2
  397.4 27.0 %fusion.37 = bf16[88,2,2,8,1024]{4,3,2,1,0:T(8,128)(2,1)} fusion(bf16[88,2,2,8,683]{4,3,2,1,0:T(8,128)(2,1)S(1)} %copy.25, pred[88]{0:T(512)(128)(4,1)S(1)} %fusion.60, pred[88,683]{1,0:T(8,128)(4,1)S(1)} %get-tuple-element.17, bf16[683,1024]{1,0:T(8,128)(2,1)S(1)} %copy-done.2, bf16[683,1024]{1,0:T(8,128)(2,1)S(1)} %copy-done.1), kind=kOutput, calls=%fused_computation.50 | convolution fusion | flops 4064952320 | bytes 12471584 | tf_op jit(solution)/shard_map/sicfn,snj->sicfj/dot_general | solution.py:92
  424.4 0.0 copy-done
  (3 shorter events, 0.0 us)
Async XLA Ops:
  128.1 132.5 %all-to-all-start = ((bf16[8,2,180224]{2,1,0:T(2,128)(2,1)}), bf16[8,2,180224]{2,1,0:T(2,128)(2,1)}, u32[]{:S(2)}, u32[]{:S(2)}) async-start(bf16[8,2,180224]{2,1,0:T(2,128)(2,1)} %reshape.302), calls=%async_computation | async-start | bytes 11534336 | tf_op jit(solution)/shard_map/all_to_all | solution.py:64
  283.6 44.7 %copy-start.3 = (s32[8]{0:T(128)S(1)}, s32[8]{0:T(128)}, u32[]{:S(2)}) copy-start(s32[8]{0:T(128)} %param.8) | copy-start | bytes 100
  321.3 52.0 %collective-permute-start = (bf16[88,2,2,8,683]{4,3,2,1,0:T(8,128)(2,1)}, bf16[88,2,2,8,683]{4,3,2,1,0:T(8,128)(2,1)}, u32[]{:S(2)}, u32[]{:S(2)}) collective-permute-start(bf16[88,2,2,8,683]{4,3,2,1,0:T(8,128)(2,1)} %bitcast_convert_fusion), channel_id=1, source_target_pairs={{0,8},{8,16},{16,24},{1,9},{9,17},{17,25},{2,10},{10,18},{18,26},{... | collective-permute-start | bytes 11539976 | tf_op jit(solution)/shard_map/ppermute | solution.py:19
  326.1 51.5 %collective-permute-start.1 = (bf16[88,2,2,8,683]{4,3,2,1,0:T(8,128)(2,1)}, bf16[88,2,2,8,683]{4,3,2,1,0:T(8,128)(2,1)}, u32[]{:S(2)}, u32[]{:S(2)}) collective-permute-start(bf16[88,2,2,8,683]{4,3,2,1,0:T(8,128)(2,1)} %bitcast_convert_fusion), channel_id=1, source_target_pairs={{8,0},{16,8},{24,16},{9,1},{17,9},{25,17},{10,2},{18,10},{26,18},{... | collective-permute-start | bytes 11539976 | tf_op jit(solution)/shard_map/ppermute | solution.py:22
  395.6 1.4 copy-start.1
  395.6 1.8 copy-start.2
  396.6 27.8 %copy-start = (bf16[88,2,2,8,683]{4,3,2,1,0:T(8,128)(2,1)}, bf16[88,2,2,8,683]{4,3,2,1,0:T(8,128)(2,1)S(1)}, u32[]{:S(2)}) copy-start(bf16[88,2,2,8,683]{4,3,2,1,0:T(8,128)(2,1)S(1)} %copy.25) | copy-start | bytes 11539972
where the time goes:
time: 426 us; the launch traced here: 424 us
  waiting for transfers between devices  150 us (35%)
  other arithmetic  95.4 us (22%)
  matrix products  90.8 us (21%)
  local copies, waits for them, and re-layouts  73.9 us (17%)
  starting transfers between devices  13.4 us (3%)
    all_to_all x1, waiting for transfers between devices, per_device(): lax.all_to_all(outgoing, 'lat', split_axis=0, concat_axis=1, tiled=True)  114 us
    dot_general x1, matrix products, forward(): jnp.einsum('sgmcfl,sngl->smcfn', coefficients, basis_split, preferred_ele...  37.6 us
    reshape x1, other arithmetic, per_device(): fourier.reshape(slots_all, 1, mem_local * 2 * field_count * lat_local)  37.1 us
    unnamed x13, local copies, waits for them, and re-layouts  36 us
    ppermute x1, waiting for transfers between devices, extended(): lax.ppermute(lax.slice_in_dim(block, block.shape[dim] - width, None, axis...  32 us
    reshape x2, local copies, waits for them, and re-layouts, per_device(): fourier.reshape(slots_all, 1, mem_local * 2 * field_count * lat_local)  31.7 us
    dot_general x1, matrix products, per_device(): jnp.einsum('sicfn,snj->sicfj', children, basis, preferred_element_type=jn...  27 us
    another operation x1, other arithmetic  25.1 us
  transfers between devices with their start and end apart: 3, of which 3 were waited for; matrix products, arithmetic and copies ran while one was open for 6% of the time, Pallas kernels for 0%

commit v1 on v0

v1 whole, which is shorter than its diff:
```python
import functools
import math

import jax
import jax.numpy as jnp
from jax import lax
from jax.experimental import pallas as pl
from jax.experimental.pallas import tpu as pltpu
from jax.sharding import PartitionSpec as P

SPREAD = 2
VMEM_BYTES = 48 * 1024 * 1024
LANES = 128


def zonal_factors(wavenumbers, longitudes, truncation):
    coarse = jnp.arange(longitudes // LANES, dtype=jnp.int32) * LANES
    fine = jnp.arange(LANES, dtype=jnp.int32)
    weight = (wavenumbers < truncation).astype(jnp.float32) / math.sqrt(longitudes)

    def angles(points):
        phase = wavenumbers[:, None] * points[None, :] % longitudes
        return phase.astype(jnp.float32) * (2.0 * math.pi / longitudes)

    coarse_angle, fine_angle = angles(coarse), angles(fine)
    return (
        jnp.cos(coarse_angle) * weight[:, None],
        jnp.sin(coarse_angle) * weight[:, None],
        jnp.cos(fine_angle),
        jnp.sin(fine_angle),
    )


def meridional_tables(truncation, latitudes):
    degree = jnp.arange(truncation, dtype=jnp.int32)
    latitude = jnp.arange(latitudes, dtype=jnp.int32)
    phase = degree[:, None] * (2 * latitude + 1)[None, :] % (4 * latitudes)
    angle = phase.astype(jnp.float32) * (math.pi / (2 * latitudes))
    factor = math.sqrt(2.0 / latitudes)
    even_table = (jnp.cos(angle) * factor).astype(jnp.bfloat16)
    odd_table = (jnp.sin(angle) * factor).astype(jnp.bfloat16)
    return even_table, odd_table


def zonal_kernel(
    fields_step, fields, cos_c, sin_c, cos_f, sin_f, velocity, tracer, out, table, total
):
    step = pl.program_id(0)
    rows = cos_f.shape[0]
    lat_local, longitudes = velocity.shape[2:]
    out_rows = out.shape[1]

    @pl.when(step == 0)
    def _():
        cos_b, sin_b = cos_f[...], sin_f[...]
        for at in range(longitudes // LANES):
            cos_a, sin_a = cos_c[:, at : at + 1], sin_c[:, at : at + 1]
            columns = slice(at * LANES, (at + 1) * LANES)
            table[:rows, columns] = (cos_a * cos_b - sin_a * sin_b).astype(table.dtype)
            table[rows:, columns] = (-sin_a * cos_b - cos_a * sin_b).astype(table.dtype)

    product = velocity[...].astype(jnp.float32) * tracer[...].astype(jnp.float32)
    product = product.astype(jnp.bfloat16).reshape(fields_step * lat_local, longitudes)
    sums = lax.dot_general(
        table[...], product, (((1,), (1,)), ((), ())), preferred_element_type=jnp.float32
    )
    steps_per_member = fields // fields_step
    member = step // steps_per_member
    first_field = step % steps_per_member * fields_step
    for part in range(2):
        for field in range(fields_step):
            row = (member * 2 + part) * fields + first_field + field
            total[pl.ds(row, rows, stride=out_rows), :] = sums[
                part * rows : (part + 1) * rows, field * lat_local : (field + 1) * lat_local
            ]

    @pl.when(step == pl.num_programs(0) - 1)
    def _():
        out[...] = total[...].reshape(out.shape).astype(out.dtype)


def zonal_transform(factors, velocity, tracer):
    mem_local, fields, lat_local, longitudes = velocity.shape
    rows = factors[0].shape[0]
    fields_step = min(fields, max(1, 256 // lat_local))
    steps = fields // fields_step
    out_rows = mem_local * 2 * fields
    whole = lambda step: (0, 0)
    grid_block = pl.BlockSpec(
        (1, fields_step, lat_local, longitudes), lambda step: (step // steps, step % steps, 0, 0)
    )
    flops = 2 * 2 * rows * longitudes * mem_local * fields * lat_local
    moved = 2 * velocity.size * 2 + rows * out_rows * lat_local * 2
    return pl.pallas_call(
        functools.partial(zonal_kernel, fields_step, fields),
        grid=(mem_local * steps,),
        in_specs=[pl.BlockSpec(f.shape, whole) for f in factors] + [grid_block, grid_block],
        out_specs=pl.BlockSpec((rows, out_rows, lat_local), lambda step: (0, 0, 0)),
        out_shape=jax.ShapeDtypeStruct((rows, out_rows, lat_local), jnp.bfloat16),
        scratch_shapes=[
            pltpu.VMEM((2 * rows, longitudes), jnp.bfloat16),
            pltpu.VMEM((rows * out_rows, lat_local), jnp.float32),
        ],
        compiler_params=pltpu.CompilerParams(vmem_limit_bytes=VMEM_BYTES),
        cost_estimate=pl.CostEstimate(flops=flops, bytes_accessed=moved, transcendentals=0),
        name="zonal",
    )(*factors, velocity, tracer)


def forward_kernel(first, block, waves, received, even, odd, out):
    truncation = even.shape[0]
    step = pl.program_id(0)
    per_slot = received.shape[1] // block
    rows = jnp.concatenate([received[g] for g in range(received.shape[0])], axis=-1)
    contract = (((1,), (1,)), ((), ()))
    by_even = lax.dot_general(rows, even[...], contract, preferred_element_type=jnp.float32)
    by_odd = lax.dot_general(rows, odd[...], contract, preferred_element_type=jnp.float32)
    degree = lax.broadcasted_iota(jnp.int32, (per_slot, truncation), 1)
    for slot in range(block):
        wave = waves[first + step * block + slot]
        least = jnp.where(wave < truncation, wave, truncation)
        here = slice(slot * per_slot, (slot + 1) * per_slot)
        chosen = jnp.where(wave % 2 == 1, by_odd[here], by_even[here])
        chosen = jnp.where(degree >= least, chosen, 0.0)
        out[slot] = chosen.astype(out.dtype).reshape(out.shape[1:])


def forward_transform(waves, first, block, received, even, odd, mem_local):
    groups, all_rows, lat_local = received.shape
    truncation, latitudes = even.shape
    slots = all_rows // (waves[1] * mem_local)
    out_shape = (slots, mem_local, waves[1], truncation)
    per_block = block * mem_local * waves[1]
    table = pl.BlockSpec(even.shape, lambda step, w: (0, 0))
    return pl.pallas_call(
        functools.partial(forward_kernel, first, block),
        grid_spec=pltpu.PrefetchScalarGridSpec(
            num_scalar_prefetch=1,
            grid=(slots // block,),
            in_specs=[
                pl.BlockSpec((groups, per_block, lat_local), lambda step, w: (0, step, 0)),
                table,
                table,
            ],
            out_specs=pl.BlockSpec((block,) + out_shape[1:], lambda step, w: (step, 0, 0, 0)),
        ),
        out_shape=jax.ShapeDtypeStruct(out_shape, jnp.bfloat16),
        compiler_params=pltpu.CompilerParams(vmem_limit_bytes=VMEM_BYTES),
        cost_estimate=pl.CostEstimate(
            flops=4 * all_rows * truncation * latitudes,
            bytes_accessed=2 * (received.size + 2 * even.size + all_rows * truncation),
            transcendentals=0,
        ),
        name="forward",
    )(waves[0], received, even, odd)


def inverse_kernel(first, block, waves, offsets, low, own, high, noise, even, odd, *rest):
    spectra_out, fourier_out = rest[-2:]
    truncation, latitudes = even.shape
    step = pl.program_id(0)
    mem_local, parts, fields = noise.shape[1:4]
    degree = lax.broadcasted_iota(jnp.int32, (fields, truncation), 1)
    sources = [low[:, m] for m in range(low.shape[1])]
    sources += [own[:, m] for m in range(own.shape[1])]
    sources += [high[:, m] for m in range(high.shape[1])]
    even_rows, odd_rows = [], []
    parents = []
    for child in range(mem_local):
        parent = sources[0]
        for at in range(1, len(sources)):
            parent = jnp.where(offsets[child] == at, sources[at], parent)
        parents.append(parent)
    for slot in range(block):
        wave = waves[first + step * block + slot]
        least = jnp.where(wave < truncation, wave, truncation)
        is_odd = wave % 2 == 1
        active = degree >= least
        for child in range(mem_local):
            parent = parents[child][slot].astype(jnp.float32)
            parent = parent.reshape(parts, fields, truncation)
            added = jnp.where(active[None], noise[slot, child].astype(jnp.float32), 0.0)
            total = parent + added
            spectra_out[slot, child] = total.astype(spectra_out.dtype)
            rows = total.reshape(parts * fields, truncation)
            even_rows.append(jnp.where(is_odd, 0.0, rows).astype(jnp.bfloat16))
            odd_rows.append(jnp.where(is_odd, rows, 0.0).astype(jnp.bfloat16))
    result = jnp.dot(
        jnp.concatenate(even_rows, axis=0), even[...], preferred_element_type=jnp.float32
    )
    result += jnp.dot(
        jnp.concatenate(odd_rows, axis=0), odd[...], preferred_element_type=jnp.float32
    )
    fourier_out[...] = result.reshape(fourier_out.shape).astype(fourier_out.dtype)


def inverse_transform(waves, offsets, first, block, low, own, high, noise, even, odd, outs):
    slots_all, mem_local, parts, fields, truncation = noise.shape
    latitudes = even.shape[1]
    slots = own.shape[0]
    at = first // block
    near = lambda step, w, o: (step, 0, 0, 0)
    far = lambda step, w, o: (at + step, 0, 0, 0, 0)
    table = pl.BlockSpec(even.shape, lambda step, w, o: (0, 0))
    noise_block = pl.BlockSpec((block,) + noise.shape[1:], far)
    fourier_shape = noise.shape[:4] + (latitudes,)
    fourier_block = pl.BlockSpec((block,) + fourier_shape[1:], far)
    operands = [low, own, high, noise, even, odd]
    in_specs = [pl.BlockSpec((block,) + a.shape[1:], near) for a in operands[:3]]
    in_specs += [noise_block, table, table]
    aliases = {}
    if outs is not None:
        aliases = {8: 0, 9: 1}
        operands += list(outs)
        in_specs += [pl.BlockSpec(memory_space=pl.ANY)] * 2
    rows = slots * mem_local * parts * fields
    return pl.pallas_call(
        functools.partial(inverse_kernel, first, block),
        grid_spec=pltpu.PrefetchScalarGridSpec(
            num_scalar_prefetch=2,
            grid=(slots // block,),
            in_specs=in_specs,
            out_specs=[noise_block, fourier_block],
        ),
        out_shape=[
            jax.ShapeDtypeStruct(noise.shape, jnp.bfloat16),
            jax.ShapeDtypeStruct(fourier_shape, jnp.bfloat16),
        ],
        input_output_aliases=aliases,
        compiler_params=pltpu.CompilerParams(vmem_limit_bytes=VMEM_BYTES),
        cost_estimate=pl.CostEstimate(
            flops=4 * rows * truncation * latitudes,
            bytes_accessed=2 * rows * (5 * truncation + latitudes) + 4 * even.size,
            transcendentals=0,
        ),
        name="inverse",
    )(waves, offsets, *operands)


def chunk_bounds(slots_here, block):
    blocks = slots_here // block
    count = min(4, blocks)
    edges = [blocks * at // count * block for at in range(count + 1)]
    return list(zip(edges[:-1], edges[1:]))


def per_device(velocity, tracer, wave_slots, parents, noise):
    lat_count = lax.axis_size("lat")
    lat_index = lax.axis_index("lat")
    mem_count = lax.axis_size("member")
    group_index = lax.axis_index("member")
    mem_local, fields, lat_local, longitudes = velocity.shape
    slots_here, truncation = noise.shape[0], noise.shape[-1]
    block = math.gcd(slots_here, 8)
    per_slot = mem_local * 2 * fields
    latitudes = lat_count * lat_local
    own_waves = lax.dynamic_slice_in_dim(wave_slots, lat_index * slots_here, slots_here)
    first_member = group_index * mem_local
    own_parents = lax.dynamic_slice_in_dim(parents, first_member, mem_local)
    offsets = own_parents - first_member + SPREAD
    even, odd = meridional_tables(truncation, latitudes)
    upward = [(i, i + 1) for i in range(mem_count - 1)]
    downward = [(target, source) for source, target in upward]
    slot_grid = wave_slots.reshape(lat_count, slots_here)
    outs = None
    for start, stop in chunk_bounds(slots_here, block):
        slots = stop - start
        factors = zonal_factors(slot_grid[:, start:stop].reshape(-1), longitudes, truncation)
        outgoing = zonal_transform(factors, velocity, tracer)
        outgoing = outgoing.reshape(lat_count, slots * per_slot, lat_local)
        received = lax.all_to_all(outgoing, "lat", split_axis=0, concat_axis=0, tiled=True)
        if lat_local % LANES != 0:
            received = jnp.swapaxes(received, 0, 1).reshape(1, slots * per_slot, latitudes)
        own = forward_transform(
            (own_waves, 2 * fields), start, block, received, even, odd, mem_local
        )
        low = lax.ppermute(own[:, mem_local - SPREAD :], "member", upward)
        high = lax.ppermute(own[:, :SPREAD], "member", downward)
        outs = inverse_transform(
            own_waves, offsets, start, block, low, own, high, noise, even, odd, outs
        )
    return tuple(outs)


def solution(mesh):
    in_specs = (
        P("member", None, "lat", None),
        P("member", None, "lat", None),
        P(),
        P(),
        P("lat", "member", None, None, None),
    )
    out_specs = (P("lat", "member", None, None, None), P("lat", "member", None, None, None))
    return jax.shard_map(
        per_device, mesh=mesh, in_specs=in_specs, out_specs=out_specs, check_vma=False
    )
```

time: 426 us -> 222 us (0.52)
  Pallas kernels: 0 us -> 96.2 us
  waiting for transfers between devices: 150 us -> 57.8 us
  matrix products: 90.8 us -> 0 us
  other arithmetic: 95.4 us -> 14.9 us
  local copies, waits for them, and re-layouts: 73.9 us -> 7.25 us
  starting transfers between devices: 13.4 us -> 43.2 us
    pallas_call x0 -> x12, Pallas kernels: none -> 96.2 us  [the longest x4 52.1 us: zonal_transform(): pl.pallas_call(functools.partial(zonal_kernel, fields_step, fields), grid...]
    dot_general x4 -> x0, matrix products: 90.8 us -> none  [the longest x1 37.6 us: forward(): jnp.einsum('sgmcfl,sngl->smcfn', coefficients, basis_split, preferred_ele...]
    all_to_all x1 -> x4, waiting for transfers between devices: 114 us -> 53.8 us  [per_device(): lax.all_to_all(outgoing, 'lat', split_axis=0, concat_axis=0, tiled=True)]
    reshape x1 -> x0, other arithmetic: 37.1 us -> none  [per_device(): fourier.reshape(slots_all, 1, mem_local * 2 * field_count * lat_local)]
    ppermute x2 -> x8, waiting for transfers between devices: 36.4 us -> 4.08 us  [the longest x4 3.81 us: per_device(): low = lax.ppermute(own[:, mem_local - SPREAD:], 'member', upward)]
    unnamed x13 -> x20, local copies, waits for them, and re-layouts: 36 us -> 4.93 us
    reshape x2 -> x1, local copies, waits for them, and re-layouts: 31.7 us -> 0.76 us  [per_device(): slot_grid = wave_slots.reshape(lat_count, slots_here)]
    another operation x1 -> x0, other arithmetic: 25.1 us -> none
  transfers between devices with their start and end apart: 3 -> 12, of which waited for: 3 -> 5; matrix products, arithmetic and copies ran while one was open for 6% -> 7% of each run, Pallas kernels for 0% -> 35%
where the time goes in v1:
time: 222 us; the launch traced here: 220 us
  Pallas kernels  96.2 us (43%)
  waiting for transfers between devices  57.8 us (26%)
  starting transfers between devices  43.2 us (19%)
  other arithmetic  14.9 us (7%)
  local copies, waits for them, and re-layouts  7.25 us (3%)
    all_to_all x4, waiting for transfers between devices, per_device(): lax.all_to_all(outgoing, 'lat', split_axis=0, concat_axis=0, tiled=True)  53.8 us
    pallas_call x4, Pallas kernels, zonal_transform(): pl.pallas_call(functools.partial(zonal_kernel, fields_step, fields), grid...  52.1 us
    pallas_call x4, Pallas kernels, inverse_transform(): pl.pallas_call(functools.partial(inverse_kernel, first, block), grid_spec...  26 us
    all_to_all x4, starting transfers between devices, per_device(): lax.all_to_all(outgoing, 'lat', split_axis=0, concat_axis=0, tiled=True)  20.3 us
    pallas_call x4, Pallas kernels, forward_transform(): pl.pallas_call(functools.partial(forward_kernel, first, block), grid_spec...  18 us
    ppermute x4, starting transfers between devices, per_device(): low = lax.ppermute(own[:, mem_local - SPREAD:], 'member', upward)  14.7 us
    convert_element_type x1, other arithmetic, meridional_tables(): odd_table = (jnp.sin(angle) * factor).astype(jnp.bfloat16)  11.6 us
    ppermute x4, starting transfers between devices, per_device(): high = lax.ppermute(own[:, :SPREAD], 'member', downward)  8.21 us
  transfers between devices with their start and end apart: 12, of which 5 were waited for; matrix products, arithmetic and copies ran while one was open for 7% of the time, Pallas kernels for 35%

profile of v1, /device:TPU:1, one launch (start us, length us, event | category | flops | bytes accessed | tf_op | source)
XLA Modules:
  0.0 220.3 jit_solution(3975989805274556891)
XLA Ops:
  0.6 0.8 reshape.60
  1.5 0.3 fusion.36
  1.9 0.1 copy.16
  2.0 0.2 sine_multiply_fusion.3
  2.3 11.9 %zonal.7 = bf16[128,32,128]{2,1,0:T(8,128)(2,1)} custom-call(f32[128,16]{1,0:T(8,128)S(1)} %get-tuple-element.21.cos_c, f32[128,16]{1,0:T(8,128)S(1)} %get-tuple-element.20.sin_c, f32[128,128]{1,0:T(8,128)S(1)} %get-tuple-element.34.cos_f, f32[128,128]{1,0:T(8,128)S(1)} %get-tuple-element.33.sin_f, bf16[2,8,128,2048]{3,2,1,0:T(8,128)(2,1)} %velocity.7, ...), custom_call_target="tpu_custom_call" | custom-call | flops 2147483648 | bytes 17825792 | tf_op jit(solution)/shard_map/zonal/pallas_call | solution.py:94
  14.1 6.4 %all-to-all-start.3 = ((bf16[8,512,128]{2,1,0:T(8,128)(2,1)}), bf16[8,512,128]{2,1,0:T(8,128)(2,1)S(1)}, u32[]{:S(2)}, u32[]{:S(2)}) async-start(bf16[8,512,128]{2,1,0:T(8,128)(2,1)} %bitcast.3), calls=%async_computation.3 | async-start | bytes 2097152 | tf_op jit(solution)/shard_map/all_to_all | solution.py:271
  20.8 0.1 fusion.40
  20.9 0.1 copy.15
  21.0 0.5 fusion.30
  21.5 0.4 sine_multiply_fusion
  21.9 13.4 %zonal.6 = bf16[192,32,128]{2,1,0:T(8,128)(2,1)} custom-call(f32[192,16]{1,0:T(8,128)S(1)} %get-tuple-element.15.cos_c, f32[192,16]{1,0:T(8,128)S(1)} %get-tuple-element.14.sin_c, f32[192,128]{1,0:T(8,128)S(1)} %get-tuple-element.28.cos_f, f32[192,128]{1,0:T(8,128)S(1)} %get-tuple-element.27.sin_f, bf16[2,8,128,2048]{3,2,1,0:T(8,128)(2,1)} %velocity.7, ...), custom_call_target="tpu_custom_call" | custom-call | flops 3221225472 | bytes 18350080 | tf_op jit(solution)/shard_map/zonal/pallas_call | solution.py:94
  35.3 9.8 %all-to-all-done.3.received = bf16[8,512,128]{2,1,0:T(8,128)(2,1)S(1)} async-done(((bf16[8,512,128]{2,1,0:T(8,128)(2,1)}), bf16[8,512,128]{2,1,0:T(8,128)(2,1)S(1)}, u32[]{:S(2)}, u32[]{:S(2)}) %all-to-all-start.3) | async-done | bytes 1048608 | tf_op jit(solution)/shard_map/all_to_all | solution.py:271
  45.1 1.0 copy-done.5
  46.1 4.9 %all-to-all-start.2 = ((bf16[8,768,128]{2,1,0:T(8,128)(2,1)}), bf16[8,768,128]{2,1,0:T(8,128)(2,1)S(1)}, u32[]{:S(2)}, u32[]{:S(2)}) async-start(bf16[8,768,128]{2,1,0:T(8,128)(2,1)} %bitcast.2), calls=%async_computation.2 | async-start | bytes 3145728 | tf_op jit(solution)/shard_map/all_to_all | solution.py:271
  51.1 0.5 fusion.32
  51.6 0.4 sine_multiply_fusion.1
  52.0 13.4 %zonal.5 = bf16[192,32,128]{2,1,0:T(8,128)(2,1)} custom-call(f32[192,16]{1,0:T(8,128)S(1)} %get-tuple-element.17.cos_c, f32[192,16]{1,0:T(8,128)S(1)} %get-tuple-element.16.sin_c, f32[192,128]{1,0:T(8,128)S(1)} %get-tuple-element.30.cos_f, f32[192,128]{1,0:T(8,128)S(1)} %get-tuple-element.29.sin_f, bf16[2,8,128,2048]{3,2,1,0:T(8,128)(2,1)} %velocity.7, ...), custom_call_target="tpu_custom_call" | custom-call | flops 3221225472 | bytes 18350080 | tf_op jit(solution)/shard_map/zonal/pallas_call | solution.py:94
  65.4 22.0 %all-to-all-done.2.received = bf16[8,768,128]{2,1,0:T(8,128)(2,1)S(1)} async-done(((bf16[8,768,128]{2,1,0:T(8,128)(2,1)}), bf16[8,768,128]{2,1,0:T(8,128)(2,1)S(1)}, u32[]{:S(2)}, u32[]{:S(2)}) %all-to-all-start.2) | async-done | bytes 1572896 | tf_op jit(solution)/shard_map/all_to_all | solution.py:271
  87.4 4.5 %all-to-all-start.1 = ((bf16[8,768,128]{2,1,0:T(8,128)(2,1)}), bf16[8,768,128]{2,1,0:T(8,128)(2,1)S(1)}, u32[]{:S(2)}, u32[]{:S(2)}) async-start(bf16[8,768,128]{2,1,0:T(8,128)(2,1)} %bitcast.1), calls=%async_computation.1 | async-start | bytes 3145728 | tf_op jit(solution)/shard_map/all_to_all | solution.py:271
  91.9 0.1 copy.13
  92.0 0.5 fusion.34
  92.4 0.4 sine_multiply_fusion.2
  92.8 13.4 %zonal.4 = bf16[192,32,128]{2,1,0:T(8,128)(2,1)} custom-call(f32[192,16]{1,0:T(8,128)S(1)} %get-tuple-element.19.cos_c, f32[192,16]{1,0:T(8,128)S(1)} %get-tuple-element.18.sin_c, f32[192,128]{1,0:T(8,128)S(1)} %get-tuple-element.32.cos_f, f32[192,128]{1,0:T(8,128)S(1)} %get-tuple-element.31.sin_f, bf16[2,8,128,2048]{3,2,1,0:T(8,128)(2,1)} %velocity.7, ...), custom_call_target="tpu_custom_call" | custom-call | flops 3221225472 | bytes 18350080 | tf_op jit(solution)/shard_map/zonal/pallas_call | solution.py:94
  106.2 22.0 %all-to-all-done.1.received = bf16[8,768,128]{2,1,0:T(8,128)(2,1)S(1)} async-done(((bf16[8,768,128]{2,1,0:T(8,128)(2,1)}), bf16[8,768,128]{2,1,0:T(8,128)(2,1)S(1)}, u32[]{:S(2)}, u32[]{:S(2)}) %all-to-all-start.1) | async-done | bytes 1572896 | tf_op jit(solution)/shard_map/all_to_all | solution.py:271
  128.2 4.5 %all-to-all-start = ((bf16[8,768,128]{2,1,0:T(8,128)(2,1)}), bf16[8,768,128]{2,1,0:T(8,128)(2,1)}, u32[]{:S(2)}, u32[]{:S(2)}) async-start(bf16[8,768,128]{2,1,0:T(8,128)(2,1)} %bitcast), calls=%async_computation | async-start | bytes 3145728 | tf_op jit(solution)/shard_map/all_to_all | solution.py:271
  132.7 0.8 dynamic_slice.6.waves
  133.5 11.6 %multiply_convert_fusion = (bf16[683,1024]{1,0:T(8,128)(2,1)S(1)}, bf16[683,1024]{1,0:T(8,128)(2,1)S(1)}) fusion(s32[1024]{0:T(1024)S(1)} %multiply_add_fusion), kind=kLoop, calls=%fused_computation.6 | loop fusion | flops 12589056 | bytes 2801664 | tf_op jit(solution)/shard_map/convert_element_type | solution.py:41
  145.1 1.9 copy-done.2
  147.0 4.5 %forward.6.own = bf16[24,2,16,683]{3,2,1,0:T(8,128)(2,1)} custom-call(s32[88]{0:T(128)S(1)} %dynamic_slice.6.waves, bf16[8,768,128]{2,1,0:T(8,128)(2,1)S(1)} %copy-done.2, bf16[683,1024]{1,0:T(8,128)(2,1)S(1)} %get-tuple-element.26.even, bf16[683,1024]{1,0:T(8,128)(2,1)S(1)} %get-tuple-element.25.odd), custom_call_target="tpu_custom_call" | custom-call | flops 2148532224 | bytes 5419520 | tf_op jit(solution)/shard_map/forward/pallas_call | solution.py:135
  151.5 4.7 %collective-permute-start.4 = (bf16[24,2,16,683]{3,2,1,0:T(8,128)(2,1)}, bf16[24,2,16,683]{3,2,1,0:T(8,128)(2,1)}, u32[]{:S(2)}, u32[]{:S(2)}) collective-permute-start(bf16[24,2,16,683]{3,2,1,0:T(8,128)(2,1)} %forward.6.own), channel_id=1, source_target_pairs={{0,8},{8,16},{16,24},{1,9},{9,17},{17,25},{2,10},{10,18},{18,26},{... | collective-permute-start | bytes 3147272 | tf_op jit(solution)/shard_map/ppermute | solution.py:277
  156.2 3.5 %forward.7.own = bf16[16,2,16,683]{3,2,1,0:T(8,128)(2,1)} custom-call(s32[88]{0:T(128)S(1)} %dynamic_slice.6.waves, bf16[8,512,128]{2,1,0:T(8,128)(2,1)S(1)} %copy-done.6, bf16[683,1024]{1,0:T(8,128)(2,1)S(1)} %get-tuple-element.26.even, bf16[683,1024]{1,0:T(8,128)(2,1)S(1)} %get-tuple-element.25.odd), custom_call_target="tpu_custom_call" | custom-call | flops 1432354816 | bytes 4545536 | tf_op jit(solution)/shard_map/forward/pallas_call | solution.py:135
  159.7 1.9 collective-permute-start.6
  161.6 2.5 %collective-permute-start.7 = (bf16[16,2,16,683]{3,2,1,0:T(8,128)(2,1)}, bf16[16,2,16,683]{3,2,1,0:T(8,128)(2,1)}, u32[]{:S(2)}, u32[]{:S(2)}) collective-permute-start(bf16[16,2,16,683]{3,2,1,0:T(8,128)(2,1)} %forward.7.own), channel_id=1, source_target_pairs={{8,0},{16,8},{24,16},{9,1},{17,9},{25,17},{10,2},{18,10},{26,18},{... | collective-permute-start | bytes 2098184 | tf_op jit(solution)/shard_map/ppermute | solution.py:278
  164.1 1.9 collective-permute-start.5
  166.0 4.5 %forward.5.own = bf16[24,2,16,683]{3,2,1,0:T(8,128)(2,1)} custom-call(s32[88]{0:T(128)S(1)} %dynamic_slice.6.waves, bf16[8,768,128]{2,1,0:T(8,128)(2,1)S(1)} %copy-done.4, bf16[683,1024]{1,0:T(8,128)(2,1)S(1)} %get-tuple-element.26.even, bf16[683,1024]{1,0:T(8,128)(2,1)S(1)} %get-tuple-element.25.odd), custom_call_target="tpu_custom_call" | custom-call | flops 2148532224 | bytes 5419520 | tf_op jit(solution)/shard_map/forward/pallas_call | solution.py:135
  170.5 3.8 %collective-permute-start.2 = (bf16[24,2,16,683]{3,2,1,0:T(8,128)(2,1)}, bf16[24,2,16,683]{3,2,1,0:T(8,128)(2,1)}, u32[]{:S(2)}, u32[]{:S(2)}) collective-permute-start(bf16[24,2,16,683]{3,2,1,0:T(8,128)(2,1)} %forward.5.own), channel_id=1, source_target_pairs={{0,8},{8,16},{16,24},{1,9},{9,17},{17,25},{2,10},{10,18},{18,26},{... | collective-permute-start | bytes 3147272 | tf_op jit(solution)/shard_map/ppermute | solution.py:277
  174.3 3.8 %collective-permute-done.6.low = bf16[16,2,16,683]{3,2,1,0:T(8,128)(2,1)S(1)} collective-permute-done((bf16[16,2,16,683]{3,2,1,0:T(8,128)(2,1)}, bf16[16,2,16,683]{3,2,1,0:T(8,128)(2,1)S(1)}, u32[]{:S(2)}, u32[]{:S(2)}) %collective-permute-start.6) | collective-permute-done | bytes 699424 | tf_op jit(solution)/shard_map/ppermute | solution.py:277
  178.1 0.9 copy-done.7
  179.0 1.9 collective-permute-start.3
  180.9 5.6 %forward.4.own = bf16[24,2,16,683]{3,2,1,0:T(8,128)(2,1)} custom-call(s32[88]{0:T(128)S(1)} %dynamic_slice.6.waves, bf16[8,768,128]{2,1,0:T(8,128)(2,1)} %all-to-all-done.received, bf16[683,1024]{1,0:T(8,128)(2,1)S(1)} %get-tuple-element.26.even, bf16[683,1024]{1,0:T(8,128)(2,1)S(1)} %get-tuple-element.25.odd), custom_call_target="tpu_custom_call" | custom-call | flops 2148532224 | bytes 5419520 | tf_op jit(solution)/shard_map/forward/pallas_call | solution.py:135
  186.5 4.3 %collective-permute-start = (bf16[24,2,16,683]{3,2,1,0:T(8,128)(2,1)}, bf16[24,2,16,683]{3,2,1,0:T(8,128)(2,1)}, u32[]{:S(2)}, u32[]{:S(2)}) collective-permute-start(bf16[24,2,16,683]{3,2,1,0:T(8,128)(2,1)} %forward.4.own), channel_id=1, source_target_pairs={{0,8},{8,16},{16,24},{1,9},{9,17},{17,25},{2,10},{10,18},{18,26},{... | collective-permute-start | bytes 3147272 | tf_op jit(solution)/shard_map/ppermute | solution.py:277
  190.8 1.9 collective-permute-start.1
  192.8 1.1 copy-done.8
  193.9 4.7 %inverse.4 = (bf16[88,2,2,8,683]{4,3,2,1,0:T(8,128)(2,1)}, bf16[88,2,2,8,1024]{4,3,2,1,0:T(8,128)(2,1)}) custom-call(s32[88]{0:T(128)S(1)} %dynamic_slice.6.waves, s32[2]{0:T(128)S(1)} %subtract_add_fusion.offsets, bf16[16,2,16,683]{3,2,1,0:T(8,128)(2,1)S(1)} %copy-done.8, bf16[16,2,16,683]{3,2,1,0:T(8,128)(2,1)} %forward.7.own, ...), custom_call_target="tpu_custom_call" | custom-call | flops 1432354816 | bytes 7343104 | tf_op jit(solution)/shard_map/inverse/pallas_call | solution.py:217
  198.7 7.1 %inverse.5 = (bf16[88,2,2,8,683]{4,3,2,1,0:T(8,128)(2,1)}, bf16[88,2,2,8,1024]{4,3,2,1,0:T(8,128)(2,1)}) custom-call(s32[88]{0:T(128)S(1)} %dynamic_slice.6.waves, s32[2]{0:T(128)S(1)} %subtract_add_fusion.offsets, bf16[24,2,16,683]{3,2,1,0:T(8,128)(2,1)} %collective-permute-done.4.low, ...), custom_call_target="tpu_custom_call", output_to_operand_aliasing={{0}: (8, {}), {1}: (9, {})} | custom-call | flops 2148532224 | bytes 9615872 | tf_op jit(solution)/shard_map/inverse/pallas_call | solution.py:217
  205.8 7.1 %inverse.6 = (bf16[88,2,2,8,683]{4,3,2,1,0:T(8,128)(2,1)}, bf16[88,2,2,8,1024]{4,3,2,1,0:T(8,128)(2,1)}) custom-call(s32[88]{0:T(128)S(1)} %dynamic_slice.6.waves, s32[2]{0:T(128)S(1)} %subtract_add_fusion.offsets, bf16[24,2,16,683]{3,2,1,0:T(8,128)(2,1)} %collective-permute-done.2.low, ...), custom_call_target="tpu_custom_call", output_to_operand_aliasing={{0}: (8, {}), {1}: (9, {})} | custom-call | flops 2148532224 | bytes 9615872 | tf_op jit(solution)/shard_map/inverse/pallas_call | solution.py:217
  212.9 0.3 collective-permute-done.1.high
  213.2 7.1 %inverse.7 = (bf16[88,2,2,8,683]{4,3,2,1,0:T(8,128)(2,1)}, bf16[88,2,2,8,1024]{4,3,2,1,0:T(8,128)(2,1)}) custom-call(s32[88]{0:T(128)S(1)} %dynamic_slice.6.waves, s32[2]{0:T(128)S(1)} %subtract_add_fusion.offsets, bf16[24,2,16,683]{3,2,1,0:T(8,128)(2,1)} %collective-permute-done.low, ...), custom_call_target="tpu_custom_call", output_to_operand_aliasing={{0}: (8, {}), {1}: (9, {})} | custom-call | flops 2148532224 | bytes 9615872 | tf_op jit(solution)/shard_map/inverse/pallas_call | solution.py:217
  (37 shorter events, 0.7 us)
Async XLA Ops:
  14.1 31.0 %all-to-all-start.3 = ((bf16[8,512,128]{2,1,0:T(8,128)(2,1)}), bf16[8,512,128]{2,1,0:T(8,128)(2,1)S(1)}, u32[]{:S(2)}, u32[]{:S(2)}) async-start(bf16[8,512,128]{2,1,0:T(8,128)(2,1)} %bitcast.3), calls=%async_computation.3 | async-start | bytes 2097152 | tf_op jit(solution)/shard_map/all_to_all | solution.py:271
  45.1 1.0 copy-start.5
  46.1 41.3 %all-to-all-start.2 = ((bf16[8,768,128]{2,1,0:T(8,128)(2,1)}), bf16[8,768,128]{2,1,0:T(8,128)(2,1)S(1)}, u32[]{:S(2)}, u32[]{:S(2)}) async-start(bf16[8,768,128]{2,1,0:T(8,128)(2,1)} %bitcast.2), calls=%async_computation.2 | async-start | bytes 3145728 | tf_op jit(solution)/shard_map/all_to_all | solution.py:271
  87.4 18.9 %copy-start.1 = (bf16[8,768,128]{2,1,0:T(8,128)(2,1)}, bf16[8,768,128]{2,1,0:T(8,128)(2,1)S(1)}, u32[]{:S(2)}) copy-start(bf16[8,768,128]{2,1,0:T(8,128)(2,1)S(1)} %all-to-all-done.2.received) | copy-start | bytes 4718596
  87.4 40.8 %all-to-all-start.1 = ((bf16[8,768,128]{2,1,0:T(8,128)(2,1)}), bf16[8,768,128]{2,1,0:T(8,128)(2,1)S(1)}, u32[]{:S(2)}, u32[]{:S(2)}) async-start(bf16[8,768,128]{2,1,0:T(8,128)(2,1)} %bitcast.1), calls=%async_computation.1 | async-start | bytes 3145728 | tf_op jit(solution)/shard_map/all_to_all | solution.py:271
  128.2 5.3 %copy-start.3 = (bf16[8,768,128]{2,1,0:T(8,128)(2,1)}, bf16[8,768,128]{2,1,0:T(8,128)(2,1)S(1)}, u32[]{:S(2)}) copy-start(bf16[8,768,128]{2,1,0:T(8,128)(2,1)S(1)} %all-to-all-done.1.received) | copy-start | bytes 4718596
  128.2 52.7 %all-to-all-start = ((bf16[8,768,128]{2,1,0:T(8,128)(2,1)}), bf16[8,768,128]{2,1,0:T(8,128)(2,1)}, u32[]{:S(2)}, u32[]{:S(2)}) async-start(bf16[8,768,128]{2,1,0:T(8,128)(2,1)} %bitcast), calls=%async_computation | async-start | bytes 3145728 | tf_op jit(solution)/shard_map/all_to_all | solution.py:271
  145.0 47.8 %copy-start = (bf16[683,1024]{1,0:T(8,128)(2,1)}, bf16[683,1024]{1,0:T(8,128)(2,1)S(1)}, u32[]{:S(2)}) copy-start(bf16[683,1024]{1,0:T(8,128)(2,1)S(1)} %get-tuple-element.25.odd) | copy-start | bytes 4196356
  145.0 1.9 copy-start.2
  147.0 9.3 %copy-start.6 = (bf16[8,512,128]{2,1,0:T(8,128)(2,1)S(1)}, bf16[8,512,128]{2,1,0:T(8,128)(2,1)}, u32[]{:S(2)}) copy-start(bf16[8,512,128]{2,1,0:T(8,128)(2,1)} %copy-done.5) | copy-start | bytes 3145732
  151.5 14.5 %copy-start.4 = (bf16[8,768,128]{2,1,0:T(8,128)(2,1)S(1)}, bf16[8,768,128]{2,1,0:T(8,128)(2,1)}, u32[]{:S(2)}) copy-start(bf16[8,768,128]{2,1,0:T(8,128)(2,1)} %copy-done.3) | copy-start | bytes 4718596
  151.5 39.3 %collective-permute-start.4 = (bf16[24,2,16,683]{3,2,1,0:T(8,128)(2,1)}, bf16[24,2,16,683]{3,2,1,0:T(8,128)(2,1)}, u32[]{:S(2)}, u32[]{:S(2)}) collective-permute-start(bf16[24,2,16,683]{3,2,1,0:T(8,128)(2,1)} %forward.6.own), channel_id=1, source_target_pairs={{0,8},{8,16},{16,24},{1,9},{9,17},{17,25},{2,10},{10,18},{18,26},{... | collective-permute-start | bytes 3147272 | tf_op jit(solution)/shard_map/ppermute | solution.py:277
  159.7 18.4 %collective-permute-start.6 = (bf16[16,2,16,683]{3,2,1,0:T(8,128)(2,1)}, bf16[16,2,16,683]{3,2,1,0:T(8,128)(2,1)S(1)}, u32[]{:S(2)}, u32[]{:S(2)}) collective-permute-start(bf16[16,2,16,683]{3,2,1,0:T(8,128)(2,1)} %forward.7.own), channel_id=1, source_target_pairs={{0,8},{8,16},{16,24},{1,9},{9,17},{17,25},{2,10},{10,18},{18,26},{... | collective-permute-start | bytes 2098184 | tf_op jit(solution)/shard_map/ppermute | solution.py:277
  161.6 24.9 %collective-permute-start.7 = (bf16[16,2,16,683]{3,2,1,0:T(8,128)(2,1)}, bf16[16,2,16,683]{3,2,1,0:T(8,128)(2,1)}, u32[]{:S(2)}, u32[]{:S(2)}) collective-permute-start(bf16[16,2,16,683]{3,2,1,0:T(8,128)(2,1)} %forward.7.own), channel_id=1, source_target_pairs={{8,0},{16,8},{24,16},{9,1},{17,9},{25,17},{10,2},{18,10},{26,18},{... | collective-permute-start | bytes 2098184 | tf_op jit(solution)/shard_map/ppermute | solution.py:278
  164.1 34.6 %collective-permute-start.5 = (bf16[24,2,16,683]{3,2,1,0:T(8,128)(2,1)}, bf16[24,2,16,683]{3,2,1,0:T(8,128)(2,1)}, u32[]{:S(2)}, u32[]{:S(2)}) collective-permute-start(bf16[24,2,16,683]{3,2,1,0:T(8,128)(2,1)} %forward.6.own), channel_id=1, source_target_pairs={{8,0},{16,8},{24,16},{9,1},{17,9},{25,17},{10,2},{18,10},{26,18},{... | collective-permute-start | bytes 3147272 | tf_op jit(solution)/shard_map/ppermute | solution.py:278
  170.5 22.2 %copy-start.9 = (s32[8]{0:T(128)S(1)}, s32[8]{0:T(128)}, u32[]{:S(2)}) copy-start(s32[8]{0:T(128)} %param.8) | copy-start | bytes 100
  170.5 35.2 %collective-permute-start.2 = (bf16[24,2,16,683]{3,2,1,0:T(8,128)(2,1)}, bf16[24,2,16,683]{3,2,1,0:T(8,128)(2,1)}, u32[]{:S(2)}, u32[]{:S(2)}) collective-permute-start(bf16[24,2,16,683]{3,2,1,0:T(8,128)(2,1)} %forward.5.own), channel_id=1, source_target_pairs={{0,8},{8,16},{16,24},{1,9},{9,17},{17,25},{2,10},{10,18},{18,26},{... | collective-permute-start | bytes 3147272 | tf_op jit(solution)/shard_map/ppermute | solution.py:277
  178.1 0.9 copy-start.7
  179.0 26.8 %collective-permute-start.3 = (bf16[24,2,16,683]{3,2,1,0:T(8,128)(2,1)}, bf16[24,2,16,683]{3,2,1,0:T(8,128)(2,1)}, u32[]{:S(2)}, u32[]{:S(2)}) collective-permute-start(bf16[24,2,16,683]{3,2,1,0:T(8,128)(2,1)} %forward.5.own), channel_id=1, source_target_pairs={{8,0},{16,8},{24,16},{9,1},{17,9},{25,17},{10,2},{18,10},{26,18},{... | collective-permute-start | bytes 3147272 | tf_op jit(solution)/shard_map/ppermute | solution.py:278
  186.5 26.4 %collective-permute-start = (bf16[24,2,16,683]{3,2,1,0:T(8,128)(2,1)}, bf16[24,2,16,683]{3,2,1,0:T(8,128)(2,1)}, u32[]{:S(2)}, u32[]{:S(2)}) collective-permute-start(bf16[24,2,16,683]{3,2,1,0:T(8,128)(2,1)} %forward.4.own), channel_id=1, source_target_pairs={{0,8},{8,16},{16,24},{1,9},{9,17},{17,25},{2,10},{10,18},{18,26},{... | collective-permute-start | bytes 3147272 | tf_op jit(solution)/shard_map/ppermute | solution.py:277
  190.8 22.4 %collective-permute-start.1 = (bf16[24,2,16,683]{3,2,1,0:T(8,128)(2,1)}, bf16[24,2,16,683]{3,2,1,0:T(8,128)(2,1)}, u32[]{:S(2)}, u32[]{:S(2)}) collective-permute-start(bf16[24,2,16,683]{3,2,1,0:T(8,128)(2,1)} %forward.4.own), channel_id=1, source_target_pairs={{8,0},{16,8},{24,16},{9,1},{17,9},{25,17},{10,2},{18,10},{26,18},{... | collective-permute-start | bytes 3147272 | tf_op jit(solution)/shard_map/ppermute | solution.py:278
  192.8 1.1 copy-start.8

commit v2 on v1

--- a/solution.py
+++ b/solution.py
@@ -11,6 +11,7 @@
 SPREAD = 2
 VMEM_BYTES = 48 * 1024 * 1024
 LANES = 128
+TOKEN = (8, 128)
 
 
 def zonal_factors(wavenumbers, longitudes, truncation):
@@ -31,24 +32,52 @@
     )
 
 
-def meridional_tables(truncation, latitudes):
+def meridional_factors(truncation, latitudes, starts, width):
     degree = jnp.arange(truncation, dtype=jnp.int32)
-    latitude = jnp.arange(latitudes, dtype=jnp.int32)
-    phase = degree[:, None] * (2 * latitude + 1)[None, :] % (4 * latitudes)
-    angle = phase.astype(jnp.float32) * (math.pi / (2 * latitudes))
+
+    def angles(points):
+        phase = degree[:, None] * points[None, :] % (4 * latitudes)
+        return phase.astype(jnp.float32) * (math.pi / (2 * latitudes))
+
+    coarse = angles(2 * starts)
+    fine = angles(2 * jnp.arange(width, dtype=jnp.int32) + 1)
     factor = math.sqrt(2.0 / latitudes)
-    even_table = (jnp.cos(angle) * factor).astype(jnp.bfloat16)
-    odd_table = (jnp.sin(angle) * factor).astype(jnp.bfloat16)
-    return even_table, odd_table
+    return jnp.cos(coarse) * factor, jnp.sin(coarse) * factor, jnp.cos(fine), jnp.sin(fine)
+
+
+def tables_kernel(cos_c, sin_c, cos_f, sin_f, even, odd):
+    width = cos_f.shape[1]
+    cos_b, sin_b = cos_f[...], sin_f[...]
+    for at in range(cos_c.shape[1]):
+        cos_a, sin_a = cos_c[:, at : at + 1], sin_c[:, at : at + 1]
+        columns = slice(at * width, (at + 1) * width)
+        even[:, columns] = (cos_a * cos_b - sin_a * sin_b).astype(even.dtype)
+        odd[:, columns] = (sin_a * cos_b + cos_a * sin_b).astype(odd.dtype)
+
+
+def meridional_tables(truncation, latitudes, starts, width):
+    factors = meridional_factors(truncation, latitudes, starts, width)
+    shape = jax.ShapeDtypeStruct((truncation, starts.shape[0] * width), jnp.bfloat16)
+    return pl.pallas_call(
+        tables_kernel,
+        out_shape=[shape, shape],
+        compiler_params=pltpu.CompilerParams(vmem_limit_bytes=VMEM_BYTES),
+        cost_estimate=pl.CostEstimate(
+            flops=6 * truncation * latitudes, bytes_accessed=4 * truncation * latitudes,
+            transcendentals=0,
+        ),
+        name="tables",
+    )(*factors)
 
 
 def zonal_kernel(
-    fields_step, fields, cos_c, sin_c, cos_f, sin_f, velocity, tracer, out, table, total
+    fields_step, fields, tokens, cos_c, sin_c, cos_f, sin_f, velocity, tracer, *rest
 ):
+    outs, (table, total) = rest[tokens:-2], rest[-2:]
     step = pl.program_id(0)
     rows = cos_f.shape[0]
     lat_local, longitudes = velocity.shape[2:]
-    out_rows = out.shape[1]
+    out_rows = outs[0].shape[1]
 
     @pl.when(step == 0)
     def _():
@@ -76,15 +105,19 @@
 
     @pl.when(step == pl.num_programs(0) - 1)
     def _():
-        out[...] = total[...].reshape(out.shape).astype(out.dtype)
-
-
-def zonal_transform(factors, velocity, tracer):
+        for at, out in enumerate(outs):
+            size = out.shape[0] * out_rows
+            part = total[at * size : (at + 1) * size, :]
+            out[...] = part.reshape(out.shape).astype(out.dtype)
+
+
+def zonal_transform(factors, velocity, tracer, pieces, tokens):
     mem_local, fields, lat_local, longitudes = velocity.shape
     rows = factors[0].shape[0]
-    fields_step = min(fields, max(1, 256 // lat_local))
+    fields_step = min(fields, max(1, 512 // lat_local))
     steps = fields // fields_step
     out_rows = mem_local * 2 * fields
+    piece = (rows // pieces, out_rows, lat_local)
     whole = lambda step: (0, 0)
     grid_block = pl.BlockSpec(
         (1, fields_step, lat_local, longitudes), lambda step: (step // steps, step % steps, 0, 0)
@@ -92,11 +125,13 @@
     flops = 2 * 2 * rows * longitudes * mem_local * fields * lat_local
     moved = 2 * velocity.size * 2 + rows * out_rows * lat_local * 2
     return pl.pallas_call(
-        functools.partial(zonal_kernel, fields_step, fields),
+        functools.partial(zonal_kernel, fields_step, fields, len(tokens)),
         grid=(mem_local * steps,),
-        in_specs=[pl.BlockSpec(f.shape, whole) for f in factors] + [grid_block, grid_block],
-        out_specs=pl.BlockSpec((rows, out_rows, lat_local), lambda step: (0, 0, 0)),
-        out_shape=jax.ShapeDtypeStruct((rows, out_rows, lat_local), jnp.bfloat16),
+        in_specs=[pl.BlockSpec(f.shape, whole) for f in factors]
+        + [grid_block, grid_block]
+        + [pl.BlockSpec(memory_space=pl.ANY)] * len(tokens),
+        out_specs=[pl.BlockSpec(piece, lambda step: (0, 0, 0))] * pieces,
+        out_shape=[jax.ShapeDtypeStruct(piece, jnp.bfloat16)] * pieces,
         scratch_shapes=[
             pltpu.VMEM((2 * rows, longitudes), jnp.bfloat16),
             pltpu.VMEM((rows * out_rows, lat_local), jnp.float32),
@@ -104,14 +139,15 @@
         compiler_params=pltpu.CompilerParams(vmem_limit_bytes=VMEM_BYTES),
         cost_estimate=pl.CostEstimate(flops=flops, bytes_accessed=moved, transcendentals=0),
         name="zonal",
-    )(*factors, velocity, tracer)
-
-
-def forward_kernel(first, block, waves, received, even, odd, out):
+    )(*factors, velocity, tracer, *tokens)
+
+
+def forward_kernel(first, block, waves, *refs):
+    received, (even, odd, out, token) = refs[:-4], refs[-4:]
     truncation = even.shape[0]
     step = pl.program_id(0)
-    per_slot = received.shape[1] // block
-    rows = jnp.concatenate([received[g] for g in range(received.shape[0])], axis=-1)
+    per_slot = received[0].shape[0] // block
+    rows = jnp.concatenate([piece[...] for piece in received], axis=-1)
     contract = (((1,), (1,)), ((), ()))
     by_even = lax.dot_general(rows, even[...], contract, preferred_element_type=jnp.float32)
     by_odd = lax.dot_general(rows, odd[...], contract, preferred_element_type=jnp.float32)
@@ -123,10 +159,11 @@
         chosen = jnp.where(wave % 2 == 1, by_odd[here], by_even[here])
         chosen = jnp.where(degree >= least, chosen, 0.0)
         out[slot] = chosen.astype(out.dtype).reshape(out.shape[1:])
+    token[...] = jnp.zeros_like(token)
 
 
 def forward_transform(waves, first, block, received, even, odd, mem_local):
-    groups, all_rows, lat_local = received.shape
+    all_rows, lat_local = received[0].shape
     truncation, latitudes = even.shape
     slots = all_rows // (waves[1] * mem_local)
     out_shape = (slots, mem_local, waves[1], truncation)
@@ -137,26 +174,31 @@
         grid_spec=pltpu.PrefetchScalarGridSpec(
             num_scalar_prefetch=1,
             grid=(slots // block,),
-            in_specs=[
-                pl.BlockSpec((groups, per_block, lat_local), lambda step, w: (0, step, 0)),
-                table,
-                table,
+            in_specs=[pl.BlockSpec((per_block, lat_local), lambda step, w: (step, 0))]
+            * len(received)
+            + [table, table],
+            out_specs=[
+                pl.BlockSpec((block,) + out_shape[1:], lambda step, w: (step, 0, 0, 0)),
+                pl.BlockSpec(TOKEN, lambda step, w: (0, 0)),
             ],
-            out_specs=pl.BlockSpec((block,) + out_shape[1:], lambda step, w: (step, 0, 0, 0)),
-        ),
-        out_shape=jax.ShapeDtypeStruct(out_shape, jnp.bfloat16),
+        ),
+        out_shape=[
+            jax.ShapeDtypeStruct(out_shape, jnp.bfloat16),
+            jax.ShapeDtypeStruct(TOKEN, jnp.float32),
+        ],
         compiler_params=pltpu.CompilerParams(vmem_limit_bytes=VMEM_BYTES),
         cost_estimate=pl.CostEstimate(
             flops=4 * all_rows * truncation * latitudes,
-            bytes_accessed=2 * (received.size + 2 * even.size + all_rows * truncation),
+            bytes_accessed=2 * (all_rows * latitudes + 2 * even.size + all_rows * truncation),
             transcendentals=0,
         ),
         name="forward",
-    )(waves[0], received, even, odd)
+    )(waves[0], *received, even, odd)
 
 
 def inverse_kernel(first, block, waves, offsets, low, own, high, noise, even, odd, *rest):
-    spectra_out, fourier_out = rest[-2:]
+    spectra_out, fourier_out, token = rest[-3:]
+    token[...] = jnp.zeros_like(token)
     truncation, latitudes = even.shape
     step = pl.program_id(0)
     mem_local, parts, fields = noise.shape[1:4]
@@ -220,11 +262,16 @@
             num_scalar_prefetch=2,
             grid=(slots // block,),
             in_specs=in_specs,
-            out_specs=[noise_block, fourier_block],
+            out_specs=[
+                noise_block,
+                fourier_block,
+                pl.BlockSpec(TOKEN, lambda step, w, o: (0, 0)),
+            ],
         ),
         out_shape=[
             jax.ShapeDtypeStruct(noise.shape, jnp.bfloat16),
             jax.ShapeDtypeStruct(fourier_shape, jnp.bfloat16),
+            jax.ShapeDtypeStruct(TOKEN, jnp.float32),
         ],
         input_output_aliases=aliases,
         compiler_params=pltpu.CompilerParams(vmem_limit_bytes=VMEM_BYTES),
@@ -239,8 +286,11 @@
 
 def chunk_bounds(slots_here, block):
     blocks = slots_here // block
-    count = min(4, blocks)
-    edges = [blocks * at // count * block for at in range(count + 1)]
+    edges = [0, 2, 5, 8, 10, 11]
+    if blocks < edges[-1]:
+        edges = list(range(blocks + 1))
+    edges[-1] = blocks
+    edges = [edge * block for edge in edges]
     return list(zip(edges[:-1], edges[1:]))
 
 
@@ -258,27 +308,60 @@
     first_member = group_index * mem_local
     own_parents = lax.dynamic_slice_in_dim(parents, first_member, mem_local)
     offsets = own_parents - first_member + SPREAD
-    even, odd = meridional_tables(truncation, latitudes)
     upward = [(i, i + 1) for i in range(mem_count - 1)]
     downward = [(target, source) for source, target in upward]
-    slot_grid = wave_slots.reshape(lat_count, slots_here)
+    partners = jnp.arange(lat_count, dtype=jnp.int32) ^ lat_index
+    slot_grid = wave_slots.reshape(lat_count, slots_here)[partners]
+    bounds = chunk_bounds(slots_here, block)
+    count = len(bounds)
+    inner = min(lat_local, LANES)
+    order = jnp.arange(latitudes // inner, dtype=jnp.int32) * inner
+    swapped = (partners[:, None] * lat_local + jnp.arange(0, lat_local, inner)[None, :]).reshape(-1)
+    received, own, edges, tokens = {}, {}, {}, {}
     outs = None
-    for start, stop in chunk_bounds(slots_here, block):
-        slots = stop - start
-        factors = zonal_factors(slot_grid[:, start:stop].reshape(-1), longitudes, truncation)
-        outgoing = zonal_transform(factors, velocity, tracer)
-        outgoing = outgoing.reshape(lat_count, slots * per_slot, lat_local)
-        received = lax.all_to_all(outgoing, "lat", split_axis=0, concat_axis=0, tiled=True)
+
+    def send(at):
+        start, stop = bounds[at]
+        waves = slot_grid[:, start:stop].reshape(-1)
+        factors = zonal_factors(waves, longitudes, truncation)
+        after = [tokens[key] for key in (("f", at - 2), ("i", at - 3)) if key in tokens]
+        pieces = zonal_transform(factors, velocity, tracer, lat_count, after)
+        pieces = [piece.reshape(-1, lat_local) for piece in pieces]
+        moved = [pieces[0]] + [None] * (lat_count - 1)
+        for k in reversed(range(1, lat_count)):
+            moved[k] = lax.ppermute(pieces[k], "lat", [(i, i ^ k) for i in range(lat_count)])
         if lat_local % LANES != 0:
-            received = jnp.swapaxes(received, 0, 1).reshape(1, slots * per_slot, latitudes)
-        own = forward_transform(
-            (own_waves, 2 * fields), start, block, received, even, odd, mem_local
+            moved = [jnp.concatenate(moved, axis=-1)]
+        received[at] = moved
+
+    def forward(at):
+        start, _ = bounds[at]
+        spectra, tokens["f", at] = forward_transform(
+            (own_waves, 2 * fields), start, block, received[at], even_swapped, odd_swapped, mem_local
         )
-        low = lax.ppermute(own[:, mem_local - SPREAD :], "member", upward)
-        high = lax.ppermute(own[:, :SPREAD], "member", downward)
-        outs = inverse_transform(
-            own_waves, offsets, start, block, low, own, high, noise, even, odd, outs
+        low = lax.ppermute(spectra[:, mem_local - SPREAD :], "member", upward)
+        high = lax.ppermute(spectra[:, :SPREAD], "member", downward)
+        own[at] = (low, spectra, high)
+
+    def inverse(at, outs):
+        start, _ = bounds[at]
+        *outs, tokens["i", at] = inverse_transform(
+            own_waves, offsets, start, block, *own[at], noise, even, odd, outs
         )
+        return outs
+
+    send(0)
+    even_swapped, odd_swapped = meridional_tables(truncation, latitudes, swapped, inner)
+    even, odd = meridional_tables(truncation, latitudes, order, inner)
+    if count > 1:
+        send(1)
+    for at in range(count):
+        forward(at)
+        if at >= 1:
+            outs = inverse(at - 1, outs)
+        if at + 2 < count:
+            send(at + 2)
+    outs = inverse(count - 1, outs)
     return tuple(outs)
 
 

time: 222 us -> 251 us (1.13)
  starting transfers between devices: 43.2 us -> 98.8 us
  waiting for transfers between devices: 57.8 us -> 40.4 us
  other arithmetic: 14.9 us -> 7.73 us
    ppermute x8 -> x45, starting transfers between devices: 22.9 us -> 98.8 us  [the longest x35 49.5 us: send(): lax.ppermute(pieces[k], 'lat', [(i, i ^ k) for i in range(lat_count)])]
    all_to_all x4 -> x0, waiting for transfers between devices: 53.8 us -> none  [per_device(): lax.all_to_all(outgoing, 'lat', split_axis=0, concat_axis=0, tiled=True)]
    ppermute x8 -> x45, waiting for transfers between devices: 4.08 us -> 40.4 us  [the longest x35 40.4 us: send(): lax.ppermute(pieces[k], 'lat', [(i, i ^ k) for i in range(lat_count)])]
    all_to_all x4 -> x0, starting transfers between devices: 20.3 us -> none  [per_device(): lax.all_to_all(outgoing, 'lat', split_axis=0, concat_axis=0, tiled=True)]
    convert_element_type x1 -> x2, other arithmetic: 11.6 us -> 0.17 us  [angles(): return phase.astype(jnp.float32) * (math.pi / (2 * latitudes))]
    mul x0 -> x4, other arithmetic: none -> 2.63 us  [the longest x2 2.63 us: meridional_factors(): jnp.sin(coarse) * factor]
    pallas_call x4 -> x5, Pallas kernels: 18 us -> 17 us  [forward_transform(): pl.pallas_call(functools.partial(forward_kernel, first, block), grid_spec...]
    pallas_call x4 -> x5, Pallas kernels: 26 us -> 25.3 us  [inverse_transform(): pl.pallas_call(functools.partial(inverse_kernel, first, block), grid_spec...]
  transfers between devices with their start and end apart: 12 -> 45, of which waited for: 5 -> 10; matrix products, arithmetic and copies ran while one was open for 7% -> 4% of each run, Pallas kernels for 35% -> 33%
where the time goes in v2:
time: 251 us; the launch traced here: 250 us
  starting transfers between devices  98.8 us (39%)
  Pallas kernels  94.9 us (38%)
  waiting for transfers between devices  40.4 us (16%)
  other arithmetic  7.73 us (3%)
  local copies, waits for them, and re-layouts  7.08 us (3%)
    ppermute x35, starting transfers between devices, send(): lax.ppermute(pieces[k], 'lat', [(i, i ^ k) for i in range(lat_count)])  49.5 us
    pallas_call x5, Pallas kernels, zonal_transform(): pl.pallas_call(functools.partial(zonal_kernel, fields_step, fields, len(t...  49.1 us
    ppermute x35, waiting for transfers between devices, send(): lax.ppermute(pieces[k], 'lat', [(i, i ^ k) for i in range(lat_count)])  40.4 us
    ppermute x5, starting transfers between devices, forward(): low = lax.ppermute(spectra[:, mem_local - SPREAD:], 'member', upward)  34.1 us
    pallas_call x5, Pallas kernels, inverse_transform(): pl.pallas_call(functools.partial(inverse_kernel, first, block), grid_spec...  25.3 us
    pallas_call x5, Pallas kernels, forward_transform(): pl.pallas_call(functools.partial(forward_kernel, first, block), grid_spec...  17 us
    ppermute x5, starting transfers between devices, forward(): high = lax.ppermute(spectra[:, :SPREAD], 'member', downward)  15.1 us
  transfers between devices with their start and end apart: 45, of which 10 were waited for; matrix products, arithmetic and copies ran while one was open for 4% of the time, Pallas kernels for 33%

profile of v2, /device:TPU:1, one launch (start us, length us, event | category | flops | bytes accessed | tf_op | source)
XLA Modules:
  0.0 250.1 jit_solution(15098445752500377081)
XLA Ops:
  3.0 9.9 %zonal.5 = (bf16[16,32,128]{2,1,0:T(8,128)(2,1)S(1)}, bf16[16,32,128]{2,1,0:T(8,128)(2,1)}, bf16[16,32,128]{2,1,0:T(8,128)(2,1)}, bf16[16,32,128]{2,1,0:T(8,128)...) custom-call(f32[128,16]{1,0:T(8,128)S(1)} %get-tuple-element.141.cos, ...), custom_call_target="tpu_custom_call" | custom-call | flops 2147483648 | bytes 17825792 | tf_op jit(solution)/shard_map/zonal/pallas_call | solution.py:127
  13.6 2.1 collective-permute-start
  17.0 2.4 collective-permute-start.3
  27.7 11.3 %zonal.7 = (bf16[24,32,128]{2,1,0:T(8,128)(2,1)S(1)}, bf16[24,32,128]{2,1,0:T(8,128)(2,1)}, bf16[24,32,128]{2,1,0:T(8,128)(2,1)}, bf16[24,32,128]{2,1,0:T(8,128)...) custom-call(f32[192,16]{1,0:T(8,128)S(1)} %get-tuple-element.135.cos, ...), custom_call_target="tpu_custom_call" | custom-call | flops 3221225472 | bytes 18350080 | tf_op jit(solution)/shard_map/zonal/pallas_call | solution.py:127
  40.7 3.4 %collective-permute-start.5 = (bf16[512,128]{1,0:T(8,128)(2,1)S(1)}, bf16[512,128]{1,0:T(8,128)(2,1)S(1)}, u32[]{:S(2)}, u32[]{:S(2)}) collective-permute-start(bf16[512,128]{1,0:T(8,128)(2,1)S(1)} %bitcast.56), channel_id=1, source_target_pairs={{0,6},{1,7},{2,4},{3,5},{4,2},{5,3},{6,0},{7,1},{8,14},{9,15},{10,... | collective-permute-start | bytes 393224 | tf_op jit(solution)/shard_map/ppermute | solution.py:332
  47.7 2.0 collective-permute-start.17
  50.5 1.8 tables.2
  52.3 1.7 tables.3
  56.3 3.6 %forward.5 = (bf16[16,2,16,683]{3,2,1,0:T(8,128)(2,1)S(1)}, f32[8,128]{1,0:T(8,128)S(1)}) custom-call(s32[88]{0:T(128)S(1)} %dynamic_slice.6.waves, bf16[512,128]{1,0:T(8,128)(2,1)S(1)} %bitcast.55, bf16[512,128]{1,0:T(8,128)(2,1)} %collective-permute-done.refs_1_, bf16[512,128]{1,0:T(8,128)(2,1)} %collective-permute-done.1.refs_2_, ...), custom_call_target="tpu_custom_call" | custom-call | flops 1432354816 | bytes 4545536 | tf_op jit(solution)/shard_map/forward/pallas_call | solution.py:172
  59.9 3.3 %collective-permute-start.19 = (bf16[768,128]{1,0:T(8,128)(2,1)S(1)}, bf16[768,128]{1,0:T(8,128)(2,1)S(1)}, u32[]{:S(2)}, u32[]{:S(2)}) collective-permute-start(bf16[768,128]{1,0:T(8,128)(2,1)S(1)} %bitcast.45), channel_id=1, source_target_pairs={{0,6},{1,7},{2,4},{3,5},{4,2},{5,3},{6,0},{7,1},{8,14},{9,15},{10,... | collective-permute-start | bytes 589832 | tf_op jit(solution)/shard_map/ppermute | solution.py:332
  64.0 10.6 %collective-permute-start.23 = (bf16[16,2,16,683]{3,2,1,0:T(8,128)(2,1)S(1)}, bf16[16,2,16,683]{3,2,1,0:T(8,128)(2,1)S(1)}, u32[]{:S(2)}, u32[]{:S(2)}) collective-permute-start(bf16[16,2,16,683]{3,2,1,0:T(8,128)(2,1)S(1)} %get-tuple-element.97.own), channel_id=1, source_target_pairs={{0,8},{8,16},{16,24},{1,9},{9,17},{17,25},{2,10},{10,18},{18,26},{... | collective-permute-start | bytes 2098184 | tf_op jit(solution)/shard_map/ppermute | solution.py:342
  74.5 7.4 %collective-permute-start.24 = (bf16[16,2,16,683]{3,2,1,0:T(8,128)(2,1)S(1)}, bf16[16,2,16,683]{3,2,1,0:T(8,128)(2,1)S(1)}, u32[]{:S(2)}, u32[]{:S(2)}) collective-permute-start(bf16[16,2,16,683]{3,2,1,0:T(8,128)(2,1)S(1)} %get-tuple-element.97.own), channel_id=1, source_target_pairs={{8,0},{16,8},{24,16},{9,1},{17,9},{25,17},{10,2},{18,10},{26,18},{... | collective-permute-start | bytes 2098184 | tf_op jit(solution)/shard_map/ppermute | solution.py:343
  82.0 10.4 %zonal.6 = (bf16[24,32,128]{2,1,0:T(8,128)(2,1)S(1)}, bf16[24,32,128]{2,1,0:T(8,128)(2,1)S(1)}, bf16[24,32,128]{2,1,0:T(8,128)(2,1)S(1)}, bf16[24,32,128]{2,1,0:...) custom-call(f32[192,16]{1,0:T(8,128)S(1)} %get-tuple-element.137.cos, ...), custom_call_target="tpu_custom_call" | custom-call | flops 3221225472 | bytes 18350080 | tf_op jit(solution)/shard_map/zonal/pallas_call | solution.py:127
  92.5 4.6 %forward.7 = (bf16[24,2,16,683]{3,2,1,0:T(8,128)(2,1)S(1)}, f32[8,128]{1,0:T(8,128)S(1)}) custom-call(s32[88]{0:T(128)S(1)} %dynamic_slice.6.waves, bf16[768,128]{1,0:T(8,128)(2,1)S(1)} %bitcast.43, bf16[768,128]{1,0:T(8,128)(2,1)} %collective-permute-done.14.refs_1_, bf16[768,128]{1,0:T(8,128)(2,1)} %collective-permute-done.15.refs_2_, ...), custom_call_target="tpu_custom_call" | custom-call | flops 2148532224 | bytes 5419520 | tf_op jit(solution)/shard_map/forward/pallas_call | solution.py:172
  97.2 3.0 %collective-permute-start.21 = (bf16[24,2,16,683]{3,2,1,0:T(8,128)(2,1)S(1)}, bf16[24,2,16,683]{3,2,1,0:T(8,128)(2,1)S(1)}, u32[]{:S(2)}, u32[]{:S(2)}) collective-permute-start(bf16[24,2,16,683]{3,2,1,0:T(8,128)(2,1)S(1)} %get-tuple-element.94.own), channel_id=1, source_target_pairs={{0,8},{8,16},{16,24},{1,9},{9,17},{17,25},{2,10},{10,18},{18,26},{... | collective-permute-start | bytes 3147272 | tf_op jit(solution)/shard_map/ppermute | solution.py:342
  100.2 1.9 collective-permute-start.22
  103.3 1.6 collective-permute-start.11
  106.2 3.0 %collective-permute-start.13 = (bf16[768,128]{1,0:T(8,128)(2,1)S(1)}, bf16[768,128]{1,0:T(8,128)(2,1)S(1)}, u32[]{:S(2)}, u32[]{:S(2)}) collective-permute-start(bf16[768,128]{1,0:T(8,128)(2,1)S(1)} %bitcast.51), channel_id=1, source_target_pairs={{0,7},{1,6},{2,5},{3,4},{4,3},{5,2},{6,1},{7,0},{8,15},{9,14},{10,... | collective-permute-start | bytes 589832 | tf_op jit(solution)/shard_map/ppermute | solution.py:332
  109.2 4.7 %inverse.5 = (bf16[88,2,2,8,683]{4,3,2,1,0:T(8,128)(2,1)}, bf16[88,2,2,8,1024]{4,3,2,1,0:T(8,128)(2,1)}, f32[8,128]{1,0:T(8,128)S(1)}) custom-call(s32[88]{0:T(128)S(1)} %dynamic_slice.6.waves, s32[2]{0:T(128)S(1)} %subtract_add_fusion.offsets, bf16[16,2,16,683]{3,2,1,0:T(8,128)(2,1)S(1)} %collective-permute-done.23.low, ...), custom_call_target="tpu_custom_call" | custom-call | flops 1432354816 | bytes 7343104 | tf_op jit(solution)/shard_map/inverse/pallas_call | solution.py:259
  113.9 10.5 %collective-permute-done.11.refs_5_ = bf16[768,128]{1,0:T(8,128)(2,1)S(1)} collective-permute-done((bf16[768,128]{1,0:T(8,128)(2,1)S(1)}, bf16[768,128]{1,0:T(8,128)(2,1)S(1)}, u32[]{:S(2)}, u32[]{:S(2)}) %collective-permute-start.11) | collective-permute-done | bytes 196640 | tf_op jit(solution)/shard_map/ppermute | solution.py:332
  124.4 3.1 %collective-permute-start.8 = (bf16[768,128]{1,0:T(8,128)(2,1)S(1)}, bf16[768,128]{1,0:T(8,128)(2,1)S(1)}, u32[]{:S(2)}, u32[]{:S(2)}) collective-permute-start(bf16[768,128]{1,0:T(8,128)(2,1)S(1)} %bitcast.49), channel_id=1, source_target_pairs={{0,2},{1,3},{2,0},{3,1},{4,6},{5,7},{6,4},{7,5},{8,10},{9,11},{10,... | collective-permute-start | bytes 589832 | tf_op jit(solution)/shard_map/ppermute | solution.py:332
  127.6 5.2 %collective-permute-start.9 = (bf16[768,128]{1,0:T(8,128)(2,1)S(1)}, bf16[768,128]{1,0:T(8,128)(2,1)S(1)}, u32[]{:S(2)}, u32[]{:S(2)}) collective-permute-start(bf16[768,128]{1,0:T(8,128)(2,1)S(1)} %bitcast.48), channel_id=1, source_target_pairs={{0,3},{1,2},{2,1},{3,0},{4,7},{5,6},{6,5},{7,4},{8,11},{9,10},{10,... | collective-permute-start | bytes 589832 | tf_op jit(solution)/shard_map/ppermute | solution.py:332
  132.7 9.0 %zonal.9 = (bf16[16,32,128]{2,1,0:T(8,128)(2,1)S(1)}, bf16[16,32,128]{2,1,0:T(8,128)(2,1)S(1)}, bf16[16,32,128]{2,1,0:T(8,128)(2,1)S(1)}, bf16[16,32,128]{2,1,0:...) custom-call(f32[128,16]{1,0:T(8,128)S(1)} %get-tuple-element.139.cos, ...), custom_call_target="tpu_custom_call" | custom-call | flops 2147483648 | bytes 17825792 | tf_op jit(solution)/shard_map/zonal/pallas_call | solution.py:127
  141.7 1.7 collective-permute-start.34
  144.7 3.6 %forward.6 = (bf16[24,2,16,683]{3,2,1,0:T(8,128)(2,1)S(1)}, f32[8,128]{1,0:T(8,128)S(1)}) custom-call(s32[88]{0:T(128)S(1)} %dynamic_slice.6.waves, bf16[768,128]{1,0:T(8,128)(2,1)S(1)} %bitcast.47, bf16[768,128]{1,0:T(8,128)(2,1)S(1)} %collective-permute-done.7.refs_1_, bf16[768,128]{1,0:T(8,128)(2,1)S(1)} %collective-permute-done.8.refs_2_, ...), custom_call_target="tpu_custom_call" | custom-call | flops 2148532224 | bytes 5419520 | tf_op jit(solution)/shard_map/forward/pallas_call | solution.py:172
  148.4 5.1 %collective-permute-start.43 = (bf16[24,2,16,683]{3,2,1,0:T(8,128)(2,1)S(1)}, bf16[24,2,16,683]{3,2,1,0:T(8,128)(2,1)S(1)}, u32[]{:S(2)}, u32[]{:S(2)}) collective-permute-start(bf16[24,2,16,683]{3,2,1,0:T(8,128)(2,1)S(1)} %get-tuple-element.121.own), channel_id=1, source_target_pairs={{0,8},{8,16},{16,24},{1,9},{9,17},{17,25},{2,10},{10,18},{18,26},{... | collective-permute-start | bytes 3147272 | tf_op jit(solution)/shard_map/ppermute | solution.py:342
  153.5 1.9 collective-permute-start.44
  156.3 5.5 %collective-permute-done.37.refs_4_ = bf16[512,128]{1,0:T(8,128)(2,1)S(1)} collective-permute-done((bf16[512,128]{1,0:T(8,128)(2,1)S(1)}, bf16[512,128]{1,0:T(8,128)(2,1)S(1)}, u32[]{:S(2)}, u32[]{:S(2)}) %collective-permute-start.37) | collective-permute-done | bytes 131104 | tf_op jit(solution)/shard_map/ppermute | solution.py:332
  162.3 1.6 collective-permute-start.39
  164.0 2.1 collective-permute-start.40
  166.0 6.6 %inverse.6 = (bf16[88,2,2,8,683]{4,3,2,1,0:T(8,128)(2,1)}, bf16[88,2,2,8,1024]{4,3,2,1,0:T(8,128)(2,1)}, f32[8,128]{1,0:T(8,128)S(1)}) custom-call(s32[88]{0:T(128)S(1)} %dynamic_slice.6.waves, s32[2]{0:T(128)S(1)} %subtract_add_fusion.offsets, ...), custom_call_target="tpu_custom_call", output_to_operand_aliasing={{0}: (8, {}), {1}: (9, {})} | custom-call | flops 2148532224 | bytes 9615872 | tf_op jit(solution)/shard_map/inverse/pallas_call | solution.py:259
  172.6 8.4 %zonal.8 = (bf16[8,32,128]{2,1,0:T(8,128)(2,1)S(1)}, bf16[8,32,128]{2,1,0:T(8,128)(2,1)S(1)}, bf16[8,32,128]{2,1,0:T(8,128)(2,1)S(1)}, bf16[8,32,128]{2,1,0:T(8,...) custom-call(f32[64,16]{1,0:T(8,128)S(1)} %get-tuple-element.143.cos_, ...), custom_call_target="tpu_custom_call" | custom-call | flops 1073741824 | bytes 17301504 | tf_op jit(solution)/shard_map/zonal/pallas_call | solution.py:127
  181.8 3.1 %forward.9 = (bf16[16,2,16,683]{3,2,1,0:T(8,128)(2,1)S(1)}, f32[8,128]{1,0:T(8,128)}) custom-call(s32[88]{0:T(128)S(1)} %dynamic_slice.6.waves, bf16[512,128]{1,0:T(8,128)(2,1)S(1)} %bitcast.57, bf16[512,128]{1,0:T(8,128)(2,1)S(1)} %collective-permute-done.34.refs_1_, bf16[512,128]{1,0:T(8,128)(2,1)S(1)} %collective-permute-done.35.refs_2_, ...), custom_call_target="tpu_custom_call" | custom-call | flops 1432354816 | bytes 4545536 | tf_op jit(solution)/shard_map/forward/pallas_call | solution.py:172
  184.9 5.8 %collective-permute-start.41 = (bf16[16,2,16,683]{3,2,1,0:T(8,128)(2,1)S(1)}, bf16[16,2,16,683]{3,2,1,0:T(8,128)(2,1)S(1)}, u32[]{:S(2)}, u32[]{:S(2)}) collective-permute-start(bf16[16,2,16,683]{3,2,1,0:T(8,128)(2,1)S(1)} %get-tuple-element.120.own), channel_id=1, source_target_pairs={{0,8},{8,16},{16,24},{1,9},{9,17},{17,25},{2,10},{10,18},{18,26},{... | collective-permute-start | bytes 2098184 | tf_op jit(solution)/shard_map/ppermute | solution.py:342
  190.7 1.9 collective-permute-start.42
  193.7 2.1 collective-permute-done.26.refs_2_
  196.8 3.1 %collective-permute-done.27.refs_3_ = bf16[256,128]{1,0:T(8,128)(2,1)S(1)} collective-permute-done((bf16[256,128]{1,0:T(8,128)(2,1)S(1)}, bf16[256,128]{1,0:T(8,128)(2,1)S(1)}, u32[]{:S(2)}, u32[]{:S(2)}) %collective-permute-start.27) | collective-permute-done | bytes 65568 | tf_op jit(solution)/shard_map/ppermute | solution.py:332
  201.1 3.6 %collective-permute-done.28.refs_4_ = bf16[256,128]{1,0:T(8,128)(2,1)S(1)} collective-permute-done((bf16[256,128]{1,0:T(8,128)(2,1)S(1)}, bf16[256,128]{1,0:T(8,128)(2,1)S(1)}, u32[]{:S(2)}, u32[]{:S(2)}) %collective-permute-start.28) | collective-permute-done | bytes 65568 | tf_op jit(solution)/shard_map/ppermute | solution.py:332
  205.1 6.5 %collective-permute-done.29.refs_5_ = bf16[256,128]{1,0:T(8,128)(2,1)S(1)} collective-permute-done((bf16[256,128]{1,0:T(8,128)(2,1)S(1)}, bf16[256,128]{1,0:T(8,128)(2,1)S(1)}, u32[]{:S(2)}, u32[]{:S(2)}) %collective-permute-start.29) | collective-permute-done | bytes 65568 | tf_op jit(solution)/shard_map/ppermute | solution.py:332
  211.6 1.7 collective-permute-start.30
  213.3 3.2 %collective-permute-done.30.refs_6_ = bf16[256,128]{1,0:T(8,128)(2,1)S(1)} collective-permute-done((bf16[256,128]{1,0:T(8,128)(2,1)S(1)}, bf16[256,128]{1,0:T(8,128)(2,1)S(1)}, u32[]{:S(2)}, u32[]{:S(2)}) %collective-permute-start.30) | collective-permute-done | bytes 65568 | tf_op jit(solution)/shard_map/ppermute | solution.py:332
  218.1 4.2 %collective-permute-done.31.refs_7_ = bf16[256,128]{1,0:T(8,128)(2,1)S(1)} collective-permute-done((bf16[256,128]{1,0:T(8,128)(2,1)S(1)}, bf16[256,128]{1,0:T(8,128)(2,1)S(1)}, u32[]{:S(2)}, u32[]{:S(2)}) %collective-permute-start.31) | collective-permute-done | bytes 65568 | tf_op jit(solution)/shard_map/ppermute | solution.py:332
  222.4 2.0 forward.8
  224.4 9.6 %collective-permute-start.32 = (bf16[8,2,16,683]{3,2,1,0:T(8,128)(2,1)S(1)}, bf16[8,2,16,683]{3,2,1,0:T(8,128)(2,1)S(1)}, u32[]{:S(2)}, u32[]{:S(2)}) collective-permute-start(bf16[8,2,16,683]{3,2,1,0:T(8,128)(2,1)S(1)} %get-tuple-element.109.own), channel_id=1, source_target_pairs={{0,8},{8,16},{16,24},{1,9},{9,17},{17,25},{2,10},{10,18},{18,26},{... | collective-permute-start | bytes 1049096 | tf_op jit(solution)/shard_map/ppermute | solution.py:342
  234.0 1.9 collective-permute-start.33
  236.0 6.2 %inverse.7 = (bf16[88,2,2,8,683]{4,3,2,1,0:T(8,128)(2,1)}, bf16[88,2,2,8,1024]{4,3,2,1,0:T(8,128)(2,1)}, f32[8,128]{1,0:T(8,128)}) custom-call(s32[88]{0:T(128)S(1)} %dynamic_slice.6.waves, s32[2]{0:T(128)S(1)} %subtract_add_fusion.offsets, bf16[24,2,16,683]{3,2,1,0:T(8,128)(2,1)S(1)} %collective-permute-done.43.low, ...), custom_call_target="tpu_custom_call", output_to_operand_aliasing={{0}: (8, {}), {1}: (9, {})} | custom-call | flops 2148532224 | bytes 9615872 | tf_op jit(solution)/shard_map/inverse/pallas_call | solution.py:259
  242.2 4.5 %inverse.8 = (bf16[88,2,2,8,683]{4,3,2,1,0:T(8,128)(2,1)}, bf16[88,2,2,8,1024]{4,3,2,1,0:T(8,128)(2,1)}, f32[8,128]{1,0:T(8,128)}) custom-call(s32[88]{0:T(128)S(1)} %dynamic_slice.6.waves, s32[2]{0:T(128)S(1)} %subtract_add_fusion.offsets, bf16[16,2,16,683]{3,2,1,0:T(8,128)(2,1)S(1)} %collective-permute-done.41.low, ...), custom_call_target="tpu_custom_call", output_to_operand_aliasing={{0}: (8, {}), {1}: (9, {})} | custom-call | flops 1432354816 | bytes 7343104 | tf_op jit(solution)/shard_map/inverse/pallas_call | solution.py:259
  246.7 3.4 %inverse.9 = (bf16[88,2,2,8,683]{4,3,2,1,0:T(8,128)(2,1)}, bf16[88,2,2,8,1024]{4,3,2,1,0:T(8,128)(2,1)}, f32[8,128]{1,0:T(8,128)}) custom-call(s32[88]{0:T(128)S(1)} %dynamic_slice.6.waves, s32[2]{0:T(128)S(1)} %subtract_add_fusion.offsets, bf16[8,2,16,683]{3,2,1,0:T(8,128)(2,1)S(1)} %collective-permute-done.32.low, ...), custom_call_target="tpu_custom_call", output_to_operand_aliasing={{0}: (8, {}), {1}: (9, {})} | custom-call | flops 716177408 | bytes 5070336 | tf_op jit(solution)/shard_map/inverse/pallas_call | solution.py:259
  (127 shorter events, 32.7 us)
Async XLA Ops:
  13.6 27.1 %collective-permute-start = (bf16[512,128]{1,0:T(8,128)(2,1)}, bf16[512,128]{1,0:T(8,128)(2,1)}, u32[]{:S(2)}, u32[]{:S(2)}) collective-permute-start(bf16[512,128]{1,0:T(8,128)(2,1)} %bitcast.2), channel_id=1, source_target_pairs={{0,1},{1,0},{2,3},{3,2},{4,5},{5,4},{6,7},{7,6},{8,9},{9,8},{10,11... | collective-permute-start | bytes 393224 | tf_op jit(solution)/shard_map/ppermute | solution.py:332
  15.7 28.6 %collective-permute-start.1 = (bf16[512,128]{1,0:T(8,128)(2,1)}, bf16[512,128]{1,0:T(8,128)(2,1)}, u32[]{:S(2)}, u32[]{:S(2)}) collective-permute-start(bf16[512,128]{1,0:T(8,128)(2,1)} %bitcast.3), channel_id=1, source_target_pairs={{0,2},{1,3},{2,0},{3,1},{4,6},{5,7},{6,4},{7,5},{8,10},{9,11},{10,... | collective-permute-start | bytes 393224 | tf_op jit(solution)/shard_map/ppermute | solution.py:332
  17.0 27.3 %collective-permute-start.2 = (bf16[512,128]{1,0:T(8,128)(2,1)}, bf16[512,128]{1,0:T(8,128)(2,1)}, u32[]{:S(2)}, u32[]{:S(2)}) collective-permute-start(bf16[512,128]{1,0:T(8,128)(2,1)} %bitcast.4), channel_id=1, source_target_pairs={{0,3},{1,2},{2,1},{3,0},{4,7},{5,6},{6,5},{7,4},{8,11},{9,10},{10,... | collective-permute-start | bytes 393224 | tf_op jit(solution)/shard_map/ppermute | solution.py:332
  17.0 28.5 %collective-permute-start.3 = (bf16[512,128]{1,0:T(8,128)(2,1)}, bf16[512,128]{1,0:T(8,128)(2,1)}, u32[]{:S(2)}, u32[]{:S(2)}) collective-permute-start(bf16[512,128]{1,0:T(8,128)(2,1)} %bitcast.5), channel_id=1, source_target_pairs={{0,4},{1,5},{2,6},{3,7},{4,0},{5,1},{6,2},{7,3},{8,12},{9,13},{10,... | collective-permute-start | bytes 393224 | tf_op jit(solution)/shard_map/ppermute | solution.py:332
  19.4 26.1 %collective-permute-start.4 = (bf16[512,128]{1,0:T(8,128)(2,1)}, bf16[512,128]{1,0:T(8,128)(2,1)}, u32[]{:S(2)}, u32[]{:S(2)}) collective-permute-start(bf16[512,128]{1,0:T(8,128)(2,1)} %bitcast.6), channel_id=1, source_target_pairs={{0,5},{1,4},{2,7},{3,6},{4,1},{5,0},{6,3},{7,2},{8,13},{9,12},{10,... | collective-permute-start | bytes 393224 | tf_op jit(solution)/shard_map/ppermute | solution.py:332
  40.7 19.2 %copy-start.3 = (bf16[24,32,128]{2,1,0:T(8,128)(2,1)S(1)}, bf16[24,32,128]{2,1,0:T(8,128)(2,1)}, u32[]{:S(2)}) copy-start(bf16[24,32,128]{2,1,0:T(8,128)(2,1)} %copy-done.2) | copy-start | bytes 589828
  40.7 6.3 %collective-permute-start.5 = (bf16[512,128]{1,0:T(8,128)(2,1)S(1)}, bf16[512,128]{1,0:T(8,128)(2,1)S(1)}, u32[]{:S(2)}, u32[]{:S(2)}) collective-permute-start(bf16[512,128]{1,0:T(8,128)(2,1)S(1)} %bitcast.56), channel_id=1, source_target_pairs={{0,6},{1,7},{2,4},{3,5},{4,2},{5,3},{6,0},{7,1},{8,14},{9,15},{10,... | collective-permute-start | bytes 393224 | tf_op jit(solution)/shard_map/ppermute | solution.py:332
  44.2 9.9 %collective-permute-start.6 = (bf16[512,128]{1,0:T(8,128)(2,1)}, bf16[512,128]{1,0:T(8,128)(2,1)}, u32[]{:S(2)}, u32[]{:S(2)}) collective-permute-start(bf16[512,128]{1,0:T(8,128)(2,1)} %bitcast.8), channel_id=1, source_target_pairs={{0,7},{1,6},{2,5},{3,4},{4,3},{5,2},{6,1},{7,0},{8,15},{9,14},{10,... | collective-permute-start | bytes 393224 | tf_op jit(solution)/shard_map/ppermute | solution.py:332
  44.3 15.6 %collective-permute-start.14 = (bf16[768,128]{1,0:T(8,128)(2,1)}, bf16[768,128]{1,0:T(8,128)(2,1)}, u32[]{:S(2)}, u32[]{:S(2)}) collective-permute-start(bf16[768,128]{1,0:T(8,128)(2,1)} %bitcast.18), channel_id=1, source_target_pairs={{0,1},{1,0},{2,3},{3,2},{4,5},{5,4},{6,7},{7,6},{8,9},{9,8},{10,11... | collective-permute-start | bytes 589832 | tf_op jit(solution)/shard_map/ppermute | solution.py:332
  45.5 17.8 %collective-permute-start.15 = (bf16[768,128]{1,0:T(8,128)(2,1)}, bf16[768,128]{1,0:T(8,128)(2,1)}, u32[]{:S(2)}, u32[]{:S(2)}) collective-permute-start(bf16[768,128]{1,0:T(8,128)(2,1)} %bitcast.19), channel_id=1, source_target_pairs={{0,2},{1,3},{2,0},{3,1},{4,6},{5,7},{6,4},{7,5},{8,10},{9,11},{10,... | collective-permute-start | bytes 589832 | tf_op jit(solution)/shard_map/ppermute | solution.py:332
  45.5 18.5 %collective-permute-start.16 = (bf16[768,128]{1,0:T(8,128)(2,1)}, bf16[768,128]{1,0:T(8,128)(2,1)}, u32[]{:S(2)}, u32[]{:S(2)}) collective-permute-start(bf16[768,128]{1,0:T(8,128)(2,1)} %bitcast.20), channel_id=1, source_target_pairs={{0,3},{1,2},{2,1},{3,0},{4,7},{5,6},{6,5},{7,4},{8,11},{9,10},{10,... | collective-permute-start | bytes 589832 | tf_op jit(solution)/shard_map/ppermute | solution.py:332
  47.7 26.8 %collective-permute-start.17 = (bf16[768,128]{1,0:T(8,128)(2,1)}, bf16[768,128]{1,0:T(8,128)(2,1)}, u32[]{:S(2)}, u32[]{:S(2)}) collective-permute-start(bf16[768,128]{1,0:T(8,128)(2,1)} %bitcast.21), channel_id=1, source_target_pairs={{0,4},{1,5},{2,6},{3,7},{4,0},{5,1},{6,2},{7,3},{8,12},{9,13},{10,... | collective-permute-start | bytes 589832 | tf_op jit(solution)/shard_map/ppermute | solution.py:332
  54.1 55.1 %copy-start = (bf16[683,1024]{1,0:T(8,128)(2,1)}, bf16[683,1024]{1,0:T(8,128)(2,1)S(1)}, u32[]{:S(2)}) copy-start(bf16[683,1024]{1,0:T(8,128)(2,1)S(1)} %get-tuple-element.96.odd) | copy-start | bytes 4196356
  54.1 38.3 %collective-permute-start.18 = (bf16[768,128]{1,0:T(8,128)(2,1)}, bf16[768,128]{1,0:T(8,128)(2,1)S(1)}, u32[]{:S(2)}, u32[]{:S(2)}) collective-permute-start(bf16[768,128]{1,0:T(8,128)(2,1)} %bitcast.46), channel_id=1, source_target_pairs={{0,5},{1,4},{2,7},{3,6},{4,1},{5,0},{6,3},{7,2},{8,13},{9,12},{10,... | collective-permute-start | bytes 589832 | tf_op jit(solution)/shard_map/ppermute | solution.py:332
  59.9 32.6 %collective-permute-start.19 = (bf16[768,128]{1,0:T(8,128)(2,1)S(1)}, bf16[768,128]{1,0:T(8,128)(2,1)S(1)}, u32[]{:S(2)}, u32[]{:S(2)}) collective-permute-start(bf16[768,128]{1,0:T(8,128)(2,1)S(1)} %bitcast.45), channel_id=1, source_target_pairs={{0,6},{1,7},{2,4},{3,5},{4,2},{5,3},{6,0},{7,1},{8,14},{9,15},{10,... | collective-permute-start | bytes 589832 | tf_op jit(solution)/shard_map/ppermute | solution.py:332
  63.3 29.3 %collective-permute-start.20 = (bf16[768,128]{1,0:T(8,128)(2,1)S(1)}, bf16[768,128]{1,0:T(8,128)(2,1)S(1)}, u32[]{:S(2)}, u32[]{:S(2)}) collective-permute-start(bf16[768,128]{1,0:T(8,128)(2,1)S(1)} %bitcast.44), channel_id=1, source_target_pairs={{0,7},{1,6},{2,5},{3,4},{4,3},{5,2},{6,1},{7,0},{8,15},{9,14},{10,... | collective-permute-start | bytes 589832 | tf_op jit(solution)/shard_map/ppermute | solution.py:332
  64.0 40.9 %collective-permute-start.23 = (bf16[16,2,16,683]{3,2,1,0:T(8,128)(2,1)S(1)}, bf16[16,2,16,683]{3,2,1,0:T(8,128)(2,1)S(1)}, u32[]{:S(2)}, u32[]{:S(2)}) collective-permute-start(bf16[16,2,16,683]{3,2,1,0:T(8,128)(2,1)S(1)} %get-tuple-element.97.own), channel_id=1, source_target_pairs={{0,8},{8,16},{16,24},{1,9},{9,17},{17,25},{2,10},{10,18},{18,26},{... | collective-permute-start | bytes 2098184 | tf_op jit(solution)/shard_map/ppermute | solution.py:342
  74.5 31.6 %collective-permute-start.24 = (bf16[16,2,16,683]{3,2,1,0:T(8,128)(2,1)S(1)}, bf16[16,2,16,683]{3,2,1,0:T(8,128)(2,1)S(1)}, u32[]{:S(2)}, u32[]{:S(2)}) collective-permute-start(bf16[16,2,16,683]{3,2,1,0:T(8,128)(2,1)S(1)} %get-tuple-element.97.own), channel_id=1, source_target_pairs={{8,0},{16,8},{24,16},{9,1},{17,9},{25,17},{10,2},{18,10},{26,18},{... | collective-permute-start | bytes 2098184 | tf_op jit(solution)/shard_map/ppermute | solution.py:343
  92.4 16.7 %copy-start.9 = (s32[8]{0:T(128)S(1)}, s32[8]{0:T(128)}, u32[]{:S(2)}) copy-start(s32[8]{0:T(128)} %param.8) | copy-start | bytes 100
  92.4 10.8 %collective-permute-start.10 = (bf16[768,128]{1,0:T(8,128)(2,1)S(1)}, bf16[768,128]{1,0:T(8,128)(2,1)S(1)}, u32[]{:S(2)}, u32[]{:S(2)}) collective-permute-start(bf16[768,128]{1,0:T(8,128)(2,1)S(1)} %bitcast.54), channel_id=1, source_target_pairs={{0,4},{1,5},{2,6},{3,7},{4,0},{5,1},{6,2},{7,3},{8,12},{9,13},{10,... | collective-permute-start | bytes 589832 | tf_op jit(solution)/shard_map/ppermute | solution.py:332
  97.2 65.2 %collective-permute-start.21 = (bf16[24,2,16,683]{3,2,1,0:T(8,128)(2,1)S(1)}, bf16[24,2,16,683]{3,2,1,0:T(8,128)(2,1)S(1)}, u32[]{:S(2)}, u32[]{:S(2)}) collective-permute-start(bf16[24,2,16,683]{3,2,1,0:T(8,128)(2,1)S(1)} %get-tuple-element.94.own), channel_id=1, source_target_pairs={{0,8},{8,16},{16,24},{1,9},{9,17},{17,25},{2,10},{10,18},{18,26},{... | collective-permute-start | bytes 3147272 | tf_op jit(solution)/shard_map/ppermute | solution.py:342
  100.2 63.8 %collective-permute-start.22 = (bf16[24,2,16,683]{3,2,1,0:T(8,128)(2,1)S(1)}, bf16[24,2,16,683]{3,2,1,0:T(8,128)(2,1)}, u32[]{:S(2)}, u32[]{:S(2)}) collective-permute-start(bf16[24,2,16,683]{3,2,1,0:T(8,128)(2,1)S(1)} %get-tuple-element.94.own), channel_id=1, source_target_pairs={{8,0},{16,8},{24,16},{9,1},{17,9},{25,17},{10,2},{18,10},{26,18},{... | collective-permute-start | bytes 3147272 | tf_op jit(solution)/shard_map/ppermute | solution.py:343
  103.3 21.2 %collective-permute-start.11 = (bf16[768,128]{1,0:T(8,128)(2,1)S(1)}, bf16[768,128]{1,0:T(8,128)(2,1)S(1)}, u32[]{:S(2)}, u32[]{:S(2)}) collective-permute-start(bf16[768,128]{1,0:T(8,128)(2,1)S(1)} %bitcast.53), channel_id=1, source_target_pairs={{0,5},{1,4},{2,7},{3,6},{4,1},{5,0},{6,3},{7,2},{8,13},{9,12},{10,... | collective-permute-start | bytes 589832 | tf_op jit(solution)/shard_map/ppermute | solution.py:332
  104.9 19.5 %collective-permute-start.12 = (bf16[768,128]{1,0:T(8,128)(2,1)S(1)}, bf16[768,128]{1,0:T(8,128)(2,1)S(1)}, u32[]{:S(2)}, u32[]{:S(2)}) collective-permute-start(bf16[768,128]{1,0:T(8,128)(2,1)S(1)} %bitcast.52), channel_id=1, source_target_pairs={{0,6},{1,7},{2,4},{3,5},{4,2},{5,3},{6,0},{7,1},{8,14},{9,15},{10,... | collective-permute-start | bytes 589832 | tf_op jit(solution)/shard_map/ppermute | solution.py:332
  106.2 21.4 %collective-permute-start.13 = (bf16[768,128]{1,0:T(8,128)(2,1)S(1)}, bf16[768,128]{1,0:T(8,128)(2,1)S(1)}, u32[]{:S(2)}, u32[]{:S(2)}) collective-permute-start(bf16[768,128]{1,0:T(8,128)(2,1)S(1)} %bitcast.51), channel_id=1, source_target_pairs={{0,7},{1,6},{2,5},{3,4},{4,3},{5,2},{6,1},{7,0},{8,15},{9,14},{10,... | collective-permute-start | bytes 589832 | tf_op jit(solution)/shard_map/ppermute | solution.py:332
  124.4 17.3 %collective-permute-start.7 = (bf16[768,128]{1,0:T(8,128)(2,1)S(1)}, bf16[768,128]{1,0:T(8,128)(2,1)S(1)}, u32[]{:S(2)}, u32[]{:S(2)}) collective-permute-start(bf16[768,128]{1,0:T(8,128)(2,1)S(1)} %bitcast.50), channel_id=1, source_target_pairs={{0,1},{1,0},{2,3},{3,2},{4,5},{5,4},{6,7},{7,6},{8,9},{9,8},{10,11... | collective-permute-start | bytes 589832 | tf_op jit(solution)/shard_map/ppermute | solution.py:332
  124.4 19.0 %collective-permute-start.8 = (bf16[768,128]{1,0:T(8,128)(2,1)S(1)}, bf16[768,128]{1,0:T(8,128)(2,1)S(1)}, u32[]{:S(2)}, u32[]{:S(2)}) collective-permute-start(bf16[768,128]{1,0:T(8,128)(2,1)S(1)} %bitcast.49), channel_id=1, source_target_pairs={{0,2},{1,3},{2,0},{3,1},{4,6},{5,7},{6,4},{7,5},{8,10},{9,11},{10,... | collective-permute-start | bytes 589832 | tf_op jit(solution)/shard_map/ppermute | solution.py:332
  127.6 15.9 %collective-permute-start.9 = (bf16[768,128]{1,0:T(8,128)(2,1)S(1)}, bf16[768,128]{1,0:T(8,128)(2,1)S(1)}, u32[]{:S(2)}, u32[]{:S(2)}) collective-permute-start(bf16[768,128]{1,0:T(8,128)(2,1)S(1)} %bitcast.48), channel_id=1, source_target_pairs={{0,3},{1,2},{2,1},{3,0},{4,7},{5,6},{6,5},{7,4},{8,11},{9,10},{10,... | collective-permute-start | bytes 589832 | tf_op jit(solution)/shard_map/ppermute | solution.py:332
  141.7 6.6 %collective-permute-start.34 = (bf16[512,128]{1,0:T(8,128)(2,1)S(1)}, bf16[512,128]{1,0:T(8,128)(2,1)S(1)}, u32[]{:S(2)}, u32[]{:S(2)}) collective-permute-start(bf16[512,128]{1,0:T(8,128)(2,1)S(1)} %bitcast.64), channel_id=1, source_target_pairs={{0,1},{1,0},{2,3},{3,2},{4,5},{5,4},{6,7},{7,6},{8,9},{9,8},{10,11... | collective-permute-start | bytes 393224 | tf_op jit(solution)/shard_map/ppermute | solution.py:332
  143.4 10.1 %collective-permute-start.35 = (bf16[512,128]{1,0:T(8,128)(2,1)S(1)}, bf16[512,128]{1,0:T(8,128)(2,1)S(1)}, u32[]{:S(2)}, u32[]{:S(2)}) collective-permute-start(bf16[512,128]{1,0:T(8,128)(2,1)S(1)} %bitcast.63), channel_id=1, source_target_pairs={{0,2},{1,3},{2,0},{3,1},{4,6},{5,7},{6,4},{7,5},{8,10},{9,11},{10,... | collective-permute-start | bytes 393224 | tf_op jit(solution)/shard_map/ppermute | solution.py:332
  143.4 12.0 %collective-permute-start.36 = (bf16[512,128]{1,0:T(8,128)(2,1)S(1)}, bf16[512,128]{1,0:T(8,128)(2,1)S(1)}, u32[]{:S(2)}, u32[]{:S(2)}) collective-permute-start(bf16[512,128]{1,0:T(8,128)(2,1)S(1)} %bitcast.62), channel_id=1, source_target_pairs={{0,3},{1,2},{2,1},{3,0},{4,7},{5,6},{6,5},{7,4},{8,11},{9,10},{10,... | collective-permute-start | bytes 393224 | tf_op jit(solution)/shard_map/ppermute | solution.py:332
  148.4 85.7 %collective-permute-start.43 = (bf16[24,2,16,683]{3,2,1,0:T(8,128)(2,1)S(1)}, bf16[24,2,16,683]{3,2,1,0:T(8,128)(2,1)S(1)}, u32[]{:S(2)}, u32[]{:S(2)}) collective-permute-start(bf16[24,2,16,683]{3,2,1,0:T(8,128)(2,1)S(1)} %get-tuple-element.121.own), channel_id=1, source_target_pairs={{0,8},{8,16},{16,24},{1,9},{9,17},{17,25},{2,10},{10,18},{18,26},{... | collective-permute-start | bytes 3147272 | tf_op jit(solution)/shard_map/ppermute | solution.py:342
  153.5 82.5 %collective-permute-start.44 = (bf16[24,2,16,683]{3,2,1,0:T(8,128)(2,1)S(1)}, bf16[24,2,16,683]{3,2,1,0:T(8,128)(2,1)S(1)}, u32[]{:S(2)}, u32[]{:S(2)}) collective-permute-start(bf16[24,2,16,683]{3,2,1,0:T(8,128)(2,1)S(1)} %get-tuple-element.121.own), channel_id=1, source_target_pairs={{8,0},{16,8},{24,16},{9,1},{17,9},{25,17},{10,2},{18,10},{26,18},{... | collective-permute-start | bytes 3147272 | tf_op jit(solution)/shard_map/ppermute | solution.py:343
  155.4 6.4 %collective-permute-start.37 = (bf16[512,128]{1,0:T(8,128)(2,1)S(1)}, bf16[512,128]{1,0:T(8,128)(2,1)S(1)}, u32[]{:S(2)}, u32[]{:S(2)}) collective-permute-start(bf16[512,128]{1,0:T(8,128)(2,1)S(1)} %bitcast.61), channel_id=1, source_target_pairs={{0,4},{1,5},{2,6},{3,7},{4,0},{5,1},{6,2},{7,3},{8,12},{9,13},{10,... | collective-permute-start | bytes 393224 | tf_op jit(solution)/shard_map/ppermute | solution.py:332
  161.8 19.2 %collective-permute-start.38 = (bf16[512,128]{1,0:T(8,128)(2,1)S(1)}, bf16[512,128]{1,0:T(8,128)(2,1)S(1)}, u32[]{:S(2)}, u32[]{:S(2)}) collective-permute-start(bf16[512,128]{1,0:T(8,128)(2,1)S(1)} %bitcast.60), channel_id=1, source_target_pairs={{0,5},{1,4},{2,7},{3,6},{4,1},{5,0},{6,3},{7,2},{8,13},{9,12},{10,... | collective-permute-start | bytes 393224 | tf_op jit(solution)/shard_map/ppermute | solution.py:332
  162.3 19.5 %collective-permute-start.39 = (bf16[512,128]{1,0:T(8,128)(2,1)S(1)}, bf16[512,128]{1,0:T(8,128)(2,1)S(1)}, u32[]{:S(2)}, u32[]{:S(2)}) collective-permute-start(bf16[512,128]{1,0:T(8,128)(2,1)S(1)} %bitcast.59), channel_id=1, source_target_pairs={{0,6},{1,7},{2,4},{3,5},{4,2},{5,3},{6,0},{7,1},{8,14},{9,15},{10,... | collective-permute-start | bytes 393224 | tf_op jit(solution)/shard_map/ppermute | solution.py:332
  164.0 17.9 %collective-permute-start.40 = (bf16[512,128]{1,0:T(8,128)(2,1)S(1)}, bf16[512,128]{1,0:T(8,128)(2,1)S(1)}, u32[]{:S(2)}, u32[]{:S(2)}) collective-permute-start(bf16[512,128]{1,0:T(8,128)(2,1)S(1)} %bitcast.58), channel_id=1, source_target_pairs={{0,7},{1,6},{2,5},{3,4},{4,3},{5,2},{6,1},{7,0},{8,15},{9,14},{10,... | collective-permute-start | bytes 393224 | tf_op jit(solution)/shard_map/ppermute | solution.py:332
  181.0 11.6 %collective-permute-start.25 = (bf16[256,128]{1,0:T(8,128)(2,1)S(1)}, bf16[256,128]{1,0:T(8,128)(2,1)S(1)}, u32[]{:S(2)}, u32[]{:S(2)}) collective-permute-start(bf16[256,128]{1,0:T(8,128)(2,1)S(1)} %bitcast.71), channel_id=1, source_target_pairs={{0,1},{1,0},{2,3},{3,2},{4,5},{5,4},{6,7},{7,6},{8,9},{9,8},{10,11... | collective-permute-start | bytes 196616 | tf_op jit(solution)/shard_map/ppermute | solution.py:332
  184.9 57.3 %collective-permute-start.41 = (bf16[16,2,16,683]{3,2,1,0:T(8,128)(2,1)S(1)}, bf16[16,2,16,683]{3,2,1,0:T(8,128)(2,1)S(1)}, u32[]{:S(2)}, u32[]{:S(2)}) collective-permute-start(bf16[16,2,16,683]{3,2,1,0:T(8,128)(2,1)S(1)} %get-tuple-element.120.own), channel_id=1, source_target_pairs={{0,8},{8,16},{16,24},{1,9},{9,17},{17,25},{2,10},{10,18},{18,26},{... | collective-permute-start | bytes 2098184 | tf_op jit(solution)/shard_map/ppermute | solution.py:342
  190.7 51.5 %collective-permute-start.42 = (bf16[16,2,16,683]{3,2,1,0:T(8,128)(2,1)S(1)}, bf16[16,2,16,683]{3,2,1,0:T(8,128)(2,1)S(1)}, u32[]{:S(2)}, u32[]{:S(2)}) collective-permute-start(bf16[16,2,16,683]{3,2,1,0:T(8,128)(2,1)S(1)} %get-tuple-element.120.own), channel_id=1, source_target_pairs={{8,0},{16,8},{24,16},{9,1},{17,9},{25,17},{10,2},{18,10},{26,18},{... | collective-permute-start | bytes 2098184 | tf_op jit(solution)/shard_map/ppermute | solution.py:343
  192.6 3.2 %collective-permute-start.26 = (bf16[256,128]{1,0:T(8,128)(2,1)S(1)}, bf16[256,128]{1,0:T(8,128)(2,1)S(1)}, u32[]{:S(2)}, u32[]{:S(2)}) collective-permute-start(bf16[256,128]{1,0:T(8,128)(2,1)S(1)} %bitcast.70), channel_id=1, source_target_pairs={{0,2},{1,3},{2,0},{3,1},{4,6},{5,7},{6,4},{7,5},{8,10},{9,11},{10,... | collective-permute-start | bytes 196616 | tf_op jit(solution)/shard_map/ppermute | solution.py:332
  195.8 4.0 %collective-permute-start.27 = (bf16[256,128]{1,0:T(8,128)(2,1)S(1)}, bf16[256,128]{1,0:T(8,128)(2,1)S(1)}, u32[]{:S(2)}, u32[]{:S(2)}) collective-permute-start(bf16[256,128]{1,0:T(8,128)(2,1)S(1)} %bitcast.69), channel_id=1, source_target_pairs={{0,3},{1,2},{2,1},{3,0},{4,7},{5,6},{6,5},{7,4},{8,11},{9,10},{10,... | collective-permute-start | bytes 196616 | tf_op jit(solution)/shard_map/ppermute | solution.py:332
  199.8 4.9 %collective-permute-start.28 = (bf16[256,128]{1,0:T(8,128)(2,1)S(1)}, bf16[256,128]{1,0:T(8,128)(2,1)S(1)}, u32[]{:S(2)}, u32[]{:S(2)}) collective-permute-start(bf16[256,128]{1,0:T(8,128)(2,1)S(1)} %bitcast.68), channel_id=1, source_target_pairs={{0,4},{1,5},{2,6},{3,7},{4,0},{5,1},{6,2},{7,3},{8,12},{9,13},{10,... | collective-permute-start | bytes 196616 | tf_op jit(solution)/shard_map/ppermute | solution.py:332
  204.7 6.8 %collective-permute-start.29 = (bf16[256,128]{1,0:T(8,128)(2,1)S(1)}, bf16[256,128]{1,0:T(8,128)(2,1)S(1)}, u32[]{:S(2)}, u32[]{:S(2)}) collective-permute-start(bf16[256,128]{1,0:T(8,128)(2,1)S(1)} %bitcast.67), channel_id=1, source_target_pairs={{0,5},{1,4},{2,7},{3,6},{4,1},{5,0},{6,3},{7,2},{8,13},{9,12},{10,... | collective-permute-start | bytes 196616 | tf_op jit(solution)/shard_map/ppermute | solution.py:332
  211.6 5.0 %collective-permute-start.30 = (bf16[256,128]{1,0:T(8,128)(2,1)S(1)}, bf16[256,128]{1,0:T(8,128)(2,1)S(1)}, u32[]{:S(2)}, u32[]{:S(2)}) collective-permute-start(bf16[256,128]{1,0:T(8,128)(2,1)S(1)} %bitcast.66), channel_id=1, source_target_pairs={{0,6},{1,7},{2,4},{3,5},{4,2},{5,3},{6,0},{7,1},{8,14},{9,15},{10,... | collective-permute-start | bytes 196616 | tf_op jit(solution)/shard_map/ppermute | solution.py:332
  216.5 5.8 %collective-permute-start.31 = (bf16[256,128]{1,0:T(8,128)(2,1)S(1)}, bf16[256,128]{1,0:T(8,128)(2,1)S(1)}, u32[]{:S(2)}, u32[]{:S(2)}) collective-permute-start(bf16[256,128]{1,0:T(8,128)(2,1)S(1)} %bitcast.65), channel_id=1, source_target_pairs={{0,7},{1,6},{2,5},{3,4},{4,3},{5,2},{6,1},{7,0},{8,15},{9,14},{10,... | collective-permute-start | bytes 196616 | tf_op jit(solution)/shard_map/ppermute | solution.py:332
  224.4 22.3 %collective-permute-start.32 = (bf16[8,2,16,683]{3,2,1,0:T(8,128)(2,1)S(1)}, bf16[8,2,16,683]{3,2,1,0:T(8,128)(2,1)S(1)}, u32[]{:S(2)}, u32[]{:S(2)}) collective-permute-start(bf16[8,2,16,683]{3,2,1,0:T(8,128)(2,1)S(1)} %get-tuple-element.109.own), channel_id=1, source_target_pairs={{0,8},{8,16},{16,24},{1,9},{9,17},{17,25},{2,10},{10,18},{18,26},{... | collective-permute-start | bytes 1049096 | tf_op jit(solution)/shard_map/ppermute | solution.py:342
  234.0 12.7 %collective-permute-start.33 = (bf16[8,2,16,683]{3,2,1,0:T(8,128)(2,1)S(1)}, bf16[8,2,16,683]{3,2,1,0:T(8,128)(2,1)S(1)}, u32[]{:S(2)}, u32[]{:S(2)}) collective-permute-start(bf16[8,2,16,683]{3,2,1,0:T(8,128)(2,1)S(1)} %get-tuple-element.109.own), channel_id=1, source_target_pairs={{8,0},{16,8},{24,16},{9,1},{17,9},{25,17},{10,2},{18,10},{26,18},{... | collective-permute-start | bytes 1049096 | tf_op jit(solution)/shard_map/ppermute | solution.py:343
  (7 other events, 22.8 us)

commit v3 on v2

--- a/solution.py
+++ b/solution.py
@@ -73,11 +73,11 @@
 def zonal_kernel(
     fields_step, fields, tokens, cos_c, sin_c, cos_f, sin_f, velocity, tracer, *rest
 ):
-    outs, (table, total) = rest[tokens:-2], rest[-2:]
+    out, table, total = rest[tokens:]
     step = pl.program_id(0)
     rows = cos_f.shape[0]
     lat_local, longitudes = velocity.shape[2:]
-    out_rows = outs[0].shape[1]
+    out_rows = out.shape[1]
 
     @pl.when(step == 0)
     def _():
@@ -105,19 +105,15 @@
 
     @pl.when(step == pl.num_programs(0) - 1)
     def _():
-        for at, out in enumerate(outs):
-            size = out.shape[0] * out_rows
-            part = total[at * size : (at + 1) * size, :]
-            out[...] = part.reshape(out.shape).astype(out.dtype)
-
-
-def zonal_transform(factors, velocity, tracer, pieces, tokens):
+        out[...] = total[...].reshape(out.shape).astype(out.dtype)
+
+
+def zonal_transform(factors, velocity, tracer, tokens):
     mem_local, fields, lat_local, longitudes = velocity.shape
     rows = factors[0].shape[0]
     fields_step = min(fields, max(1, 512 // lat_local))
     steps = fields // fields_step
     out_rows = mem_local * 2 * fields
-    piece = (rows // pieces, out_rows, lat_local)
     whole = lambda step: (0, 0)
     grid_block = pl.BlockSpec(
         (1, fields_step, lat_local, longitudes), lambda step: (step // steps, step % steps, 0, 0)
@@ -130,8 +126,8 @@
         in_specs=[pl.BlockSpec(f.shape, whole) for f in factors]
         + [grid_block, grid_block]
         + [pl.BlockSpec(memory_space=pl.ANY)] * len(tokens),
-        out_specs=[pl.BlockSpec(piece, lambda step: (0, 0, 0))] * pieces,
-        out_shape=[jax.ShapeDtypeStruct(piece, jnp.bfloat16)] * pieces,
+        out_specs=pl.BlockSpec((rows, out_rows, lat_local), lambda step: (0, 0, 0)),
+        out_shape=jax.ShapeDtypeStruct((rows, out_rows, lat_local), jnp.bfloat16),
         scratch_shapes=[
             pltpu.VMEM((2 * rows, longitudes), jnp.bfloat16),
             pltpu.VMEM((rows * out_rows, lat_local), jnp.float32),
@@ -142,12 +138,11 @@
     )(*factors, velocity, tracer, *tokens)
 
 
-def forward_kernel(first, block, waves, *refs):
-    received, (even, odd, out, token) = refs[:-4], refs[-4:]
+def forward_kernel(first, block, waves, received, even, odd, out, token):
     truncation = even.shape[0]
     step = pl.program_id(0)
-    per_slot = received[0].shape[0] // block
-    rows = jnp.concatenate([piece[...] for piece in received], axis=-1)
+    per_slot = received.shape[1] // block
+    rows = jnp.concatenate([received[g] for g in range(received.shape[0])], axis=-1)
     contract = (((1,), (1,)), ((), ()))
     by_even = lax.dot_general(rows, even[...], contract, preferred_element_type=jnp.float32)
     by_odd = lax.dot_general(rows, odd[...], contract, preferred_element_type=jnp.float32)
@@ -163,7 +158,7 @@
 
 
 def forward_transform(waves, first, block, received, even, odd, mem_local):
-    all_rows, lat_local = received[0].shape
+    groups, all_rows, lat_local = received.shape
     truncation, latitudes = even.shape
     slots = all_rows // (waves[1] * mem_local)
     out_shape = (slots, mem_local, waves[1], truncation)
@@ -174,9 +169,11 @@
         grid_spec=pltpu.PrefetchScalarGridSpec(
             num_scalar_prefetch=1,
             grid=(slots // block,),
-            in_specs=[pl.BlockSpec((per_block, lat_local), lambda step, w: (step, 0))]
-            * len(received)
-            + [table, table],
+            in_specs=[
+                pl.BlockSpec((groups, per_block, lat_local), lambda step, w: (0, step, 0)),
+                table,
+                table,
+            ],
             out_specs=[
                 pl.BlockSpec((block,) + out_shape[1:], lambda step, w: (step, 0, 0, 0)),
                 pl.BlockSpec(TOKEN, lambda step, w: (0, 0)),
@@ -193,7 +190,7 @@
             transcendentals=0,
         ),
         name="forward",
-    )(waves[0], *received, even, odd)
+    )(waves[0], received, even, odd)
 
 
 def inverse_kernel(first, block, waves, offsets, low, own, high, noise, even, odd, *rest):
@@ -286,7 +283,7 @@
 
 def chunk_bounds(slots_here, block):
     blocks = slots_here // block
-    edges = [0, 2, 5, 8, 10, 11]
+    edges = [0, 2, 6, 9, 11]
     if blocks < edges[-1]:
         edges = list(range(blocks + 1))
     edges[-1] = blocks
@@ -310,14 +307,12 @@
     offsets = own_parents - first_member + SPREAD
     upward = [(i, i + 1) for i in range(mem_count - 1)]
     downward = [(target, source) for source, target in upward]
-    partners = jnp.arange(lat_count, dtype=jnp.int32) ^ lat_index
-    slot_grid = wave_slots.reshape(lat_count, slots_here)[partners]
+    slot_grid = wave_slots.reshape(lat_count, slots_here)
     bounds = chunk_bounds(slots_here, block)
     count = len(bounds)
     inner = min(lat_local, LANES)
-    order = jnp.arange(latitudes // inner, dtype=jnp.int32) * inner
-    swapped = (partners[:, None] * lat_local + jnp.arange(0, lat_local, inner)[None, :]).reshape(-1)
-    received, own, edges, tokens = {}, {}, {}, {}
+    starts = jnp.arange(latitudes // inner, dtype=jnp.int32) * inner
+    received, own, tokens = {}, {}, {}
     outs = None
 
     def send(at):
@@ -325,19 +320,18 @@
         waves = slot_grid[:, start:stop].reshape(-1)
         factors = zonal_factors(waves, longitudes, truncation)
         after = [tokens[key] for key in (("f", at - 2), ("i", at - 3)) if key in tokens]
-        pieces = zonal_transform(factors, velocity, tracer, lat_count, after)
-        pieces = [piece.reshape(-1, lat_local) for piece in pieces]
-        moved = [pieces[0]] + [None] * (lat_count - 1)
-        for k in reversed(range(1, lat_count)):
-            moved[k] = lax.ppermute(pieces[k], "lat", [(i, i ^ k) for i in range(lat_count)])
+        outgoing = zonal_transform(factors, velocity, tracer, after)
+        rows = (stop - start) * per_slot
+        outgoing = outgoing.reshape(lat_count, rows, lat_local)
+        moved = lax.all_to_all(outgoing, "lat", split_axis=0, concat_axis=0, tiled=True)
         if lat_local % LANES != 0:
-            moved = [jnp.concatenate(moved, axis=-1)]
+            moved = jnp.swapaxes(moved, 0, 1).reshape(1, rows, latitudes)
         received[at] = moved
 
     def forward(at):
         start, _ = bounds[at]
         spectra, tokens["f", at] = forward_transform(
-            (own_waves, 2 * fields), start, block, received[at], even_swapped, odd_swapped, mem_local
+            (own_waves, 2 * fields), start, block, received[at], even, odd, mem_local
         )
         low = lax.ppermute(spectra[:, mem_local - SPREAD :], "member", upward)
         high = lax.ppermute(spectra[:, :SPREAD], "member", downward)
@@ -351,8 +345,7 @@
         return outs
 
     send(0)
-    even_swapped, odd_swapped = meridional_tables(truncation, latitudes, swapped, inner)
-    even, odd = meridional_tables(truncation, latitudes, order, inner)
+    even, odd = meridional_tables(truncation, latitudes, starts, inner)
     if count > 1:
         send(1)
     for at in range(count):

time: 251 us -> 199 us (0.79)
  starting transfers between devices: 98.8 us -> 43.8 us
  waiting for transfers between devices: 40.4 us -> 51 us
  Pallas kernels: 94.9 us -> 86.2 us
  local copies, waits for them, and re-layouts: 7.08 us -> 10.1 us
    ppermute x35 -> x0, starting transfers between devices: 49.5 us -> none  [send(): lax.ppermute(pieces[k], 'lat', [(i, i ^ k) for i in range(lat_count)])]
    ppermute x35 -> x0, waiting for transfers between devices: 40.4 us -> none  [send(): lax.ppermute(pieces[k], 'lat', [(i, i ^ k) for i in range(lat_count)])]
    all_to_all x0 -> x4, waiting for transfers between devices: none -> 40 us  [send(): lax.all_to_all(outgoing, 'lat', split_axis=0, concat_axis=0, tiled=True)]
    ppermute x5 -> x4, starting transfers between devices: 34.1 us -> 10.4 us  [forward(): low = lax.ppermute(spectra[:, mem_local - SPREAD:], 'member', upward)]
    all_to_all x0 -> x4, starting transfers between devices: none -> 22 us  [send(): lax.all_to_all(outgoing, 'lat', split_axis=0, concat_axis=0, tiled=True)]
    pallas_call x5 -> x4, Pallas kernels: 49.1 us -> 42.6 us  [zonal_transform(): pl.pallas_call(functools.partial(zonal_kernel, fields_step, fields, len(t...]
    ppermute x5 -> x4, waiting for transfers between devices: 0.01 us -> 6.29 us  [forward(): low = lax.ppermute(spectra[:, mem_local - SPREAD:], 'member', upward)]
    ppermute x5 -> x4, waiting for transfers between devices: 0.01 us -> 4.7 us  [forward(): high = lax.ppermute(spectra[:, :SPREAD], 'member', downward)]
  transfers between devices with their start and end apart: 45 -> 12, of which waited for: 10 -> 5; matrix products, arithmetic and copies ran while one was open for 4% -> 4% of each run, Pallas kernels for 33% -> 36%
where the time goes in v3:
time: 199 us; the launch traced here: 198 us
  Pallas kernels  86.2 us (43%)
  waiting for transfers between devices  51 us (26%)
  starting transfers between devices  43.8 us (22%)
  local copies, waits for them, and re-layouts  10.1 us (5%)
  other arithmetic  6.22 us (3%)
    pallas_call x4, Pallas kernels, zonal_transform(): pl.pallas_call(functools.partial(zonal_kernel, fields_step, fields, len(t...  42.6 us
    all_to_all x4, waiting for transfers between devices, send(): lax.all_to_all(outgoing, 'lat', split_axis=0, concat_axis=0, tiled=True)  40 us
    pallas_call x4, Pallas kernels, inverse_transform(): pl.pallas_call(functools.partial(inverse_kernel, first, block), grid_spec...  23.8 us
    all_to_all x4, starting transfers between devices, send(): lax.all_to_all(outgoing, 'lat', split_axis=0, concat_axis=0, tiled=True)  22 us
    pallas_call x4, Pallas kernels, forward_transform(): pl.pallas_call(functools.partial(forward_kernel, first, block), grid_spec...  18.1 us
    ppermute x4, starting transfers between devices, forward(): high = lax.ppermute(spectra[:, :SPREAD], 'member', downward)  11.5 us
    ppermute x4, starting transfers between devices, forward(): low = lax.ppermute(spectra[:, mem_local - SPREAD:], 'member', upward)  10.4 us
    unnamed x22, local copies, waits for them, and re-layouts  7.49 us
  transfers between devices with their start and end apart: 12, of which 5 were waited for; matrix products, arithmetic and copies ran while one was open for 4% of the time, Pallas kernels for 36%

profile of v3, /device:TPU:1, one launch (start us, length us, event | category | flops | bytes accessed | tf_op | source)
XLA Modules:
  0.0 198.3 jit_solution(12468260470224430237)
XLA Ops:
  0.6 0.8 reshape.64
  1.6 0.3 fusion.36
  2.4 9.9 %zonal.5 = bf16[128,32,128]{2,1,0:T(8,128)(2,1)} custom-call(f32[128,16]{1,0:T(8,128)S(1)} %get-tuple-element.43.cos_c, f32[128,16]{1,0:T(8,128)S(1)} %get-tuple-element.42.sin_c, f32[128,128]{1,0:T(8,128)S(1)} %get-tuple-element.53.cos_f, f32[128,128]{1,0:T(8,128)S(1)} %get-tuple-element.52.sin_f, bf16[2,8,128,2048]{3,2,1,0:T(8,128)(2,1)} %velocity.7, ...), custom_call_target="tpu_custom_call" | custom-call | flops 2147483648 | bytes 17825792 | tf_op jit(solution)/shard_map/zonal/pallas_call | solution.py:123
  12.4 6.4 %all-to-all-start.1 = ((bf16[8,512,128]{2,1,0:T(8,128)(2,1)}), bf16[8,512,128]{2,1,0:T(8,128)(2,1)S(1)}, u32[]{:S(2)}, u32[]{:S(2)}) async-start(bf16[8,512,128]{2,1,0:T(8,128)(2,1)} %bitcast.1), calls=%async_computation.1 | async-start | bytes 2097152 | tf_op jit(solution)/shard_map/all_to_all | solution.py:326
  19.1 0.6 fusion.28
  19.7 0.5 sine_multiply_fusion.1
  20.2 13.2 %zonal.4 = bf16[256,32,128]{2,1,0:T(8,128)(2,1)} custom-call(f32[256,16]{1,0:T(8,128)S(1)} %get-tuple-element.39.cos_c, f32[256,16]{1,0:T(8,128)S(1)} %get-tuple-element.38.sin_c, f32[256,128]{1,0:T(8,128)S(1)} %get-tuple-element.51.cos_f, f32[256,128]{1,0:T(8,128)S(1)} %get-tuple-element.50.sin_f, bf16[2,8,128,2048]{3,2,1,0:T(8,128)(2,1)} %velocity.7, ...), custom_call_target="tpu_custom_call" | custom-call | flops 4294967296 | bytes 18874368 | tf_op jit(solution)/shard_map/zonal/pallas_call | solution.py:123
  33.4 10.0 %all-to-all-done.1.received = bf16[8,512,128]{2,1,0:T(8,128)(2,1)S(1)} async-done(((bf16[8,512,128]{2,1,0:T(8,128)(2,1)}), bf16[8,512,128]{2,1,0:T(8,128)(2,1)S(1)}, u32[]{:S(2)}, u32[]{:S(2)}) %all-to-all-start.1) | async-done | bytes 1048608 | tf_op jit(solution)/shard_map/all_to_all | solution.py:326
  43.4 1.0 copy-done.6
  44.4 4.9 %all-to-all-start = ((bf16[8,1024,128]{2,1,0:T(8,128)(2,1)}), bf16[8,1024,128]{2,1,0:T(8,128)(2,1)}, u32[]{:S(2)}, u32[]{:S(2)}) async-start(bf16[8,1024,128]{2,1,0:T(8,128)(2,1)} %bitcast), calls=%async_computation | async-start | bytes 4194304 | tf_op jit(solution)/shard_map/all_to_all | solution.py:326
  49.4 0.8 dynamic_slice.6.waves
  50.7 1.4 fusion.6
  52.0 1.3 sine_multiply_fusion
  53.4 1.8 tables.1
  55.2 0.5 fusion.34
  55.6 0.4 sine_multiply_fusion.2
  56.0 1.2 copy-done.7
  57.2 2.7 %forward.5 = (bf16[16,2,16,683]{3,2,1,0:T(8,128)(2,1)S(1)}, f32[8,128]{1,0:T(8,128)S(1)}) custom-call(s32[88]{0:T(128)S(1)} %dynamic_slice.6.waves, bf16[8,512,128]{2,1,0:T(8,128)(2,1)S(1)} %copy-done.7, bf16[683,1024]{1,0:T(8,128)(2,1)S(1)} %get-tuple-element.19.even, bf16[683,1024]{1,0:T(8,128)(2,1)S(1)} %get-tuple-element.20.odd), custom_call_target="tpu_custom_call" | custom-call | flops 1432354816 | bytes 4545536 | tf_op jit(solution)/shard_map/forward/pallas_call | solution.py:167
  60.0 0.9 copy-done.8
  60.8 10.4 %zonal.7 = bf16[192,32,128]{2,1,0:T(8,128)(2,1)S(1)} custom-call(f32[192,16]{1,0:T(8,128)S(1)} %get-tuple-element.41.cos_c, f32[192,16]{1,0:T(8,128)S(1)} %get-tuple-element.40.sin_c, f32[192,128]{1,0:T(8,128)S(1)} %get-tuple-element.49.cos_f, f32[192,128]{1,0:T(8,128)S(1)} %get-tuple-element.48.sin_f, bf16[2,8,128,2048]{3,2,1,0:T(8,128)(2,1)} %velocity.7, ...), custom_call_target="tpu_custom_call" | custom-call | flops 3221225472 | bytes 18350080 | tf_op jit(solution)/shard_map/zonal/pallas_call | solution.py:123
  71.2 1.1 copy-done.2
  72.4 24.0 %all-to-all-done.received = bf16[8,1024,128]{2,1,0:T(8,128)(2,1)} async-done(((bf16[8,1024,128]{2,1,0:T(8,128)(2,1)}), bf16[8,1024,128]{2,1,0:T(8,128)(2,1)}, u32[]{:S(2)}, u32[]{:S(2)}) %all-to-all-start) | async-done | bytes 2097184 | tf_op jit(solution)/shard_map/all_to_all | solution.py:326
  96.4 5.1 %all-to-all-start.3 = ((bf16[8,768,128]{2,1,0:T(8,128)(2,1)}), bf16[8,768,128]{2,1,0:T(8,128)(2,1)}, u32[]{:S(2)}, u32[]{:S(2)}) async-start(bf16[8,768,128]{2,1,0:T(8,128)(2,1)} %bitcast.4), calls=%async_computation.3 | async-start | bytes 3145728 | tf_op jit(solution)/shard_map/all_to_all | solution.py:326
  101.4 4.5 %collective-permute-start = (bf16[16,2,16,683]{3,2,1,0:T(8,128)(2,1)}, bf16[16,2,16,683]{3,2,1,0:T(8,128)(2,1)}, u32[]{:S(2)}, u32[]{:S(2)}) collective-permute-start(bf16[16,2,16,683]{3,2,1,0:T(8,128)(2,1)} %copy-done.8), channel_id=1, source_target_pairs={{0,8},{8,16},{16,24},{1,9},{9,17},{17,25},{2,10},{10,18},{18,26},{... | collective-permute-start | bytes 2098184 | tf_op jit(solution)/shard_map/ppermute | solution.py:336
  106.0 2.1 %collective-permute-start.1 = (bf16[16,2,16,683]{3,2,1,0:T(8,128)(2,1)}, bf16[16,2,16,683]{3,2,1,0:T(8,128)(2,1)}, u32[]{:S(2)}, u32[]{:S(2)}) collective-permute-start(bf16[16,2,16,683]{3,2,1,0:T(8,128)(2,1)} %copy-done.8), channel_id=1, source_target_pairs={{8,0},{16,8},{24,16},{9,1},{17,9},{25,17},{10,2},{18,10},{26,18},{... | collective-permute-start | bytes 2098184 | tf_op jit(solution)/shard_map/ppermute | solution.py:337
  108.3 0.3 fusion.38
  108.7 0.2 sine_multiply_fusion.4
  108.9 6.3 %collective-permute-done.low = bf16[16,2,16,683]{3,2,1,0:T(8,128)(2,1)} collective-permute-done((bf16[16,2,16,683]{3,2,1,0:T(8,128)(2,1)}, bf16[16,2,16,683]{3,2,1,0:T(8,128)(2,1)}, u32[]{:S(2)}, u32[]{:S(2)}) %collective-permute-start) | collective-permute-done | bytes 699424 | tf_op jit(solution)/shard_map/ppermute | solution.py:336
  115.2 4.7 %collective-permute-done.1.high = bf16[16,2,16,683]{3,2,1,0:T(8,128)(2,1)} collective-permute-done((bf16[16,2,16,683]{3,2,1,0:T(8,128)(2,1)}, bf16[16,2,16,683]{3,2,1,0:T(8,128)(2,1)}, u32[]{:S(2)}, u32[]{:S(2)}) %collective-permute-start.1) | collective-permute-done | bytes 699424 | tf_op jit(solution)/shard_map/ppermute | solution.py:337
  119.9 1.1 copy-done.9
  121.0 4.7 %inverse.4 = (bf16[88,2,2,8,683]{4,3,2,1,0:T(8,128)(2,1)}, bf16[88,2,2,8,1024]{4,3,2,1,0:T(8,128)(2,1)}, f32[8,128]{1,0:T(8,128)S(1)}) custom-call(s32[88]{0:T(128)S(1)} %dynamic_slice.6.waves, s32[2]{0:T(128)S(1)} %subtract_add_fusion.offsets, bf16[16,2,16,683]{3,2,1,0:T(8,128)(2,1)} %collective-permute-done.low, bf16[16,2,16,683]{3,2,1,0:T(8,128)(2,1)S(1)} %copy-done.9, ...), custom_call_target="tpu_custom_call" | custom-call | flops 1432354816 | bytes 7343104 | tf_op jit(solution)/shard_map/inverse/pallas_call | solution.py:256
  125.8 5.7 %forward.4 = (bf16[32,2,16,683]{3,2,1,0:T(8,128)(2,1)S(1)}, f32[8,128]{1,0:T(8,128)S(1)}) custom-call(s32[88]{0:T(128)S(1)} %dynamic_slice.6.waves, bf16[8,1024,128]{2,1,0:T(8,128)(2,1)} %all-to-all-done.received, bf16[683,1024]{1,0:T(8,128)(2,1)S(1)} %get-tuple-element.19.even, bf16[683,1024]{1,0:T(8,128)(2,1)S(1)} %get-tuple-element.20.odd), custom_call_target="tpu_custom_call" | custom-call | flops 2864709632 | bytes 6293504 | tf_op jit(solution)/shard_map/forward/pallas_call | solution.py:167
  131.5 1.1 copy-done.4
  132.7 9.0 %zonal.6 = bf16[128,32,128]{2,1,0:T(8,128)(2,1)S(1)} custom-call(f32[128,16]{1,0:T(8,128)S(1)} %get-tuple-element.45.cos_c, f32[128,16]{1,0:T(8,128)S(1)} %get-tuple-element.44.sin_c, f32[128,128]{1,0:T(8,128)S(1)} %get-tuple-element.59.cos_f, f32[128,128]{1,0:T(8,128)S(1)} %get-tuple-element.58.sin_f, bf16[2,8,128,2048]{3,2,1,0:T(8,128)(2,1)} %velocity.7, ...), custom_call_target="tpu_custom_call" | custom-call | flops 2147483648 | bytes 17825792 | tf_op jit(solution)/shard_map/zonal/pallas_call | solution.py:123
  141.7 1.0 copy-done.3
  142.7 5.6 %all-to-all-start.2 = ((bf16[8,512,128]{2,1,0:T(8,128)(2,1)}), bf16[8,512,128]{2,1,0:T(8,128)(2,1)}, u32[]{:S(2)}, u32[]{:S(2)}) async-start(bf16[8,512,128]{2,1,0:T(8,128)(2,1)} %bitcast.5), calls=%async_computation.2 | async-start | bytes 2097152 | tf_op jit(solution)/shard_map/all_to_all | solution.py:326
  148.3 1.9 collective-permute-start.6
  150.2 3.5 %collective-permute-start.7 = (bf16[32,2,16,683]{3,2,1,0:T(8,128)(2,1)}, bf16[32,2,16,683]{3,2,1,0:T(8,128)(2,1)}, u32[]{:S(2)}, u32[]{:S(2)}) collective-permute-start(bf16[32,2,16,683]{3,2,1,0:T(8,128)(2,1)} %copy-done.4), channel_id=1, source_target_pairs={{8,0},{16,8},{24,16},{9,1},{17,9},{25,17},{10,2},{18,10},{26,18},{... | collective-permute-start | bytes 4196360 | tf_op jit(solution)/shard_map/ppermute | solution.py:337
  153.7 5.6 %forward.7 = (bf16[24,2,16,683]{3,2,1,0:T(8,128)(2,1)}, f32[8,128]{1,0:T(8,128)}) custom-call(s32[88]{0:T(128)S(1)} %dynamic_slice.6.waves, bf16[8,768,128]{2,1,0:T(8,128)(2,1)} %all-to-all-done.3.received, bf16[683,1024]{1,0:T(8,128)(2,1)S(1)} %get-tuple-element.19.even, bf16[683,1024]{1,0:T(8,128)(2,1)S(1)} %get-tuple-element.20.odd), custom_call_target="tpu_custom_call" | custom-call | flops 2148532224 | bytes 5419520 | tf_op jit(solution)/shard_map/forward/pallas_call | solution.py:167
  159.3 2.0 %collective-permute-start.4 = (bf16[24,2,16,683]{3,2,1,0:T(8,128)(2,1)}, bf16[24,2,16,683]{3,2,1,0:T(8,128)(2,1)}, u32[]{:S(2)}, u32[]{:S(2)}) collective-permute-start(bf16[24,2,16,683]{3,2,1,0:T(8,128)(2,1)} %get-tuple-element.26.own), channel_id=1, source_target_pairs={{0,8},{8,16},{16,24},{1,9},{9,17},{17,25},{2,10},{10,18},{18,26},{... | collective-permute-start | bytes 3147272 | tf_op jit(solution)/shard_map/ppermute | solution.py:336
  161.3 3.3 %collective-permute-start.5 = (bf16[24,2,16,683]{3,2,1,0:T(8,128)(2,1)}, bf16[24,2,16,683]{3,2,1,0:T(8,128)(2,1)}, u32[]{:S(2)}, u32[]{:S(2)}) collective-permute-start(bf16[24,2,16,683]{3,2,1,0:T(8,128)(2,1)} %get-tuple-element.26.own), channel_id=1, source_target_pairs={{8,0},{16,8},{24,16},{9,1},{17,9},{25,17},{10,2},{18,10},{26,18},{... | collective-permute-start | bytes 3147272 | tf_op jit(solution)/shard_map/ppermute | solution.py:337
  164.7 6.0 %all-to-all-done.2.received = bf16[8,512,128]{2,1,0:T(8,128)(2,1)} async-done(((bf16[8,512,128]{2,1,0:T(8,128)(2,1)}), bf16[8,512,128]{2,1,0:T(8,128)(2,1)}, u32[]{:S(2)}, u32[]{:S(2)}) %all-to-all-start.2) | async-done | bytes 1048608 | tf_op jit(solution)/shard_map/all_to_all | solution.py:326
  170.7 4.1 %forward.6 = (bf16[16,2,16,683]{3,2,1,0:T(8,128)(2,1)S(1)}, f32[8,128]{1,0:T(8,128)}) custom-call(s32[88]{0:T(128)S(1)} %dynamic_slice.6.waves, bf16[8,512,128]{2,1,0:T(8,128)(2,1)} %all-to-all-done.2.received, bf16[683,1024]{1,0:T(8,128)(2,1)S(1)} %get-tuple-element.19.even, bf16[683,1024]{1,0:T(8,128)(2,1)S(1)} %get-tuple-element.20.odd), custom_call_target="tpu_custom_call" | custom-call | flops 1432354816 | bytes 4545536 | tf_op jit(solution)/shard_map/forward/pallas_call | solution.py:167
  174.8 1.9 collective-permute-start.2
  176.7 2.5 %collective-permute-start.3 = (bf16[16,2,16,683]{3,2,1,0:T(8,128)(2,1)S(1)}, bf16[16,2,16,683]{3,2,1,0:T(8,128)(2,1)S(1)}, u32[]{:S(2)}, u32[]{:S(2)}) collective-permute-start(bf16[16,2,16,683]{3,2,1,0:T(8,128)(2,1)S(1)} %get-tuple-element.24.own), channel_id=1, source_target_pairs={{8,0},{16,8},{24,16},{9,1},{17,9},{25,17},{10,2},{18,10},{26,18},{... | collective-permute-start | bytes 2098184 | tf_op jit(solution)/shard_map/ppermute | solution.py:337
  179.2 7.3 %inverse.5 = (bf16[88,2,2,8,683]{4,3,2,1,0:T(8,128)(2,1)}, bf16[88,2,2,8,1024]{4,3,2,1,0:T(8,128)(2,1)}, f32[8,128]{1,0:T(8,128)}) custom-call(s32[88]{0:T(128)S(1)} %dynamic_slice.6.waves, s32[2]{0:T(128)S(1)} %subtract_add_fusion.offsets, bf16[32,2,16,683]{3,2,1,0:T(8,128)(2,1)} %collective-permute-done.6.low, ...), custom_call_target="tpu_custom_call", output_to_operand_aliasing={{0}: (8, {}), {1}: (9, {})} | custom-call | flops 2864709632 | bytes 11888640 | tf_op jit(solution)/shard_map/inverse/pallas_call | solution.py:256
  186.6 7.2 %inverse.6 = (bf16[88,2,2,8,683]{4,3,2,1,0:T(8,128)(2,1)}, bf16[88,2,2,8,1024]{4,3,2,1,0:T(8,128)(2,1)}, f32[8,128]{1,0:T(8,128)}) custom-call(s32[88]{0:T(128)S(1)} %dynamic_slice.6.waves, s32[2]{0:T(128)S(1)} %subtract_add_fusion.offsets, bf16[24,2,16,683]{3,2,1,0:T(8,128)(2,1)} %collective-permute-done.4.low, ...), custom_call_target="tpu_custom_call", output_to_operand_aliasing={{0}: (8, {}), {1}: (9, {})} | custom-call | flops 2148532224 | bytes 9615872 | tf_op jit(solution)/shard_map/inverse/pallas_call | solution.py:256
  193.8 4.5 %inverse.7 = (bf16[88,2,2,8,683]{4,3,2,1,0:T(8,128)(2,1)}, bf16[88,2,2,8,1024]{4,3,2,1,0:T(8,128)(2,1)}, f32[8,128]{1,0:T(8,128)}) custom-call(s32[88]{0:T(128)S(1)} %dynamic_slice.6.waves, s32[2]{0:T(128)S(1)} %subtract_add_fusion.offsets, bf16[16,2,16,683]{3,2,1,0:T(8,128)(2,1)S(1)} %collective-permute-done.2.low, ...), custom_call_target="tpu_custom_call", output_to_operand_aliasing={{0}: (8, {}), {1}: (9, {})} | custom-call | flops 1432354816 | bytes 7343104 | tf_op jit(solution)/shard_map/inverse/pallas_call | solution.py:256
  (47 shorter events, 1.8 us)
Async XLA Ops:
  12.4 31.0 %all-to-all-start.1 = ((bf16[8,512,128]{2,1,0:T(8,128)(2,1)}), bf16[8,512,128]{2,1,0:T(8,128)(2,1)S(1)}, u32[]{:S(2)}, u32[]{:S(2)}) async-start(bf16[8,512,128]{2,1,0:T(8,128)(2,1)} %bitcast.1), calls=%async_computation.1 | async-start | bytes 2097152 | tf_op jit(solution)/shard_map/all_to_all | solution.py:326
  43.4 1.0 copy-start.6
  44.4 52.0 %all-to-all-start = ((bf16[8,1024,128]{2,1,0:T(8,128)(2,1)}), bf16[8,1024,128]{2,1,0:T(8,128)(2,1)}, u32[]{:S(2)}, u32[]{:S(2)}) async-start(bf16[8,1024,128]{2,1,0:T(8,128)(2,1)} %bitcast), calls=%async_computation | async-start | bytes 4194304 | tf_op jit(solution)/shard_map/all_to_all | solution.py:326
  55.2 124.0 %copy-start = (bf16[683,1024]{1,0:T(8,128)(2,1)}, bf16[683,1024]{1,0:T(8,128)(2,1)S(1)}, u32[]{:S(2)}) copy-start(bf16[683,1024]{1,0:T(8,128)(2,1)S(1)} %get-tuple-element.20.odd) | copy-start | bytes 4196356
  56.0 1.2 copy-start.7
  59.9 0.9 copy-start.8
  71.2 1.1 copy-start.2
  72.4 35.8 %copy-start.10 = (s32[8]{0:T(128)S(1)}, s32[8]{0:T(128)}, u32[]{:S(2)}) copy-start(s32[8]{0:T(128)} %param.8) | copy-start | bytes 100
  96.4 46.3 %all-to-all-start.3 = ((bf16[8,768,128]{2,1,0:T(8,128)(2,1)}), bf16[8,768,128]{2,1,0:T(8,128)(2,1)}, u32[]{:S(2)}, u32[]{:S(2)}) async-start(bf16[8,768,128]{2,1,0:T(8,128)(2,1)} %bitcast.4), calls=%async_computation.3 | async-start | bytes 3145728 | tf_op jit(solution)/shard_map/all_to_all | solution.py:326
  101.4 13.8 %collective-permute-start = (bf16[16,2,16,683]{3,2,1,0:T(8,128)(2,1)}, bf16[16,2,16,683]{3,2,1,0:T(8,128)(2,1)}, u32[]{:S(2)}, u32[]{:S(2)}) collective-permute-start(bf16[16,2,16,683]{3,2,1,0:T(8,128)(2,1)} %copy-done.8), channel_id=1, source_target_pairs={{0,8},{8,16},{16,24},{1,9},{9,17},{17,25},{2,10},{10,18},{18,26},{... | collective-permute-start | bytes 2098184 | tf_op jit(solution)/shard_map/ppermute | solution.py:336
  106.0 13.9 %collective-permute-start.1 = (bf16[16,2,16,683]{3,2,1,0:T(8,128)(2,1)}, bf16[16,2,16,683]{3,2,1,0:T(8,128)(2,1)}, u32[]{:S(2)}, u32[]{:S(2)}) collective-permute-start(bf16[16,2,16,683]{3,2,1,0:T(8,128)(2,1)} %copy-done.8), channel_id=1, source_target_pairs={{8,0},{16,8},{24,16},{9,1},{17,9},{25,17},{10,2},{18,10},{26,18},{... | collective-permute-start | bytes 2098184 | tf_op jit(solution)/shard_map/ppermute | solution.py:337
  119.9 1.1 copy-start.9
  131.5 1.2 copy-start.4
  141.7 1.0 copy-start.3
  142.7 28.0 %all-to-all-start.2 = ((bf16[8,512,128]{2,1,0:T(8,128)(2,1)}), bf16[8,512,128]{2,1,0:T(8,128)(2,1)}, u32[]{:S(2)}, u32[]{:S(2)}) async-start(bf16[8,512,128]{2,1,0:T(8,128)(2,1)} %bitcast.5), calls=%async_computation.2 | async-start | bytes 2097152 | tf_op jit(solution)/shard_map/all_to_all | solution.py:326
  148.3 28.4 %collective-permute-start.6 = (bf16[32,2,16,683]{3,2,1,0:T(8,128)(2,1)}, bf16[32,2,16,683]{3,2,1,0:T(8,128)(2,1)}, u32[]{:S(2)}, u32[]{:S(2)}) collective-permute-start(bf16[32,2,16,683]{3,2,1,0:T(8,128)(2,1)} %copy-done.4), channel_id=1, source_target_pairs={{0,8},{8,16},{16,24},{1,9},{9,17},{17,25},{2,10},{10,18},{18,26},{... | collective-permute-start | bytes 4196360 | tf_op jit(solution)/shard_map/ppermute | solution.py:336
  150.2 29.0 %collective-permute-start.7 = (bf16[32,2,16,683]{3,2,1,0:T(8,128)(2,1)}, bf16[32,2,16,683]{3,2,1,0:T(8,128)(2,1)}, u32[]{:S(2)}, u32[]{:S(2)}) collective-permute-start(bf16[32,2,16,683]{3,2,1,0:T(8,128)(2,1)} %copy-done.4), channel_id=1, source_target_pairs={{8,0},{16,8},{24,16},{9,1},{17,9},{25,17},{10,2},{18,10},{26,18},{... | collective-permute-start | bytes 4196360 | tf_op jit(solution)/shard_map/ppermute | solution.py:337
  159.3 27.2 %collective-permute-start.4 = (bf16[24,2,16,683]{3,2,1,0:T(8,128)(2,1)}, bf16[24,2,16,683]{3,2,1,0:T(8,128)(2,1)}, u32[]{:S(2)}, u32[]{:S(2)}) collective-permute-start(bf16[24,2,16,683]{3,2,1,0:T(8,128)(2,1)} %get-tuple-element.26.own), channel_id=1, source_target_pairs={{0,8},{8,16},{16,24},{1,9},{9,17},{17,25},{2,10},{10,18},{18,26},{... | collective-permute-start | bytes 3147272 | tf_op jit(solution)/shard_map/ppermute | solution.py:336
  161.3 25.2 %collective-permute-start.5 = (bf16[24,2,16,683]{3,2,1,0:T(8,128)(2,1)}, bf16[24,2,16,683]{3,2,1,0:T(8,128)(2,1)}, u32[]{:S(2)}, u32[]{:S(2)}) collective-permute-start(bf16[24,2,16,683]{3,2,1,0:T(8,128)(2,1)} %get-tuple-element.26.own), channel_id=1, source_target_pairs={{8,0},{16,8},{24,16},{9,1},{17,9},{25,17},{10,2},{18,10},{26,18},{... | collective-permute-start | bytes 3147272 | tf_op jit(solution)/shard_map/ppermute | solution.py:337
  170.7 8.5 %copy-start.5 = (bf16[32,2,16,683]{3,2,1,0:T(8,128)(2,1)S(1)}, bf16[32,2,16,683]{3,2,1,0:T(8,128)(2,1)}, u32[]{:S(2)}) copy-start(bf16[32,2,16,683]{3,2,1,0:T(8,128)(2,1)} %copy-done.4) | copy-start | bytes 4196356
  174.8 19.0 %collective-permute-start.2 = (bf16[16,2,16,683]{3,2,1,0:T(8,128)(2,1)S(1)}, bf16[16,2,16,683]{3,2,1,0:T(8,128)(2,1)S(1)}, u32[]{:S(2)}, u32[]{:S(2)}) collective-permute-start(bf16[16,2,16,683]{3,2,1,0:T(8,128)(2,1)S(1)} %get-tuple-element.24.own), channel_id=1, source_target_pairs={{0,8},{8,16},{16,24},{1,9},{9,17},{17,25},{2,10},{10,18},{18,26},{... | collective-permute-start | bytes 2098184 | tf_op jit(solution)/shard_map/ppermute | solution.py:336
  176.7 17.1 %collective-permute-start.3 = (bf16[16,2,16,683]{3,2,1,0:T(8,128)(2,1)S(1)}, bf16[16,2,16,683]{3,2,1,0:T(8,128)(2,1)S(1)}, u32[]{:S(2)}, u32[]{:S(2)}) collective-permute-start(bf16[16,2,16,683]{3,2,1,0:T(8,128)(2,1)S(1)} %get-tuple-element.24.own), channel_id=1, source_target_pairs={{8,0},{16,8},{24,16},{9,1},{17,9},{25,17},{10,2},{18,10},{26,18},{... | collective-permute-start | bytes 2098184 | tf_op jit(solution)/shard_map/ppermute | solution.py:337
  186.6 7.2 %copy-start.1 = (bf16[683,1024]{1,0:T(8,128)(2,1)S(1)}, bf16[683,1024]{1,0:T(8,128)(2,1)}, u32[]{:S(2)}) copy-start(bf16[683,1024]{1,0:T(8,128)(2,1)} %copy-done) | copy-start | bytes 4196356

commit v4 on v3

--- a/solution.py
+++ b/solution.py
@@ -138,7 +138,8 @@
     )(*factors, velocity, tracer, *tokens)
 
 
-def forward_kernel(first, block, waves, received, even, odd, out, token):
+def forward_kernel(first, block, waves, received, even, odd, *rest):
+    out, token = rest[-2:]
     truncation = even.shape[0]
     step = pl.program_id(0)
     per_slot = received.shape[1] // block
@@ -157,7 +158,7 @@
     token[...] = jnp.zeros_like(token)
 
 
-def forward_transform(waves, first, block, received, even, odd, mem_local):
+def forward_transform(waves, first, block, received, even, odd, mem_local, tokens):
     groups, all_rows, lat_local = received.shape
     truncation, latitudes = even.shape
     slots = all_rows // (waves[1] * mem_local)
@@ -173,7 +174,8 @@
                 pl.BlockSpec((groups, per_block, lat_local), lambda step, w: (0, step, 0)),
                 table,
                 table,
-            ],
+            ]
+            + [pl.BlockSpec(memory_space=pl.ANY)] * len(tokens),
             out_specs=[
                 pl.BlockSpec((block,) + out_shape[1:], lambda step, w: (step, 0, 0, 0)),
                 pl.BlockSpec(TOKEN, lambda step, w: (0, 0)),
@@ -190,7 +192,7 @@
             transcendentals=0,
         ),
         name="forward",
-    )(waves[0], received, even, odd)
+    )(waves[0], received, even, odd, *tokens)
 
 
 def inverse_kernel(first, block, waves, offsets, low, own, high, noise, even, odd, *rest):
@@ -283,7 +285,7 @@
 
 def chunk_bounds(slots_here, block):
     blocks = slots_here // block
-    edges = [0, 2, 6, 9, 11]
+    edges = [0, 3, 7, 10, 11]
     if blocks < edges[-1]:
         edges = list(range(blocks + 1))
     edges[-1] = blocks
@@ -319,7 +321,7 @@
         start, stop = bounds[at]
         waves = slot_grid[:, start:stop].reshape(-1)
         factors = zonal_factors(waves, longitudes, truncation)
-        after = [tokens[key] for key in (("f", at - 2), ("i", at - 3)) if key in tokens]
+        after = [tokens["f", at - 2]] if at >= 2 else []
         outgoing = zonal_transform(factors, velocity, tracer, after)
         rows = (stop - start) * per_slot
         outgoing = outgoing.reshape(lat_count, rows, lat_local)
@@ -330,8 +332,9 @@
 
     def forward(at):
         start, _ = bounds[at]
+        after = [tokens["i", at - 2]] if at >= 2 else []
         spectra, tokens["f", at] = forward_transform(
-            (own_waves, 2 * fields), start, block, received[at], even, odd, mem_local
+            (own_waves, 2 * fields), start, block, received[at], even, odd, mem_local, after
         )
         low = lax.ppermute(spectra[:, mem_local - SPREAD :], "member", upward)
         high = lax.ppermute(spectra[:, :SPREAD], "member", downward)

time: 199 us -> 195 us (0.980)
  local copies, waits for them, and re-layouts: 10.1 us -> 6.01 us
  waiting for transfers between devices: 51 us -> 47 us
  Pallas kernels: 86.2 us -> 88.5 us
    all_to_all x4, waiting for transfers between devices: 40 us -> 46.3 us  [send(): lax.all_to_all(outgoing, 'lat', split_axis=0, concat_axis=0, tiled=True)]
    ppermute x4, waiting for transfers between devices: 6.29 us -> 0.01 us  [forward(): low = lax.ppermute(spectra[:, mem_local - SPREAD:], 'member', upward)]
    ppermute x4, starting transfers between devices: 10.4 us -> 15.6 us  [forward(): low = lax.ppermute(spectra[:, mem_local - SPREAD:], 'member', upward)]
    unnamed x22 -> x18, local copies, waits for them, and re-layouts: 7.49 us -> 3.41 us
    ppermute x4, waiting for transfers between devices: 4.7 us -> 0.74 us  [forward(): high = lax.ppermute(spectra[:, :SPREAD], 'member', downward)]
    ppermute x4, starting transfers between devices: 11.5 us -> 7.9 us  [forward(): high = lax.ppermute(spectra[:, :SPREAD], 'member', downward)]
  transfers between devices with their start and end apart: 12 -> 12, of which waited for: 5 -> 4; matrix products, arithmetic and copies ran while one was open for 4% -> 4% of each run, Pallas kernels for 36% -> 38%
where the time goes in v4:
time: 195 us; the launch traced here: 194 us
  Pallas kernels  88.5 us (45%)
  waiting for transfers between devices  47 us (24%)
  starting transfers between devices  44.8 us (23%)
  other arithmetic  6.22 us (3%)
  local copies, waits for them, and re-layouts  6.01 us (3%)
    all_to_all x4, waiting for transfers between devices, send(): lax.all_to_all(outgoing, 'lat', split_axis=0, concat_axis=0, tiled=True)  46.3 us
    pallas_call x4, Pallas kernels, zonal_transform(): pl.pallas_call(functools.partial(zonal_kernel, fields_step, fields, len(t...  44.4 us
    pallas_call x4, Pallas kernels, inverse_transform(): pl.pallas_call(functools.partial(inverse_kernel, first, block), grid_spec...  24.4 us
    all_to_all x4, starting transfers between devices, send(): lax.all_to_all(outgoing, 'lat', split_axis=0, concat_axis=0, tiled=True)  21.3 us
    pallas_call x4, Pallas kernels, forward_transform(): pl.pallas_call(functools.partial(forward_kernel, first, block), grid_spec...  18 us
    ppermute x4, starting transfers between devices, forward(): low = lax.ppermute(spectra[:, mem_local - SPREAD:], 'member', upward)  15.6 us
    ppermute x4, starting transfers between devices, forward(): high = lax.ppermute(spectra[:, :SPREAD], 'member', downward)  7.9 us
  transfers between devices with their start and end apart: 12, of which 4 were waited for; matrix products, arithmetic and copies ran while one was open for 4% of the time, Pallas kernels for 38%

profile of v4, /device:TPU:1, one launch (start us, length us, event | category | flops | bytes accessed | tf_op | source)
XLA Modules:
  0.0 193.6 jit_solution(1586374304237912875)
XLA Ops:
  0.6 0.8 reshape.64
  1.6 0.5 fusion.30
  2.2 0.1 copy.16
  2.3 0.4 sine_multiply_fusion.3
  2.7 11.5 %zonal.6 = bf16[192,32,128]{2,1,0:T(8,128)(2,1)} custom-call(f32[192,16]{1,0:T(8,128)S(1)} %get-tuple-element.45.cos_c, f32[192,16]{1,0:T(8,128)S(1)} %get-tuple-element.44.sin_c, f32[192,128]{1,0:T(8,128)S(1)} %get-tuple-element.53.cos_f, f32[192,128]{1,0:T(8,128)S(1)} %get-tuple-element.52.sin_f, bf16[2,8,128,2048]{3,2,1,0:T(8,128)(2,1)} %velocity.7, ...), custom_call_target="tpu_custom_call" | custom-call | flops 3221225472 | bytes 18350080 | tf_op jit(solution)/shard_map/zonal/pallas_call | solution.py:123
  14.2 6.4 %all-to-all-start.2 = ((bf16[8,768,128]{2,1,0:T(8,128)(2,1)}), bf16[8,768,128]{2,1,0:T(8,128)(2,1)S(1)}, u32[]{:S(2)}, u32[]{:S(2)}) async-start(bf16[8,768,128]{2,1,0:T(8,128)(2,1)} %bitcast.2), calls=%async_computation.2 | async-start | bytes 3145728 | tf_op jit(solution)/shard_map/all_to_all | solution.py:328
  20.8 0.1 copy.14
  20.9 0.6 fusion.26
  21.5 0.5 sine_multiply_fusion.1
  22.0 13.2 %zonal.4 = bf16[256,32,128]{2,1,0:T(8,128)(2,1)} custom-call(f32[256,16]{1,0:T(8,128)S(1)} %get-tuple-element.41.cos_c, f32[256,16]{1,0:T(8,128)S(1)} %get-tuple-element.40.sin_c, f32[256,128]{1,0:T(8,128)S(1)} %get-tuple-element.55.cos_f, f32[256,128]{1,0:T(8,128)S(1)} %get-tuple-element.54.sin_f, bf16[2,8,128,2048]{3,2,1,0:T(8,128)(2,1)} %velocity.7, ...), custom_call_target="tpu_custom_call" | custom-call | flops 4294967296 | bytes 18874368 | tf_op jit(solution)/shard_map/zonal/pallas_call | solution.py:123
  35.2 21.5 %all-to-all-done.2.received = bf16[8,768,128]{2,1,0:T(8,128)(2,1)S(1)} async-done(((bf16[8,768,128]{2,1,0:T(8,128)(2,1)}), bf16[8,768,128]{2,1,0:T(8,128)(2,1)S(1)}, u32[]{:S(2)}, u32[]{:S(2)}) %all-to-all-start.2) | async-done | bytes 1572896 | tf_op jit(solution)/shard_map/all_to_all | solution.py:328
  56.7 1.1 copy-done.4
  57.9 4.7 %all-to-all-start = ((bf16[8,1024,128]{2,1,0:T(8,128)(2,1)}), bf16[8,1024,128]{2,1,0:T(8,128)(2,1)}, u32[]{:S(2)}, u32[]{:S(2)}) async-start(bf16[8,1024,128]{2,1,0:T(8,128)(2,1)} %bitcast), calls=%async_computation | async-start | bytes 4194304 | tf_op jit(solution)/shard_map/all_to_all | solution.py:328
  62.5 0.8 dynamic_slice.6.waves
  63.4 0.2 copy.15
  63.6 0.1 copy.17
  63.7 1.4 fusion.6
  65.1 1.3 sine_multiply_fusion
  66.4 1.8 tables.1
  68.2 0.5 fusion.28
  68.7 0.4 sine_multiply_fusion.2
  69.1 3.8 %forward.5 = (bf16[24,2,16,683]{3,2,1,0:T(8,128)(2,1)S(1)}, f32[8,128]{1,0:T(8,128)S(1)}) custom-call(s32[88]{0:T(128)S(1)} %dynamic_slice.6.waves, bf16[8,768,128]{2,1,0:T(8,128)(2,1)S(1)} %copy-done.5, bf16[683,1024]{1,0:T(8,128)(2,1)S(1)} %get-tuple-element.20.even, bf16[683,1024]{1,0:T(8,128)(2,1)S(1)} %get-tuple-element.21.odd), custom_call_target="tpu_custom_call" | custom-call | flops 2148532224 | bytes 5419520 | tf_op jit(solution)/shard_map/forward/pallas_call | solution.py:168
  72.8 1.0 copy-done.6
  73.8 10.4 %zonal.7 = bf16[192,32,128]{2,1,0:T(8,128)(2,1)S(1)} custom-call(f32[192,16]{1,0:T(8,128)S(1)} %get-tuple-element.43.cos_c, f32[192,16]{1,0:T(8,128)S(1)} %get-tuple-element.42.sin_c, f32[192,128]{1,0:T(8,128)S(1)} %get-tuple-element.51.cos_f, f32[192,128]{1,0:T(8,128)S(1)} %get-tuple-element.50.sin_f, bf16[2,8,128,2048]{3,2,1,0:T(8,128)(2,1)} %velocity.7, ...), custom_call_target="tpu_custom_call" | custom-call | flops 3221225472 | bytes 18350080 | tf_op jit(solution)/shard_map/zonal/pallas_call | solution.py:123
  84.2 1.2 copy-done.3
  85.5 24.2 %all-to-all-done.received = bf16[8,1024,128]{2,1,0:T(8,128)(2,1)} async-done(((bf16[8,1024,128]{2,1,0:T(8,128)(2,1)}), bf16[8,1024,128]{2,1,0:T(8,128)(2,1)}, u32[]{:S(2)}, u32[]{:S(2)}) %all-to-all-start) | async-done | bytes 2097184 | tf_op jit(solution)/shard_map/all_to_all | solution.py:328
  109.7 5.0 %all-to-all-start.3 = ((bf16[8,768,128]{2,1,0:T(8,128)(2,1)}), bf16[8,768,128]{2,1,0:T(8,128)(2,1)}, u32[]{:S(2)}, u32[]{:S(2)}) async-start(bf16[8,768,128]{2,1,0:T(8,128)(2,1)} %bitcast.4), calls=%async_computation.3 | async-start | bytes 3145728 | tf_op jit(solution)/shard_map/all_to_all | solution.py:328
  115.0 4.5 %collective-permute-start.2 = (bf16[24,2,16,683]{3,2,1,0:T(8,128)(2,1)}, bf16[24,2,16,683]{3,2,1,0:T(8,128)(2,1)S(1)}, u32[]{:S(2)}, u32[]{:S(2)}) collective-permute-start(bf16[24,2,16,683]{3,2,1,0:T(8,128)(2,1)} %copy-done.6), channel_id=1, source_target_pairs={{0,8},{8,16},{16,24},{1,9},{9,17},{17,25},{2,10},{10,18},{18,26},{... | collective-permute-start | bytes 3147272 | tf_op jit(solution)/shard_map/ppermute | solution.py:339
  119.6 1.9 collective-permute-start.3
  121.5 0.2 fusion.49
  121.8 6.6 %forward.4 = (bf16[32,2,16,683]{3,2,1,0:T(8,128)(2,1)}, f32[8,128]{1,0:T(8,128)S(1)}) custom-call(s32[88]{0:T(128)S(1)} %dynamic_slice.6.waves, bf16[8,1024,128]{2,1,0:T(8,128)(2,1)} %all-to-all-done.received, bf16[683,1024]{1,0:T(8,128)(2,1)S(1)} %get-tuple-element.20.even, bf16[683,1024]{1,0:T(8,128)(2,1)S(1)} %get-tuple-element.21.odd), custom_call_target="tpu_custom_call" | custom-call | flops 2864709632 | bytes 6293504 | tf_op jit(solution)/shard_map/forward/pallas_call | solution.py:168
  128.4 3.6 %collective-permute-start = (bf16[32,2,16,683]{3,2,1,0:T(8,128)(2,1)}, bf16[32,2,16,683]{3,2,1,0:T(8,128)(2,1)}, u32[]{:S(2)}, u32[]{:S(2)}) collective-permute-start(bf16[32,2,16,683]{3,2,1,0:T(8,128)(2,1)} %get-tuple-element.23.own), channel_id=1, source_target_pairs={{0,8},{8,16},{16,24},{1,9},{9,17},{17,25},{2,10},{10,18},{18,26},{... | collective-permute-start | bytes 4196360 | tf_op jit(solution)/shard_map/ppermute | solution.py:339
  132.0 2.1 %collective-permute-start.1 = (bf16[32,2,16,683]{3,2,1,0:T(8,128)(2,1)}, bf16[32,2,16,683]{3,2,1,0:T(8,128)(2,1)}, u32[]{:S(2)}, u32[]{:S(2)}) collective-permute-start(bf16[32,2,16,683]{3,2,1,0:T(8,128)(2,1)} %get-tuple-element.23.own), channel_id=1, source_target_pairs={{8,0},{16,8},{24,16},{9,1},{17,9},{25,17},{10,2},{18,10},{26,18},{... | collective-permute-start | bytes 4196360 | tf_op jit(solution)/shard_map/ppermute | solution.py:340
  134.3 0.1 sine_multiply_fusion.4
  134.4 9.3 %zonal.5 = bf16[64,32,128]{2,1,0:T(8,128)(2,1)} custom-call(f32[64,16]{1,0:T(8,128)S(1)} %get-tuple-element.47.cos_c, f32[64,16]{1,0:T(8,128)S(1)} %get-tuple-element.46.sin_c, f32[64,128]{1,0:T(8,128)S(1)} %get-tuple-element.61.cos_f, f32[64,128]{1,0:T(8,128)S(1)} %get-tuple-element.60.sin_f, bf16[2,8,128,2048]{3,2,1,0:T(8,128)(2,1)} %velocity.7, ...), custom_call_target="tpu_custom_call" | custom-call | flops 1073741824 | bytes 17301504 | tf_op jit(solution)/shard_map/zonal/pallas_call | solution.py:123
  143.8 6.2 %inverse.4 = (bf16[88,2,2,8,683]{4,3,2,1,0:T(8,128)(2,1)}, bf16[88,2,2,8,1024]{4,3,2,1,0:T(8,128)(2,1)}, f32[8,128]{1,0:T(8,128)S(1)}) custom-call(s32[88]{0:T(128)S(1)} %dynamic_slice.6.waves, s32[2]{0:T(128)S(1)} %subtract_add_fusion.offsets, bf16[24,2,16,683]{3,2,1,0:T(8,128)(2,1)S(1)} %collective-permute-done.2.low, ...), custom_call_target="tpu_custom_call" | custom-call | flops 2148532224 | bytes 9615872 | tf_op jit(solution)/shard_map/inverse/pallas_call | solution.py:258
  149.9 0.6 all-to-all-done.3.received
  150.5 5.2 %all-to-all-start.1 = ((bf16[8,256,128]{2,1,0:T(8,128)(2,1)}), bf16[8,256,128]{2,1,0:T(8,128)(2,1)S(1)}, u32[]{:S(2)}, u32[]{:S(2)}) async-start(bf16[8,256,128]{2,1,0:T(8,128)(2,1)} %bitcast.1), calls=%async_computation.1 | async-start | bytes 1048576 | tf_op jit(solution)/shard_map/all_to_all | solution.py:328
  155.6 5.6 %forward.7 = (bf16[24,2,16,683]{3,2,1,0:T(8,128)(2,1)}, f32[8,128]{1,0:T(8,128)}) custom-call(s32[88]{0:T(128)S(1)} %dynamic_slice.6.waves, bf16[8,768,128]{2,1,0:T(8,128)(2,1)} %all-to-all-done.3.received, bf16[683,1024]{1,0:T(8,128)(2,1)S(1)} %get-tuple-element.20.even, bf16[683,1024]{1,0:T(8,128)(2,1)S(1)} %copy-done.1, ...), custom_call_target="tpu_custom_call" | custom-call | flops 2148532224 | bytes 5419520 | tf_op jit(solution)/shard_map/forward/pallas_call | solution.py:168
  161.3 3.8 %collective-permute-start.6 = (bf16[24,2,16,683]{3,2,1,0:T(8,128)(2,1)}, bf16[24,2,16,683]{3,2,1,0:T(8,128)(2,1)}, u32[]{:S(2)}, u32[]{:S(2)}) collective-permute-start(bf16[24,2,16,683]{3,2,1,0:T(8,128)(2,1)} %get-tuple-element.31.own), channel_id=1, source_target_pairs={{0,8},{8,16},{16,24},{1,9},{9,17},{17,25},{2,10},{10,18},{18,26},{... | collective-permute-start | bytes 3147272 | tf_op jit(solution)/shard_map/ppermute | solution.py:339
  165.1 1.9 collective-permute-start.7
  167.0 7.6 %inverse.5 = (bf16[88,2,2,8,683]{4,3,2,1,0:T(8,128)(2,1)}, bf16[88,2,2,8,1024]{4,3,2,1,0:T(8,128)(2,1)}, f32[8,128]{1,0:T(8,128)S(1)}) custom-call(s32[88]{0:T(128)S(1)} %dynamic_slice.6.waves, s32[2]{0:T(128)S(1)} %subtract_add_fusion.offsets, bf16[32,2,16,683]{3,2,1,0:T(8,128)(2,1)} %collective-permute-done.low, ...), custom_call_target="tpu_custom_call", output_to_operand_aliasing={{0}: (8, {}), {1}: (9, {})} | custom-call | flops 2864709632 | bytes 11888640 | tf_op jit(solution)/shard_map/inverse/pallas_call | solution.py:258
  174.6 2.0 %forward.6 = (bf16[8,2,16,683]{3,2,1,0:T(8,128)(2,1)S(1)}, f32[8,128]{1,0:T(8,128)}) custom-call(s32[88]{0:T(128)S(1)} %dynamic_slice.6.waves, bf16[8,256,128]{2,1,0:T(8,128)(2,1)S(1)} %all-to-all-done.1.received, bf16[683,1024]{1,0:T(8,128)(2,1)S(1)} %get-tuple-element.20.even, bf16[683,1024]{1,0:T(8,128)(2,1)S(1)} %copy-done.1, ...), custom_call_target="tpu_custom_call" | custom-call | flops 716177408 | bytes 3671552 | tf_op jit(solution)/shard_map/forward/pallas_call | solution.py:168
  176.6 3.6 %collective-permute-start.4 = (bf16[8,2,16,683]{3,2,1,0:T(8,128)(2,1)S(1)}, bf16[8,2,16,683]{3,2,1,0:T(8,128)(2,1)S(1)}, u32[]{:S(2)}, u32[]{:S(2)}) collective-permute-start(bf16[8,2,16,683]{3,2,1,0:T(8,128)(2,1)S(1)} %get-tuple-element.28.own), channel_id=1, source_target_pairs={{0,8},{8,16},{16,24},{1,9},{9,17},{17,25},{2,10},{10,18},{18,26},{... | collective-permute-start | bytes 1049096 | tf_op jit(solution)/shard_map/ppermute | solution.py:339
  180.2 1.9 collective-permute-start.5
  182.2 0.7 collective-permute-done.7.high
  182.9 7.2 %inverse.6 = (bf16[88,2,2,8,683]{4,3,2,1,0:T(8,128)(2,1)}, bf16[88,2,2,8,1024]{4,3,2,1,0:T(8,128)(2,1)}, f32[8,128]{1,0:T(8,128)}) custom-call(s32[88]{0:T(128)S(1)} %dynamic_slice.6.waves, s32[2]{0:T(128)S(1)} %subtract_add_fusion.offsets, bf16[24,2,16,683]{3,2,1,0:T(8,128)(2,1)} %collective-permute-done.6.low, ...), custom_call_target="tpu_custom_call", output_to_operand_aliasing={{0}: (8, {}), {1}: (9, {})} | custom-call | flops 2148532224 | bytes 9615872 | tf_op jit(solution)/shard_map/inverse/pallas_call | solution.py:258
  190.2 3.4 %inverse.7 = (bf16[88,2,2,8,683]{4,3,2,1,0:T(8,128)(2,1)}, bf16[88,2,2,8,1024]{4,3,2,1,0:T(8,128)(2,1)}, f32[8,128]{1,0:T(8,128)}) custom-call(s32[88]{0:T(128)S(1)} %dynamic_slice.6.waves, s32[2]{0:T(128)S(1)} %subtract_add_fusion.offsets, bf16[8,2,16,683]{3,2,1,0:T(8,128)(2,1)S(1)} %collective-permute-done.4.low, ...), custom_call_target="tpu_custom_call", output_to_operand_aliasing={{0}: (8, {}), {1}: (9, {})} | custom-call | flops 716177408 | bytes 5070336 | tf_op jit(solution)/shard_map/inverse/pallas_call | solution.py:258
  (43 shorter events, 1.1 us)
Async XLA Ops:
  14.2 42.5 %all-to-all-start.2 = ((bf16[8,768,128]{2,1,0:T(8,128)(2,1)}), bf16[8,768,128]{2,1,0:T(8,128)(2,1)S(1)}, u32[]{:S(2)}, u32[]{:S(2)}) async-start(bf16[8,768,128]{2,1,0:T(8,128)(2,1)} %bitcast.2), calls=%async_computation.2 | async-start | bytes 3145728 | tf_op jit(solution)/shard_map/all_to_all | solution.py:328
  56.7 1.1 copy-start.4
  57.9 51.8 %all-to-all-start = ((bf16[8,1024,128]{2,1,0:T(8,128)(2,1)}), bf16[8,1024,128]{2,1,0:T(8,128)(2,1)}, u32[]{:S(2)}, u32[]{:S(2)}) async-start(bf16[8,1024,128]{2,1,0:T(8,128)(2,1)} %bitcast), calls=%async_computation | async-start | bytes 4194304 | tf_op jit(solution)/shard_map/all_to_all | solution.py:328
  65.1 4.0 %copy-start.5 = (bf16[8,768,128]{2,1,0:T(8,128)(2,1)S(1)}, bf16[8,768,128]{2,1,0:T(8,128)(2,1)}, u32[]{:S(2)}) copy-start(bf16[8,768,128]{2,1,0:T(8,128)(2,1)} %copy-done.4) | copy-start | bytes 4718596
  68.2 53.6 %copy-start = (bf16[683,1024]{1,0:T(8,128)(2,1)}, bf16[683,1024]{1,0:T(8,128)(2,1)S(1)}, u32[]{:S(2)}) copy-start(bf16[683,1024]{1,0:T(8,128)(2,1)S(1)} %get-tuple-element.21.odd) | copy-start | bytes 4196356
  72.8 1.0 copy-start.6
  84.2 1.2 copy-start.3
  109.7 40.8 %all-to-all-start.3 = ((bf16[8,768,128]{2,1,0:T(8,128)(2,1)}), bf16[8,768,128]{2,1,0:T(8,128)(2,1)}, u32[]{:S(2)}, u32[]{:S(2)}) async-start(bf16[8,768,128]{2,1,0:T(8,128)(2,1)} %bitcast.4), calls=%async_computation.3 | async-start | bytes 3145728 | tf_op jit(solution)/shard_map/all_to_all | solution.py:328
  115.0 28.7 %collective-permute-start.2 = (bf16[24,2,16,683]{3,2,1,0:T(8,128)(2,1)}, bf16[24,2,16,683]{3,2,1,0:T(8,128)(2,1)S(1)}, u32[]{:S(2)}, u32[]{:S(2)}) collective-permute-start(bf16[24,2,16,683]{3,2,1,0:T(8,128)(2,1)} %copy-done.6), channel_id=1, source_target_pairs={{0,8},{8,16},{16,24},{1,9},{9,17},{17,25},{2,10},{10,18},{18,26},{... | collective-permute-start | bytes 3147272 | tf_op jit(solution)/shard_map/ppermute | solution.py:339
  119.6 24.2 %collective-permute-start.3 = (bf16[24,2,16,683]{3,2,1,0:T(8,128)(2,1)}, bf16[24,2,16,683]{3,2,1,0:T(8,128)(2,1)S(1)}, u32[]{:S(2)}, u32[]{:S(2)}) collective-permute-start(bf16[24,2,16,683]{3,2,1,0:T(8,128)(2,1)} %copy-done.6), channel_id=1, source_target_pairs={{8,0},{16,8},{24,16},{9,1},{17,9},{25,17},{10,2},{18,10},{26,18},{... | collective-permute-start | bytes 3147272 | tf_op jit(solution)/shard_map/ppermute | solution.py:340
  121.8 12.4 %copy-start.8 = (s32[8]{0:T(128)S(1)}, s32[8]{0:T(128)}, u32[]{:S(2)}) copy-start(s32[8]{0:T(128)} %param.8) | copy-start | bytes 100
  128.4 38.6 %collective-permute-start = (bf16[32,2,16,683]{3,2,1,0:T(8,128)(2,1)}, bf16[32,2,16,683]{3,2,1,0:T(8,128)(2,1)}, u32[]{:S(2)}, u32[]{:S(2)}) collective-permute-start(bf16[32,2,16,683]{3,2,1,0:T(8,128)(2,1)} %get-tuple-element.23.own), channel_id=1, source_target_pairs={{0,8},{8,16},{16,24},{1,9},{9,17},{17,25},{2,10},{10,18},{18,26},{... | collective-permute-start | bytes 4196360 | tf_op jit(solution)/shard_map/ppermute | solution.py:339
  132.0 35.0 %collective-permute-start.1 = (bf16[32,2,16,683]{3,2,1,0:T(8,128)(2,1)}, bf16[32,2,16,683]{3,2,1,0:T(8,128)(2,1)}, u32[]{:S(2)}, u32[]{:S(2)}) collective-permute-start(bf16[32,2,16,683]{3,2,1,0:T(8,128)(2,1)} %get-tuple-element.23.own), channel_id=1, source_target_pairs={{8,0},{16,8},{24,16},{9,1},{17,9},{25,17},{10,2},{18,10},{26,18},{... | collective-permute-start | bytes 4196360 | tf_op jit(solution)/shard_map/ppermute | solution.py:340
  134.4 9.3 %copy-start.7 = (bf16[24,2,16,683]{3,2,1,0:T(8,128)(2,1)S(1)}, bf16[24,2,16,683]{3,2,1,0:T(8,128)(2,1)}, u32[]{:S(2)}) copy-start(bf16[24,2,16,683]{3,2,1,0:T(8,128)(2,1)} %copy-done.6) | copy-start | bytes 3147268
  143.7 11.9 %copy-start.1 = (bf16[683,1024]{1,0:T(8,128)(2,1)S(1)}, bf16[683,1024]{1,0:T(8,128)(2,1)}, u32[]{:S(2)}) copy-start(bf16[683,1024]{1,0:T(8,128)(2,1)} %copy-done) | copy-start | bytes 4196356
  150.5 24.1 %all-to-all-start.1 = ((bf16[8,256,128]{2,1,0:T(8,128)(2,1)}), bf16[8,256,128]{2,1,0:T(8,128)(2,1)S(1)}, u32[]{:S(2)}, u32[]{:S(2)}) async-start(bf16[8,256,128]{2,1,0:T(8,128)(2,1)} %bitcast.1), calls=%async_computation.1 | async-start | bytes 1048576 | tf_op jit(solution)/shard_map/all_to_all | solution.py:328
  161.3 20.9 %collective-permute-start.6 = (bf16[24,2,16,683]{3,2,1,0:T(8,128)(2,1)}, bf16[24,2,16,683]{3,2,1,0:T(8,128)(2,1)}, u32[]{:S(2)}, u32[]{:S(2)}) collective-permute-start(bf16[24,2,16,683]{3,2,1,0:T(8,128)(2,1)} %get-tuple-element.31.own), channel_id=1, source_target_pairs={{0,8},{8,16},{16,24},{1,9},{9,17},{17,25},{2,10},{10,18},{18,26},{... | collective-permute-start | bytes 3147272 | tf_op jit(solution)/shard_map/ppermute | solution.py:339
  165.1 17.8 %collective-permute-start.7 = (bf16[24,2,16,683]{3,2,1,0:T(8,128)(2,1)}, bf16[24,2,16,683]{3,2,1,0:T(8,128)(2,1)}, u32[]{:S(2)}, u32[]{:S(2)}) collective-permute-start(bf16[24,2,16,683]{3,2,1,0:T(8,128)(2,1)} %get-tuple-element.31.own), channel_id=1, source_target_pairs={{8,0},{16,8},{24,16},{9,1},{17,9},{25,17},{10,2},{18,10},{26,18},{... | collective-permute-start | bytes 3147272 | tf_op jit(solution)/shard_map/ppermute | solution.py:340
  176.6 13.6 %collective-permute-start.4 = (bf16[8,2,16,683]{3,2,1,0:T(8,128)(2,1)S(1)}, bf16[8,2,16,683]{3,2,1,0:T(8,128)(2,1)S(1)}, u32[]{:S(2)}, u32[]{:S(2)}) collective-permute-start(bf16[8,2,16,683]{3,2,1,0:T(8,128)(2,1)S(1)} %get-tuple-element.28.own), channel_id=1, source_target_pairs={{0,8},{8,16},{16,24},{1,9},{9,17},{17,25},{2,10},{10,18},{18,26},{... | collective-permute-start | bytes 1049096 | tf_op jit(solution)/shard_map/ppermute | solution.py:339
  180.2 9.9 %collective-permute-start.5 = (bf16[8,2,16,683]{3,2,1,0:T(8,128)(2,1)S(1)}, bf16[8,2,16,683]{3,2,1,0:T(8,128)(2,1)S(1)}, u32[]{:S(2)}, u32[]{:S(2)}) collective-permute-start(bf16[8,2,16,683]{3,2,1,0:T(8,128)(2,1)S(1)} %get-tuple-element.28.own), channel_id=1, source_target_pairs={{8,0},{16,8},{24,16},{9,1},{17,9},{25,17},{10,2},{18,10},{26,18},{... | collective-permute-start | bytes 1049096 | tf_op jit(solution)/shard_map/ppermute | solution.py:340
  182.9 7.3 %copy-start.2 = (bf16[683,1024]{1,0:T(8,128)(2,1)S(1)}, bf16[683,1024]{1,0:T(8,128)(2,1)}, u32[]{:S(2)}) copy-start(bf16[683,1024]{1,0:T(8,128)(2,1)} %copy-done) | copy-start | bytes 4196356

commit v5 on v4

--- a/solution.py
+++ b/solution.py
@@ -73,11 +73,12 @@
 def zonal_kernel(
     fields_step, fields, tokens, cos_c, sin_c, cos_f, sin_f, velocity, tracer, *rest
 ):
-    out, table, total = rest[tokens:]
+    *outs, token, table, total = rest[tokens:]
+    token[...] = jnp.zeros_like(token)
     step = pl.program_id(0)
     rows = cos_f.shape[0]
     lat_local, longitudes = velocity.shape[2:]
-    out_rows = out.shape[1]
+    out_rows = outs[0].shape[1]
 
     @pl.when(step == 0)
     def _():
@@ -105,15 +106,19 @@
 
     @pl.when(step == pl.num_programs(0) - 1)
     def _():
-        out[...] = total[...].reshape(out.shape).astype(out.dtype)
-
-
-def zonal_transform(factors, velocity, tracer, tokens):
+        size = outs[0].shape[0] * out_rows
+        for at, out in enumerate(outs):
+            part = total[at * size : (at + 1) * size, :]
+            out[...] = part.reshape(out.shape).astype(out.dtype)
+
+
+def zonal_transform(factors, velocity, tracer, pieces, tokens):
     mem_local, fields, lat_local, longitudes = velocity.shape
     rows = factors[0].shape[0]
     fields_step = min(fields, max(1, 512 // lat_local))
     steps = fields // fields_step
     out_rows = mem_local * 2 * fields
+    piece = (rows // pieces, out_rows, lat_local)
     whole = lambda step: (0, 0)
     grid_block = pl.BlockSpec(
         (1, fields_step, lat_local, longitudes), lambda step: (step // steps, step % steps, 0, 0)
@@ -126,8 +131,10 @@
         in_specs=[pl.BlockSpec(f.shape, whole) for f in factors]
         + [grid_block, grid_block]
         + [pl.BlockSpec(memory_space=pl.ANY)] * len(tokens),
-        out_specs=pl.BlockSpec((rows, out_rows, lat_local), lambda step: (0, 0, 0)),
-        out_shape=jax.ShapeDtypeStruct((rows, out_rows, lat_local), jnp.bfloat16),
+        out_specs=[pl.BlockSpec(piece, lambda step: (0, 0, 0))] * pieces
+        + [pl.BlockSpec(TOKEN, lambda step: (0, 0))],
+        out_shape=[jax.ShapeDtypeStruct(piece, jnp.bfloat16)] * pieces
+        + [jax.ShapeDtypeStruct(TOKEN, jnp.float32)],
         scratch_shapes=[
             pltpu.VMEM((2 * rows, longitudes), jnp.bfloat16),
             pltpu.VMEM((rows * out_rows, lat_local), jnp.float32),
@@ -138,12 +145,13 @@
     )(*factors, velocity, tracer, *tokens)
 
 
-def forward_kernel(first, block, waves, received, even, odd, *rest):
-    out, token = rest[-2:]
+def forward_kernel(first, block, pieces, waves, *refs):
+    received, (even, odd), (out, token) = refs[:pieces], refs[pieces : pieces + 2], refs[-2:]
     truncation = even.shape[0]
     step = pl.program_id(0)
-    per_slot = received.shape[1] // block
-    rows = jnp.concatenate([received[g] for g in range(received.shape[0])], axis=-1)
+    per_slot = received[0].shape[1] // block
+    rows = [piece[g] for piece in received for g in range(piece.shape[0])]
+    rows = jnp.concatenate(rows, axis=-1)
     contract = (((1,), (1,)), ((), ()))
     by_even = lax.dot_general(rows, even[...], contract, preferred_element_type=jnp.float32)
     by_odd = lax.dot_general(rows, odd[...], contract, preferred_element_type=jnp.float32)
@@ -159,22 +167,22 @@
 
 
 def forward_transform(waves, first, block, received, even, odd, mem_local, tokens):
-    groups, all_rows, lat_local = received.shape
+    groups, all_rows, lat_local = received[0].shape
     truncation, latitudes = even.shape
     slots = all_rows // (waves[1] * mem_local)
     out_shape = (slots, mem_local, waves[1], truncation)
     per_block = block * mem_local * waves[1]
     table = pl.BlockSpec(even.shape, lambda step, w: (0, 0))
     return pl.pallas_call(
-        functools.partial(forward_kernel, first, block),
+        functools.partial(forward_kernel, first, block, len(received)),
         grid_spec=pltpu.PrefetchScalarGridSpec(
             num_scalar_prefetch=1,
             grid=(slots // block,),
             in_specs=[
-                pl.BlockSpec((groups, per_block, lat_local), lambda step, w: (0, step, 0)),
-                table,
-                table,
+                pl.BlockSpec((groups, per_block, lat_local), lambda step, w: (0, step, 0))
             ]
+            * len(received)
+            + [table, table]
             + [pl.BlockSpec(memory_space=pl.ANY)] * len(tokens),
             out_specs=[
                 pl.BlockSpec((block,) + out_shape[1:], lambda step, w: (step, 0, 0, 0)),
@@ -192,7 +200,7 @@
             transcendentals=0,
         ),
         name="forward",
-    )(waves[0], received, even, odd, *tokens)
+    )(waves[0], *received, even, odd, *tokens)
 
 
 def inverse_kernel(first, block, waves, offsets, low, own, high, noise, even, odd, *rest):
@@ -285,12 +293,13 @@
 
 def chunk_bounds(slots_here, block):
     blocks = slots_here // block
-    edges = [0, 3, 7, 10, 11]
-    if blocks < edges[-1]:
-        edges = list(range(blocks + 1))
-    edges[-1] = blocks
+    shares = (2, 5, 3)
+    edges = [0]
+    for share in shares:
+        edges.append(min(blocks, edges[-1] + max(1, blocks * share // 11)))
+    edges.append(blocks)
     edges = [edge * block for edge in edges]
-    return list(zip(edges[:-1], edges[1:]))
+    return [(start, stop) for start, stop in zip(edges[:-1], edges[1:]) if stop > start]
 
 
 def per_device(velocity, tracer, wave_slots, parents, noise):
@@ -313,28 +322,50 @@
     bounds = chunk_bounds(slots_here, block)
     count = len(bounds)
     inner = min(lat_local, LANES)
-    starts = jnp.arange(latitudes // inner, dtype=jnp.int32) * inner
+    partners = jnp.arange(lat_count, dtype=jnp.int32) ^ lat_index
+    lanes_at = jnp.arange(0, lat_local, inner, dtype=jnp.int32)[None, :]
+
+    def tables_of(devices):
+        starts = (devices[:, None] * lat_local + lanes_at).reshape(-1)
+        return meridional_tables(truncation, latitudes, starts, inner)
+
     received, own, tokens = {}, {}, {}
     outs = None
 
-    def send(at):
+    def joined(pieces):
+        if lat_local % LANES == 0:
+            return pieces
+        pieces = jnp.concatenate(pieces, axis=0)
+        return [jnp.swapaxes(pieces, 0, 1).reshape(1, -1, latitudes)]
+
+    def transform(at, grid, pieces, after):
         start, stop = bounds[at]
-        waves = slot_grid[:, start:stop].reshape(-1)
-        factors = zonal_factors(waves, longitudes, truncation)
-        after = [tokens["f", at - 2]] if at >= 2 else []
-        outgoing = zonal_transform(factors, velocity, tracer, after)
-        rows = (stop - start) * per_slot
-        outgoing = outgoing.reshape(lat_count, rows, lat_local)
+        factors = zonal_factors(grid[:, start:stop].reshape(-1), longitudes, truncation)
+        after = [tokens[key] for key in after]
+        *pieces, tokens["z", at] = zonal_transform(factors, velocity, tracer, pieces, after)
+        return [piece.reshape(-1, (stop - start) * per_slot, lat_local) for piece in pieces]
+
+    def send(at, *after):
+        (outgoing,) = transform(at, slot_grid, 1, after)
         moved = lax.all_to_all(outgoing, "lat", split_axis=0, concat_axis=0, tiled=True)
-        if lat_local % LANES != 0:
-            moved = jnp.swapaxes(moved, 0, 1).reshape(1, rows, latitudes)
-        received[at] = moved
-
-    def forward(at):
+        received[at] = joined([moved])
+
+    def send_by_permutes(at, *after):
+        moved = transform(at, slot_grid[partners], lat_count, after)
+        for k in reversed(range(1, lat_count)):
+            moved[k] = lax.ppermute(moved[k], "lat", [(i, i ^ k) for i in range(lat_count)])
+        received[at] = joined(moved)
+
+    def forward(at, tables, *after):
         start, _ = bounds[at]
-        after = [tokens["i", at - 2]] if at >= 2 else []
         spectra, tokens["f", at] = forward_transform(
-            (own_waves, 2 * fields), start, block, received[at], even, odd, mem_local, after
+            (own_waves, 2 * fields),
+            start,
+            block,
+            received[at],
+            *tables,
+            mem_local,
+            [tokens[key] for key in after],
         )
         low = lax.ppermute(spectra[:, mem_local - SPREAD :], "member", upward)
         high = lax.ppermute(spectra[:, :SPREAD], "member", downward)
@@ -343,21 +374,27 @@
     def inverse(at, outs):
         start, _ = bounds[at]
         *outs, tokens["i", at] = inverse_transform(
-            own_waves, offsets, start, block, *own[at], noise, even, odd, outs
+            own_waves, offsets, start, block, *own[at], noise, *tables, outs
         )
         return outs
 
-    send(0)
-    even, odd = meridional_tables(truncation, latitudes, starts, inner)
-    if count > 1:
-        send(1)
-    for at in range(count):
-        forward(at)
-        if at >= 1:
-            outs = inverse(at - 1, outs)
-        if at + 2 < count:
-            send(at + 2)
-    outs = inverse(count - 1, outs)
+    send(1)
+    send_by_permutes(0)
+    swapped = tables_of(partners)
+    tables = tables_of(jnp.arange(lat_count, dtype=jnp.int32))
+    send(2, ("z", 0))
+    forward(1, tables)
+    forward(0, swapped, ("f", 1))
+    outs = inverse(1, outs)
+    if count > 3:
+        send(3, ("f", 0))
+    forward(2, tables)
+    outs = inverse(0, outs)
+    if count > 3:
+        forward(3, tables, ("i", 0))
+    outs = inverse(2, outs)
+    if count > 3:
+        outs = inverse(3, outs)
     return tuple(outs)
 
 

time: 195 us -> 219 us (1.12)
  starting transfers between devices: 44.8 us -> 58.1 us
  other arithmetic: 6.22 us -> 12.3 us
  waiting for transfers between devices: 47 us -> 41.7 us
  Pallas kernels: 88.5 us -> 93.7 us
  local copies, waits for them, and re-layouts: 6.01 us -> 10.8 us
    all_to_all x4 -> x3, waiting for transfers between devices: 46.3 us -> 28.7 us  [send(): lax.all_to_all(outgoing, 'lat', split_axis=0, concat_axis=0, tiled=True)]
    ppermute x0 -> x7, waiting for transfers between devices: none -> 12.9 us  [send_by_permutes(): lax.ppermute(moved[k], 'lat', [(i, i ^ k) for i in range(lat_count)])]
    ppermute x0 -> x7, starting transfers between devices: none -> 12.7 us  [send_by_permutes(): lax.ppermute(moved[k], 'lat', [(i, i ^ k) for i in range(lat_count)])]
    mul x1 -> x2, other arithmetic: 1.31 us -> 4.47 us  [meridional_factors(): jnp.sin(coarse) * factor]
    all_to_all x4 -> x3, starting transfers between devices: 21.3 us -> 22.7 us  [send(): lax.all_to_all(outgoing, 'lat', split_axis=0, concat_axis=0, tiled=True)]
  transfers between devices with their start and end apart: 12 -> 18, of which waited for: 4 -> 3; matrix products, arithmetic and copies ran while one was open for 4% -> 8% of each run, Pallas kernels for 38% -> 35%
where the time goes in v5:
time: 219 us; the launch traced here: 218 us
  Pallas kernels  93.7 us (43%)
  starting transfers between devices  58.1 us (27%)
  waiting for transfers between devices  41.7 us (19%)
  other arithmetic  12.3 us (6%)
  local copies, waits for them, and re-layouts  10.8 us (5%)
    pallas_call x4, Pallas kernels, zonal_transform(): pl.pallas_call(functools.partial(zonal_kernel, fields_step, fields, len(t...  45.3 us
    all_to_all x3, waiting for transfers between devices, send(): lax.all_to_all(outgoing, 'lat', split_axis=0, concat_axis=0, tiled=True)  28.7 us
    pallas_call x4, Pallas kernels, inverse_transform(): pl.pallas_call(functools.partial(inverse_kernel, first, block), grid_spec...  25 us
    all_to_all x3, starting transfers between devices, send(): lax.all_to_all(outgoing, 'lat', split_axis=0, concat_axis=0, tiled=True)  22.7 us
    pallas_call x4, Pallas kernels, forward_transform(): pl.pallas_call(functools.partial(forward_kernel, first, block, len(receiv...  19.7 us
    ppermute x4, starting transfers between devices, forward(): low = lax.ppermute(spectra[:, mem_local - SPREAD:], 'member', upward)  14.3 us
    ppermute x7, waiting for transfers between devices, send_by_permutes(): lax.ppermute(moved[k], 'lat', [(i, i ^ k) for i in range(lat_count)])  12.9 us
    ppermute x7, starting transfers between devices, send_by_permutes(): lax.ppermute(moved[k], 'lat', [(i, i ^ k) for i in range(lat_count)])  12.7 us
  transfers between devices with their start and end apart: 18, of which 3 were waited for; matrix products, arithmetic and copies ran while one was open for 8% of the time, Pallas kernels for 35%

profile of v5, /device:TPU:1, one launch (start us, length us, event | category | flops | bytes accessed | tf_op | source)
XLA Modules:
  0.0 217.5 jit_solution(13364164761061134911)
XLA Ops:
  0.6 0.8 reshape.113
  1.6 0.7 fusion.20
  3.1 15.0 %zonal.5 = (bf16[320,32,128]{2,1,0:T(8,128)(2,1)}, f32[8,128]{1,0:T(8,128)}) custom-call(f32[320,16]{1,0:T(8,128)S(1)} %get-tuple-element.69.cos_c, f32[320,16]{1,0:T(8,128)S(1)} %get-tuple-element.68.sin_c, f32[320,128]{1,0:T(8,128)S(1)} %get-tuple-element.77.cos_f, f32[320,128]{1,0:T(8,128)S(1)} %get-tuple-element.76.sin_f, ...), custom_call_target="tpu_custom_call" | custom-call | flops 5368709120 | bytes 19398656 | tf_op jit(solution)/shard_map/zonal/pallas_call | solution.py:128
  18.1 6.4 %all-to-all-start = ((bf16[8,1280,128]{2,1,0:T(8,128)(2,1)}), bf16[8,1280,128]{2,1,0:T(8,128)(2,1)S(1)}, u32[]{:S(2)}, u32[]{:S(2)}) async-start(bf16[8,1280,128]{2,1,0:T(8,128)(2,1)} %bitcast.9), calls=%async_computation | async-start | bytes 5242880 | tf_op jit(solution)/shard_map/all_to_all | solution.py:350
  26.0 9.8 %zonal.4 = (bf16[16,32,128]{2,1,0:T(8,128)(2,1)S(1)}, bf16[16,32,128]{2,1,0:T(8,128)(2,1)}, bf16[16,32,128]{2,1,0:T(8,128)(2,1)}, bf16[16,32,128]{2,1,0:T(8,128)...) custom-call(f32[128,16]{1,0:T(8,128)S(1)} %get-tuple-element.73.cos_, ...), custom_call_target="tpu_custom_call" | custom-call | flops 2147483648 | bytes 17825792 | tf_op jit(solution)/shard_map/zonal/pallas_call | solution.py:128
  39.0 1.5 collective-permute-start
  40.5 1.2 collective-permute-start.1
  42.9 11.5 %zonal.7 = (bf16[192,32,128]{2,1,0:T(8,128)(2,1)}, f32[8,128]{1,0:T(8,128)}) custom-call(f32[192,16]{1,0:T(8,128)S(1)} %get-tuple-element.71.cos_c, f32[192,16]{1,0:T(8,128)S(1)} %get-tuple-element.70.sin_c, f32[192,128]{1,0:T(8,128)S(1)} %get-tuple-element.79.cos_f, f32[192,128]{1,0:T(8,128)S(1)} %get-tuple-element.78.sin_f, ...), custom_call_target="tpu_custom_call" | custom-call | flops 3221225472 | bytes 18350080 | tf_op jit(solution)/shard_map/zonal/pallas_call | solution.py:128
  54.4 28.7 %all-to-all-done.refs_0_ = bf16[8,1280,128]{2,1,0:T(8,128)(2,1)S(1)} async-done(((bf16[8,1280,128]{2,1,0:T(8,128)(2,1)}), bf16[8,1280,128]{2,1,0:T(8,128)(2,1)S(1)}, u32[]{:S(2)}, u32[]{:S(2)}) %all-to-all-start) | async-done | bytes 2621472 | tf_op jit(solution)/shard_map/all_to_all | solution.py:350
  83.1 7.5 %all-to-all-start.2 = ((bf16[8,768,128]{2,1,0:T(8,128)(2,1)}), bf16[8,768,128]{2,1,0:T(8,128)(2,1)}, u32[]{:S(2)}, u32[]{:S(2)}) async-start(bf16[8,768,128]{2,1,0:T(8,128)(2,1)} %bitcast.11), calls=%async_computation.2 | async-start | bytes 3145728 | tf_op jit(solution)/shard_map/all_to_all | solution.py:350
  90.8 0.8 dynamic_slice.6.waves
  91.5 0.9 copy.17
  93.1 1.4 fusion.6
  94.5 2.2 %sine_multiply_fusion = (f32[683,8]{1,0:T(8,128)S(1)}, f32[683,8]{1,0:T(8,128)S(1)}) fusion(f32[683,8]{1,0:T(8,128)} %copy.17), kind=kLoop, calls=%fused_computation.7 | loop fusion | flops 16392 | bytes 65568 | tf_op jit(solution)/shard_map/mul | solution.py:45
  96.8 1.8 tables.3
  98.7 7.8 %forward.4 = (bf16[40,2,16,683]{3,2,1,0:T(8,128)(2,1)}, f32[8,128]{1,0:T(8,128)S(1)}) custom-call(s32[88]{0:T(128)S(1)} %dynamic_slice.6.waves, bf16[8,1280,128]{2,1,0:T(8,128)(2,1)} %copy-done.9, bf16[683,1024]{1,0:T(8,128)(2,1)S(1)} %get-tuple-element.44.refs_1_.even, bf16[683,1024]{1,0:T(8,128)(2,1)S(1)} %get-tuple-element.45.refs_2_.odd), custom_call_target="tpu_custom_call" | custom-call | flops 3580887040 | bytes 7167488 | tf_op jit(solution)/shard_map/forward/pallas_call | solution.py:176
  106.5 2.7 %collective-permute-start.10 = (bf16[40,2,16,683]{3,2,1,0:T(8,128)(2,1)}, bf16[40,2,16,683]{3,2,1,0:T(8,128)(2,1)}, u32[]{:S(2)}, u32[]{:S(2)}) collective-permute-start(bf16[40,2,16,683]{3,2,1,0:T(8,128)(2,1)} %get-tuple-element.50.own), channel_id=1, source_target_pairs={{8,0},{16,8},{24,16},{9,1},{17,9},{25,17},{10,2},{18,10},{26,18},{... | collective-permute-start | bytes 5245448 | tf_op jit(solution)/shard_map/ppermute | solution.py:371
  109.2 3.2 %collective-permute-start.9 = (bf16[40,2,16,683]{3,2,1,0:T(8,128)(2,1)}, bf16[40,2,16,683]{3,2,1,0:T(8,128)(2,1)}, u32[]{:S(2)}, u32[]{:S(2)}) collective-permute-start(bf16[40,2,16,683]{3,2,1,0:T(8,128)(2,1)} %get-tuple-element.50.own), channel_id=1, source_target_pairs={{0,8},{8,16},{16,24},{1,9},{9,17},{17,25},{2,10},{10,18},{18,26},{... | collective-permute-start | bytes 5245448 | tf_op jit(solution)/shard_map/ppermute | solution.py:370
  112.5 0.7 fusion.54
  113.2 0.9 copy.15
  114.1 1.4 copy.13
  115.4 2.3 %sine_multiply_fusion.1 = (f32[683,8]{1,0:T(8,128)S(1)}, f32[683,8]{1,0:T(8,128)S(1)}) fusion(f32[683,8]{1,0:T(8,128)} %copy.15), kind=kLoop, calls=%fused_computation.11 | loop fusion | flops 16392 | bytes 65568 | tf_op jit(solution)/shard_map/mul | solution.py:45
  117.7 1.8 tables.2
  119.5 0.7 compare_select_fusion.4
  120.2 2.6 %collective-permute-start.3 = (bf16[1,512,128]{2,1,0:T(8,128)(2,1)}, bf16[1,512,128]{2,1,0:T(8,128)(2,1)S(1)}, u32[]{:S(2)}, u32[]{:S(2)}) collective-permute-start(bf16[1,512,128]{2,1,0:T(8,128)(2,1)} %bitcast.19), channel_id=1, source_target_pairs={{0,4},{1,5},{2,6},{3,7},{4,0},{5,1},{6,2},{7,3},{8,12},{9,13},{10,... | collective-permute-start | bytes 393224 | tf_op jit(solution)/shard_map/ppermute | solution.py:356
  122.9 0.9 sine_multiply_fusion.5
  123.8 1.2 collective-permute-start.4
  125.0 3.0 %collective-permute-start.5 = (bf16[1,512,128]{2,1,0:T(8,128)(2,1)}, bf16[1,512,128]{2,1,0:T(8,128)(2,1)S(1)}, u32[]{:S(2)}, u32[]{:S(2)}) collective-permute-start(bf16[1,512,128]{2,1,0:T(8,128)(2,1)} %bitcast.17), channel_id=1, source_target_pairs={{0,6},{1,7},{2,4},{3,5},{4,2},{5,3},{6,0},{7,1},{8,14},{9,15},{10,... | collective-permute-start | bytes 393224 | tf_op jit(solution)/shard_map/ppermute | solution.py:356
  128.0 10.2 %collective-permute-done.3.refs_4_ = bf16[1,512,128]{2,1,0:T(8,128)(2,1)S(1)} collective-permute-done((bf16[1,512,128]{2,1,0:T(8,128)(2,1)}, bf16[1,512,128]{2,1,0:T(8,128)(2,1)S(1)}, u32[]{:S(2)}, u32[]{:S(2)}) %collective-permute-start.3) | collective-permute-done | bytes 131104 | tf_op jit(solution)/shard_map/ppermute | solution.py:356
  138.2 3.2 %collective-permute-start.6 = (bf16[1,512,128]{2,1,0:T(8,128)(2,1)}, bf16[1,512,128]{2,1,0:T(8,128)(2,1)S(1)}, u32[]{:S(2)}, u32[]{:S(2)}) collective-permute-start(bf16[1,512,128]{2,1,0:T(8,128)(2,1)} %bitcast.16), channel_id=1, source_target_pairs={{0,7},{1,6},{2,5},{3,4},{4,3},{5,2},{6,1},{7,0},{8,15},{9,14},{10,... | collective-permute-start | bytes 393224 | tf_op jit(solution)/shard_map/ppermute | solution.py:356
  141.4 0.9 fusion.52
  142.3 2.7 %collective-permute-done.6.refs_7_ = bf16[1,512,128]{2,1,0:T(8,128)(2,1)S(1)} collective-permute-done((bf16[1,512,128]{2,1,0:T(8,128)(2,1)}, bf16[1,512,128]{2,1,0:T(8,128)(2,1)S(1)}, u32[]{:S(2)}, u32[]{:S(2)}) %collective-permute-start.6) | collective-permute-done | bytes 131104 | tf_op jit(solution)/shard_map/ppermute | solution.py:356
  145.0 4.3 %forward.5 = (bf16[16,2,16,683]{3,2,1,0:T(8,128)(2,1)}, f32[8,128]{1,0:T(8,128)S(1)}) custom-call(s32[88]{0:T(128)S(1)} %dynamic_slice.6.waves, bf16[1,512,128]{2,1,0:T(8,128)(2,1)S(1)} %bitcast.15, bf16[1,512,128]{2,1,0:T(8,128)(2,1)} %collective-permute-done.refs_1_, bf16[1,512,128]{2,1,0:T(8,128)(2,1)} %collective-permute-done.1.refs_2_, ...), custom_call_target="tpu_custom_call" | custom-call | flops 1432354816 | bytes 4545536 | tf_op jit(solution)/shard_map/forward/pallas_call | solution.py:176
  149.3 9.0 %zonal.6 = (bf16[64,32,128]{2,1,0:T(8,128)(2,1)S(1)}, f32[8,128]{1,0:T(8,128)}) custom-call(f32[64,16]{1,0:T(8,128)S(1)} %get-tuple-element.75.cos_c, f32[64,16]{1,0:T(8,128)S(1)} %get-tuple-element.74.sin_c, f32[64,128]{1,0:T(8,128)S(1)} %get-tuple-element.85.cos_f, f32[64,128]{1,0:T(8,128)S(1)} %get-tuple-element.84.sin_f, ...), custom_call_target="tpu_custom_call" | custom-call | flops 1073741824 | bytes 17301504 | tf_op jit(solution)/shard_map/zonal/pallas_call | solution.py:128
  158.3 0.8 copy-done.2
  159.1 8.8 %all-to-all-start.1 = ((bf16[8,256,128]{2,1,0:T(8,128)(2,1)}), bf16[8,256,128]{2,1,0:T(8,128)(2,1)S(1)}, u32[]{:S(2)}, u32[]{:S(2)}) async-start(bf16[8,256,128]{2,1,0:T(8,128)(2,1)} %bitcast.14), calls=%async_computation.1 | async-start | bytes 1048576 | tf_op jit(solution)/shard_map/all_to_all | solution.py:350
  167.9 5.6 %forward.7 = (bf16[24,2,16,683]{3,2,1,0:T(8,128)(2,1)}, f32[8,128]{1,0:T(8,128)}) custom-call(s32[88]{0:T(128)S(1)} %dynamic_slice.6.waves, bf16[8,768,128]{2,1,0:T(8,128)(2,1)} %all-to-all-done.2.refs_0_, bf16[683,1024]{1,0:T(8,128)(2,1)S(1)} %get-tuple-element.44.refs_1_.even, bf16[683,1024]{1,0:T(8,128)(2,1)S(1)} %get-tuple-element.45.refs_2_.odd), custom_call_target="tpu_custom_call" | custom-call | flops 2148532224 | bytes 5419520 | tf_op jit(solution)/shard_map/forward/pallas_call | solution.py:176
  173.5 3.8 %collective-permute-start.7 = (bf16[16,2,16,683]{3,2,1,0:T(8,128)(2,1)}, bf16[16,2,16,683]{3,2,1,0:T(8,128)(2,1)}, u32[]{:S(2)}, u32[]{:S(2)}) collective-permute-start(bf16[16,2,16,683]{3,2,1,0:T(8,128)(2,1)} %get-tuple-element.49.own), channel_id=1, source_target_pairs={{0,8},{8,16},{16,24},{1,9},{9,17},{17,25},{2,10},{10,18},{18,26},{... | collective-permute-start | bytes 2098184 | tf_op jit(solution)/shard_map/ppermute | solution.py:370
  177.3 1.9 collective-permute-start.8
  179.2 3.6 %collective-permute-start.13 = (bf16[24,2,16,683]{3,2,1,0:T(8,128)(2,1)}, bf16[24,2,16,683]{3,2,1,0:T(8,128)(2,1)}, u32[]{:S(2)}, u32[]{:S(2)}) collective-permute-start(bf16[24,2,16,683]{3,2,1,0:T(8,128)(2,1)} %get-tuple-element.57.own), channel_id=1, source_target_pairs={{0,8},{8,16},{16,24},{1,9},{9,17},{17,25},{2,10},{10,18},{18,26},{... | collective-permute-start | bytes 3147272 | tf_op jit(solution)/shard_map/ppermute | solution.py:370
  182.9 1.9 collective-permute-start.14
  184.9 9.3 %inverse.4 = (bf16[88,2,2,8,683]{4,3,2,1,0:T(8,128)(2,1)}, bf16[88,2,2,8,1024]{4,3,2,1,0:T(8,128)(2,1)}, f32[8,128]{1,0:T(8,128)}) custom-call(s32[88]{0:T(128)S(1)} %dynamic_slice.6.waves, s32[2]{0:T(128)S(1)} %subtract_add_fusion.offsets, bf16[40,2,16,683]{3,2,1,0:T(8,128)(2,1)} %collective-permute-done.9.low, ...), custom_call_target="tpu_custom_call" | custom-call | flops 3580887040 | bytes 14161408 | tf_op jit(solution)/shard_map/inverse/pallas_call | solution.py:266
  194.2 4.9 %inverse.5 = (bf16[88,2,2,8,683]{4,3,2,1,0:T(8,128)(2,1)}, bf16[88,2,2,8,1024]{4,3,2,1,0:T(8,128)(2,1)}, f32[8,128]{1,0:T(8,128)S(1)}) custom-call(s32[88]{0:T(128)S(1)} %dynamic_slice.6.waves, s32[2]{0:T(128)S(1)} %subtract_add_fusion.offsets, bf16[16,2,16,683]{3,2,1,0:T(8,128)(2,1)} %collective-permute-done.7.low, ...), custom_call_target="tpu_custom_call", output_to_operand_aliasing={{0}: (8, {}), {1}: (9, {})} | custom-call | flops 1432354816 | bytes 7343104 | tf_op jit(solution)/shard_map/inverse/pallas_call | solution.py:266
  199.1 2.0 forward.6
  201.1 3.6 %collective-permute-start.11 = (bf16[8,2,16,683]{3,2,1,0:T(8,128)(2,1)S(1)}, bf16[8,2,16,683]{3,2,1,0:T(8,128)(2,1)S(1)}, u32[]{:S(2)}, u32[]{:S(2)}) collective-permute-start(bf16[8,2,16,683]{3,2,1,0:T(8,128)(2,1)S(1)} %get-tuple-element.54.own), channel_id=1, source_target_pairs={{0,8},{8,16},{16,24},{1,9},{9,17},{17,25},{2,10},{10,18},{18,26},{... | collective-permute-start | bytes 1049096 | tf_op jit(solution)/shard_map/ppermute | solution.py:370
  204.7 1.9 collective-permute-start.12
  206.7 7.4 %inverse.6 = (bf16[88,2,2,8,683]{4,3,2,1,0:T(8,128)(2,1)}, bf16[88,2,2,8,1024]{4,3,2,1,0:T(8,128)(2,1)}, f32[8,128]{1,0:T(8,128)}) custom-call(s32[88]{0:T(128)S(1)} %dynamic_slice.6.waves, s32[2]{0:T(128)S(1)} %subtract_add_fusion.offsets, bf16[24,2,16,683]{3,2,1,0:T(8,128)(2,1)} %collective-permute-done.13.low, ...), custom_call_target="tpu_custom_call", output_to_operand_aliasing={{0}: (8, {}), {1}: (9, {})} | custom-call | flops 2148532224 | bytes 9615872 | tf_op jit(solution)/shard_map/inverse/pallas_call | solution.py:266
  214.1 3.4 %inverse.7 = (bf16[88,2,2,8,683]{4,3,2,1,0:T(8,128)(2,1)}, bf16[88,2,2,8,1024]{4,3,2,1,0:T(8,128)(2,1)}, f32[8,128]{1,0:T(8,128)}) custom-call(s32[88]{0:T(128)S(1)} %dynamic_slice.6.waves, s32[2]{0:T(128)S(1)} %subtract_add_fusion.offsets, bf16[8,2,16,683]{3,2,1,0:T(8,128)(2,1)S(1)} %collective-permute-done.11.low, ...), custom_call_target="tpu_custom_call", output_to_operand_aliasing={{0}: (8, {}), {1}: (9, {})} | custom-call | flops 716177408 | bytes 5070336 | tf_op jit(solution)/shard_map/inverse/pallas_call | solution.py:266
  (74 shorter events, 7.9 us)
Async XLA Ops:
  0.6 41.2 %copy-start.10 = (s32[16]{0:T(128)}, s32[16]{0:T(128)S(1)}, u32[]{:S(2)}) copy-start(s32[16]{0:T(128)S(1)} %iota_multiply_fusion.1) | copy-start | bytes 196
  18.1 65.0 %all-to-all-start = ((bf16[8,1280,128]{2,1,0:T(8,128)(2,1)}), bf16[8,1280,128]{2,1,0:T(8,128)(2,1)S(1)}, u32[]{:S(2)}, u32[]{:S(2)}) async-start(bf16[8,1280,128]{2,1,0:T(8,128)(2,1)} %bitcast.9), calls=%async_computation | async-start | bytes 5242880 | tf_op jit(solution)/shard_map/all_to_all | solution.py:350
  35.8 0.7 copy-start.3
  36.4 0.6 copy-start.5
  37.1 0.7 copy-start.6
  37.7 0.7 copy-start.7
  38.4 0.7 copy-start.8
  39.0 81.2 %collective-permute-start = (bf16[1,512,128]{2,1,0:T(8,128)(2,1)}, bf16[1,512,128]{2,1,0:T(8,128)(2,1)}, u32[]{:S(2)}, u32[]{:S(2)}) collective-permute-start(bf16[1,512,128]{2,1,0:T(8,128)(2,1)} %bitcast.2), channel_id=1, source_target_pairs={{0,1},{1,0},{2,3},{3,2},{4,5},{5,4},{6,7},{7,6},{8,9},{9,8},{10,11... | collective-permute-start | bytes 393224 | tf_op jit(solution)/shard_map/ppermute | solution.py:356
  40.5 83.2 %collective-permute-start.1 = (bf16[1,512,128]{2,1,0:T(8,128)(2,1)}, bf16[1,512,128]{2,1,0:T(8,128)(2,1)}, u32[]{:S(2)}, u32[]{:S(2)}) collective-permute-start(bf16[1,512,128]{2,1,0:T(8,128)(2,1)} %bitcast.3), channel_id=1, source_target_pairs={{0,2},{1,3},{2,0},{3,1},{4,6},{5,7},{6,4},{7,5},{8,10},{9,11},{10,... | collective-permute-start | bytes 393224 | tf_op jit(solution)/shard_map/ppermute | solution.py:356
  41.7 83.3 %collective-permute-start.2 = (bf16[1,512,128]{2,1,0:T(8,128)(2,1)}, bf16[1,512,128]{2,1,0:T(8,128)(2,1)}, u32[]{:S(2)}, u32[]{:S(2)}) collective-permute-start(bf16[1,512,128]{2,1,0:T(8,128)(2,1)} %bitcast.4), channel_id=1, source_target_pairs={{0,3},{1,2},{2,1},{3,0},{4,7},{5,6},{6,5},{7,4},{8,11},{9,10},{10,... | collective-permute-start | bytes 393224 | tf_op jit(solution)/shard_map/ppermute | solution.py:356
  83.1 13.6 %copy-start.9 = (bf16[8,1280,128]{2,1,0:T(8,128)(2,1)}, bf16[8,1280,128]{2,1,0:T(8,128)(2,1)S(1)}, u32[]{:S(2)}) copy-start(bf16[8,1280,128]{2,1,0:T(8,128)(2,1)S(1)} %all-to-all-done.refs_0_) | copy-start | bytes 7864324
  83.1 76.0 %all-to-all-start.2 = ((bf16[8,768,128]{2,1,0:T(8,128)(2,1)}), bf16[8,768,128]{2,1,0:T(8,128)(2,1)}, u32[]{:S(2)}, u32[]{:S(2)}) async-start(bf16[8,768,128]{2,1,0:T(8,128)(2,1)} %bitcast.11), calls=%async_computation.2 | async-start | bytes 3145728 | tf_op jit(solution)/shard_map/all_to_all | solution.py:350
  98.6 100.5 %copy-start = (bf16[683,1024]{1,0:T(8,128)(2,1)}, bf16[683,1024]{1,0:T(8,128)(2,1)S(1)}, u32[]{:S(2)}) copy-start(bf16[683,1024]{1,0:T(8,128)(2,1)S(1)} %get-tuple-element.45.refs_2_.odd) | copy-start | bytes 4196356
  98.6 13.8 %copy-start.11 = (s32[16]{0:T(128)S(1)}, s32[16]{0:T(128)}, u32[]{:S(2)}) copy-start(s32[16]{0:T(128)} %copy-done.10) | copy-start | bytes 196
  98.6 13.8 %copy-start.12 = (s32[64]{0:T(128)S(1)}, s32[64]{0:T(128)}, u32[]{:S(2)}) copy-start(s32[64]{0:T(128)} %mul.382) | copy-start | bytes 772
  106.5 76.4 %collective-permute-start.10 = (bf16[40,2,16,683]{3,2,1,0:T(8,128)(2,1)}, bf16[40,2,16,683]{3,2,1,0:T(8,128)(2,1)}, u32[]{:S(2)}, u32[]{:S(2)}) collective-permute-start(bf16[40,2,16,683]{3,2,1,0:T(8,128)(2,1)} %get-tuple-element.50.own), channel_id=1, source_target_pairs={{8,0},{16,8},{24,16},{9,1},{17,9},{25,17},{10,2},{18,10},{26,18},{... | collective-permute-start | bytes 5245448 | tf_op jit(solution)/shard_map/ppermute | solution.py:371
  109.2 75.7 %collective-permute-start.9 = (bf16[40,2,16,683]{3,2,1,0:T(8,128)(2,1)}, bf16[40,2,16,683]{3,2,1,0:T(8,128)(2,1)}, u32[]{:S(2)}, u32[]{:S(2)}) collective-permute-start(bf16[40,2,16,683]{3,2,1,0:T(8,128)(2,1)} %get-tuple-element.50.own), channel_id=1, source_target_pairs={{0,8},{8,16},{16,24},{1,9},{9,17},{17,25},{2,10},{10,18},{18,26},{... | collective-permute-start | bytes 5245448 | tf_op jit(solution)/shard_map/ppermute | solution.py:370
  115.4 29.6 %copy-start.4 = (bf16[16,32,128]{2,1,0:T(8,128)(2,1)S(1)}, bf16[16,32,128]{2,1,0:T(8,128)(2,1)}, u32[]{:S(2)}) copy-start(bf16[16,32,128]{2,1,0:T(8,128)(2,1)} %copy-done.3) | copy-start | bytes 393220
  120.2 18.0 %collective-permute-start.3 = (bf16[1,512,128]{2,1,0:T(8,128)(2,1)}, bf16[1,512,128]{2,1,0:T(8,128)(2,1)S(1)}, u32[]{:S(2)}, u32[]{:S(2)}) collective-permute-start(bf16[1,512,128]{2,1,0:T(8,128)(2,1)} %bitcast.19), channel_id=1, source_target_pairs={{0,4},{1,5},{2,6},{3,7},{4,0},{5,1},{6,2},{7,3},{8,12},{9,13},{10,... | collective-permute-start | bytes 393224 | tf_op jit(solution)/shard_map/ppermute | solution.py:356
  123.8 18.5 %collective-permute-start.4 = (bf16[1,512,128]{2,1,0:T(8,128)(2,1)}, bf16[1,512,128]{2,1,0:T(8,128)(2,1)S(1)}, u32[]{:S(2)}, u32[]{:S(2)}) collective-permute-start(bf16[1,512,128]{2,1,0:T(8,128)(2,1)} %bitcast.18), channel_id=1, source_target_pairs={{0,5},{1,4},{2,7},{3,6},{4,1},{5,0},{6,3},{7,2},{8,13},{9,12},{10,... | collective-permute-start | bytes 393224 | tf_op jit(solution)/shard_map/ppermute | solution.py:356
  125.0 17.3 %collective-permute-start.5 = (bf16[1,512,128]{2,1,0:T(8,128)(2,1)}, bf16[1,512,128]{2,1,0:T(8,128)(2,1)S(1)}, u32[]{:S(2)}, u32[]{:S(2)}) collective-permute-start(bf16[1,512,128]{2,1,0:T(8,128)(2,1)} %bitcast.17), channel_id=1, source_target_pairs={{0,6},{1,7},{2,4},{3,5},{4,2},{5,3},{6,0},{7,1},{8,14},{9,15},{10,... | collective-permute-start | bytes 393224 | tf_op jit(solution)/shard_map/ppermute | solution.py:356
  138.2 6.8 %collective-permute-start.6 = (bf16[1,512,128]{2,1,0:T(8,128)(2,1)}, bf16[1,512,128]{2,1,0:T(8,128)(2,1)S(1)}, u32[]{:S(2)}, u32[]{:S(2)}) collective-permute-start(bf16[1,512,128]{2,1,0:T(8,128)(2,1)} %bitcast.16), channel_id=1, source_target_pairs={{0,7},{1,6},{2,5},{3,4},{4,3},{5,2},{6,1},{7,0},{8,15},{9,14},{10,... | collective-permute-start | bytes 393224 | tf_op jit(solution)/shard_map/ppermute | solution.py:356
  158.3 0.8 copy-start.2
  159.1 40.0 %all-to-all-start.1 = ((bf16[8,256,128]{2,1,0:T(8,128)(2,1)}), bf16[8,256,128]{2,1,0:T(8,128)(2,1)S(1)}, u32[]{:S(2)}, u32[]{:S(2)}) async-start(bf16[8,256,128]{2,1,0:T(8,128)(2,1)} %bitcast.14), calls=%async_computation.1 | async-start | bytes 1048576 | tf_op jit(solution)/shard_map/all_to_all | solution.py:350
  167.9 16.9 %copy-start.13 = (s32[8]{0:T(128)S(1)}, s32[8]{0:T(128)}, u32[]{:S(2)}) copy-start(s32[8]{0:T(128)} %param.8) | copy-start | bytes 100
  173.5 20.7 %collective-permute-start.7 = (bf16[16,2,16,683]{3,2,1,0:T(8,128)(2,1)}, bf16[16,2,16,683]{3,2,1,0:T(8,128)(2,1)}, u32[]{:S(2)}, u32[]{:S(2)}) collective-permute-start(bf16[16,2,16,683]{3,2,1,0:T(8,128)(2,1)} %get-tuple-element.49.own), channel_id=1, source_target_pairs={{0,8},{8,16},{16,24},{1,9},{9,17},{17,25},{2,10},{10,18},{18,26},{... | collective-permute-start | bytes 2098184 | tf_op jit(solution)/shard_map/ppermute | solution.py:370
  177.3 16.9 %collective-permute-start.8 = (bf16[16,2,16,683]{3,2,1,0:T(8,128)(2,1)}, bf16[16,2,16,683]{3,2,1,0:T(8,128)(2,1)}, u32[]{:S(2)}, u32[]{:S(2)}) collective-permute-start(bf16[16,2,16,683]{3,2,1,0:T(8,128)(2,1)} %get-tuple-element.49.own), channel_id=1, source_target_pairs={{8,0},{16,8},{24,16},{9,1},{17,9},{25,17},{10,2},{18,10},{26,18},{... | collective-permute-start | bytes 2098184 | tf_op jit(solution)/shard_map/ppermute | solution.py:371
  179.2 27.5 %collective-permute-start.13 = (bf16[24,2,16,683]{3,2,1,0:T(8,128)(2,1)}, bf16[24,2,16,683]{3,2,1,0:T(8,128)(2,1)}, u32[]{:S(2)}, u32[]{:S(2)}) collective-permute-start(bf16[24,2,16,683]{3,2,1,0:T(8,128)(2,1)} %get-tuple-element.57.own), channel_id=1, source_target_pairs={{0,8},{8,16},{16,24},{1,9},{9,17},{17,25},{2,10},{10,18},{18,26},{... | collective-permute-start | bytes 3147272 | tf_op jit(solution)/shard_map/ppermute | solution.py:370
  182.9 23.8 %collective-permute-start.14 = (bf16[24,2,16,683]{3,2,1,0:T(8,128)(2,1)}, bf16[24,2,16,683]{3,2,1,0:T(8,128)(2,1)}, u32[]{:S(2)}, u32[]{:S(2)}) collective-permute-start(bf16[24,2,16,683]{3,2,1,0:T(8,128)(2,1)} %get-tuple-element.57.own), channel_id=1, source_target_pairs={{8,0},{16,8},{24,16},{9,1},{17,9},{25,17},{10,2},{18,10},{26,18},{... | collective-permute-start | bytes 3147272 | tf_op jit(solution)/shard_map/ppermute | solution.py:371
  201.1 13.0 %collective-permute-start.11 = (bf16[8,2,16,683]{3,2,1,0:T(8,128)(2,1)S(1)}, bf16[8,2,16,683]{3,2,1,0:T(8,128)(2,1)S(1)}, u32[]{:S(2)}, u32[]{:S(2)}) collective-permute-start(bf16[8,2,16,683]{3,2,1,0:T(8,128)(2,1)S(1)} %get-tuple-element.54.own), channel_id=1, source_target_pairs={{0,8},{8,16},{16,24},{1,9},{9,17},{17,25},{2,10},{10,18},{18,26},{... | collective-permute-start | bytes 1049096 | tf_op jit(solution)/shard_map/ppermute | solution.py:370
  204.7 9.4 %collective-permute-start.12 = (bf16[8,2,16,683]{3,2,1,0:T(8,128)(2,1)S(1)}, bf16[8,2,16,683]{3,2,1,0:T(8,128)(2,1)S(1)}, u32[]{:S(2)}, u32[]{:S(2)}) collective-permute-start(bf16[8,2,16,683]{3,2,1,0:T(8,128)(2,1)S(1)} %get-tuple-element.54.own), channel_id=1, source_target_pairs={{8,0},{16,8},{24,16},{9,1},{17,9},{25,17},{10,2},{18,10},{26,18},{... | collective-permute-start | bytes 1049096 | tf_op jit(solution)/shard_map/ppermute | solution.py:371
  206.7 7.4 %copy-start.1 = (bf16[683,1024]{1,0:T(8,128)(2,1)S(1)}, bf16[683,1024]{1,0:T(8,128)(2,1)}, u32[]{:S(2)}) copy-start(bf16[683,1024]{1,0:T(8,128)(2,1)} %copy-done) | copy-start | bytes 4196356

commit v6 on v4

--- a/solution.py
+++ b/solution.py
@@ -283,14 +283,125 @@
     )(waves, offsets, *operands)
 
 
+def copy_kernel(members, pieces, offsets, low, own, high, out, sems):
+    rows_total, rows = out.shape[0], out.shape[1] // members
+    size = rows_total // pieces
+    sources = [(ref, at) for ref in (low, own, high) for at in range(ref.shape[1] // rows)]
+
+    def copy(child, piece, source):
+        ref, at = source
+        part = pl.ds(piece * size, size)
+        return pltpu.make_async_copy(
+            ref.at[part, pl.ds(at * rows, rows)],
+            out.at[part, pl.ds(child * rows, rows)],
+            sems.at[child, piece],
+        )
+
+    for child in range(members):
+        for index, source in enumerate(sources):
+
+            @pl.when(offsets[child] == index)
+            def _():
+                for piece in range(pieces):
+                    copy(child, piece, source).start()
+
+    for child in range(members):
+        for piece in range(pieces):
+            copy(child, piece, sources[0]).wait()
+
+
+def copy_parents(offsets, low, own, high):
+    members = offsets.shape[0]
+    pieces = math.gcd(own.shape[0], 4)
+    anywhere = pl.BlockSpec(memory_space=pl.ANY)
+    return pl.pallas_call(
+        functools.partial(copy_kernel, members, pieces),
+        in_specs=[pl.BlockSpec(memory_space=pltpu.SMEM)] + [anywhere] * 3,
+        out_specs=anywhere,
+        out_shape=jax.ShapeDtypeStruct(own.shape, own.dtype),
+        scratch_shapes=[pltpu.SemaphoreType.DMA((members, pieces))],
+        cost_estimate=pl.CostEstimate(flops=0, bytes_accessed=4 * own.size, transcendentals=0),
+        name="parents",
+    )(offsets, low, own, high)
+
+
+def finish_kernel(first, block, waves, received, noise, even, odd, *rest):
+    spectra_out, fourier_out = rest[-2:]
+    truncation = even.shape[0]
+    mem_local, parts, fields = noise.shape[1:4]
+    step = pl.program_id(0)
+    per_slot = received.shape[1] // block
+    rows = jnp.concatenate([received[g] for g in range(received.shape[0])], axis=-1)
+    contract = (((1,), (1,)), ((), ()))
+    by_even = lax.dot_general(rows, even[...], contract, preferred_element_type=jnp.float32)
+    by_odd = lax.dot_general(rows, odd[...], contract, preferred_element_type=jnp.float32)
+    degree = lax.broadcasted_iota(jnp.int32, (per_slot, truncation), 1)
+    even_rows, odd_rows = [], []
+    for slot in range(block):
+        wave = waves[first + step * block + slot]
+        least = jnp.where(wave < truncation, wave, truncation)
+        is_odd = wave % 2 == 1
+        active = degree >= least
+        here = slice(slot * per_slot, (slot + 1) * per_slot)
+        spectra = jnp.where(is_odd, by_odd[here], by_even[here])
+        spectra = spectra.astype(jnp.bfloat16).astype(jnp.float32)
+        added = noise[slot].astype(jnp.float32).reshape(per_slot, truncation)
+        child = jnp.where(active, spectra + added, 0.0)
+        spectra_out[slot] = child.reshape(noise.shape[1:]).astype(spectra_out.dtype)
+        even_rows.append(jnp.where(is_odd, 0.0, child).astype(jnp.bfloat16))
+        odd_rows.append(jnp.where(is_odd, child, 0.0).astype(jnp.bfloat16))
+    result = jnp.dot(
+        jnp.concatenate(even_rows, axis=0), even[...], preferred_element_type=jnp.float32
+    )
+    result += jnp.dot(
+        jnp.concatenate(odd_rows, axis=0), odd[...], preferred_element_type=jnp.float32
+    )
+    fourier_out[...] = result.reshape(fourier_out.shape).astype(fourier_out.dtype)
+
+
+def finish_transform(waves, first, block, received, noise, even, odd, outs):
+    slots_all, mem_local, parts, fields, truncation = noise.shape
+    latitudes = even.shape[1]
+    groups, all_rows, lat_local = received.shape
+    per_slot = mem_local * parts * fields
+    at = first // block
+    far = lambda step, w: (at + step, 0, 0, 0, 0)
+    table = pl.BlockSpec(even.shape, lambda step, w: (0, 0))
+    noise_block = pl.BlockSpec((block,) + noise.shape[1:], far)
+    fourier_shape = noise.shape[:4] + (latitudes,)
+    fourier_block = pl.BlockSpec((block,) + fourier_shape[1:], far)
+    received_block = pl.BlockSpec(
+        (groups, block * per_slot, lat_local), lambda step, w: (0, step, 0)
+    )
+    return pl.pallas_call(
+        functools.partial(finish_kernel, first, block),
+        grid_spec=pltpu.PrefetchScalarGridSpec(
+            num_scalar_prefetch=1,
+            grid=(all_rows // (block * per_slot),),
+            in_specs=[received_block, noise_block, table, table]
+            + [pl.BlockSpec(memory_space=pl.ANY)] * 2,
+            out_specs=[noise_block, fourier_block],
+        ),
+        out_shape=[
+            jax.ShapeDtypeStruct(noise.shape, jnp.bfloat16),
+            jax.ShapeDtypeStruct(fourier_shape, jnp.bfloat16),
+        ],
+        input_output_aliases={5: 0, 6: 1},
+        compiler_params=pltpu.CompilerParams(vmem_limit_bytes=VMEM_BYTES),
+        cost_estimate=pl.CostEstimate(
+            flops=8 * all_rows * truncation * latitudes,
+            bytes_accessed=2 * all_rows * (2 * truncation + 2 * latitudes) + 4 * even.size,
+            transcendentals=0,
+        ),
+        name="finish",
+    )(waves, received, noise, even, odd, *outs)
+
+
 def chunk_bounds(slots_here, block):
     blocks = slots_here // block
-    edges = [0, 3, 7, 10, 11]
-    if blocks < edges[-1]:
-        edges = list(range(blocks + 1))
-    edges[-1] = blocks
+    edges = [0, (blocks * 4 + 10) // 11, (blocks * 8 + 10) // 11, blocks]
     edges = [edge * block for edge in edges]
-    return list(zip(edges[:-1], edges[1:]))
+    return [(start, stop) for start, stop in zip(edges[:-1], edges[1:]) if stop > start]
 
 
 def per_device(velocity, tracer, wave_slots, parents, noise):
@@ -301,7 +412,8 @@
     mem_local, fields, lat_local, longitudes = velocity.shape
     slots_here, truncation = noise.shape[0], noise.shape[-1]
     block = math.gcd(slots_here, 8)
-    per_slot = mem_local * 2 * fields
+    per_member = 2 * fields
+    per_slot = mem_local * per_member
     latitudes = lat_count * lat_local
     own_waves = lax.dynamic_slice_in_dim(wave_slots, lat_index * slots_here, slots_here)
     first_member = group_index * mem_local
@@ -311,53 +423,38 @@
     downward = [(target, source) for source, target in upward]
     slot_grid = wave_slots.reshape(lat_count, slots_here)
     bounds = chunk_bounds(slots_here, block)
-    count = len(bounds)
     inner = min(lat_local, LANES)
     starts = jnp.arange(latitudes // inner, dtype=jnp.int32) * inner
-    received, own, tokens = {}, {}, {}
-    outs = None
-
-    def send(at):
+
+    def zonal(at):
         start, stop = bounds[at]
-        waves = slot_grid[:, start:stop].reshape(-1)
-        factors = zonal_factors(waves, longitudes, truncation)
-        after = [tokens["f", at - 2]] if at >= 2 else []
-        outgoing = zonal_transform(factors, velocity, tracer, after)
-        rows = (stop - start) * per_slot
-        outgoing = outgoing.reshape(lat_count, rows, lat_local)
+        factors = zonal_factors(slot_grid[:, start:stop].reshape(-1), longitudes, truncation)
+        return zonal_transform(factors, velocity, tracer, [])
+
+    def neighbours(rows, per_member):
+        low = lax.ppermute(rows[:, rows.shape[1] - SPREAD * per_member :], "member", upward)
+        high = lax.ppermute(rows[:, : SPREAD * per_member], "member", downward)
+        return low, rows, high
+
+    def exchanged(outgoing):
+        outgoing = outgoing.reshape(lat_count, -1, lat_local)
         moved = lax.all_to_all(outgoing, "lat", split_axis=0, concat_axis=0, tiled=True)
         if lat_local % LANES != 0:
-            moved = jnp.swapaxes(moved, 0, 1).reshape(1, rows, latitudes)
-        received[at] = moved
-
-    def forward(at):
-        start, _ = bounds[at]
-        after = [tokens["i", at - 2]] if at >= 2 else []
-        spectra, tokens["f", at] = forward_transform(
-            (own_waves, 2 * fields), start, block, received[at], even, odd, mem_local, after
-        )
-        low = lax.ppermute(spectra[:, mem_local - SPREAD :], "member", upward)
-        high = lax.ppermute(spectra[:, :SPREAD], "member", downward)
-        own[at] = (low, spectra, high)
-
-    def inverse(at, outs):
-        start, _ = bounds[at]
-        *outs, tokens["i", at] = inverse_transform(
-            own_waves, offsets, start, block, *own[at], noise, even, odd, outs
-        )
-        return outs
-
-    send(0)
+            moved = jnp.swapaxes(moved, 0, 1).reshape(1, -1, latitudes)
+        return moved
+
+    received = exchanged(zonal(0))
     even, odd = meridional_tables(truncation, latitudes, starts, inner)
-    if count > 1:
-        send(1)
-    for at in range(count):
-        forward(at)
-        if at >= 1:
-            outs = inverse(at - 1, outs)
-        if at + 2 < count:
-            send(at + 2)
-    outs = inverse(count - 1, outs)
+    later = [copy_parents(offsets, *neighbours(zonal(at), per_member)) for at in range(1, len(bounds))]
+    later = [exchanged(outgoing) for outgoing in later]
+    spectra, _ = forward_transform(
+        (own_waves, per_member), 0, block, received, even, odd, mem_local, []
+    )
+    *outs, _ = inverse_transform(
+        own_waves, offsets, 0, block, *neighbours(spectra, 1), noise, even, odd, None
+    )
+    for (start, _), received in zip(bounds[1:], later):
+        outs = finish_transform(own_waves, start, block, received, noise, even, odd, outs)
     return tuple(outs)
 
 

time: 195 us -> 292 us (1.50)
  Pallas kernels: 88.5 us -> 184 us
  waiting for transfers between devices: 47 us -> 61.4 us
  starting transfers between devices: 44.8 us -> 32.5 us
    pallas_call x0 -> x4, Pallas kernels: none -> 133 us  [the longest x2 115 us: copy_parents(): pl.pallas_call(functools.partial(copy_kernel, members, pieces), in_specs=...]
    ppermute x8 -> x6, waiting for transfers between devices: 0.75 us -> 61.4 us  [the longest x3 47.7 us: neighbours(): lax.ppermute(rows[:, rows.shape[1] - SPREAD * per_member:], 'member', upw...]
    all_to_all x4 -> x3, waiting for transfers between devices: 46.3 us -> 0.01 us  [exchanged(): lax.all_to_all(outgoing, 'lat', split_axis=0, concat_axis=0, tiled=True)]
    pallas_call x4 -> x1, Pallas kernels: 24.4 us -> 7.1 us  [inverse_transform(): pl.pallas_call(functools.partial(inverse_kernel, first, block), grid_spec...]
    pallas_call x4 -> x1, Pallas kernels: 18 us -> 6.18 us  [forward_transform(): pl.pallas_call(functools.partial(forward_kernel, first, block), grid_spec...]
    pallas_call x4 -> x3, Pallas kernels: 44.4 us -> 35.5 us  [zonal_transform(): pl.pallas_call(functools.partial(zonal_kernel, fields_step, fields, len(t...]
    ppermute x8 -> x6, starting transfers between devices: 23.5 us -> 14.9 us  [the longest x3 7.8 us: neighbours(): lax.ppermute(rows[:, rows.shape[1] - SPREAD * per_member:], 'member', upw...]
    all_to_all x4 -> x3, starting transfers between devices: 21.3 us -> 17.6 us  [exchanged(): lax.all_to_all(outgoing, 'lat', split_axis=0, concat_axis=0, tiled=True)]
  transfers between devices with their start and end apart: 12 -> 9, of which waited for: 4 -> 6; matrix products, arithmetic and copies ran while one was open for 4% -> 3% of each run, Pallas kernels for 38% -> 56%
where the time goes in v6:
time: 292 us
  Pallas kernels  184 us (63%)
  waiting for transfers between devices  61.4 us (21%)
  starting transfers between devices  32.5 us (11%)
  other arithmetic  7.28 us (2%)
  local copies, waits for them, and re-layouts  5.9 us (2%)
    pallas_call x2, Pallas kernels, copy_parents(): pl.pallas_call(functools.partial(copy_kernel, members, pieces), in_specs=...  115 us
    ppermute x3, waiting for transfers between devices, neighbours(): lax.ppermute(rows[:, rows.shape[1] - SPREAD * per_member:], 'member', upw...  47.7 us
    pallas_call x3, Pallas kernels, zonal_transform(): pl.pallas_call(functools.partial(zonal_kernel, fields_step, fields, len(t...  35.5 us
    pallas_call x2, Pallas kernels, finish_transform(): pl.pallas_call(functools.partial(finish_kernel, first, block), grid_spec=...  18.3 us
    all_to_all x3, starting transfers between devices, exchanged(): lax.all_to_all(outgoing, 'lat', split_axis=0, concat_axis=0, tiled=True)  17.6 us
    ppermute x3, waiting for transfers between devices, neighbours(): high = lax.ppermute(rows[:, :SPREAD * per_member], 'member', downward)  13.7 us
    ppermute x3, starting transfers between devices, neighbours(): lax.ppermute(rows[:, rows.shape[1] - SPREAD * per_member:], 'member', upw...  7.8 us
    ppermute x3, starting transfers between devices, neighbours(): high = lax.ppermute(rows[:, :SPREAD * per_member], 'member', downward)  7.15 us
  transfers between devices with their start and end apart: 9, of which 6 were waited for; matrix products, arithmetic and copies ran while one was open for 3% of the time, Pallas kernels for 56%

profile of v6, /device:TPU:1, one launch (start us, length us, event | category | flops | bytes accessed | tf_op | source)
XLA Modules:
  0.0 291.7 jit_solution(11872887804287329048)
XLA Ops:
  0.6 0.8 reshape.53
  1.6 0.6 fusion.26
  2.2 0.1 mul.286
  2.2 0.1 fusion.39
  2.3 0.1 copy.14
  2.4 0.5 sine_multiply_fusion.1
  2.9 13.2 %zonal.5 = bf16[256,32,128]{2,1,0:T(8,128)(2,1)} custom-call(f32[256,16]{1,0:T(8,128)S(1)} %get-tuple-element.19.cos_c, f32[256,16]{1,0:T(8,128)S(1)} %get-tuple-element.18.sin_c, f32[256,128]{1,0:T(8,128)S(1)} %get-tuple-element.27.cos_f, f32[256,128]{1,0:T(8,128)S(1)} %get-tuple-element.26.sin_f, bf16[2,8,128,2048]{3,2,1,0:T(8,128)(2,1)} %velocity.5, ...), custom_call_target="tpu_custom_call" | custom-call | flops 4294967296 | bytes 18874368 | tf_op jit(solution)/shard_map/zonal/pallas_call | solution.py:123
  16.1 6.4 %all-to-all-start.2 = ((bf16[8,1024,128]{2,1,0:T(8,128)(2,1)}), bf16[8,1024,128]{2,1,0:T(8,128)(2,1)}, u32[]{:S(2)}, u32[]{:S(2)}) async-start(bf16[8,1024,128]{2,1,0:T(8,128)(2,1)} %bitcast.2), calls=%async_computation.2 | async-start | bytes 4194304 | tf_op jit(solution)/shard_map/all_to_all | solution.py:441
  22.5 0.1 copy.13
  22.6 0.6 fusion.28
  23.2 0.5 sine_multiply_fusion.2
  23.7 11.9 %zonal.4.own = bf16[256,32,128]{2,1,0:T(8,128)(2,1)S(1)} custom-call(f32[256,16]{1,0:T(8,128)S(1)} %get-tuple-element.21.cos_c, f32[256,16]{1,0:T(8,128)S(1)} %get-tuple-element.20.sin_c, f32[256,128]{1,0:T(8,128)S(1)} %get-tuple-element.29.cos_f, f32[256,128]{1,0:T(8,128)S(1)} %get-tuple-element.28.sin_f, bf16[2,8,128,2048]{3,2,1,0:T(8,128)(2,1)} %velocity.5, ...), custom_call_target="tpu_custom_call" | custom-call | flops 4294967296 | bytes 18874368 | tf_op jit(solution)/shard_map/zonal/pallas_call | solution.py:123
  35.6 4.0 %collective-permute-start.2 = (bf16[256,32,128]{2,1,0:T(8,128)(2,1)S(1)}, bf16[256,32,128]{2,1,0:T(8,128)(2,1)}, u32[]{:S(2)}, u32[]{:S(2)}) collective-permute-start(bf16[256,32,128]{2,1,0:T(8,128)(2,1)S(1)} %zonal.4.own), channel_id=1, source_target_pairs={{0,8},{8,16},{16,24},{1,9},{9,17},{17,25},{2,10},{10,18},{18,26},{... | collective-permute-start | bytes 6291464 | tf_op jit(solution)/shard_map/ppermute | solution.py:435
  39.6 1.9 collective-permute-start.3
  41.6 0.6 subtract_add_fusion.offsets
  42.2 20.4 %collective-permute-done.2.low = bf16[256,32,128]{2,1,0:T(8,128)(2,1)} collective-permute-done((bf16[256,32,128]{2,1,0:T(8,128)(2,1)S(1)}, bf16[256,32,128]{2,1,0:T(8,128)(2,1)}, u32[]{:S(2)}, u32[]{:S(2)}) %collective-permute-start.2) | collective-permute-done | bytes 2097184 | tf_op jit(solution)/shard_map/ppermute | solution.py:435
  62.6 4.8 %collective-permute-done.3.high = bf16[256,32,128]{2,1,0:T(8,128)(2,1)} collective-permute-done((bf16[256,32,128]{2,1,0:T(8,128)(2,1)S(1)}, bf16[256,32,128]{2,1,0:T(8,128)(2,1)}, u32[]{:S(2)}, u32[]{:S(2)}) %collective-permute-start.3) | collective-permute-done | bytes 2097184 | tf_op jit(solution)/shard_map/ppermute | solution.py:436
  67.4 65.4 %parents.3 = bf16[256,32,128]{2,1,0:T(8,128)(2,1)} custom-call(s32[2]{0:T(128)} %subtract_add_fusion.offsets, bf16[256,32,128]{2,1,0:T(8,128)(2,1)} %collective-permute-done.2.low, bf16[256,32,128]{2,1,0:T(8,128)(2,1)} %copy-done, bf16[256,32,128]{2,1,0:T(8,128)(2,1)} %collective-permute-done.3.high), custom_call_target="tpu_custom_call" | custom-call | bytes 4194304 | tf_op jit(solution)/shard_map/parents/pallas_call | solution.py:317
  132.8 5.7 %all-to-all-start.1 = ((bf16[8,1024,128]{2,1,0:T(8,128)(2,1)}), bf16[8,1024,128]{2,1,0:T(8,128)(2,1)}, u32[]{:S(2)}, u32[]{:S(2)}) async-start(bf16[8,1024,128]{2,1,0:T(8,128)(2,1)} %bitcast.3), calls=%async_computation.1 | async-start | bytes 4194304 | tf_op jit(solution)/shard_map/all_to_all | solution.py:441
  138.6 0.1 mul.255
  138.7 0.1 fusion.37
  138.7 0.1 copy.11
  138.9 0.5 fusion.30
  139.3 0.4 sine_multiply_fusion.3
  139.7 10.4 %zonal.3.own = bf16[192,32,128]{2,1,0:T(8,128)(2,1)S(1)} custom-call(f32[192,16]{1,0:T(8,128)S(1)} %get-tuple-element.23.cos_c, f32[192,16]{1,0:T(8,128)S(1)} %get-tuple-element.22.sin_c, f32[192,128]{1,0:T(8,128)S(1)} %get-tuple-element.31.cos_f, f32[192,128]{1,0:T(8,128)S(1)} %get-tuple-element.30.sin_f, bf16[2,8,128,2048]{3,2,1,0:T(8,128)(2,1)} %velocity.5, ...), custom_call_target="tpu_custom_call" | custom-call | flops 3221225472 | bytes 18350080 | tf_op jit(solution)/shard_map/zonal/pallas_call | solution.py:123
  150.1 1.9 collective-permute-start
  152.0 2.5 collective-permute-start.1
  154.6 2.1 fusion.6
  156.7 12.7 %collective-permute-done.low = bf16[192,32,128]{2,1,0:T(8,128)(2,1)S(1)} collective-permute-done((bf16[192,32,128]{2,1,0:T(8,128)(2,1)S(1)}, bf16[192,32,128]{2,1,0:T(8,128)(2,1)S(1)}, u32[]{:S(2)}, u32[]{:S(2)}) %collective-permute-start) | collective-permute-done | bytes 1572896 | tf_op jit(solution)/shard_map/ppermute | solution.py:435
  169.4 4.5 %collective-permute-done.1.high = bf16[192,32,128]{2,1,0:T(8,128)(2,1)} collective-permute-done((bf16[192,32,128]{2,1,0:T(8,128)(2,1)S(1)}, bf16[192,32,128]{2,1,0:T(8,128)(2,1)}, u32[]{:S(2)}, u32[]{:S(2)}) %collective-permute-start.1) | collective-permute-done | bytes 1572896 | tf_op jit(solution)/shard_map/ppermute | solution.py:436
  173.9 49.5 %parents.2 = bf16[192,32,128]{2,1,0:T(8,128)(2,1)} custom-call(s32[2]{0:T(128)} %subtract_add_fusion.offsets, bf16[192,32,128]{2,1,0:T(8,128)(2,1)} %copy-done.7, bf16[192,32,128]{2,1,0:T(8,128)(2,1)} %copy-done.1, bf16[192,32,128]{2,1,0:T(8,128)(2,1)} %collective-permute-done.1.high), custom_call_target="tpu_custom_call" | custom-call | bytes 3145728 | tf_op jit(solution)/shard_map/parents/pallas_call | solution.py:317
  223.4 5.5 %all-to-all-start = ((bf16[8,768,128]{2,1,0:T(8,128)(2,1)}), bf16[8,768,128]{2,1,0:T(8,128)(2,1)S(1)}, u32[]{:S(2)}, u32[]{:S(2)}) async-start(bf16[8,768,128]{2,1,0:T(8,128)(2,1)} %bitcast.4), calls=%async_computation | async-start | bytes 3145728 | tf_op jit(solution)/shard_map/all_to_all | solution.py:441
  228.9 0.1 fusion.33
  228.9 0.8 dynamic_slice.6.waves
  229.7 0.2 copy.12
  229.9 1.3 sine_multiply_fusion
  231.2 1.0 copy-done.4
  232.2 1.7 tables.1
  233.9 6.2 %forward.1 = (bf16[32,2,16,683]{3,2,1,0:T(8,128)(2,1)S(1)}, f32[8,128]{1,0:T(8,128)}) custom-call(s32[88]{0:T(128)S(1)} %dynamic_slice.6.waves, bf16[8,1024,128]{2,1,0:T(8,128)(2,1)} %all-to-all-done.2.received, bf16[683,1024]{1,0:T(8,128)(2,1)S(1)} %get-tuple-element.9.even, bf16[683,1024]{1,0:T(8,128)(2,1)S(1)} %get-tuple-element.10.odd), custom_call_target="tpu_custom_call" | custom-call | flops 2864709632 | bytes 6293504 | tf_op jit(solution)/shard_map/forward/pallas_call | solution.py:168
  240.0 1.9 collective-permute-start.4
  242.0 2.7 collective-permute-start.5
  244.7 14.6 %collective-permute-done.4.low = bf16[32,2,16,683]{3,2,1,0:T(8,128)(2,1)S(1)} collective-permute-done((bf16[32,2,16,683]{3,2,1,0:T(8,128)(2,1)S(1)}, bf16[32,2,16,683]{3,2,1,0:T(8,128)(2,1)S(1)}, u32[]{:S(2)}, u32[]{:S(2)}) %collective-permute-start.4) | collective-permute-done | bytes 1398816 | tf_op jit(solution)/shard_map/ppermute | solution.py:435
  259.3 4.4 %collective-permute-done.5.high = bf16[32,2,16,683]{3,2,1,0:T(8,128)(2,1)S(1)} collective-permute-done((bf16[32,2,16,683]{3,2,1,0:T(8,128)(2,1)S(1)}, bf16[32,2,16,683]{3,2,1,0:T(8,128)(2,1)S(1)}, u32[]{:S(2)}, u32[]{:S(2)}) %collective-permute-start.5) | collective-permute-done | bytes 1398816 | tf_op jit(solution)/shard_map/ppermute | solution.py:436
  263.7 1.2 copy-done.6
  264.9 7.1 %inverse.1 = (bf16[88,2,2,8,683]{4,3,2,1,0:T(8,128)(2,1)}, bf16[88,2,2,8,1024]{4,3,2,1,0:T(8,128)(2,1)}, f32[8,128]{1,0:T(8,128)}) custom-call(s32[88]{0:T(128)S(1)} %dynamic_slice.6.waves, s32[2]{0:T(128)S(1)} %copy-done.5, bf16[32,2,16,683]{3,2,1,0:T(8,128)(2,1)S(1)} %collective-permute-done.4.low, bf16[32,2,16,683]{3,2,1,0:T(8,128)(2,1)S(1)} %get-tuple-element.11.own, ...), custom_call_target="tpu_custom_call" | custom-call | flops 2864709632 | bytes 11888640 | tf_op jit(solution)/shard_map/inverse/pallas_call | solution.py:258
  272.0 10.2 %finish.2 = (bf16[88,2,2,8,683]{4,3,2,1,0:T(8,128)(2,1)}, bf16[88,2,2,8,1024]{4,3,2,1,0:T(8,128)(2,1)}) custom-call(s32[88]{0:T(128)S(1)} %dynamic_slice.6.waves, bf16[8,1024,128]{2,1,0:T(8,128)(2,1)} %all-to-all-done.1.received, bf16[88,2,2,8,683]{4,3,2,1,0:T(8,128)(2,1)} %noise.5, ...), custom_call_target="tpu_custom_call", output_to_operand_aliasing={{0}: (5, {}), {1}: (6, {})} | custom-call | flops 5729419264 | bytes 9789440 | tf_op jit(solution)/shard_map/finish/pallas_call | solution.py:376
  282.2 1.3 copy-done.3
  283.5 8.1 %finish.3 = (bf16[88,2,2,8,683]{4,3,2,1,0:T(8,128)(2,1)}, bf16[88,2,2,8,1024]{4,3,2,1,0:T(8,128)(2,1)}) custom-call(s32[88]{0:T(128)S(1)} %dynamic_slice.6.waves, bf16[8,768,128]{2,1,0:T(8,128)(2,1)S(1)} %all-to-all-done.received, bf16[88,2,2,8,683]{4,3,2,1,0:T(8,128)(2,1)} %noise.5, ...), custom_call_target="tpu_custom_call", output_to_operand_aliasing={{0}: (5, {}), {1}: (6, {})} | custom-call | flops 4297064448 | bytes 8041472 | tf_op jit(solution)/shard_map/finish/pallas_call | solution.py:376
  (27 shorter events, 0.3 us)
Async XLA Ops:
  16.1 116.6 %all-to-all-start.2 = ((bf16[8,1024,128]{2,1,0:T(8,128)(2,1)}), bf16[8,1024,128]{2,1,0:T(8,128)(2,1)}, u32[]{:S(2)}, u32[]{:S(2)}) async-start(bf16[8,1024,128]{2,1,0:T(8,128)(2,1)} %bitcast.2), calls=%async_computation.2 | async-start | bytes 4194304 | tf_op jit(solution)/shard_map/all_to_all | solution.py:441
  23.7 17.9 %copy-start.8 = (s32[8]{0:T(128)S(1)}, s32[8]{0:T(128)}, u32[]{:S(2)}) copy-start(s32[8]{0:T(128)} %param.8) | copy-start | bytes 100
  35.6 31.8 %copy-start = (bf16[256,32,128]{2,1,0:T(8,128)(2,1)}, bf16[256,32,128]{2,1,0:T(8,128)(2,1)S(1)}, u32[]{:S(2)}) copy-start(bf16[256,32,128]{2,1,0:T(8,128)(2,1)S(1)} %zonal.4.own) | copy-start | bytes 6291460
  35.6 26.9 %collective-permute-start.2 = (bf16[256,32,128]{2,1,0:T(8,128)(2,1)S(1)}, bf16[256,32,128]{2,1,0:T(8,128)(2,1)}, u32[]{:S(2)}, u32[]{:S(2)}) collective-permute-start(bf16[256,32,128]{2,1,0:T(8,128)(2,1)S(1)} %zonal.4.own), channel_id=1, source_target_pairs={{0,8},{8,16},{16,24},{1,9},{9,17},{17,25},{2,10},{10,18},{18,26},{... | collective-permute-start | bytes 6291464 | tf_op jit(solution)/shard_map/ppermute | solution.py:435
  39.6 27.8 %collective-permute-start.3 = (bf16[256,32,128]{2,1,0:T(8,128)(2,1)S(1)}, bf16[256,32,128]{2,1,0:T(8,128)(2,1)}, u32[]{:S(2)}, u32[]{:S(2)}) collective-permute-start(bf16[256,32,128]{2,1,0:T(8,128)(2,1)S(1)} %zonal.4.own), channel_id=1, source_target_pairs={{8,0},{16,8},{24,16},{9,1},{17,9},{25,17},{10,2},{18,10},{26,18},{... | collective-permute-start | bytes 6291464 | tf_op jit(solution)/shard_map/ppermute | solution.py:436
  132.8 90.6 %all-to-all-start.1 = ((bf16[8,1024,128]{2,1,0:T(8,128)(2,1)}), bf16[8,1024,128]{2,1,0:T(8,128)(2,1)}, u32[]{:S(2)}, u32[]{:S(2)}) async-start(bf16[8,1024,128]{2,1,0:T(8,128)(2,1)} %bitcast.3), calls=%async_computation.1 | async-start | bytes 4194304 | tf_op jit(solution)/shard_map/all_to_all | solution.py:441
  150.1 23.8 %copy-start.1 = (bf16[192,32,128]{2,1,0:T(8,128)(2,1)}, bf16[192,32,128]{2,1,0:T(8,128)(2,1)S(1)}, u32[]{:S(2)}) copy-start(bf16[192,32,128]{2,1,0:T(8,128)(2,1)S(1)} %zonal.3.own) | copy-start | bytes 4718596
  150.1 19.3 %collective-permute-start = (bf16[192,32,128]{2,1,0:T(8,128)(2,1)S(1)}, bf16[192,32,128]{2,1,0:T(8,128)(2,1)S(1)}, u32[]{:S(2)}, u32[]{:S(2)}) collective-permute-start(bf16[192,32,128]{2,1,0:T(8,128)(2,1)S(1)} %zonal.3.own), channel_id=1, source_target_pairs={{0,8},{8,16},{16,24},{1,9},{9,17},{17,25},{2,10},{10,18},{18,26},{... | collective-permute-start | bytes 4718600 | tf_op jit(solution)/shard_map/ppermute | solution.py:435
  152.0 21.8 %collective-permute-start.1 = (bf16[192,32,128]{2,1,0:T(8,128)(2,1)S(1)}, bf16[192,32,128]{2,1,0:T(8,128)(2,1)}, u32[]{:S(2)}, u32[]{:S(2)}) collective-permute-start(bf16[192,32,128]{2,1,0:T(8,128)(2,1)S(1)} %zonal.3.own), channel_id=1, source_target_pairs={{8,0},{16,8},{24,16},{9,1},{17,9},{25,17},{10,2},{18,10},{26,18},{... | collective-permute-start | bytes 4718600 | tf_op jit(solution)/shard_map/ppermute | solution.py:436
  169.4 4.5 %copy-start.7 = (bf16[192,32,128]{2,1,0:T(8,128)(2,1)}, bf16[192,32,128]{2,1,0:T(8,128)(2,1)S(1)}, u32[]{:S(2)}) copy-start(bf16[192,32,128]{2,1,0:T(8,128)(2,1)S(1)} %collective-permute-done.low) | copy-start | bytes 4718596
  223.4 58.8 %all-to-all-start = ((bf16[8,768,128]{2,1,0:T(8,128)(2,1)}), bf16[8,768,128]{2,1,0:T(8,128)(2,1)S(1)}, u32[]{:S(2)}, u32[]{:S(2)}) async-start(bf16[8,768,128]{2,1,0:T(8,128)(2,1)} %bitcast.4), calls=%async_computation | async-start | bytes 3145728 | tf_op jit(solution)/shard_map/all_to_all | solution.py:441
  231.2 1.0 copy-start.4
  233.9 38.1 %copy-start.2 = (bf16[683,1024]{1,0:T(8,128)(2,1)}, bf16[683,1024]{1,0:T(8,128)(2,1)S(1)}, u32[]{:S(2)}) copy-start(bf16[683,1024]{1,0:T(8,128)(2,1)S(1)} %get-tuple-element.10.odd) | copy-start | bytes 4196356
  233.9 31.0 %copy-start.5 = (s32[2]{0:T(128)S(1)}, s32[2]{0:T(128)}, u32[]{:S(2)}) copy-start(s32[2]{0:T(128)} %subtract_add_fusion.offsets) | copy-start | bytes 28
  240.0 19.3 %collective-permute-start.4 = (bf16[32,2,16,683]{3,2,1,0:T(8,128)(2,1)S(1)}, bf16[32,2,16,683]{3,2,1,0:T(8,128)(2,1)S(1)}, u32[]{:S(2)}, u32[]{:S(2)}) collective-permute-start(bf16[32,2,16,683]{3,2,1,0:T(8,128)(2,1)S(1)} %get-tuple-element.11.own), channel_id=1, source_target_pairs={{0,8},{8,16},{16,24},{1,9},{9,17},{17,25},{2,10},{10,18},{18,26},{... | collective-permute-start | bytes 4196360 | tf_op jit(solution)/shard_map/ppermute | solution.py:435
  242.0 21.7 %collective-permute-start.5 = (bf16[32,2,16,683]{3,2,1,0:T(8,128)(2,1)S(1)}, bf16[32,2,16,683]{3,2,1,0:T(8,128)(2,1)S(1)}, u32[]{:S(2)}, u32[]{:S(2)}) collective-permute-start(bf16[32,2,16,683]{3,2,1,0:T(8,128)(2,1)S(1)} %get-tuple-element.11.own), channel_id=1, source_target_pairs={{8,0},{16,8},{24,16},{9,1},{17,9},{25,17},{10,2},{18,10},{26,18},{... | collective-permute-start | bytes 4196360 | tf_op jit(solution)/shard_map/ppermute | solution.py:436
  263.7 1.2 copy-start.6
  282.2 1.4 copy-start.3

commit v7 on v6

--- a/solution.py
+++ b/solution.py
@@ -283,44 +283,34 @@
     )(waves, offsets, *operands)
 
 
-def copy_kernel(members, pieces, offsets, low, own, high, out, sems):
-    rows_total, rows = out.shape[0], out.shape[1] // members
-    size = rows_total // pieces
-    sources = [(ref, at) for ref in (low, own, high) for at in range(ref.shape[1] // rows)]
-
-    def copy(child, piece, source):
-        ref, at = source
-        part = pl.ds(piece * size, size)
-        return pltpu.make_async_copy(
-            ref.at[part, pl.ds(at * rows, rows)],
-            out.at[part, pl.ds(child * rows, rows)],
-            sems.at[child, piece],
-        )
-
-    for child in range(members):
-        for index, source in enumerate(sources):
-
-            @pl.when(offsets[child] == index)
-            def _():
-                for piece in range(pieces):
-                    copy(child, piece, source).start()
-
-    for child in range(members):
-        for piece in range(pieces):
-            copy(child, piece, sources[0]).wait()
+def copy_kernel(offsets, low, own, high, out):
+    rows = out.shape[1] // offsets.shape[0]
+    for child in range(offsets.shape[0]):
+        index, chosen = 0, None
+        for source in (low, own, high):
+            for at in range(source.shape[1] // rows):
+                value = source[:, at * rows : (at + 1) * rows]
+                chosen = value if index == 0 else jnp.where(offsets[child] == index, value, chosen)
+                index += 1
+        out[:, child * rows : (child + 1) * rows] = chosen
 
 
 def copy_parents(offsets, low, own, high):
-    members = offsets.shape[0]
-    pieces = math.gcd(own.shape[0], 4)
-    anywhere = pl.BlockSpec(memory_space=pl.ANY)
-    return pl.pallas_call(
-        functools.partial(copy_kernel, members, pieces),
-        in_specs=[pl.BlockSpec(memory_space=pltpu.SMEM)] + [anywhere] * 3,
-        out_specs=anywhere,
+    steps = math.gcd(own.shape[0], 4)
+    block = lambda array: pl.BlockSpec(
+        (array.shape[0] // steps,) + array.shape[1:], lambda step, o: (step, 0, 0)
+    )
+    return pl.pallas_call(
+        copy_kernel,
+        grid_spec=pltpu.PrefetchScalarGridSpec(
+            num_scalar_prefetch=1,
+            grid=(steps,),
+            in_specs=[block(low), block(own), block(high)],
+            out_specs=block(own),
+        ),
         out_shape=jax.ShapeDtypeStruct(own.shape, own.dtype),
-        scratch_shapes=[pltpu.SemaphoreType.DMA((members, pieces))],
-        cost_estimate=pl.CostEstimate(flops=0, bytes_accessed=4 * own.size, transcendentals=0),
+        compiler_params=pltpu.CompilerParams(vmem_limit_bytes=VMEM_BYTES),
+        cost_estimate=pl.CostEstimate(flops=0, bytes_accessed=8 * own.size, transcendentals=0),
         name="parents",
     )(offsets, low, own, high)
 
@@ -399,7 +389,7 @@
 
 def chunk_bounds(slots_here, block):
     blocks = slots_here // block
-    edges = [0, (blocks * 4 + 10) // 11, (blocks * 8 + 10) // 11, blocks]
+    edges = [0, (blocks * 5 + 10) // 11, (blocks * 9 + 10) // 11, blocks]
     edges = [edge * block for edge in edges]
     return [(start, stop) for start, stop in zip(edges[:-1], edges[1:]) if stop > start]
 

time: 292 us -> 179 us (0.61)
  Pallas kernels: 184 us -> 80.3 us
  waiting for transfers between devices: 61.4 us -> 49.1 us
  local copies, waits for them, and re-layouts: 5.9 us -> 9.11 us
    pallas_call x2, Pallas kernels: 115 us -> 8.9 us  [copy_parents(): pl.pallas_call(copy_kernel, grid_spec=pltpu.PrefetchScalarGridSpec(num_sc...]
    ppermute x3, waiting for transfers between devices: 47.7 us -> 24 us  [neighbours(): lax.ppermute(rows[:, rows.shape[1] - SPREAD * per_member:], 'member', upw...]
    all_to_all x3, waiting for transfers between devices: 0.01 us -> 16 us  [exchanged(): lax.all_to_all(outgoing, 'lat', split_axis=0, concat_axis=0, tiled=True)]
    ppermute x3, waiting for transfers between devices: 13.7 us -> 9.09 us  [neighbours(): high = lax.ppermute(rows[:, :SPREAD * per_member], 'member', downward)]
    ppermute x3, starting transfers between devices: 7.8 us -> 11.5 us  [neighbours(): lax.ppermute(rows[:, rows.shape[1] - SPREAD * per_member:], 'member', upw...]
    unnamed x18, local copies, waits for them, and re-layouts: 3.53 us -> 6.74 us
  transfers between devices with their start and end apart: 9 -> 9, of which waited for: 6 -> 6; matrix products, arithmetic and copies ran while one was open for 3% -> 3% of each run, Pallas kernels for 56% -> 33%
where the time goes in v7:
time: 179 us; the launch traced here: 178 us
  Pallas kernels  80.3 us (45%)
  waiting for transfers between devices  49.1 us (27%)
  starting transfers between devices  32.9 us (18%)
  local copies, waits for them, and re-layouts  9.11 us (5%)
  other arithmetic  6.1 us (3%)
    pallas_call x3, Pallas kernels, zonal_transform(): pl.pallas_call(functools.partial(zonal_kernel, fields_step, fields, len(t...  35.9 us
    ppermute x3, waiting for transfers between devices, neighbours(): lax.ppermute(rows[:, rows.shape[1] - SPREAD * per_member:], 'member', upw...  24 us
    pallas_call x2, Pallas kernels, finish_transform(): pl.pallas_call(functools.partial(finish_kernel, first, block), grid_spec=...  16.2 us
    all_to_all x3, waiting for transfers between devices, exchanged(): lax.all_to_all(outgoing, 'lat', split_axis=0, concat_axis=0, tiled=True)  16 us
    all_to_all x3, starting transfers between devices, exchanged(): lax.all_to_all(outgoing, 'lat', split_axis=0, concat_axis=0, tiled=True)  15.5 us
    ppermute x3, starting transfers between devices, neighbours(): lax.ppermute(rows[:, rows.shape[1] - SPREAD * per_member:], 'member', upw...  11.5 us
    pallas_call x1, Pallas kernels, inverse_transform(): pl.pallas_call(functools.partial(inverse_kernel, first, block), grid_spec...  9.23 us
    ppermute x3, waiting for transfers between devices, neighbours(): high = lax.ppermute(rows[:, :SPREAD * per_member], 'member', downward)  9.09 us
  transfers between devices with their start and end apart: 9, of which 6 were waited for; matrix products, arithmetic and copies ran while one was open for 3% of the time, Pallas kernels for 33%

profile of v7, /device:TPU:1, one launch (start us, length us, event | category | flops | bytes accessed | tf_op | source)
XLA Modules:
  0.0 178.4 jit_solution(15129629482898932012)
XLA Ops:
  0.6 0.8 reshape.53
  1.5 0.7 fusion.20
  2.2 0.1 fusion.34
  2.3 0.1 copy.14
  2.4 0.6 sine_multiply_fusion.1
  3.0 15.0 %zonal.5 = bf16[320,32,128]{2,1,0:T(8,128)(2,1)} custom-call(f32[320,16]{1,0:T(8,128)S(1)} %get-tuple-element.19.cos_c, f32[320,16]{1,0:T(8,128)S(1)} %get-tuple-element.18.sin_c, f32[320,128]{1,0:T(8,128)S(1)} %get-tuple-element.25.cos_f, f32[320,128]{1,0:T(8,128)S(1)} %get-tuple-element.24.sin_f, bf16[2,8,128,2048]{3,2,1,0:T(8,128)(2,1)} %velocity.5, ...), custom_call_target="tpu_custom_call" | custom-call | flops 5368709120 | bytes 19398656 | tf_op jit(solution)/shard_map/zonal/pallas_call | solution.py:123
  18.0 6.4 %all-to-all-start.2 = ((bf16[8,1280,128]{2,1,0:T(8,128)(2,1)}), bf16[8,1280,128]{2,1,0:T(8,128)(2,1)}, u32[]{:S(2)}, u32[]{:S(2)}) async-start(bf16[8,1280,128]{2,1,0:T(8,128)(2,1)} %bitcast.2), calls=%async_computation.2 | async-start | bytes 5242880 | tf_op jit(solution)/shard_map/all_to_all | solution.py:431
  24.6 0.1 fusion.39
  24.7 0.1 copy.13
  24.8 0.6 fusion.25
  25.4 0.5 sine_multiply_fusion.2
  25.8 11.9 %zonal.4.own = bf16[256,32,128]{2,1,0:T(8,128)(2,1)S(1)} custom-call(f32[256,16]{1,0:T(8,128)S(1)} %get-tuple-element.21.cos_c, f32[256,16]{1,0:T(8,128)S(1)} %get-tuple-element.20.sin_c, f32[256,128]{1,0:T(8,128)S(1)} %get-tuple-element.27.cos_f, f32[256,128]{1,0:T(8,128)S(1)} %get-tuple-element.26.sin_f, bf16[2,8,128,2048]{3,2,1,0:T(8,128)(2,1)} %velocity.5, ...), custom_call_target="tpu_custom_call" | custom-call | flops 4294967296 | bytes 18874368 | tf_op jit(solution)/shard_map/zonal/pallas_call | solution.py:123
  37.8 4.0 %collective-permute-start.2 = (bf16[256,32,128]{2,1,0:T(8,128)(2,1)S(1)}, bf16[256,32,128]{2,1,0:T(8,128)(2,1)}, u32[]{:S(2)}, u32[]{:S(2)}) collective-permute-start(bf16[256,32,128]{2,1,0:T(8,128)(2,1)S(1)} %zonal.4.own), channel_id=1, source_target_pairs={{0,8},{8,16},{16,24},{1,9},{9,17},{17,25},{2,10},{10,18},{18,26},{... | collective-permute-start | bytes 6291464 | tf_op jit(solution)/shard_map/ppermute | solution.py:425
  41.8 1.9 %collective-permute-start.3 = (bf16[256,32,128]{2,1,0:T(8,128)(2,1)S(1)}, bf16[256,32,128]{2,1,0:T(8,128)(2,1)}, u32[]{:S(2)}, u32[]{:S(2)}) collective-permute-start(bf16[256,32,128]{2,1,0:T(8,128)(2,1)S(1)} %zonal.4.own), channel_id=1, source_target_pairs={{8,0},{16,8},{24,16},{9,1},{17,9},{25,17},{10,2},{18,10},{26,18},{... | collective-permute-start | bytes 6291464 | tf_op jit(solution)/shard_map/ppermute | solution.py:426
  43.8 20.9 %collective-permute-done.2.low = bf16[256,32,128]{2,1,0:T(8,128)(2,1)} collective-permute-done((bf16[256,32,128]{2,1,0:T(8,128)(2,1)S(1)}, bf16[256,32,128]{2,1,0:T(8,128)(2,1)}, u32[]{:S(2)}, u32[]{:S(2)}) %collective-permute-start.2) | collective-permute-done | bytes 2097184 | tf_op jit(solution)/shard_map/ppermute | solution.py:425
  64.7 4.5 %collective-permute-done.3.high = bf16[256,32,128]{2,1,0:T(8,128)(2,1)} collective-permute-done((bf16[256,32,128]{2,1,0:T(8,128)(2,1)S(1)}, bf16[256,32,128]{2,1,0:T(8,128)(2,1)}, u32[]{:S(2)}, u32[]{:S(2)}) %collective-permute-start.3) | collective-permute-done | bytes 2097184 | tf_op jit(solution)/shard_map/ppermute | solution.py:426
  69.2 4.5 %parents.3 = bf16[256,32,128]{2,1,0:T(8,128)(2,1)S(1)} custom-call(s32[2]{0:T(128)S(1)} %subtract_add_fusion.offsets, bf16[256,32,128]{2,1,0:T(8,128)(2,1)} %collective-permute-done.2.low, bf16[256,32,128]{2,1,0:T(8,128)(2,1)} %copy-done, bf16[256,32,128]{2,1,0:T(8,128)(2,1)} %collective-permute-done.3.high), custom_call_target="tpu_custom_call" | custom-call | bytes 8388608 | tf_op jit(solution)/shard_map/parents/pallas_call | solution.py:303
  73.8 1.3 copy-done.1
  75.1 8.1 %all-to-all-done.2.received = bf16[8,1280,128]{2,1,0:T(8,128)(2,1)} async-done(((bf16[8,1280,128]{2,1,0:T(8,128)(2,1)}), bf16[8,1280,128]{2,1,0:T(8,128)(2,1)}, u32[]{:S(2)}, u32[]{:S(2)}) %all-to-all-start.2) | async-done | bytes 2621472 | tf_op jit(solution)/shard_map/all_to_all | solution.py:431
  83.1 4.7 %all-to-all-start.1 = ((bf16[8,1024,128]{2,1,0:T(8,128)(2,1)}), bf16[8,1024,128]{2,1,0:T(8,128)(2,1)S(1)}, u32[]{:S(2)}, u32[]{:S(2)}) async-start(bf16[8,1024,128]{2,1,0:T(8,128)(2,1)} %bitcast.4), calls=%async_computation.1 | async-start | bytes 4194304 | tf_op jit(solution)/shard_map/all_to_all | solution.py:431
  87.9 0.1 mul.267
  88.0 0.1 copy.11
  88.2 0.3 fusion.30
  88.5 0.2 sine_multiply_fusion.3
  88.8 9.0 %zonal.3.own = bf16[128,32,128]{2,1,0:T(8,128)(2,1)S(1)} custom-call(f32[128,16]{1,0:T(8,128)S(1)} %get-tuple-element.23.cos_c, f32[128,16]{1,0:T(8,128)S(1)} %get-tuple-element.22.sin_c, f32[128,128]{1,0:T(8,128)S(1)} %get-tuple-element.31.cos_f, f32[128,128]{1,0:T(8,128)S(1)} %get-tuple-element.30.sin_f, bf16[2,8,128,2048]{3,2,1,0:T(8,128)(2,1)} %velocity.5, ...), custom_call_target="tpu_custom_call" | custom-call | flops 2147483648 | bytes 17825792 | tf_op jit(solution)/shard_map/zonal/pallas_call | solution.py:123
  97.8 3.9 %collective-permute-start = (bf16[128,32,128]{2,1,0:T(8,128)(2,1)S(1)}, bf16[128,32,128]{2,1,0:T(8,128)(2,1)}, u32[]{:S(2)}, u32[]{:S(2)}) collective-permute-start(bf16[128,32,128]{2,1,0:T(8,128)(2,1)S(1)} %zonal.3.own), channel_id=1, source_target_pairs={{0,8},{8,16},{16,24},{1,9},{9,17},{17,25},{2,10},{10,18},{18,26},{... | collective-permute-start | bytes 3145736 | tf_op jit(solution)/shard_map/ppermute | solution.py:425
  101.7 1.9 %collective-permute-start.1 = (bf16[128,32,128]{2,1,0:T(8,128)(2,1)S(1)}, bf16[128,32,128]{2,1,0:T(8,128)(2,1)}, u32[]{:S(2)}, u32[]{:S(2)}) collective-permute-start(bf16[128,32,128]{2,1,0:T(8,128)(2,1)S(1)} %zonal.3.own), channel_id=1, source_target_pairs={{8,0},{16,8},{24,16},{9,1},{17,9},{25,17},{10,2},{18,10},{26,18},{... | collective-permute-start | bytes 3145736 | tf_op jit(solution)/shard_map/ppermute | solution.py:426
  103.7 0.8 dynamic_slice.6.waves
  104.4 0.1 fusion.33
  104.5 0.2 copy.12
  104.7 1.4 fusion.6
  106.1 1.3 sine_multiply_fusion
  107.4 1.8 tables.1
  109.2 8.2 %forward.1 = (bf16[40,2,16,683]{3,2,1,0:T(8,128)(2,1)}, f32[8,128]{1,0:T(8,128)}) custom-call(s32[88]{0:T(128)S(1)} %dynamic_slice.6.waves, bf16[8,1280,128]{2,1,0:T(8,128)(2,1)} %all-to-all-done.2.received, bf16[683,1024]{1,0:T(8,128)(2,1)S(1)} %get-tuple-element.9.even, bf16[683,1024]{1,0:T(8,128)(2,1)S(1)} %get-tuple-element.10.odd), custom_call_target="tpu_custom_call" | custom-call | flops 3580887040 | bytes 7167488 | tf_op jit(solution)/shard_map/forward/pallas_call | solution.py:168
  117.4 3.6 %collective-permute-start.4 = (bf16[40,2,16,683]{3,2,1,0:T(8,128)(2,1)}, bf16[40,2,16,683]{3,2,1,0:T(8,128)(2,1)}, u32[]{:S(2)}, u32[]{:S(2)}) collective-permute-start(bf16[40,2,16,683]{3,2,1,0:T(8,128)(2,1)} %get-tuple-element.11.own), channel_id=1, source_target_pairs={{0,8},{8,16},{16,24},{1,9},{9,17},{17,25},{2,10},{10,18},{18,26},{... | collective-permute-start | bytes 5245448 | tf_op jit(solution)/shard_map/ppermute | solution.py:425
  121.1 2.0 %collective-permute-start.5 = (bf16[40,2,16,683]{3,2,1,0:T(8,128)(2,1)}, bf16[40,2,16,683]{3,2,1,0:T(8,128)(2,1)}, u32[]{:S(2)}, u32[]{:S(2)}) collective-permute-start(bf16[40,2,16,683]{3,2,1,0:T(8,128)(2,1)} %get-tuple-element.11.own), channel_id=1, source_target_pairs={{8,0},{16,8},{24,16},{9,1},{17,9},{25,17},{10,2},{18,10},{26,18},{... | collective-permute-start | bytes 5245448 | tf_op jit(solution)/shard_map/ppermute | solution.py:426
  123.1 4.4 %parents.2 = bf16[128,32,128]{2,1,0:T(8,128)(2,1)} custom-call(s32[2]{0:T(128)S(1)} %subtract_add_fusion.offsets, bf16[128,32,128]{2,1,0:T(8,128)(2,1)} %collective-permute-done.low, bf16[128,32,128]{2,1,0:T(8,128)(2,1)S(1)} %zonal.3.own, bf16[128,32,128]{2,1,0:T(8,128)(2,1)} %collective-permute-done.1.high), custom_call_target="tpu_custom_call" | custom-call | bytes 4194304 | tf_op jit(solution)/shard_map/parents/pallas_call | solution.py:303
  127.4 8.0 %all-to-all-done.1.received = bf16[8,1024,128]{2,1,0:T(8,128)(2,1)S(1)} async-done(((bf16[8,1024,128]{2,1,0:T(8,128)(2,1)}), bf16[8,1024,128]{2,1,0:T(8,128)(2,1)S(1)}, u32[]{:S(2)}, u32[]{:S(2)}) %all-to-all-start.1) | async-done | bytes 2097184 | tf_op jit(solution)/shard_map/all_to_all | solution.py:431
  135.4 4.4 %all-to-all-start = ((bf16[8,512,128]{2,1,0:T(8,128)(2,1)}), bf16[8,512,128]{2,1,0:T(8,128)(2,1)S(1)}, u32[]{:S(2)}, u32[]{:S(2)}) async-start(bf16[8,512,128]{2,1,0:T(8,128)(2,1)} %bitcast), calls=%async_computation | async-start | bytes 2097152 | tf_op jit(solution)/shard_map/all_to_all | solution.py:431
  139.9 3.1 %collective-permute-done.4.low = bf16[40,2,16,683]{3,2,1,0:T(8,128)(2,1)} collective-permute-done((bf16[40,2,16,683]{3,2,1,0:T(8,128)(2,1)}, bf16[40,2,16,683]{3,2,1,0:T(8,128)(2,1)}, u32[]{:S(2)}, u32[]{:S(2)}) %collective-permute-start.4) | collective-permute-done | bytes 1748512 | tf_op jit(solution)/shard_map/ppermute | solution.py:425
  142.9 4.6 %collective-permute-done.5.high = bf16[40,2,16,683]{3,2,1,0:T(8,128)(2,1)} collective-permute-done((bf16[40,2,16,683]{3,2,1,0:T(8,128)(2,1)}, bf16[40,2,16,683]{3,2,1,0:T(8,128)(2,1)}, u32[]{:S(2)}, u32[]{:S(2)}) %collective-permute-start.5) | collective-permute-done | bytes 1748512 | tf_op jit(solution)/shard_map/ppermute | solution.py:426
  147.5 1.3 copy-done.3
  148.9 1.3 copy-done.6
  150.2 9.2 %inverse.1 = (bf16[88,2,2,8,683]{4,3,2,1,0:T(8,128)(2,1)}, bf16[88,2,2,8,1024]{4,3,2,1,0:T(8,128)(2,1)}, f32[8,128]{1,0:T(8,128)}) custom-call(s32[88]{0:T(128)S(1)} %dynamic_slice.6.waves, s32[2]{0:T(128)S(1)} %subtract_add_fusion.offsets, bf16[40,2,16,683]{3,2,1,0:T(8,128)(2,1)} %collective-permute-done.4.low, ...), custom_call_target="tpu_custom_call" | custom-call | flops 3580887040 | bytes 14161408 | tf_op jit(solution)/shard_map/inverse/pallas_call | solution.py:258
  159.5 10.1 %finish.2 = (bf16[88,2,2,8,683]{4,3,2,1,0:T(8,128)(2,1)}, bf16[88,2,2,8,1024]{4,3,2,1,0:T(8,128)(2,1)}) custom-call(s32[88]{0:T(128)S(1)} %dynamic_slice.6.waves, bf16[8,1024,128]{2,1,0:T(8,128)(2,1)S(1)} %all-to-all-done.1.received, bf16[88,2,2,8,683]{4,3,2,1,0:T(8,128)(2,1)} %noise.5, ...), custom_call_target="tpu_custom_call", output_to_operand_aliasing={{0}: (5, {}), {1}: (6, {})} | custom-call | flops 5729419264 | bytes 9789440 | tf_op jit(solution)/shard_map/finish/pallas_call | solution.py:366
  169.5 1.3 copy-done.4
  170.9 1.3 copy-done.7
  172.2 6.2 %finish.3 = (bf16[88,2,2,8,683]{4,3,2,1,0:T(8,128)(2,1)}, bf16[88,2,2,8,1024]{4,3,2,1,0:T(8,128)(2,1)}) custom-call(s32[88]{0:T(128)S(1)} %dynamic_slice.6.waves, bf16[8,512,128]{2,1,0:T(8,128)(2,1)S(1)} %all-to-all-done.received, bf16[88,2,2,8,683]{4,3,2,1,0:T(8,128)(2,1)} %noise.5, ...), custom_call_target="tpu_custom_call", output_to_operand_aliasing={{0}: (5, {}), {1}: (6, {})} | custom-call | flops 2864709632 | bytes 6293504 | tf_op jit(solution)/shard_map/finish/pallas_call | solution.py:366
  (28 shorter events, 0.5 us)
Async XLA Ops:
  18.0 65.1 %all-to-all-start.2 = ((bf16[8,1280,128]{2,1,0:T(8,128)(2,1)}), bf16[8,1280,128]{2,1,0:T(8,128)(2,1)}, u32[]{:S(2)}, u32[]{:S(2)}) async-start(bf16[8,1280,128]{2,1,0:T(8,128)(2,1)} %bitcast.2), calls=%async_computation.2 | async-start | bytes 5242880 | tf_op jit(solution)/shard_map/all_to_all | solution.py:431
  25.8 17.9 %copy-start.8 = (s32[8]{0:T(128)S(1)}, s32[8]{0:T(128)}, u32[]{:S(2)}) copy-start(s32[8]{0:T(128)} %param.8) | copy-start | bytes 100
  37.8 31.4 %copy-start = (bf16[256,32,128]{2,1,0:T(8,128)(2,1)}, bf16[256,32,128]{2,1,0:T(8,128)(2,1)S(1)}, u32[]{:S(2)}) copy-start(bf16[256,32,128]{2,1,0:T(8,128)(2,1)S(1)} %zonal.4.own) | copy-start | bytes 6291460
  37.8 26.9 %collective-permute-start.2 = (bf16[256,32,128]{2,1,0:T(8,128)(2,1)S(1)}, bf16[256,32,128]{2,1,0:T(8,128)(2,1)}, u32[]{:S(2)}, u32[]{:S(2)}) collective-permute-start(bf16[256,32,128]{2,1,0:T(8,128)(2,1)S(1)} %zonal.4.own), channel_id=1, source_target_pairs={{0,8},{8,16},{16,24},{1,9},{9,17},{17,25},{2,10},{10,18},{18,26},{... | collective-permute-start | bytes 6291464 | tf_op jit(solution)/shard_map/ppermute | solution.py:425
  41.8 27.5 %collective-permute-start.3 = (bf16[256,32,128]{2,1,0:T(8,128)(2,1)S(1)}, bf16[256,32,128]{2,1,0:T(8,128)(2,1)}, u32[]{:S(2)}, u32[]{:S(2)}) collective-permute-start(bf16[256,32,128]{2,1,0:T(8,128)(2,1)S(1)} %zonal.4.own), channel_id=1, source_target_pairs={{8,0},{16,8},{24,16},{9,1},{17,9},{25,17},{10,2},{18,10},{26,18},{... | collective-permute-start | bytes 6291464 | tf_op jit(solution)/shard_map/ppermute | solution.py:426
  73.7 1.3 copy-start.1
  83.1 52.3 %all-to-all-start.1 = ((bf16[8,1024,128]{2,1,0:T(8,128)(2,1)}), bf16[8,1024,128]{2,1,0:T(8,128)(2,1)S(1)}, u32[]{:S(2)}, u32[]{:S(2)}) async-start(bf16[8,1024,128]{2,1,0:T(8,128)(2,1)} %bitcast.4), calls=%async_computation.1 | async-start | bytes 4194304 | tf_op jit(solution)/shard_map/all_to_all | solution.py:431
  97.8 25.3 %collective-permute-start = (bf16[128,32,128]{2,1,0:T(8,128)(2,1)S(1)}, bf16[128,32,128]{2,1,0:T(8,128)(2,1)}, u32[]{:S(2)}, u32[]{:S(2)}) collective-permute-start(bf16[128,32,128]{2,1,0:T(8,128)(2,1)S(1)} %zonal.3.own), channel_id=1, source_target_pairs={{0,8},{8,16},{16,24},{1,9},{9,17},{17,25},{2,10},{10,18},{18,26},{... | collective-permute-start | bytes 3145736 | tf_op jit(solution)/shard_map/ppermute | solution.py:425
  101.7 21.3 %collective-permute-start.1 = (bf16[128,32,128]{2,1,0:T(8,128)(2,1)S(1)}, bf16[128,32,128]{2,1,0:T(8,128)(2,1)}, u32[]{:S(2)}, u32[]{:S(2)}) collective-permute-start(bf16[128,32,128]{2,1,0:T(8,128)(2,1)S(1)} %zonal.3.own), channel_id=1, source_target_pairs={{8,0},{16,8},{24,16},{9,1},{17,9},{25,17},{10,2},{18,10},{26,18},{... | collective-permute-start | bytes 3145736 | tf_op jit(solution)/shard_map/ppermute | solution.py:426
  109.2 8.2 %copy-start.2 = (bf16[683,1024]{1,0:T(8,128)(2,1)}, bf16[683,1024]{1,0:T(8,128)(2,1)S(1)}, u32[]{:S(2)}) copy-start(bf16[683,1024]{1,0:T(8,128)(2,1)S(1)} %get-tuple-element.9.even) | copy-start | bytes 4196356
  109.2 8.2 %copy-start.5 = (bf16[683,1024]{1,0:T(8,128)(2,1)}, bf16[683,1024]{1,0:T(8,128)(2,1)S(1)}, u32[]{:S(2)}) copy-start(bf16[683,1024]{1,0:T(8,128)(2,1)S(1)} %get-tuple-element.10.odd) | copy-start | bytes 4196356
  117.4 25.5 %collective-permute-start.4 = (bf16[40,2,16,683]{3,2,1,0:T(8,128)(2,1)}, bf16[40,2,16,683]{3,2,1,0:T(8,128)(2,1)}, u32[]{:S(2)}, u32[]{:S(2)}) collective-permute-start(bf16[40,2,16,683]{3,2,1,0:T(8,128)(2,1)} %get-tuple-element.11.own), channel_id=1, source_target_pairs={{0,8},{8,16},{16,24},{1,9},{9,17},{17,25},{2,10},{10,18},{18,26},{... | collective-permute-start | bytes 5245448 | tf_op jit(solution)/shard_map/ppermute | solution.py:425
  121.1 26.5 %collective-permute-start.5 = (bf16[40,2,16,683]{3,2,1,0:T(8,128)(2,1)}, bf16[40,2,16,683]{3,2,1,0:T(8,128)(2,1)}, u32[]{:S(2)}, u32[]{:S(2)}) collective-permute-start(bf16[40,2,16,683]{3,2,1,0:T(8,128)(2,1)} %get-tuple-element.11.own), channel_id=1, source_target_pairs={{8,0},{16,8},{24,16},{9,1},{17,9},{25,17},{10,2},{18,10},{26,18},{... | collective-permute-start | bytes 5245448 | tf_op jit(solution)/shard_map/ppermute | solution.py:426
  135.4 34.1 %all-to-all-start = ((bf16[8,512,128]{2,1,0:T(8,128)(2,1)}), bf16[8,512,128]{2,1,0:T(8,128)(2,1)S(1)}, u32[]{:S(2)}, u32[]{:S(2)}) async-start(bf16[8,512,128]{2,1,0:T(8,128)(2,1)} %bitcast), calls=%async_computation | async-start | bytes 2097152 | tf_op jit(solution)/shard_map/all_to_all | solution.py:431
  147.5 1.4 copy-start.3
  148.9 1.4 copy-start.6
  169.5 1.4 copy-start.4
  170.9 1.4 copy-start.7

commit v8 on v7

--- a/solution.py
+++ b/solution.py
@@ -9,27 +9,11 @@
 from jax.sharding import PartitionSpec as P
 
 SPREAD = 2
-VMEM_BYTES = 48 * 1024 * 1024
+VMEM_BYTES = 24 * 1024 * 1024
+ZONAL_BYTES = 44 * 1024 * 1024
 LANES = 128
+SUBLANES = 8
 TOKEN = (8, 128)
-
-
-def zonal_factors(wavenumbers, longitudes, truncation):
-    coarse = jnp.arange(longitudes // LANES, dtype=jnp.int32) * LANES
-    fine = jnp.arange(LANES, dtype=jnp.int32)
-    weight = (wavenumbers < truncation).astype(jnp.float32) / math.sqrt(longitudes)
-
-    def angles(points):
-        phase = wavenumbers[:, None] * points[None, :] % longitudes
-        return phase.astype(jnp.float32) * (2.0 * math.pi / longitudes)
-
-    coarse_angle, fine_angle = angles(coarse), angles(fine)
-    return (
-        jnp.cos(coarse_angle) * weight[:, None],
-        jnp.sin(coarse_angle) * weight[:, None],
-        jnp.cos(fine_angle),
-        jnp.sin(fine_angle),
-    )
 
 
 def meridional_factors(truncation, latitudes, starts, width):
@@ -70,72 +54,99 @@
     )(*factors)
 
 
-def zonal_kernel(
-    fields_step, fields, tokens, cos_c, sin_c, cos_f, sin_f, velocity, tracer, *rest
-):
-    out, table, total = rest[tokens:]
-    step = pl.program_id(0)
-    rows = cos_f.shape[0]
-    lat_local, longitudes = velocity.shape[2:]
-    out_rows = out.shape[1]
-
-    @pl.when(step == 0)
-    def _():
-        cos_b, sin_b = cos_f[...], sin_f[...]
-        for at in range(longitudes // LANES):
-            cos_a, sin_a = cos_c[:, at : at + 1], sin_c[:, at : at + 1]
-            columns = slice(at * LANES, (at + 1) * LANES)
-            table[:rows, columns] = (cos_a * cos_b - sin_a * sin_b).astype(table.dtype)
-            table[rows:, columns] = (-sin_a * cos_b - cos_a * sin_b).astype(table.dtype)
-
-    product = velocity[...].astype(jnp.float32) * tracer[...].astype(jnp.float32)
-    product = product.astype(jnp.bfloat16).reshape(fields_step * lat_local, longitudes)
-    sums = lax.dot_general(
-        table[...], product, (((1,), (1,)), ((), ())), preferred_element_type=jnp.float32
-    )
-    steps_per_member = fields // fields_step
-    member = step // steps_per_member
-    first_field = step % steps_per_member * fields_step
-    for part in range(2):
-        for field in range(fields_step):
-            row = (member * 2 + part) * fields + first_field + field
-            total[pl.ds(row, rows, stride=out_rows), :] = sums[
-                part * rows : (part + 1) * rows, field * lat_local : (field + 1) * lat_local
-            ]
-
-    @pl.when(step == pl.num_programs(0) - 1)
-    def _():
-        out[...] = total[...].reshape(out.shape).astype(out.dtype)
-
-
-def zonal_transform(factors, velocity, tracer, tokens):
+def zonal_kernel(truncation, tokens, waves, velocity, tracer, *rest):
+    out, table, total, velocity_here, tracer_here, sems = rest[tokens:]
+    members, fields, lat_local, longitudes = velocity.shape
+    rows = waves.shape[0]
+    groups = velocity_here.shape[0]
+    step_fields = velocity_here.shape[1]
+    steps = fields // step_fields
+
+    def copies(step):
+        part = (step // steps, pl.ds(step % steps * step_fields, step_fields))
+        return [
+            pltpu.make_async_copy(source.at[part], target.at[step], sems.at[step, at])
+            for at, (source, target) in enumerate(
+                ((velocity, velocity_here), (tracer, tracer_here))
+            )
+        ]
+
+    for step in range(groups):
+        for copy in copies(step):
+            copy.start()
+
+    wave = waves[...]
+    weight = jnp.where(wave < truncation, 1.0 / math.sqrt(longitudes), 0.0)
+
+    def angles(count, stride):
+        points = lax.broadcasted_iota(jnp.int32, (rows, count), 1) * stride
+        phase = lax.rem(wave * points, jnp.full((), longitudes, jnp.int32))
+        return phase.astype(jnp.float32) * (2.0 * math.pi / longitudes)
+
+    coarse, fine = angles(longitudes // LANES, LANES), angles(LANES, 1)
+    cos_c, sin_c = jnp.cos(coarse) * weight, jnp.sin(coarse) * weight
+    cos_f, sin_f = jnp.cos(fine), jnp.sin(fine)
+    for at in range(longitudes // LANES):
+        cos_a, sin_a = cos_c[:, at : at + 1], sin_c[:, at : at + 1]
+        columns = slice(at * LANES, (at + 1) * LANES)
+        table[:rows, columns] = (cos_a * cos_f - sin_a * sin_f).astype(table.dtype)
+        table[rows:, columns] = (-sin_a * cos_f - cos_a * sin_f).astype(table.dtype)
+
+    def body(step, carry):
+        for copy in copies(step):
+            copy.wait()
+        product = velocity_here[step].astype(jnp.float32) * tracer_here[step].astype(jnp.float32)
+        product = product.astype(jnp.bfloat16).reshape(step_fields * lat_local, longitudes)
+        sums = lax.dot_general(
+            table[...], product, (((1,), (1,)), ((), ())), preferred_element_type=jnp.float32
+        )
+        first = step // steps * 2 * fields + step % steps * step_fields
+        for part in range(2):
+            for field in range(step_fields):
+                block = sums[
+                    part * rows : (part + 1) * rows, field * lat_local : (field + 1) * lat_local
+                ]
+                total[:, first + part * fields + field] = block.reshape(
+                    rows // SUBLANES, SUBLANES, lat_local
+                )
+        return carry
+
+    lax.fori_loop(0, groups, body, 0)
+
+    def turn(at, carry):
+        first = pl.multiple_of(at * SUBLANES, SUBLANES)
+        out[pl.ds(first, SUBLANES)] = jnp.swapaxes(total[at], 0, 1).astype(out.dtype)
+        return carry
+
+    lax.fori_loop(0, rows // SUBLANES, turn, 0)
+
+
+def zonal_transform(waves, truncation, velocity, tracer, tokens):
     mem_local, fields, lat_local, longitudes = velocity.shape
-    rows = factors[0].shape[0]
+    rows = waves.shape[0]
     fields_step = min(fields, max(1, 512 // lat_local))
-    steps = fields // fields_step
+    groups = mem_local * (fields // fields_step)
     out_rows = mem_local * 2 * fields
-    whole = lambda step: (0, 0)
-    grid_block = pl.BlockSpec(
-        (1, fields_step, lat_local, longitudes), lambda step: (step // steps, step % steps, 0, 0)
-    )
+    grid_part = pltpu.VMEM((groups, fields_step, lat_local, longitudes), velocity.dtype)
     flops = 2 * 2 * rows * longitudes * mem_local * fields * lat_local
     moved = 2 * velocity.size * 2 + rows * out_rows * lat_local * 2
     return pl.pallas_call(
-        functools.partial(zonal_kernel, fields_step, fields, len(tokens)),
-        grid=(mem_local * steps,),
-        in_specs=[pl.BlockSpec(f.shape, whole) for f in factors]
-        + [grid_block, grid_block]
-        + [pl.BlockSpec(memory_space=pl.ANY)] * len(tokens),
-        out_specs=pl.BlockSpec((rows, out_rows, lat_local), lambda step: (0, 0, 0)),
+        functools.partial(zonal_kernel, truncation, len(tokens)),
+        in_specs=[pl.BlockSpec(memory_space=pltpu.VMEM)]
+        + [pl.BlockSpec(memory_space=pl.ANY)] * (2 + len(tokens)),
+        out_specs=pl.BlockSpec(memory_space=pltpu.VMEM),
         out_shape=jax.ShapeDtypeStruct((rows, out_rows, lat_local), jnp.bfloat16),
         scratch_shapes=[
             pltpu.VMEM((2 * rows, longitudes), jnp.bfloat16),
-            pltpu.VMEM((rows * out_rows, lat_local), jnp.float32),
+            pltpu.VMEM((rows // SUBLANES, out_rows, SUBLANES, lat_local), jnp.float32),
+            grid_part,
+            grid_part,
+            pltpu.SemaphoreType.DMA((groups, 2)),
         ],
-        compiler_params=pltpu.CompilerParams(vmem_limit_bytes=VMEM_BYTES),
+        compiler_params=pltpu.CompilerParams(vmem_limit_bytes=ZONAL_BYTES),
         cost_estimate=pl.CostEstimate(flops=flops, bytes_accessed=moved, transcendentals=0),
         name="zonal",
-    )(*factors, velocity, tracer, *tokens)
+    )(waves, velocity, tracer, *tokens)
 
 
 def forward_kernel(first, block, waves, received, even, odd, *rest):
@@ -283,7 +294,8 @@
     )(waves, offsets, *operands)
 
 
-def copy_kernel(offsets, low, own, high, out):
+def copy_kernel(offsets, low, own, high, *rest):
+    out = rest[-1]
     rows = out.shape[1] // offsets.shape[0]
     for child in range(offsets.shape[0]):
         index, chosen = 0, None
@@ -295,7 +307,7 @@
         out[:, child * rows : (child + 1) * rows] = chosen
 
 
-def copy_parents(offsets, low, own, high):
+def copy_parents(offsets, low, own, high, tokens):
     steps = math.gcd(own.shape[0], 4)
     block = lambda array: pl.BlockSpec(
         (array.shape[0] // steps,) + array.shape[1:], lambda step, o: (step, 0, 0)
@@ -305,14 +317,15 @@
         grid_spec=pltpu.PrefetchScalarGridSpec(
             num_scalar_prefetch=1,
             grid=(steps,),
-            in_specs=[block(low), block(own), block(high)],
+            in_specs=[block(low), block(own), block(high)]
+            + [pl.BlockSpec(memory_space=pl.ANY)] * len(tokens),
             out_specs=block(own),
         ),
         out_shape=jax.ShapeDtypeStruct(own.shape, own.dtype),
         compiler_params=pltpu.CompilerParams(vmem_limit_bytes=VMEM_BYTES),
         cost_estimate=pl.CostEstimate(flops=0, bytes_accessed=8 * own.size, transcendentals=0),
         name="parents",
-    )(offsets, low, own, high)
+    )(offsets, low, own, high, *tokens)
 
 
 def finish_kernel(first, block, waves, received, noise, even, odd, *rest):
@@ -389,7 +402,7 @@
 
 def chunk_bounds(slots_here, block):
     blocks = slots_here // block
-    edges = [0, (blocks * 5 + 10) // 11, (blocks * 9 + 10) // 11, blocks]
+    edges = [0, (blocks * 5 + 10) // 11, (blocks * 10 + 10) // 11, blocks]
     edges = [edge * block for edge in edges]
     return [(start, stop) for start, stop in zip(edges[:-1], edges[1:]) if stop > start]
 
@@ -418,8 +431,8 @@
 
     def zonal(at):
         start, stop = bounds[at]
-        factors = zonal_factors(slot_grid[:, start:stop].reshape(-1), longitudes, truncation)
-        return zonal_transform(factors, velocity, tracer, [])
+        waves = slot_grid[:, start:stop].reshape(-1, 1)
+        return zonal_transform(waves, truncation, velocity, tracer, [])
 
     def neighbours(rows, per_member):
         low = lax.ppermute(rows[:, rows.shape[1] - SPREAD * per_member :], "member", upward)
@@ -433,16 +446,19 @@
             moved = jnp.swapaxes(moved, 0, 1).reshape(1, -1, latitudes)
         return moved
 
+    def copied(at, tokens):
+        return copy_parents(offsets, *neighbours(zonal(at), per_member), tokens)
+
     received = exchanged(zonal(0))
     even, odd = meridional_tables(truncation, latitudes, starts, inner)
-    later = [copy_parents(offsets, *neighbours(zonal(at), per_member)) for at in range(1, len(bounds))]
-    later = [exchanged(outgoing) for outgoing in later]
+    later = [exchanged(copied(1, []))] if len(bounds) > 1 else []
     spectra, _ = forward_transform(
         (own_waves, per_member), 0, block, received, even, odd, mem_local, []
     )
-    *outs, _ = inverse_transform(
+    *outs, token = inverse_transform(
         own_waves, offsets, 0, block, *neighbours(spectra, 1), noise, even, odd, None
     )
+    later += [exchanged(copied(at, [token])) for at in range(2, len(bounds))]
     for (start, _), received in zip(bounds[1:], later):
         outs = finish_transform(own_waves, start, block, received, noise, even, odd, outs)
     return tuple(outs)

time: 179 us -> 174 us (0.972)
  Pallas kernels: 80.3 us -> 67.2 us
  local copies, waits for them, and re-layouts: 9.11 us -> 19.1 us
  other arithmetic: 6.1 us -> 2.88 us
    unnamed x18 -> x36, local copies, waits for them, and re-layouts: 6.74 us -> 17 us
    ppermute x3, waiting for transfers between devices: 24 us -> 32.2 us  [neighbours(): lax.ppermute(rows[:, rows.shape[1] - SPREAD * per_member:], 'member', upw...]
    all_to_all x3, waiting for transfers between devices: 16 us -> 8.46 us  [exchanged(): lax.all_to_all(outgoing, 'lat', split_axis=0, concat_axis=0, tiled=True)]
    pallas_call x3, Pallas kernels: 35.9 us -> 28.4 us  [zonal_transform(): pl.pallas_call(functools.partial(zonal_kernel, truncation, len(tokens)),...]
    pallas_call x2, Pallas kernels: 16.2 us -> 14.3 us  [finish_transform(): pl.pallas_call(functools.partial(finish_kernel, first, block), grid_spec=...]
  transfers between devices with their start and end apart: 9 -> 9, of which waited for: 6 -> 6; matrix products, arithmetic and copies ran while one was open for 3% -> 2% of each run, Pallas kernels for 33% -> 31%
where the time goes in v8:
time: 174 us; the launch traced here: 172 us
  Pallas kernels  67.2 us (39%)
  waiting for transfers between devices  49.4 us (28%)
  starting transfers between devices  32.8 us (19%)
  local copies, waits for them, and re-layouts  19.1 us (11%)
  other arithmetic  2.88 us (2%)
    ppermute x3, waiting for transfers between devices, neighbours(): lax.ppermute(rows[:, rows.shape[1] - SPREAD * per_member:], 'member', upw...  32.2 us
    pallas_call x3, Pallas kernels, zonal_transform(): pl.pallas_call(functools.partial(zonal_kernel, truncation, len(tokens)),...  28.4 us
    unnamed x36, local copies, waits for them, and re-layouts  17 us
    all_to_all x3, starting transfers between devices, exchanged(): lax.all_to_all(outgoing, 'lat', split_axis=0, concat_axis=0, tiled=True)  15.5 us
    pallas_call x2, Pallas kernels, finish_transform(): pl.pallas_call(functools.partial(finish_kernel, first, block), grid_spec=...  14.3 us
    ppermute x3, starting transfers between devices, neighbours(): lax.ppermute(rows[:, rows.shape[1] - SPREAD * per_member:], 'member', upw...  11.6 us
    pallas_call x1, Pallas kernels, inverse_transform(): pl.pallas_call(functools.partial(inverse_kernel, first, block), grid_spec...  8.87 us
    ppermute x3, waiting for transfers between devices, neighbours(): high = lax.ppermute(rows[:, :SPREAD * per_member], 'member', downward)  8.8 us
  transfers between devices with their start and end apart: 9, of which 6 were waited for; matrix products, arithmetic and copies ran while one was open for 2% of the time, Pallas kernels for 31%

profile of v8, /device:TPU:1, one launch (start us, length us, event | category | flops | bytes accessed | tf_op | source)
XLA Modules:
  0.0 172.4 jit_solution(13125241535628534164)
XLA Ops:
  0.6 0.8 reshape.34
  1.4 0.1 fusion.13
  1.5 0.1 reshape.42.waves
  1.6 10.7 %zonal.4 = bf16[320,32,128]{2,1,0:T(8,128)(2,1)S(1)} custom-call(s32[320,1]{1,0:T(8,128)S(1)} %reshape.42.waves, bf16[2,8,128,2048]{3,2,1,0:T(8,128)(2,1)} %velocity.5, bf16[2,8,128,2048]{3,2,1,0:T(8,128)(2,1)} %tracer.5), custom_call_target="tpu_custom_call" | custom-call | flops 5368709120 | bytes 19398656 | tf_op jit(solution)/shard_map/zonal/pallas_call | solution.py:133
  12.3 1.5 copy-done.5
  13.8 6.4 %all-to-all-start = ((bf16[8,1280,128]{2,1,0:T(8,128)(2,1)}), bf16[8,1280,128]{2,1,0:T(8,128)(2,1)S(1)}, u32[]{:S(2)}, u32[]{:S(2)}) async-start(bf16[8,1280,128]{2,1,0:T(8,128)(2,1)} %bitcast.5), calls=%async_computation | async-start | bytes 5242880 | tf_op jit(solution)/shard_map/all_to_all | solution.py:444
  20.2 0.1 reshape.43.waves
  20.3 12.2 %zonal.5.own = bf16[320,32,128]{2,1,0:T(8,128)(2,1)} custom-call(s32[320,1]{1,0:T(8,128)S(1)} %reshape.43.waves, bf16[2,8,128,2048]{3,2,1,0:T(8,128)(2,1)} %velocity.5, bf16[2,8,128,2048]{3,2,1,0:T(8,128)(2,1)} %tracer.5), custom_call_target="tpu_custom_call" | custom-call | flops 5368709120 | bytes 19398656 | tf_op jit(solution)/shard_map/zonal/pallas_call | solution.py:133
  32.5 4.0 %collective-permute-start.4 = (bf16[320,32,128]{2,1,0:T(8,128)(2,1)}, bf16[320,32,128]{2,1,0:T(8,128)(2,1)}, u32[]{:S(2)}, u32[]{:S(2)}) collective-permute-start(bf16[320,32,128]{2,1,0:T(8,128)(2,1)} %zonal.5.own), channel_id=1, source_target_pairs={{0,8},{8,16},{16,24},{1,9},{9,17},{17,25},{2,10},{10,18},{18,26},{... | collective-permute-start | bytes 7864328 | tf_op jit(solution)/shard_map/ppermute | solution.py:438
  36.5 1.9 %collective-permute-start.5 = (bf16[320,32,128]{2,1,0:T(8,128)(2,1)}, bf16[320,32,128]{2,1,0:T(8,128)(2,1)}, u32[]{:S(2)}, u32[]{:S(2)}) collective-permute-start(bf16[320,32,128]{2,1,0:T(8,128)(2,1)} %zonal.5.own), channel_id=1, source_target_pairs={{8,0},{16,8},{24,16},{9,1},{17,9},{25,17},{10,2},{18,10},{26,18},{... | collective-permute-start | bytes 7864328 | tf_op jit(solution)/shard_map/ppermute | solution.py:439
  38.4 0.1 subtract_add_fusion.offsets
  38.5 26.9 %collective-permute-done.4.low = bf16[320,32,128]{2,1,0:T(8,128)(2,1)} collective-permute-done((bf16[320,32,128]{2,1,0:T(8,128)(2,1)}, bf16[320,32,128]{2,1,0:T(8,128)(2,1)}, u32[]{:S(2)}, u32[]{:S(2)}) %collective-permute-start.4) | collective-permute-done | bytes 2621472 | tf_op jit(solution)/shard_map/ppermute | solution.py:438
  65.4 4.4 %collective-permute-done.5.high = bf16[320,32,128]{2,1,0:T(8,128)(2,1)} collective-permute-done((bf16[320,32,128]{2,1,0:T(8,128)(2,1)}, bf16[320,32,128]{2,1,0:T(8,128)(2,1)}, u32[]{:S(2)}, u32[]{:S(2)}) %collective-permute-start.5) | collective-permute-done | bytes 2621472 | tf_op jit(solution)/shard_map/ppermute | solution.py:439
  69.8 6.3 %parents.3 = bf16[320,32,128]{2,1,0:T(8,128)(2,1)} custom-call(s32[2]{0:T(128)S(1)} %subtract_add_fusion.offsets, bf16[320,32,128]{2,1,0:T(8,128)(2,1)} %collective-permute-done.4.low, bf16[320,32,128]{2,1,0:T(8,128)(2,1)} %zonal.5.own, bf16[320,32,128]{2,1,0:T(8,128)(2,1)} %collective-permute-done.5.high), custom_call_target="tpu_custom_call" | custom-call | bytes 10485760 | tf_op jit(solution)/shard_map/parents/pallas_call | solution.py:315
  76.1 2.7 %all-to-all-done.received = bf16[8,1280,128]{2,1,0:T(8,128)(2,1)S(1)} async-done(((bf16[8,1280,128]{2,1,0:T(8,128)(2,1)}), bf16[8,1280,128]{2,1,0:T(8,128)(2,1)S(1)}, u32[]{:S(2)}, u32[]{:S(2)}) %all-to-all-start) | async-done | bytes 2621472 | tf_op jit(solution)/shard_map/all_to_all | solution.py:444
  78.8 1.5 copy-done.3
  80.3 4.7 %all-to-all-start.2 = ((bf16[8,1280,128]{2,1,0:T(8,128)(2,1)}), bf16[8,1280,128]{2,1,0:T(8,128)(2,1)S(1)}, u32[]{:S(2)}, u32[]{:S(2)}) async-start(bf16[8,1280,128]{2,1,0:T(8,128)(2,1)} %bitcast.2), calls=%async_computation.2 | async-start | bytes 5242880 | tf_op jit(solution)/shard_map/all_to_all | solution.py:444
  85.0 0.8 dynamic_slice.6.waves
  85.7 0.1 fusion.9
  85.8 0.2 copy.17
  86.0 1.4 fusion.6
  87.4 1.3 sine_multiply_fusion
  88.7 1.7 tables.1
  90.4 0.0 slice-start
  90.5 6.7 %forward.1 = (bf16[40,2,16,683]{3,2,1,0:T(8,128)(2,1)}, f32[8,128]{1,0:T(8,128)}) custom-call(s32[88]{0:T(128)S(1)} %dynamic_slice.6.waves, bf16[8,1280,128]{2,1,0:T(8,128)(2,1)S(1)} %copy-done.4, bf16[683,1024]{1,0:T(8,128)(2,1)S(1)} %get-tuple-element.10.even, bf16[683,1024]{1,0:T(8,128)(2,1)S(1)} %get-tuple-element.11.odd), custom_call_target="tpu_custom_call" | custom-call | flops 3580887040 | bytes 7167488 | tf_op jit(solution)/shard_map/forward/pallas_call | solution.py:179
  97.1 4.0 %collective-permute-start.2 = (bf16[40,2,16,683]{3,2,1,0:T(8,128)(2,1)}, bf16[40,2,16,683]{3,2,1,0:T(8,128)(2,1)}, u32[]{:S(2)}, u32[]{:S(2)}) collective-permute-start(bf16[40,2,16,683]{3,2,1,0:T(8,128)(2,1)} %get-tuple-element.12.own), channel_id=1, source_target_pairs={{0,8},{8,16},{16,24},{1,9},{9,17},{17,25},{2,10},{10,18},{18,26},{... | collective-permute-start | bytes 5245448 | tf_op jit(solution)/shard_map/ppermute | solution.py:438
  101.1 1.9 %collective-permute-start.3 = (bf16[40,2,16,683]{3,2,1,0:T(8,128)(2,1)}, bf16[40,2,16,683]{3,2,1,0:T(8,128)(2,1)}, u32[]{:S(2)}, u32[]{:S(2)}) collective-permute-start(bf16[40,2,16,683]{3,2,1,0:T(8,128)(2,1)} %get-tuple-element.12.own), channel_id=1, source_target_pairs={{8,0},{16,8},{24,16},{9,1},{17,9},{25,17},{10,2},{18,10},{26,18},{... | collective-permute-start | bytes 5245448 | tf_op jit(solution)/shard_map/ppermute | solution.py:439
  103.0 0.1 slice.9
  103.1 0.1 reshape.41.waves
  103.2 3.4 %copy-done = bf16[2,8,128,2048]{3,2,1,0:T(8,128)(2,1)S(1)} copy-done((bf16[2,8,128,2048]{3,2,1,0:T(8,128)(2,1)S(1)}, bf16[2,8,128,2048]{3,2,1,0:T(8,128)(2,1)}, u32[]{:S(2)}) %copy-start) | copy-done | bytes 8388632
  106.6 5.5 %zonal.3.own = bf16[64,32,128]{2,1,0:T(8,128)(2,1)S(1)} custom-call(s32[64,1]{1,0:T(8,128)S(1)} %reshape.41.waves, bf16[2,8,128,2048]{3,2,1,0:T(8,128)(2,1)S(1)} %copy-done, bf16[2,8,128,2048]{3,2,1,0:T(8,128)(2,1)} %tracer.5), custom_call_target="tpu_custom_call" | custom-call | flops 1073741824 | bytes 17301504 | tf_op jit(solution)/shard_map/zonal/pallas_call | solution.py:133
  112.1 3.6 %collective-permute-start = (bf16[64,32,128]{2,1,0:T(8,128)(2,1)S(1)}, bf16[64,32,128]{2,1,0:T(8,128)(2,1)S(1)}, u32[]{:S(2)}, u32[]{:S(2)}) collective-permute-start(bf16[64,32,128]{2,1,0:T(8,128)(2,1)S(1)} %zonal.3.own), channel_id=1, source_target_pairs={{0,8},{8,16},{16,24},{1,9},{9,17},{17,25},{2,10},{10,18},{18,26},{... | collective-permute-start | bytes 1572872 | tf_op jit(solution)/shard_map/ppermute | solution.py:438
  115.7 1.9 %collective-permute-start.1 = (bf16[64,32,128]{2,1,0:T(8,128)(2,1)S(1)}, bf16[64,32,128]{2,1,0:T(8,128)(2,1)S(1)}, u32[]{:S(2)}, u32[]{:S(2)}) collective-permute-start(bf16[64,32,128]{2,1,0:T(8,128)(2,1)S(1)} %zonal.3.own), channel_id=1, source_target_pairs={{8,0},{16,8},{24,16},{9,1},{17,9},{25,17},{10,2},{18,10},{26,18},{... | collective-permute-start | bytes 1572872 | tf_op jit(solution)/shard_map/ppermute | solution.py:439
  117.6 5.3 %collective-permute-done.2.low = bf16[40,2,16,683]{3,2,1,0:T(8,128)(2,1)} collective-permute-done((bf16[40,2,16,683]{3,2,1,0:T(8,128)(2,1)}, bf16[40,2,16,683]{3,2,1,0:T(8,128)(2,1)}, u32[]{:S(2)}, u32[]{:S(2)}) %collective-permute-start.2) | collective-permute-done | bytes 1748512 | tf_op jit(solution)/shard_map/ppermute | solution.py:438
  123.0 4.4 %collective-permute-done.3.high = bf16[40,2,16,683]{3,2,1,0:T(8,128)(2,1)} collective-permute-done((bf16[40,2,16,683]{3,2,1,0:T(8,128)(2,1)}, bf16[40,2,16,683]{3,2,1,0:T(8,128)(2,1)}, u32[]{:S(2)}, u32[]{:S(2)}) %collective-permute-start.3) | collective-permute-done | bytes 1748512 | tf_op jit(solution)/shard_map/ppermute | solution.py:439
  127.4 8.9 %inverse.1 = (bf16[88,2,2,8,683]{4,3,2,1,0:T(8,128)(2,1)}, bf16[88,2,2,8,1024]{4,3,2,1,0:T(8,128)(2,1)}, f32[8,128]{1,0:T(8,128)S(1)}) custom-call(s32[88]{0:T(128)S(1)} %dynamic_slice.6.waves, s32[2]{0:T(128)S(1)} %subtract_add_fusion.offsets, bf16[40,2,16,683]{3,2,1,0:T(8,128)(2,1)} %collective-permute-done.2.low, ...), custom_call_target="tpu_custom_call" | custom-call | flops 3580887040 | bytes 14161408 | tf_op jit(solution)/shard_map/inverse/pallas_call | solution.py:269
  136.3 1.0 parents.2
  137.2 0.8 copy-done.6
  138.0 5.8 %all-to-all-done.2.received = bf16[8,1280,128]{2,1,0:T(8,128)(2,1)S(1)} async-done(((bf16[8,1280,128]{2,1,0:T(8,128)(2,1)}), bf16[8,1280,128]{2,1,0:T(8,128)(2,1)S(1)}, u32[]{:S(2)}, u32[]{:S(2)}) %all-to-all-start.2) | async-done | bytes 2621472 | tf_op jit(solution)/shard_map/all_to_all | solution.py:444
  143.8 4.4 %all-to-all-start.1 = ((bf16[8,256,128]{2,1,0:T(8,128)(2,1)}), bf16[8,256,128]{2,1,0:T(8,128)(2,1)S(1)}, u32[]{:S(2)}, u32[]{:S(2)}) async-start(bf16[8,256,128]{2,1,0:T(8,128)(2,1)} %bitcast.6), calls=%async_computation.1 | async-start | bytes 1048576 | tf_op jit(solution)/shard_map/all_to_all | solution.py:444
  148.2 2.2 %copy-done.1 = bf16[88,2,2,8,683]{4,3,2,1,0:T(8,128)(2,1)S(1)} copy-done((bf16[88,2,2,8,683]{4,3,2,1,0:T(8,128)(2,1)S(1)}, bf16[88,2,2,8,683]{4,3,2,1,0:T(8,128)(2,1)}, u32[]{:S(2)}) %copy-start.1) | copy-done | bytes 3846680
  150.5 1.3 copy-done.9
  151.8 1.3 copy-done.13
  153.2 11.1 %finish.2 = (bf16[88,2,2,8,683]{4,3,2,1,0:T(8,128)(2,1)}, bf16[88,2,2,8,1024]{4,3,2,1,0:T(8,128)(2,1)}) custom-call(s32[88]{0:T(128)S(1)} %dynamic_slice.6.waves, bf16[8,1280,128]{2,1,0:T(8,128)(2,1)S(1)} %all-to-all-done.2.received, bf16[88,2,2,8,683]{4,3,2,1,0:T(8,128)(2,1)S(1)} %copy-done.1, ...), custom_call_target="tpu_custom_call", output_to_operand_aliasing={{0}: (5, {}), {1}: (6, {})} | custom-call | flops 7161774080 | bytes 11537408 | tf_op jit(solution)/shard_map/finish/pallas_call | solution.py:379
  164.2 2.2 %copy-done.2 = bf16[88,2,2,8,683]{4,3,2,1,0:T(8,128)(2,1)S(1)} copy-done((bf16[88,2,2,8,683]{4,3,2,1,0:T(8,128)(2,1)S(1)}, bf16[88,2,2,8,683]{4,3,2,1,0:T(8,128)(2,1)}, u32[]{:S(2)}) %copy-start.2) | copy-done | bytes 3846680
  166.5 1.3 copy-done.10
  167.8 1.3 copy-done.14
  169.2 3.2 %finish.3 = (bf16[88,2,2,8,683]{4,3,2,1,0:T(8,128)(2,1)}, bf16[88,2,2,8,1024]{4,3,2,1,0:T(8,128)(2,1)}) custom-call(s32[88]{0:T(128)S(1)} %dynamic_slice.6.waves, bf16[8,256,128]{2,1,0:T(8,128)(2,1)S(1)} %all-to-all-done.1.received, bf16[88,2,2,8,683]{4,3,2,1,0:T(8,128)(2,1)S(1)} %copy-done.2, ...), custom_call_target="tpu_custom_call", output_to_operand_aliasing={{0}: (5, {}), {1}: (6, {})} | custom-call | flops 1432354816 | bytes 4545536 | tf_op jit(solution)/shard_map/finish/pallas_call | solution.py:379
  (31 shorter events, 0.1 us)
Async XLA Ops:
  12.3 1.5 copy-start.5
  13.8 65.0 %all-to-all-start = ((bf16[8,1280,128]{2,1,0:T(8,128)(2,1)}), bf16[8,1280,128]{2,1,0:T(8,128)(2,1)S(1)}, u32[]{:S(2)}, u32[]{:S(2)}) async-start(bf16[8,1280,128]{2,1,0:T(8,128)(2,1)} %bitcast.5), calls=%async_computation | async-start | bytes 5242880 | tf_op jit(solution)/shard_map/all_to_all | solution.py:444
  20.3 18.1 %copy-start.15 = (s32[8]{0:T(128)S(1)}, s32[8]{0:T(128)}, u32[]{:S(2)}) copy-start(s32[8]{0:T(128)} %param.8) | copy-start | bytes 100
  32.5 32.9 %collective-permute-start.4 = (bf16[320,32,128]{2,1,0:T(8,128)(2,1)}, bf16[320,32,128]{2,1,0:T(8,128)(2,1)}, u32[]{:S(2)}, u32[]{:S(2)}) collective-permute-start(bf16[320,32,128]{2,1,0:T(8,128)(2,1)} %zonal.5.own), channel_id=1, source_target_pairs={{0,8},{8,16},{16,24},{1,9},{9,17},{17,25},{2,10},{10,18},{18,26},{... | collective-permute-start | bytes 7864328 | tf_op jit(solution)/shard_map/ppermute | solution.py:438
  36.5 33.3 %collective-permute-start.5 = (bf16[320,32,128]{2,1,0:T(8,128)(2,1)}, bf16[320,32,128]{2,1,0:T(8,128)(2,1)}, u32[]{:S(2)}, u32[]{:S(2)}) collective-permute-start(bf16[320,32,128]{2,1,0:T(8,128)(2,1)} %zonal.5.own), channel_id=1, source_target_pairs={{8,0},{16,8},{24,16},{9,1},{17,9},{25,17},{10,2},{18,10},{26,18},{... | collective-permute-start | bytes 7864328 | tf_op jit(solution)/shard_map/ppermute | solution.py:439
  78.8 1.5 copy-start.3
  80.3 63.5 %all-to-all-start.2 = ((bf16[8,1280,128]{2,1,0:T(8,128)(2,1)}), bf16[8,1280,128]{2,1,0:T(8,128)(2,1)S(1)}, u32[]{:S(2)}, u32[]{:S(2)}) async-start(bf16[8,1280,128]{2,1,0:T(8,128)(2,1)} %bitcast.2), calls=%async_computation.2 | async-start | bytes 5242880 | tf_op jit(solution)/shard_map/all_to_all | solution.py:444
  86.0 4.5 %copy-start.4 = (bf16[8,1280,128]{2,1,0:T(8,128)(2,1)S(1)}, bf16[8,1280,128]{2,1,0:T(8,128)(2,1)}, u32[]{:S(2)}) copy-start(bf16[8,1280,128]{2,1,0:T(8,128)(2,1)} %copy-done.3) | copy-start | bytes 7864324
  90.4 6.7 %copy-start.7 = (bf16[683,1024]{1,0:T(8,128)(2,1)}, bf16[683,1024]{1,0:T(8,128)(2,1)S(1)}, u32[]{:S(2)}) copy-start(bf16[683,1024]{1,0:T(8,128)(2,1)S(1)} %get-tuple-element.10.even) | copy-start | bytes 4196356
  90.4 6.7 %copy-start.11 = (bf16[683,1024]{1,0:T(8,128)(2,1)}, bf16[683,1024]{1,0:T(8,128)(2,1)S(1)}, u32[]{:S(2)}) copy-start(bf16[683,1024]{1,0:T(8,128)(2,1)S(1)} %get-tuple-element.11.odd) | copy-start | bytes 4196356
  90.4 36.9 %slice-start = ((s8[4325376]{0:T(1024)(128)(4,1)}), s8[131072]{0:T(1024)(128)(4,1)S(1)}, s32[]{:S(2)}) async-start(s8[4325376]{0:T(1024)(128)(4,1)} %bitcast.3), calls=%async_computation.3 | async-start | bytes 262144
  97.1 25.8 %collective-permute-start.2 = (bf16[40,2,16,683]{3,2,1,0:T(8,128)(2,1)}, bf16[40,2,16,683]{3,2,1,0:T(8,128)(2,1)}, u32[]{:S(2)}, u32[]{:S(2)}) collective-permute-start(bf16[40,2,16,683]{3,2,1,0:T(8,128)(2,1)} %get-tuple-element.12.own), channel_id=1, source_target_pairs={{0,8},{8,16},{16,24},{1,9},{9,17},{17,25},{2,10},{10,18},{18,26},{... | collective-permute-start | bytes 5245448 | tf_op jit(solution)/shard_map/ppermute | solution.py:438
  101.1 26.3 %collective-permute-start.3 = (bf16[40,2,16,683]{3,2,1,0:T(8,128)(2,1)}, bf16[40,2,16,683]{3,2,1,0:T(8,128)(2,1)}, u32[]{:S(2)}, u32[]{:S(2)}) collective-permute-start(bf16[40,2,16,683]{3,2,1,0:T(8,128)(2,1)} %get-tuple-element.12.own), channel_id=1, source_target_pairs={{8,0},{16,8},{24,16},{9,1},{17,9},{25,17},{10,2},{18,10},{26,18},{... | collective-permute-start | bytes 5245448 | tf_op jit(solution)/shard_map/ppermute | solution.py:439
  103.2 3.4 %copy-start = (bf16[2,8,128,2048]{3,2,1,0:T(8,128)(2,1)S(1)}, bf16[2,8,128,2048]{3,2,1,0:T(8,128)(2,1)}, u32[]{:S(2)}) copy-start(bf16[2,8,128,2048]{3,2,1,0:T(8,128)(2,1)} %velocity.5) | copy-start | bytes 25165828
  106.6 20.8 %slice-start.1 = ((s8[4325376]{0:T(1024)(128)(4,1)}), s8[4194304]{0:T(1024)(128)(4,1)S(1)}, s32[]{:S(2)}) async-start(s8[4325376]{0:T(1024)(128)(4,1)} %bitcast.3), calls=%async_computation.4 | async-start | bytes 8388608
  106.6 20.8 %copy-start.8 = (bf16[683,1024]{1,0:T(8,128)(2,1)S(1)}, bf16[683,1024]{1,0:T(8,128)(2,1)}, u32[]{:S(2)}) copy-start(bf16[683,1024]{1,0:T(8,128)(2,1)} %copy-done.7) | copy-start | bytes 4196356
  106.6 20.8 %copy-start.12 = (bf16[683,1024]{1,0:T(8,128)(2,1)S(1)}, bf16[683,1024]{1,0:T(8,128)(2,1)}, u32[]{:S(2)}) copy-start(bf16[683,1024]{1,0:T(8,128)(2,1)} %copy-done.11) | copy-start | bytes 4196356
  112.1 24.2 %collective-permute-start = (bf16[64,32,128]{2,1,0:T(8,128)(2,1)S(1)}, bf16[64,32,128]{2,1,0:T(8,128)(2,1)S(1)}, u32[]{:S(2)}, u32[]{:S(2)}) collective-permute-start(bf16[64,32,128]{2,1,0:T(8,128)(2,1)S(1)} %zonal.3.own), channel_id=1, source_target_pairs={{0,8},{8,16},{16,24},{1,9},{9,17},{17,25},{2,10},{10,18},{18,26},{... | collective-permute-start | bytes 1572872 | tf_op jit(solution)/shard_map/ppermute | solution.py:438
  115.7 20.5 %collective-permute-start.1 = (bf16[64,32,128]{2,1,0:T(8,128)(2,1)S(1)}, bf16[64,32,128]{2,1,0:T(8,128)(2,1)S(1)}, u32[]{:S(2)}, u32[]{:S(2)}) collective-permute-start(bf16[64,32,128]{2,1,0:T(8,128)(2,1)S(1)} %zonal.3.own), channel_id=1, source_target_pairs={{8,0},{16,8},{24,16},{9,1},{17,9},{25,17},{10,2},{18,10},{26,18},{... | collective-permute-start | bytes 1572872 | tf_op jit(solution)/shard_map/ppermute | solution.py:439
  137.2 0.8 copy-start.6
  143.8 20.4 %all-to-all-start.1 = ((bf16[8,256,128]{2,1,0:T(8,128)(2,1)}), bf16[8,256,128]{2,1,0:T(8,128)(2,1)S(1)}, u32[]{:S(2)}, u32[]{:S(2)}) async-start(bf16[8,256,128]{2,1,0:T(8,128)(2,1)} %bitcast.6), calls=%async_computation.1 | async-start | bytes 1048576 | tf_op jit(solution)/shard_map/all_to_all | solution.py:444
  148.2 2.2 %copy-start.1 = (bf16[88,2,2,8,683]{4,3,2,1,0:T(8,128)(2,1)S(1)}, bf16[88,2,2,8,683]{4,3,2,1,0:T(8,128)(2,1)}, u32[]{:S(2)}) copy-start(bf16[88,2,2,8,683]{4,3,2,1,0:T(8,128)(2,1)} %noise.5) | copy-start | bytes 11539972
  150.5 1.4 copy-start.9
  151.8 1.4 copy-start.13
  164.2 2.2 %copy-start.2 = (bf16[88,2,2,8,683]{4,3,2,1,0:T(8,128)(2,1)S(1)}, bf16[88,2,2,8,683]{4,3,2,1,0:T(8,128)(2,1)}, u32[]{:S(2)}) copy-start(bf16[88,2,2,8,683]{4,3,2,1,0:T(8,128)(2,1)} %noise.5) | copy-start | bytes 11539972
  166.5 1.4 copy-start.10
  167.8 1.4 copy-start.14

commit v9 on v8

--- a/solution.py
+++ b/solution.py
@@ -14,6 +14,14 @@
 LANES = 128
 SUBLANES = 8
 TOKEN = (8, 128)
+
+
+def in_hbm(*arrays):
+    return [pltpu.with_memory_space_constraint(array, pltpu.HBM) for array in arrays]
+
+
+def in_vmem(*arrays):
+    return [pltpu.with_memory_space_constraint(array, pltpu.VMEM) for array in arrays]
 
 
 def meridional_factors(truncation, latitudes, starts, width):
@@ -41,7 +49,7 @@
 
 def meridional_tables(truncation, latitudes, starts, width):
     factors = meridional_factors(truncation, latitudes, starts, width)
-    shape = jax.ShapeDtypeStruct((truncation, starts.shape[0] * width), jnp.bfloat16)
+    shape = pltpu.VMEM((truncation, starts.shape[0] * width), jnp.bfloat16)
     return pl.pallas_call(
         tables_kernel,
         out_shape=[shape, shape],
@@ -55,7 +63,7 @@
 
 
 def zonal_kernel(truncation, tokens, waves, velocity, tracer, *rest):
-    out, table, total, velocity_here, tracer_here, sems = rest[tokens:]
+    out, table, total, turned, velocity_here, tracer_here, sems, out_sems = rest[tokens:]
     members, fields, lat_local, longitudes = velocity.shape
     rows = waves.shape[0]
     groups = velocity_here.shape[0]
@@ -113,12 +121,27 @@
 
     lax.fori_loop(0, groups, body, 0)
 
+    tiles = rows // SUBLANES
+    batch = math.gcd(tiles, 4)
+
+    def leave(at):
+        part = pl.ds(pl.multiple_of(at * batch * SUBLANES, SUBLANES), batch * SUBLANES)
+        return pltpu.make_async_copy(turned.at[part], out.at[part], out_sems.at[at])
+
     def turn(at, carry):
-        first = pl.multiple_of(at * SUBLANES, SUBLANES)
-        out[pl.ds(first, SUBLANES)] = jnp.swapaxes(total[at], 0, 1).astype(out.dtype)
+        for tile in range(batch):
+            first = pl.multiple_of((at * batch + tile) * SUBLANES, SUBLANES)
+            tiles_here = jnp.swapaxes(total[at * batch + tile], 0, 1)
+            turned[pl.ds(first, SUBLANES)] = tiles_here.astype(out.dtype)
+        leave(at).start()
         return carry
 
-    lax.fori_loop(0, rows // SUBLANES, turn, 0)
+    def end(at, carry):
+        leave(at).wait()
+        return carry
+
+    lax.fori_loop(0, tiles // batch, turn, 0)
+    lax.fori_loop(0, tiles // batch, end, 0)
 
 
 def zonal_transform(waves, truncation, velocity, tracer, tokens):
@@ -134,19 +157,21 @@
         functools.partial(zonal_kernel, truncation, len(tokens)),
         in_specs=[pl.BlockSpec(memory_space=pltpu.VMEM)]
         + [pl.BlockSpec(memory_space=pl.ANY)] * (2 + len(tokens)),
-        out_specs=pl.BlockSpec(memory_space=pltpu.VMEM),
-        out_shape=jax.ShapeDtypeStruct((rows, out_rows, lat_local), jnp.bfloat16),
+        out_specs=pl.BlockSpec(memory_space=pl.ANY),
+        out_shape=pltpu.HBM((rows, out_rows, lat_local), jnp.bfloat16),
         scratch_shapes=[
             pltpu.VMEM((2 * rows, longitudes), jnp.bfloat16),
             pltpu.VMEM((rows // SUBLANES, out_rows, SUBLANES, lat_local), jnp.float32),
+            pltpu.VMEM((rows, out_rows, lat_local), jnp.bfloat16),
             grid_part,
             grid_part,
             pltpu.SemaphoreType.DMA((groups, 2)),
+            pltpu.SemaphoreType.DMA((rows // SUBLANES,)),
         ],
         compiler_params=pltpu.CompilerParams(vmem_limit_bytes=ZONAL_BYTES),
         cost_estimate=pl.CostEstimate(flops=flops, bytes_accessed=moved, transcendentals=0),
         name="zonal",
-    )(waves, velocity, tracer, *tokens)
+    )(waves, *in_hbm(velocity, tracer), *tokens)
 
 
 def forward_kernel(first, block, waves, received, even, odd, *rest):
@@ -193,7 +218,7 @@
             ],
         ),
         out_shape=[
-            jax.ShapeDtypeStruct(out_shape, jnp.bfloat16),
+            pltpu.HBM(out_shape, jnp.bfloat16),
             jax.ShapeDtypeStruct(TOKEN, jnp.float32),
         ],
         compiler_params=pltpu.CompilerParams(vmem_limit_bytes=VMEM_BYTES),
@@ -203,7 +228,7 @@
             transcendentals=0,
         ),
         name="forward",
-    )(waves[0], received, even, odd, *tokens)
+    )(waves[0], *in_hbm(received), *in_vmem(even, odd), *tokens)
 
 
 def inverse_kernel(first, block, waves, offsets, low, own, high, noise, even, odd, *rest):
@@ -257,13 +282,13 @@
     noise_block = pl.BlockSpec((block,) + noise.shape[1:], far)
     fourier_shape = noise.shape[:4] + (latitudes,)
     fourier_block = pl.BlockSpec((block,) + fourier_shape[1:], far)
-    operands = [low, own, high, noise, even, odd]
+    operands = [low, *in_hbm(own), high, *in_hbm(noise), *in_vmem(even, odd)]
     in_specs = [pl.BlockSpec((block,) + a.shape[1:], near) for a in operands[:3]]
     in_specs += [noise_block, table, table]
     aliases = {}
     if outs is not None:
         aliases = {8: 0, 9: 1}
-        operands += list(outs)
+        operands += in_hbm(*outs)
         in_specs += [pl.BlockSpec(memory_space=pl.ANY)] * 2
     rows = slots * mem_local * parts * fields
     return pl.pallas_call(
@@ -321,11 +346,11 @@
             + [pl.BlockSpec(memory_space=pl.ANY)] * len(tokens),
             out_specs=block(own),
         ),
-        out_shape=jax.ShapeDtypeStruct(own.shape, own.dtype),
+        out_shape=pltpu.HBM(own.shape, own.dtype),
         compiler_params=pltpu.CompilerParams(vmem_limit_bytes=VMEM_BYTES),
         cost_estimate=pl.CostEstimate(flops=0, bytes_accessed=8 * own.size, transcendentals=0),
         name="parents",
-    )(offsets, low, own, high, *tokens)
+    )(offsets, low, *in_hbm(own), high, *tokens)
 
 
 def finish_kernel(first, block, waves, received, noise, even, odd, *rest):
@@ -397,7 +422,7 @@
             transcendentals=0,
         ),
         name="finish",
-    )(waves, received, noise, even, odd, *outs)
+    )(waves, *in_hbm(received, noise), *in_vmem(even, odd), *in_hbm(*outs))
 
 
 def chunk_bounds(slots_here, block):

time: 174 us -> 168 us (0.966)
  local copies, waits for them, and re-layouts: 19.1 us -> 2.91 us
  Pallas kernels: 67.2 us -> 76 us
    unnamed x36 -> x4, local copies, waits for them, and re-layouts: 17 us -> 0.8 us
    pallas_call x3, Pallas kernels: 28.4 us -> 30.9 us  [zonal_transform(): pl.pallas_call(functools.partial(zonal_kernel, truncation, len(tokens)),...]
    all_to_all x3, waiting for transfers between devices: 8.46 us -> 6.1 us  [exchanged(): lax.all_to_all(outgoing, 'lat', split_axis=0, concat_axis=0, tiled=True)]
    pallas_call x2, Pallas kernels: 14.3 us -> 16.6 us  [finish_transform(): pl.pallas_call(functools.partial(finish_kernel, first, block), grid_spec=...]
    pallas_call x2, Pallas kernels: 7.3 us -> 9.59 us  [copy_parents(): pl.pallas_call(copy_kernel, grid_spec=pltpu.PrefetchScalarGridSpec(num_sc...]
  transfers between devices with their start and end apart: 9 -> 9, of which waited for: 6 -> 7; matrix products, arithmetic and copies ran while one was open for 2% -> 2% of each run, Pallas kernels for 31% -> 36%
where the time goes in v9:
time: 168 us; the launch traced here: 165 us
  Pallas kernels  76 us (45%)
  waiting for transfers between devices  48.3 us (29%)
  starting transfers between devices  34.3 us (20%)
  local copies, waits for them, and re-layouts  2.91 us (2%)
  other arithmetic  2.88 us (2%)
    ppermute x3, waiting for transfers between devices, neighbours(): lax.ppermute(rows[:, rows.shape[1] - SPREAD * per_member:], 'member', upw...  33.4 us
    pallas_call x3, Pallas kernels, zonal_transform(): pl.pallas_call(functools.partial(zonal_kernel, truncation, len(tokens)),...  30.9 us
    pallas_call x2, Pallas kernels, finish_transform(): pl.pallas_call(functools.partial(finish_kernel, first, block), grid_spec=...  16.6 us
    all_to_all x3, starting transfers between devices, exchanged(): lax.all_to_all(outgoing, 'lat', split_axis=0, concat_axis=0, tiled=True)  16.2 us
    ppermute x3, starting transfers between devices, neighbours(): lax.ppermute(rows[:, rows.shape[1] - SPREAD * per_member:], 'member', upw...  12.3 us
    pallas_call x2, Pallas kernels, copy_parents(): pl.pallas_call(copy_kernel, grid_spec=pltpu.PrefetchScalarGridSpec(num_sc...  9.59 us
    pallas_call x1, Pallas kernels, inverse_transform(): pl.pallas_call(functools.partial(inverse_kernel, first, block), grid_spec...  9.27 us
    ppermute x3, waiting for transfers between devices, neighbours(): high = lax.ppermute(rows[:, :SPREAD * per_member], 'member', downward)  8.8 us
  transfers between devices with their start and end apart: 9, of which 7 were waited for; matrix products, arithmetic and copies ran while one was open for 2% of the time, Pallas kernels for 36%

profile of v9, /device:TPU:1, one launch (start us, length us, event | category | flops | bytes accessed | tf_op | source)
XLA Modules:
  0.0 165.0 jit_solution(13494902520236937613)
XLA Ops:
  0.6 0.8 reshape.34
  1.4 0.1 fusion.13
  1.5 0.1 reshape.42.waves
  1.6 11.6 %zonal.4 = bf16[320,32,128]{2,1,0:T(8,128)(2,1)} custom-call(s32[320,1]{1,0:T(8,128)S(1)} %reshape.42.waves, bf16[2,8,128,2048]{3,2,1,0:T(8,128)(2,1)} %velocity.5, bf16[2,8,128,2048]{3,2,1,0:T(8,128)(2,1)} %tracer.5), custom_call_target="tpu_custom_call" | custom-call | flops 5368709120 | bytes 19398656 | tf_op jit(solution)/shard_map/zonal/pallas_call | solution.py:156
  13.2 6.4 %all-to-all-start = ((bf16[8,1280,128]{2,1,0:T(8,128)(2,1)}), bf16[8,1280,128]{2,1,0:T(8,128)(2,1)}, u32[]{:S(2)}, u32[]{:S(2)}) async-start(bf16[8,1280,128]{2,1,0:T(8,128)(2,1)} %bitcast.4), calls=%async_computation | async-start | bytes 5242880 | tf_op jit(solution)/shard_map/all_to_all | solution.py:469
  19.6 0.1 reshape.43.waves
  19.7 0.0 copy-start.1
  19.7 11.6 %zonal.5.own = bf16[320,32,128]{2,1,0:T(8,128)(2,1)} custom-call(s32[320,1]{1,0:T(8,128)S(1)} %reshape.43.waves, bf16[2,8,128,2048]{3,2,1,0:T(8,128)(2,1)} %velocity.5, bf16[2,8,128,2048]{3,2,1,0:T(8,128)(2,1)} %tracer.5), custom_call_target="tpu_custom_call" | custom-call | flops 5368709120 | bytes 19398656 | tf_op jit(solution)/shard_map/zonal/pallas_call | solution.py:156
  31.3 4.0 %collective-permute-start.4 = (bf16[320,32,128]{2,1,0:T(8,128)(2,1)}, bf16[320,32,128]{2,1,0:T(8,128)(2,1)S(1)}, u32[]{:S(2)}, u32[]{:S(2)}) collective-permute-start(bf16[320,32,128]{2,1,0:T(8,128)(2,1)} %zonal.5.own), channel_id=1, source_target_pairs={{0,8},{8,16},{16,24},{1,9},{9,17},{17,25},{2,10},{10,18},{18,26},{... | collective-permute-start | bytes 7864328 | tf_op jit(solution)/shard_map/ppermute | solution.py:463
  35.3 1.9 %collective-permute-start.5 = (bf16[320,32,128]{2,1,0:T(8,128)(2,1)}, bf16[320,32,128]{2,1,0:T(8,128)(2,1)}, u32[]{:S(2)}, u32[]{:S(2)}) collective-permute-start(bf16[320,32,128]{2,1,0:T(8,128)(2,1)} %zonal.5.own), channel_id=1, source_target_pairs={{8,0},{16,8},{24,16},{9,1},{17,9},{25,17},{10,2},{18,10},{26,18},{... | collective-permute-start | bytes 7864328 | tf_op jit(solution)/shard_map/ppermute | solution.py:464
  37.2 0.0 copy-done.1
  37.2 0.1 subtract_add_fusion.offsets
  37.3 26.9 %collective-permute-done.4.low = bf16[320,32,128]{2,1,0:T(8,128)(2,1)S(1)} collective-permute-done((bf16[320,32,128]{2,1,0:T(8,128)(2,1)}, bf16[320,32,128]{2,1,0:T(8,128)(2,1)S(1)}, u32[]{:S(2)}, u32[]{:S(2)}) %collective-permute-start.4) | collective-permute-done | bytes 2621472 | tf_op jit(solution)/shard_map/ppermute | solution.py:463
  64.1 4.4 %collective-permute-done.5.high = bf16[320,32,128]{2,1,0:T(8,128)(2,1)} collective-permute-done((bf16[320,32,128]{2,1,0:T(8,128)(2,1)}, bf16[320,32,128]{2,1,0:T(8,128)(2,1)}, u32[]{:S(2)}, u32[]{:S(2)}) %collective-permute-start.5) | collective-permute-done | bytes 2621472 | tf_op jit(solution)/shard_map/ppermute | solution.py:464
  68.5 5.7 %parents.3 = bf16[320,32,128]{2,1,0:T(8,128)(2,1)} custom-call(s32[2]{0:T(128)S(1)} %subtract_add_fusion.offsets, bf16[320,32,128]{2,1,0:T(8,128)(2,1)S(1)} %collective-permute-done.4.low, bf16[320,32,128]{2,1,0:T(8,128)(2,1)} %zonal.5.own, bf16[320,32,128]{2,1,0:T(8,128)(2,1)} %collective-permute-done.5.high), custom_call_target="tpu_custom_call" | custom-call | bytes 10485760 | tf_op jit(solution)/shard_map/parents/pallas_call | solution.py:340
  74.3 4.0 %all-to-all-done.received = bf16[8,1280,128]{2,1,0:T(8,128)(2,1)} async-done(((bf16[8,1280,128]{2,1,0:T(8,128)(2,1)}), bf16[8,1280,128]{2,1,0:T(8,128)(2,1)}, u32[]{:S(2)}, u32[]{:S(2)}) %all-to-all-start) | async-done | bytes 2621472 | tf_op jit(solution)/shard_map/all_to_all | solution.py:469
  78.3 4.7 %all-to-all-start.2 = ((bf16[8,1280,128]{2,1,0:T(8,128)(2,1)}), bf16[8,1280,128]{2,1,0:T(8,128)(2,1)}, u32[]{:S(2)}, u32[]{:S(2)}) async-start(bf16[8,1280,128]{2,1,0:T(8,128)(2,1)} %bitcast.3), calls=%async_computation.2 | async-start | bytes 5242880 | tf_op jit(solution)/shard_map/all_to_all | solution.py:469
  83.0 0.8 dynamic_slice.6.waves
  83.7 0.1 fusion.9
  83.8 0.2 copy.17
  84.0 1.4 fusion.6
  85.4 1.3 sine_multiply_fusion
  86.7 1.8 %tables.1 = (bf16[683,1024]{1,0:T(8,128)(2,1)S(1)}, bf16[683,1024]{1,0:T(8,128)(2,1)S(1)}) custom-call(f32[683,8]{1,0:T(8,128)S(1)} %get-tuple-element.19.cos_c, f32[683,8]{1,0:T(8,128)S(1)} %get-tuple-element.18.sin_c, f32[683,128]{1,0:T(8,128)S(1)} %get-tuple-element.23.cos_f, f32[683,128]{1,0:T(8,128)S(1)} %get-tuple-element.22.sin_f), custom_call_target="tpu_custom_call" | custom-call | flops 4196352 | bytes 2797568 | tf_op jit(solution)/shard_map/tables/pallas_call | solution.py:53
  88.5 7.8 %forward.1 = (bf16[40,2,16,683]{3,2,1,0:T(8,128)(2,1)}, f32[8,128]{1,0:T(8,128)}) custom-call(s32[88]{0:T(128)S(1)} %dynamic_slice.6.waves, bf16[8,1280,128]{2,1,0:T(8,128)(2,1)} %all-to-all-done.received, bf16[683,1024]{1,0:T(8,128)(2,1)S(1)} %get-tuple-element.10.even, bf16[683,1024]{1,0:T(8,128)(2,1)S(1)} %get-tuple-element.11.odd), custom_call_target="tpu_custom_call" | custom-call | flops 3580887040 | bytes 7167488 | tf_op jit(solution)/shard_map/forward/pallas_call | solution.py:204
  96.4 4.7 %collective-permute-start.2 = (bf16[40,2,16,683]{3,2,1,0:T(8,128)(2,1)}, bf16[40,2,16,683]{3,2,1,0:T(8,128)(2,1)}, u32[]{:S(2)}, u32[]{:S(2)}) collective-permute-start(bf16[40,2,16,683]{3,2,1,0:T(8,128)(2,1)} %get-tuple-element.12.own), channel_id=1, source_target_pairs={{0,8},{8,16},{16,24},{1,9},{9,17},{17,25},{2,10},{10,18},{18,26},{... | collective-permute-start | bytes 5245448 | tf_op jit(solution)/shard_map/ppermute | solution.py:463
  101.1 1.9 %collective-permute-start.3 = (bf16[40,2,16,683]{3,2,1,0:T(8,128)(2,1)}, bf16[40,2,16,683]{3,2,1,0:T(8,128)(2,1)}, u32[]{:S(2)}, u32[]{:S(2)}) collective-permute-start(bf16[40,2,16,683]{3,2,1,0:T(8,128)(2,1)} %get-tuple-element.12.own), channel_id=1, source_target_pairs={{8,0},{16,8},{24,16},{9,1},{17,9},{25,17},{10,2},{18,10},{26,18},{... | collective-permute-start | bytes 5245448 | tf_op jit(solution)/shard_map/ppermute | solution.py:464
  103.0 0.1 slice.9
  103.1 0.1 reshape.41.waves
  103.2 7.7 %zonal.3.own = bf16[64,32,128]{2,1,0:T(8,128)(2,1)} custom-call(s32[64,1]{1,0:T(8,128)S(1)} %reshape.41.waves, bf16[2,8,128,2048]{3,2,1,0:T(8,128)(2,1)} %velocity.5, bf16[2,8,128,2048]{3,2,1,0:T(8,128)(2,1)} %tracer.5), custom_call_target="tpu_custom_call" | custom-call | flops 1073741824 | bytes 17301504 | tf_op jit(solution)/shard_map/zonal/pallas_call | solution.py:156
  110.9 3.6 %collective-permute-start = (bf16[64,32,128]{2,1,0:T(8,128)(2,1)}, bf16[64,32,128]{2,1,0:T(8,128)(2,1)S(1)}, u32[]{:S(2)}, u32[]{:S(2)}) collective-permute-start(bf16[64,32,128]{2,1,0:T(8,128)(2,1)} %zonal.3.own), channel_id=1, source_target_pairs={{0,8},{8,16},{16,24},{1,9},{9,17},{17,25},{2,10},{10,18},{18,26},{... | collective-permute-start | bytes 1572872 | tf_op jit(solution)/shard_map/ppermute | solution.py:463
  114.5 1.9 %collective-permute-start.1 = (bf16[64,32,128]{2,1,0:T(8,128)(2,1)}, bf16[64,32,128]{2,1,0:T(8,128)(2,1)S(1)}, u32[]{:S(2)}, u32[]{:S(2)}) collective-permute-start(bf16[64,32,128]{2,1,0:T(8,128)(2,1)} %zonal.3.own), channel_id=1, source_target_pairs={{8,0},{16,8},{24,16},{9,1},{17,9},{25,17},{10,2},{18,10},{26,18},{... | collective-permute-start | bytes 1572872 | tf_op jit(solution)/shard_map/ppermute | solution.py:464
  116.5 6.5 %collective-permute-done.2.low = bf16[40,2,16,683]{3,2,1,0:T(8,128)(2,1)} collective-permute-done((bf16[40,2,16,683]{3,2,1,0:T(8,128)(2,1)}, bf16[40,2,16,683]{3,2,1,0:T(8,128)(2,1)}, u32[]{:S(2)}, u32[]{:S(2)}) %collective-permute-start.2) | collective-permute-done | bytes 1748512 | tf_op jit(solution)/shard_map/ppermute | solution.py:463
  123.0 4.4 %collective-permute-done.3.high = bf16[40,2,16,683]{3,2,1,0:T(8,128)(2,1)} collective-permute-done((bf16[40,2,16,683]{3,2,1,0:T(8,128)(2,1)}, bf16[40,2,16,683]{3,2,1,0:T(8,128)(2,1)}, u32[]{:S(2)}, u32[]{:S(2)}) %collective-permute-start.3) | collective-permute-done | bytes 1748512 | tf_op jit(solution)/shard_map/ppermute | solution.py:464
  127.4 9.3 %inverse.1 = (bf16[88,2,2,8,683]{4,3,2,1,0:T(8,128)(2,1)}, bf16[88,2,2,8,1024]{4,3,2,1,0:T(8,128)(2,1)}, f32[8,128]{1,0:T(8,128)S(1)}) custom-call(s32[88]{0:T(128)S(1)} %dynamic_slice.6.waves, s32[2]{0:T(128)S(1)} %subtract_add_fusion.offsets, bf16[40,2,16,683]{3,2,1,0:T(8,128)(2,1)} %collective-permute-done.2.low, ...), custom_call_target="tpu_custom_call" | custom-call | flops 3580887040 | bytes 14161408 | tf_op jit(solution)/shard_map/inverse/pallas_call | solution.py:294
  136.6 0.0 collective-permute-done.low
  136.6 0.0 collective-permute-done.1.high
  136.6 3.9 %parents.2 = bf16[64,32,128]{2,1,0:T(8,128)(2,1)} custom-call(s32[2]{0:T(128)S(1)} %subtract_add_fusion.offsets, bf16[64,32,128]{2,1,0:T(8,128)(2,1)S(1)} %collective-permute-done.low, bf16[64,32,128]{2,1,0:T(8,128)(2,1)} %zonal.3.own, bf16[64,32,128]{2,1,0:T(8,128)(2,1)S(1)} %collective-permute-done.1.high, f32[8,128]{1,0:T(8,128)S(1)} %get-tuple-element.13.rest_0_), custom_call_target="tpu_custom_call" | custom-call | bytes 2097152 | tf_op jit(solution)/shard_map/parents/pallas_call | solution.py:340
  140.5 0.8 all-to-all-done.2.received
  141.3 5.1 %all-to-all-start.1 = ((bf16[8,256,128]{2,1,0:T(8,128)(2,1)}), bf16[8,256,128]{2,1,0:T(8,128)(2,1)S(1)}, u32[]{:S(2)}, u32[]{:S(2)}) async-start(bf16[8,256,128]{2,1,0:T(8,128)(2,1)} %bitcast.5), calls=%async_computation.1 | async-start | bytes 1048576 | tf_op jit(solution)/shard_map/all_to_all | solution.py:469
  146.4 12.2 %finish.2 = (bf16[88,2,2,8,683]{4,3,2,1,0:T(8,128)(2,1)}, bf16[88,2,2,8,1024]{4,3,2,1,0:T(8,128)(2,1)}) custom-call(s32[88]{0:T(128)S(1)} %dynamic_slice.6.waves, bf16[8,1280,128]{2,1,0:T(8,128)(2,1)} %all-to-all-done.2.received, bf16[88,2,2,8,683]{4,3,2,1,0:T(8,128)(2,1)} %noise.5, ...), custom_call_target="tpu_custom_call", output_to_operand_aliasing={{0}: (5, {}), {1}: (6, {})} | custom-call | flops 7161774080 | bytes 11537408 | tf_op jit(solution)/shard_map/finish/pallas_call | solution.py:404
  158.6 1.3 all-to-all-done.1.received
  159.9 0.0 copy-start
  159.9 0.8 copy-done
  160.6 4.4 %finish.3 = (bf16[88,2,2,8,683]{4,3,2,1,0:T(8,128)(2,1)}, bf16[88,2,2,8,1024]{4,3,2,1,0:T(8,128)(2,1)}) custom-call(s32[88]{0:T(128)S(1)} %dynamic_slice.6.waves, bf16[8,256,128]{2,1,0:T(8,128)(2,1)} %copy-done, bf16[88,2,2,8,683]{4,3,2,1,0:T(8,128)(2,1)} %noise.5, ...), custom_call_target="tpu_custom_call", output_to_operand_aliasing={{0}: (5, {}), {1}: (6, {})} | custom-call | flops 1432354816 | bytes 4545536 | tf_op jit(solution)/shard_map/finish/pallas_call | solution.py:404
  (2 shorter events, 0.0 us)
Async XLA Ops:
  13.2 65.1 %all-to-all-start = ((bf16[8,1280,128]{2,1,0:T(8,128)(2,1)}), bf16[8,1280,128]{2,1,0:T(8,128)(2,1)}, u32[]{:S(2)}, u32[]{:S(2)}) async-start(bf16[8,1280,128]{2,1,0:T(8,128)(2,1)} %bitcast.4), calls=%async_computation | async-start | bytes 5242880 | tf_op jit(solution)/shard_map/all_to_all | solution.py:469
  19.7 17.5 %copy-start.1 = (s32[8]{0:T(128)S(1)}, s32[8]{0:T(128)}, u32[]{:S(2)}) copy-start(s32[8]{0:T(128)} %param.8) | copy-start | bytes 100
  31.3 32.9 %collective-permute-start.4 = (bf16[320,32,128]{2,1,0:T(8,128)(2,1)}, bf16[320,32,128]{2,1,0:T(8,128)(2,1)S(1)}, u32[]{:S(2)}, u32[]{:S(2)}) collective-permute-start(bf16[320,32,128]{2,1,0:T(8,128)(2,1)} %zonal.5.own), channel_id=1, source_target_pairs={{0,8},{8,16},{16,24},{1,9},{9,17},{17,25},{2,10},{10,18},{18,26},{... | collective-permute-start | bytes 7864328 | tf_op jit(solution)/shard_map/ppermute | solution.py:463
  35.3 33.3 %collective-permute-start.5 = (bf16[320,32,128]{2,1,0:T(8,128)(2,1)}, bf16[320,32,128]{2,1,0:T(8,128)(2,1)}, u32[]{:S(2)}, u32[]{:S(2)}) collective-permute-start(bf16[320,32,128]{2,1,0:T(8,128)(2,1)} %zonal.5.own), channel_id=1, source_target_pairs={{8,0},{16,8},{24,16},{9,1},{17,9},{25,17},{10,2},{18,10},{26,18},{... | collective-permute-start | bytes 7864328 | tf_op jit(solution)/shard_map/ppermute | solution.py:464
  78.3 63.0 %all-to-all-start.2 = ((bf16[8,1280,128]{2,1,0:T(8,128)(2,1)}), bf16[8,1280,128]{2,1,0:T(8,128)(2,1)}, u32[]{:S(2)}, u32[]{:S(2)}) async-start(bf16[8,1280,128]{2,1,0:T(8,128)(2,1)} %bitcast.3), calls=%async_computation.2 | async-start | bytes 5242880 | tf_op jit(solution)/shard_map/all_to_all | solution.py:469
  96.4 26.6 %collective-permute-start.2 = (bf16[40,2,16,683]{3,2,1,0:T(8,128)(2,1)}, bf16[40,2,16,683]{3,2,1,0:T(8,128)(2,1)}, u32[]{:S(2)}, u32[]{:S(2)}) collective-permute-start(bf16[40,2,16,683]{3,2,1,0:T(8,128)(2,1)} %get-tuple-element.12.own), channel_id=1, source_target_pairs={{0,8},{8,16},{16,24},{1,9},{9,17},{17,25},{2,10},{10,18},{18,26},{... | collective-permute-start | bytes 5245448 | tf_op jit(solution)/shard_map/ppermute | solution.py:463
  101.1 26.3 %collective-permute-start.3 = (bf16[40,2,16,683]{3,2,1,0:T(8,128)(2,1)}, bf16[40,2,16,683]{3,2,1,0:T(8,128)(2,1)}, u32[]{:S(2)}, u32[]{:S(2)}) collective-permute-start(bf16[40,2,16,683]{3,2,1,0:T(8,128)(2,1)} %get-tuple-element.12.own), channel_id=1, source_target_pairs={{8,0},{16,8},{24,16},{9,1},{17,9},{25,17},{10,2},{18,10},{26,18},{... | collective-permute-start | bytes 5245448 | tf_op jit(solution)/shard_map/ppermute | solution.py:464
  110.9 25.7 %collective-permute-start = (bf16[64,32,128]{2,1,0:T(8,128)(2,1)}, bf16[64,32,128]{2,1,0:T(8,128)(2,1)S(1)}, u32[]{:S(2)}, u32[]{:S(2)}) collective-permute-start(bf16[64,32,128]{2,1,0:T(8,128)(2,1)} %zonal.3.own), channel_id=1, source_target_pairs={{0,8},{8,16},{16,24},{1,9},{9,17},{17,25},{2,10},{10,18},{18,26},{... | collective-permute-start | bytes 1572872 | tf_op jit(solution)/shard_map/ppermute | solution.py:463
  114.5 22.1 %collective-permute-start.1 = (bf16[64,32,128]{2,1,0:T(8,128)(2,1)}, bf16[64,32,128]{2,1,0:T(8,128)(2,1)S(1)}, u32[]{:S(2)}, u32[]{:S(2)}) collective-permute-start(bf16[64,32,128]{2,1,0:T(8,128)(2,1)} %zonal.3.own), channel_id=1, source_target_pairs={{8,0},{16,8},{24,16},{9,1},{17,9},{25,17},{10,2},{18,10},{26,18},{... | collective-permute-start | bytes 1572872 | tf_op jit(solution)/shard_map/ppermute | solution.py:464
  141.3 18.6 %all-to-all-start.1 = ((bf16[8,256,128]{2,1,0:T(8,128)(2,1)}), bf16[8,256,128]{2,1,0:T(8,128)(2,1)S(1)}, u32[]{:S(2)}, u32[]{:S(2)}) async-start(bf16[8,256,128]{2,1,0:T(8,128)(2,1)} %bitcast.5), calls=%async_computation.1 | async-start | bytes 1048576 | tf_op jit(solution)/shard_map/all_to_all | solution.py:469
  159.9 0.8 copy-start

commit v10 on v9

--- a/solution.py
+++ b/solution.py
@@ -353,11 +353,9 @@
     )(offsets, low, *in_hbm(own), high, *tokens)
 
 
-def finish_kernel(first, block, waves, received, noise, even, odd, *rest):
-    spectra_out, fourier_out = rest[-2:]
+def finish_block(first, waves, received, noise, even, odd, spectra_out, fourier_out, ready, store):
     truncation = even.shape[0]
-    mem_local, parts, fields = noise.shape[1:4]
-    step = pl.program_id(0)
+    block, mem_local, parts, fields = noise.shape[:4]
     per_slot = received.shape[1] // block
     rows = jnp.concatenate([received[g] for g in range(received.shape[0])], axis=-1)
     contract = (((1,), (1,)), ((), ()))
@@ -365,8 +363,9 @@
     by_odd = lax.dot_general(rows, odd[...], contract, preferred_element_type=jnp.float32)
     degree = lax.broadcasted_iota(jnp.int32, (per_slot, truncation), 1)
     even_rows, odd_rows = [], []
+    ready()
     for slot in range(block):
-        wave = waves[first + step * block + slot]
+        wave = waves[first + slot]
         least = jnp.where(wave < truncation, wave, truncation)
         is_odd = wave % 2 == 1
         active = degree >= least
@@ -378,6 +377,7 @@
         spectra_out[slot] = child.reshape(noise.shape[1:]).astype(spectra_out.dtype)
         even_rows.append(jnp.where(is_odd, 0.0, child).astype(jnp.bfloat16))
         odd_rows.append(jnp.where(is_odd, child, 0.0).astype(jnp.bfloat16))
+    store()
     result = jnp.dot(
         jnp.concatenate(even_rows, axis=0), even[...], preferred_element_type=jnp.float32
     )
@@ -385,6 +385,70 @@
         jnp.concatenate(odd_rows, axis=0), odd[...], preferred_element_type=jnp.float32
     )
     fourier_out[...] = result.reshape(fourier_out.shape).astype(fourier_out.dtype)
+
+
+def finish_kernel(first, block, waves, received, noise, even, odd, *rest):
+    start = first + pl.program_id(0) * block
+    nothing = lambda: None
+    finish_block(start, waves, received, noise, even, odd, *rest[-2:], nothing, nothing)
+
+
+def last_kernel(first, waves, received, noise, even, odd, *rest):
+    spectra_out, fourier_out, noise_here, spectra_here, fourier_here, sems = rest[-6:]
+    part = pl.ds(first, noise_here.shape[0])
+    fetch = pltpu.make_async_copy(noise.at[part], noise_here, sems.at[0])
+    leave = pltpu.make_async_copy(spectra_here, spectra_out.at[part], sems.at[1])
+    leave_too = pltpu.make_async_copy(fourier_here, fourier_out.at[part], sems.at[2])
+    fetch.start()
+    finish_block(
+        first,
+        waves,
+        received,
+        noise_here,
+        even,
+        odd,
+        spectra_here,
+        fourier_here,
+        fetch.wait,
+        leave.start,
+    )
+    leave_too.start()
+    leave.wait()
+    leave_too.wait()
+
+
+def last_transform(waves, first, received, noise, even, odd, outs):
+    slots_all, mem_local, parts, fields, truncation = noise.shape
+    latitudes = even.shape[1]
+    all_rows = received.shape[1]
+    block = all_rows // (mem_local * parts * fields)
+    fourier_shape = noise.shape[:4] + (latitudes,)
+    here = pl.BlockSpec(memory_space=pltpu.VMEM)
+    anywhere = pl.BlockSpec(memory_space=pl.ANY)
+    return pl.pallas_call(
+        functools.partial(last_kernel, first),
+        in_specs=[pl.BlockSpec(memory_space=pltpu.SMEM), here, anywhere, here, here]
+        + [anywhere] * 2,
+        out_specs=[anywhere, anywhere],
+        out_shape=[
+            jax.ShapeDtypeStruct(noise.shape, jnp.bfloat16),
+            jax.ShapeDtypeStruct(fourier_shape, jnp.bfloat16),
+        ],
+        scratch_shapes=[
+            pltpu.VMEM((block,) + noise.shape[1:], jnp.bfloat16),
+            pltpu.VMEM((block,) + noise.shape[1:], jnp.bfloat16),
+            pltpu.VMEM((block,) + fourier_shape[1:], jnp.bfloat16),
+            pltpu.SemaphoreType.DMA((3,)),
+        ],
+        input_output_aliases={5: 0, 6: 1},
+        compiler_params=pltpu.CompilerParams(vmem_limit_bytes=VMEM_BYTES),
+        cost_estimate=pl.CostEstimate(
+            flops=8 * all_rows * truncation * latitudes,
+            bytes_accessed=2 * all_rows * (2 * truncation + 2 * latitudes) + 4 * even.size,
+            transcendentals=0,
+        ),
+        name="last",
+    )(waves, received, *in_hbm(noise), *in_vmem(even, odd), *in_hbm(*outs))
 
 
 def finish_transform(waves, first, block, received, noise, even, odd, outs):
@@ -484,8 +548,11 @@
         own_waves, offsets, 0, block, *neighbours(spectra, 1), noise, even, odd, None
     )
     later += [exchanged(copied(at, [token])) for at in range(2, len(bounds))]
-    for (start, _), received in zip(bounds[1:], later):
-        outs = finish_transform(own_waves, start, block, received, noise, even, odd, outs)
+    for (start, stop), received in zip(bounds[1:], later):
+        if stop - start == block:
+            outs = last_transform(own_waves, start, received, noise, even, odd, outs)
+        else:
+            outs = finish_transform(own_waves, start, block, received, noise, even, odd, outs)
     return tuple(outs)
 
 

time: 168 us -> 166 us (0.988)
    pallas_call x2 -> x1, Pallas kernels: 16.6 us -> 12.2 us  [finish_transform(): pl.pallas_call(functools.partial(finish_kernel, first, block), grid_spec=...]
    pallas_call x0 -> x1, Pallas kernels: none -> 3.41 us  [last_transform(): pl.pallas_call(functools.partial(last_kernel, first), in_specs=[pl.BlockS...]
  transfers between devices with their start and end apart: 9 -> 9, of which waited for: 7 -> 7; matrix products, arithmetic and copies ran while one was open for 2% -> 2% of each run, Pallas kernels for 36% -> 37%
where the time goes in v10:
time: 166 us; the launch traced here: 163 us
  Pallas kernels  75 us (45%)
  waiting for transfers between devices  48.3 us (29%)
  starting transfers between devices  34.3 us (21%)
  other arithmetic  2.88 us (2%)
  local copies, waits for them, and re-layouts  2.12 us (1%)
    ppermute x3, waiting for transfers between devices, neighbours(): lax.ppermute(rows[:, rows.shape[1] - SPREAD * per_member:], 'member', upw...  33.4 us
    pallas_call x3, Pallas kernels, zonal_transform(): pl.pallas_call(functools.partial(zonal_kernel, truncation, len(tokens)),...  30.9 us
    all_to_all x3, starting transfers between devices, exchanged(): lax.all_to_all(outgoing, 'lat', split_axis=0, concat_axis=0, tiled=True)  16.2 us
    ppermute x3, starting transfers between devices, neighbours(): lax.ppermute(rows[:, rows.shape[1] - SPREAD * per_member:], 'member', upw...  12.3 us
    pallas_call x1, Pallas kernels, finish_transform(): pl.pallas_call(functools.partial(finish_kernel, first, block), grid_spec=...  12.2 us
    pallas_call x2, Pallas kernels, copy_parents(): pl.pallas_call(copy_kernel, grid_spec=pltpu.PrefetchScalarGridSpec(num_sc...  9.59 us
    pallas_call x1, Pallas kernels, inverse_transform(): pl.pallas_call(functools.partial(inverse_kernel, first, block), grid_spec...  9.27 us
    ppermute x3, waiting for transfers between devices, neighbours(): high = lax.ppermute(rows[:, :SPREAD * per_member], 'member', downward)  8.8 us
  transfers between devices with their start and end apart: 9, of which 7 were waited for; matrix products, arithmetic and copies ran while one was open for 2% of the time, Pallas kernels for 37%

profile of v10, /device:TPU:1, one launch (start us, length us, event | category | flops | bytes accessed | tf_op | source)
XLA Modules:
  0.0 163.4 jit_solution(1377807716288064323)
XLA Ops:
  0.6 0.8 reshape.34
  1.4 0.1 fusion.13
  1.5 0.1 reshape.42.waves
  1.6 11.6 %zonal.4 = bf16[320,32,128]{2,1,0:T(8,128)(2,1)} custom-call(s32[320,1]{1,0:T(8,128)S(1)} %reshape.42.waves, bf16[2,8,128,2048]{3,2,1,0:T(8,128)(2,1)} %velocity.5, bf16[2,8,128,2048]{3,2,1,0:T(8,128)(2,1)} %tracer.5), custom_call_target="tpu_custom_call" | custom-call | flops 5368709120 | bytes 19398656 | tf_op jit(solution)/shard_map/zonal/pallas_call | solution.py:156
  13.2 6.4 %all-to-all-start = ((bf16[8,1280,128]{2,1,0:T(8,128)(2,1)}), bf16[8,1280,128]{2,1,0:T(8,128)(2,1)}, u32[]{:S(2)}, u32[]{:S(2)}) async-start(bf16[8,1280,128]{2,1,0:T(8,128)(2,1)} %bitcast.4), calls=%async_computation | async-start | bytes 5242880 | tf_op jit(solution)/shard_map/all_to_all | solution.py:533
  19.6 0.1 reshape.43.waves
  19.7 0.0 copy-start
  19.7 11.6 %zonal.5.own = bf16[320,32,128]{2,1,0:T(8,128)(2,1)} custom-call(s32[320,1]{1,0:T(8,128)S(1)} %reshape.43.waves, bf16[2,8,128,2048]{3,2,1,0:T(8,128)(2,1)} %velocity.5, bf16[2,8,128,2048]{3,2,1,0:T(8,128)(2,1)} %tracer.5), custom_call_target="tpu_custom_call" | custom-call | flops 5368709120 | bytes 19398656 | tf_op jit(solution)/shard_map/zonal/pallas_call | solution.py:156
  31.3 4.0 %collective-permute-start.4 = (bf16[320,32,128]{2,1,0:T(8,128)(2,1)}, bf16[320,32,128]{2,1,0:T(8,128)(2,1)S(1)}, u32[]{:S(2)}, u32[]{:S(2)}) collective-permute-start(bf16[320,32,128]{2,1,0:T(8,128)(2,1)} %zonal.5.own), channel_id=1, source_target_pairs={{0,8},{8,16},{16,24},{1,9},{9,17},{17,25},{2,10},{10,18},{18,26},{... | collective-permute-start | bytes 7864328 | tf_op jit(solution)/shard_map/ppermute | solution.py:527
  35.3 1.9 %collective-permute-start.5 = (bf16[320,32,128]{2,1,0:T(8,128)(2,1)}, bf16[320,32,128]{2,1,0:T(8,128)(2,1)}, u32[]{:S(2)}, u32[]{:S(2)}) collective-permute-start(bf16[320,32,128]{2,1,0:T(8,128)(2,1)} %zonal.5.own), channel_id=1, source_target_pairs={{8,0},{16,8},{24,16},{9,1},{17,9},{25,17},{10,2},{18,10},{26,18},{... | collective-permute-start | bytes 7864328 | tf_op jit(solution)/shard_map/ppermute | solution.py:528
  37.2 0.0 copy-done
  37.2 0.1 subtract_add_fusion.offsets
  37.3 26.9 %collective-permute-done.4.low = bf16[320,32,128]{2,1,0:T(8,128)(2,1)S(1)} collective-permute-done((bf16[320,32,128]{2,1,0:T(8,128)(2,1)}, bf16[320,32,128]{2,1,0:T(8,128)(2,1)S(1)}, u32[]{:S(2)}, u32[]{:S(2)}) %collective-permute-start.4) | collective-permute-done | bytes 2621472 | tf_op jit(solution)/shard_map/ppermute | solution.py:527
  64.1 4.4 %collective-permute-done.5.high = bf16[320,32,128]{2,1,0:T(8,128)(2,1)} collective-permute-done((bf16[320,32,128]{2,1,0:T(8,128)(2,1)}, bf16[320,32,128]{2,1,0:T(8,128)(2,1)}, u32[]{:S(2)}, u32[]{:S(2)}) %collective-permute-start.5) | collective-permute-done | bytes 2621472 | tf_op jit(solution)/shard_map/ppermute | solution.py:528
  68.5 5.7 %parents.3 = bf16[320,32,128]{2,1,0:T(8,128)(2,1)} custom-call(s32[2]{0:T(128)S(1)} %subtract_add_fusion.offsets, bf16[320,32,128]{2,1,0:T(8,128)(2,1)S(1)} %collective-permute-done.4.low, bf16[320,32,128]{2,1,0:T(8,128)(2,1)} %zonal.5.own, bf16[320,32,128]{2,1,0:T(8,128)(2,1)} %collective-permute-done.5.high), custom_call_target="tpu_custom_call" | custom-call | bytes 10485760 | tf_op jit(solution)/shard_map/parents/pallas_call | solution.py:340
  74.3 4.0 %all-to-all-done.received = bf16[8,1280,128]{2,1,0:T(8,128)(2,1)} async-done(((bf16[8,1280,128]{2,1,0:T(8,128)(2,1)}), bf16[8,1280,128]{2,1,0:T(8,128)(2,1)}, u32[]{:S(2)}, u32[]{:S(2)}) %all-to-all-start) | async-done | bytes 2621472 | tf_op jit(solution)/shard_map/all_to_all | solution.py:533
  78.3 4.7 %all-to-all-start.2 = ((bf16[8,1280,128]{2,1,0:T(8,128)(2,1)}), bf16[8,1280,128]{2,1,0:T(8,128)(2,1)}, u32[]{:S(2)}, u32[]{:S(2)}) async-start(bf16[8,1280,128]{2,1,0:T(8,128)(2,1)} %bitcast.3), calls=%async_computation.2 | async-start | bytes 5242880 | tf_op jit(solution)/shard_map/all_to_all | solution.py:533
  83.0 0.8 dynamic_slice.6.waves
  83.7 0.1 fusion.9
  83.8 0.2 copy.17
  84.0 1.4 fusion.6
  85.4 1.3 sine_multiply_fusion
  86.7 1.8 %tables.1 = (bf16[683,1024]{1,0:T(8,128)(2,1)S(1)}, bf16[683,1024]{1,0:T(8,128)(2,1)S(1)}) custom-call(f32[683,8]{1,0:T(8,128)S(1)} %get-tuple-element.19.cos_c, f32[683,8]{1,0:T(8,128)S(1)} %get-tuple-element.18.sin_c, f32[683,128]{1,0:T(8,128)S(1)} %get-tuple-element.23.cos_f, f32[683,128]{1,0:T(8,128)S(1)} %get-tuple-element.22.sin_f), custom_call_target="tpu_custom_call" | custom-call | flops 4196352 | bytes 2797568 | tf_op jit(solution)/shard_map/tables/pallas_call | solution.py:53
  88.5 7.8 %forward.1 = (bf16[40,2,16,683]{3,2,1,0:T(8,128)(2,1)}, f32[8,128]{1,0:T(8,128)}) custom-call(s32[88]{0:T(128)S(1)} %dynamic_slice.6.waves, bf16[8,1280,128]{2,1,0:T(8,128)(2,1)} %all-to-all-done.received, bf16[683,1024]{1,0:T(8,128)(2,1)S(1)} %get-tuple-element.10.even, bf16[683,1024]{1,0:T(8,128)(2,1)S(1)} %get-tuple-element.11.odd), custom_call_target="tpu_custom_call" | custom-call | flops 3580887040 | bytes 7167488 | tf_op jit(solution)/shard_map/forward/pallas_call | solution.py:204
  96.3 4.7 %collective-permute-start.2 = (bf16[40,2,16,683]{3,2,1,0:T(8,128)(2,1)}, bf16[40,2,16,683]{3,2,1,0:T(8,128)(2,1)}, u32[]{:S(2)}, u32[]{:S(2)}) collective-permute-start(bf16[40,2,16,683]{3,2,1,0:T(8,128)(2,1)} %get-tuple-element.12.own), channel_id=1, source_target_pairs={{0,8},{8,16},{16,24},{1,9},{9,17},{17,25},{2,10},{10,18},{18,26},{... | collective-permute-start | bytes 5245448 | tf_op jit(solution)/shard_map/ppermute | solution.py:527
  101.1 1.9 %collective-permute-start.3 = (bf16[40,2,16,683]{3,2,1,0:T(8,128)(2,1)}, bf16[40,2,16,683]{3,2,1,0:T(8,128)(2,1)}, u32[]{:S(2)}, u32[]{:S(2)}) collective-permute-start(bf16[40,2,16,683]{3,2,1,0:T(8,128)(2,1)} %get-tuple-element.12.own), channel_id=1, source_target_pairs={{8,0},{16,8},{24,16},{9,1},{17,9},{25,17},{10,2},{18,10},{26,18},{... | collective-permute-start | bytes 5245448 | tf_op jit(solution)/shard_map/ppermute | solution.py:528
  103.0 0.1 slice.9
  103.1 0.1 reshape.41.waves
  103.2 7.7 %zonal.3.own = bf16[64,32,128]{2,1,0:T(8,128)(2,1)} custom-call(s32[64,1]{1,0:T(8,128)S(1)} %reshape.41.waves, bf16[2,8,128,2048]{3,2,1,0:T(8,128)(2,1)} %velocity.5, bf16[2,8,128,2048]{3,2,1,0:T(8,128)(2,1)} %tracer.5), custom_call_target="tpu_custom_call" | custom-call | flops 1073741824 | bytes 17301504 | tf_op jit(solution)/shard_map/zonal/pallas_call | solution.py:156
  110.9 3.6 %collective-permute-start = (bf16[64,32,128]{2,1,0:T(8,128)(2,1)}, bf16[64,32,128]{2,1,0:T(8,128)(2,1)S(1)}, u32[]{:S(2)}, u32[]{:S(2)}) collective-permute-start(bf16[64,32,128]{2,1,0:T(8,128)(2,1)} %zonal.3.own), channel_id=1, source_target_pairs={{0,8},{8,16},{16,24},{1,9},{9,17},{17,25},{2,10},{10,18},{18,26},{... | collective-permute-start | bytes 1572872 | tf_op jit(solution)/shard_map/ppermute | solution.py:527
  114.5 1.9 %collective-permute-start.1 = (bf16[64,32,128]{2,1,0:T(8,128)(2,1)}, bf16[64,32,128]{2,1,0:T(8,128)(2,1)S(1)}, u32[]{:S(2)}, u32[]{:S(2)}) collective-permute-start(bf16[64,32,128]{2,1,0:T(8,128)(2,1)} %zonal.3.own), channel_id=1, source_target_pairs={{8,0},{16,8},{24,16},{9,1},{17,9},{25,17},{10,2},{18,10},{26,18},{... | collective-permute-start | bytes 1572872 | tf_op jit(solution)/shard_map/ppermute | solution.py:528
  116.5 6.5 %collective-permute-done.2.low = bf16[40,2,16,683]{3,2,1,0:T(8,128)(2,1)} collective-permute-done((bf16[40,2,16,683]{3,2,1,0:T(8,128)(2,1)}, bf16[40,2,16,683]{3,2,1,0:T(8,128)(2,1)}, u32[]{:S(2)}, u32[]{:S(2)}) %collective-permute-start.2) | collective-permute-done | bytes 1748512 | tf_op jit(solution)/shard_map/ppermute | solution.py:527
  122.9 4.4 %collective-permute-done.3.high = bf16[40,2,16,683]{3,2,1,0:T(8,128)(2,1)} collective-permute-done((bf16[40,2,16,683]{3,2,1,0:T(8,128)(2,1)}, bf16[40,2,16,683]{3,2,1,0:T(8,128)(2,1)}, u32[]{:S(2)}, u32[]{:S(2)}) %collective-permute-start.3) | collective-permute-done | bytes 1748512 | tf_op jit(solution)/shard_map/ppermute | solution.py:528
  127.3 9.3 %inverse.1 = (bf16[88,2,2,8,683]{4,3,2,1,0:T(8,128)(2,1)}, bf16[88,2,2,8,1024]{4,3,2,1,0:T(8,128)(2,1)}, f32[8,128]{1,0:T(8,128)S(1)}) custom-call(s32[88]{0:T(128)S(1)} %dynamic_slice.6.waves, s32[2]{0:T(128)S(1)} %subtract_add_fusion.offsets, bf16[40,2,16,683]{3,2,1,0:T(8,128)(2,1)} %collective-permute-done.2.low, ...), custom_call_target="tpu_custom_call" | custom-call | flops 3580887040 | bytes 14161408 | tf_op jit(solution)/shard_map/inverse/pallas_call | solution.py:294
  136.6 0.0 collective-permute-done.low
  136.6 0.0 collective-permute-done.1.high
  136.6 3.9 %parents.2 = bf16[64,32,128]{2,1,0:T(8,128)(2,1)} custom-call(s32[2]{0:T(128)S(1)} %subtract_add_fusion.offsets, bf16[64,32,128]{2,1,0:T(8,128)(2,1)S(1)} %collective-permute-done.low, bf16[64,32,128]{2,1,0:T(8,128)(2,1)} %zonal.3.own, bf16[64,32,128]{2,1,0:T(8,128)(2,1)S(1)} %collective-permute-done.1.high, f32[8,128]{1,0:T(8,128)S(1)} %get-tuple-element.13.rest_0_), custom_call_target="tpu_custom_call" | custom-call | bytes 2097152 | tf_op jit(solution)/shard_map/parents/pallas_call | solution.py:340
  140.5 0.8 all-to-all-done.2.received
  141.3 5.1 %all-to-all-start.1 = ((bf16[8,256,128]{2,1,0:T(8,128)(2,1)}), bf16[8,256,128]{2,1,0:T(8,128)(2,1)S(1)}, u32[]{:S(2)}, u32[]{:S(2)}) async-start(bf16[8,256,128]{2,1,0:T(8,128)(2,1)} %bitcast.5), calls=%async_computation.1 | async-start | bytes 1048576 | tf_op jit(solution)/shard_map/all_to_all | solution.py:533
  146.4 12.2 %finish.1 = (bf16[88,2,2,8,683]{4,3,2,1,0:T(8,128)(2,1)}, bf16[88,2,2,8,1024]{4,3,2,1,0:T(8,128)(2,1)}) custom-call(s32[88]{0:T(128)S(1)} %dynamic_slice.6.waves, bf16[8,1280,128]{2,1,0:T(8,128)(2,1)} %all-to-all-done.2.received, bf16[88,2,2,8,683]{4,3,2,1,0:T(8,128)(2,1)} %noise.5, ...), custom_call_target="tpu_custom_call", output_to_operand_aliasing={{0}: (5, {}), {1}: (6, {})} | custom-call | flops 7161774080 | bytes 11537408 | tf_op jit(solution)/shard_map/finish/pallas_call | solution.py:468
  158.6 1.3 all-to-all-done.1.received
  159.9 3.4 %last.1 = (bf16[88,2,2,8,683]{4,3,2,1,0:T(8,128)(2,1)}, bf16[88,2,2,8,1024]{4,3,2,1,0:T(8,128)(2,1)}) custom-call(s32[88]{0:T(128)S(1)} %dynamic_slice.6.waves, bf16[8,256,128]{2,1,0:T(8,128)(2,1)S(1)} %all-to-all-done.1.received, bf16[88,2,2,8,683]{4,3,2,1,0:T(8,128)(2,1)} %noise.5, ...), custom_call_target="tpu_custom_call", output_to_operand_aliasing={{0}: (5, {}), {1}: (6, {})} | custom-call | flops 1432354816 | bytes 4545536 | tf_op jit(solution)/shard_map/last/pallas_call | solution.py:428
  (2 shorter events, 0.0 us)
Async XLA Ops:
  13.2 65.1 %all-to-all-start = ((bf16[8,1280,128]{2,1,0:T(8,128)(2,1)}), bf16[8,1280,128]{2,1,0:T(8,128)(2,1)}, u32[]{:S(2)}, u32[]{:S(2)}) async-start(bf16[8,1280,128]{2,1,0:T(8,128)(2,1)} %bitcast.4), calls=%async_computation | async-start | bytes 5242880 | tf_op jit(solution)/shard_map/all_to_all | solution.py:533
  19.7 17.5 %copy-start = (s32[8]{0:T(128)S(1)}, s32[8]{0:T(128)}, u32[]{:S(2)}) copy-start(s32[8]{0:T(128)} %param.8) | copy-start | bytes 100
  31.3 32.9 %collective-permute-start.4 = (bf16[320,32,128]{2,1,0:T(8,128)(2,1)}, bf16[320,32,128]{2,1,0:T(8,128)(2,1)S(1)}, u32[]{:S(2)}, u32[]{:S(2)}) collective-permute-start(bf16[320,32,128]{2,1,0:T(8,128)(2,1)} %zonal.5.own), channel_id=1, source_target_pairs={{0,8},{8,16},{16,24},{1,9},{9,17},{17,25},{2,10},{10,18},{18,26},{... | collective-permute-start | bytes 7864328 | tf_op jit(solution)/shard_map/ppermute | solution.py:527
  35.3 33.3 %collective-permute-start.5 = (bf16[320,32,128]{2,1,0:T(8,128)(2,1)}, bf16[320,32,128]{2,1,0:T(8,128)(2,1)}, u32[]{:S(2)}, u32[]{:S(2)}) collective-permute-start(bf16[320,32,128]{2,1,0:T(8,128)(2,1)} %zonal.5.own), channel_id=1, source_target_pairs={{8,0},{16,8},{24,16},{9,1},{17,9},{25,17},{10,2},{18,10},{26,18},{... | collective-permute-start | bytes 7864328 | tf_op jit(solution)/shard_map/ppermute | solution.py:528
  78.3 63.0 %all-to-all-start.2 = ((bf16[8,1280,128]{2,1,0:T(8,128)(2,1)}), bf16[8,1280,128]{2,1,0:T(8,128)(2,1)}, u32[]{:S(2)}, u32[]{:S(2)}) async-start(bf16[8,1280,128]{2,1,0:T(8,128)(2,1)} %bitcast.3), calls=%async_computation.2 | async-start | bytes 5242880 | tf_op jit(solution)/shard_map/all_to_all | solution.py:533
  96.3 26.6 %collective-permute-start.2 = (bf16[40,2,16,683]{3,2,1,0:T(8,128)(2,1)}, bf16[40,2,16,683]{3,2,1,0:T(8,128)(2,1)}, u32[]{:S(2)}, u32[]{:S(2)}) collective-permute-start(bf16[40,2,16,683]{3,2,1,0:T(8,128)(2,1)} %get-tuple-element.12.own), channel_id=1, source_target_pairs={{0,8},{8,16},{16,24},{1,9},{9,17},{17,25},{2,10},{10,18},{18,26},{... | collective-permute-start | bytes 5245448 | tf_op jit(solution)/shard_map/ppermute | solution.py:527
  101.1 26.3 %collective-permute-start.3 = (bf16[40,2,16,683]{3,2,1,0:T(8,128)(2,1)}, bf16[40,2,16,683]{3,2,1,0:T(8,128)(2,1)}, u32[]{:S(2)}, u32[]{:S(2)}) collective-permute-start(bf16[40,2,16,683]{3,2,1,0:T(8,128)(2,1)} %get-tuple-element.12.own), channel_id=1, source_target_pairs={{8,0},{16,8},{24,16},{9,1},{17,9},{25,17},{10,2},{18,10},{26,18},{... | collective-permute-start | bytes 5245448 | tf_op jit(solution)/shard_map/ppermute | solution.py:528
  110.9 25.7 %collective-permute-start = (bf16[64,32,128]{2,1,0:T(8,128)(2,1)}, bf16[64,32,128]{2,1,0:T(8,128)(2,1)S(1)}, u32[]{:S(2)}, u32[]{:S(2)}) collective-permute-start(bf16[64,32,128]{2,1,0:T(8,128)(2,1)} %zonal.3.own), channel_id=1, source_target_pairs={{0,8},{8,16},{16,24},{1,9},{9,17},{17,25},{2,10},{10,18},{18,26},{... | collective-permute-start | bytes 1572872 | tf_op jit(solution)/shard_map/ppermute | solution.py:527
  114.5 22.1 %collective-permute-start.1 = (bf16[64,32,128]{2,1,0:T(8,128)(2,1)}, bf16[64,32,128]{2,1,0:T(8,128)(2,1)S(1)}, u32[]{:S(2)}, u32[]{:S(2)}) collective-permute-start(bf16[64,32,128]{2,1,0:T(8,128)(2,1)} %zonal.3.own), channel_id=1, source_target_pairs={{8,0},{16,8},{24,16},{9,1},{17,9},{25,17},{10,2},{18,10},{26,18},{... | collective-permute-start | bytes 1572872 | tf_op jit(solution)/shard_map/ppermute | solution.py:528
  141.3 18.6 %all-to-all-start.1 = ((bf16[8,256,128]{2,1,0:T(8,128)(2,1)}), bf16[8,256,128]{2,1,0:T(8,128)(2,1)S(1)}, u32[]{:S(2)}, u32[]{:S(2)}) async-start(bf16[8,256,128]{2,1,0:T(8,128)(2,1)} %bitcast.5), calls=%async_computation.1 | async-start | bytes 1048576 | tf_op jit(solution)/shard_map/all_to_all | solution.py:533

commit v11 on v9

--- a/solution.py
+++ b/solution.py
@@ -86,14 +86,29 @@
     wave = waves[...]
     weight = jnp.where(wave < truncation, 1.0 / math.sqrt(longitudes), 0.0)
 
-    def angles(count, stride):
+    def cos_sin(count, stride):
         points = lax.broadcasted_iota(jnp.int32, (rows, count), 1) * stride
         phase = lax.rem(wave * points, jnp.full((), longitudes, jnp.int32))
-        return phase.astype(jnp.float32) * (2.0 * math.pi / longitudes)
-
-    coarse, fine = angles(longitudes // LANES, LANES), angles(LANES, 1)
-    cos_c, sin_c = jnp.cos(coarse) * weight, jnp.sin(coarse) * weight
-    cos_f, sin_f = jnp.cos(fine), jnp.sin(fine)
+        quarter = longitudes // 4
+        turns = lax.div(phase + quarter // 2, jnp.full((), quarter, jnp.int32))
+        angle = (phase - turns * quarter).astype(jnp.float32) * (2.0 * math.pi / longitudes)
+        square = angle * angle
+        cos, sin = 1.0 / 40320, -1.0 / 5040
+        for power in (6, 4, 2, 0):
+            sign = -1.0 if power % 4 else 1.0
+            cos = cos * square + sign / math.factorial(power)
+        for power in (5, 3, 1):
+            sign = -1.0 if power % 4 == 3 else 1.0
+            sin = sin * square + sign / math.factorial(power)
+        sin = sin * angle
+        swap = turns % 2 == 1
+        cos, sin = jnp.where(swap, sin, cos), jnp.where(swap, cos, sin)
+        cos = jnp.where((turns == 1) | (turns == 2), -cos, cos)
+        sin = jnp.where((turns == 2) | (turns == 3), -sin, sin)
+        return cos, sin
+
+    (cos_c, sin_c), (cos_f, sin_f) = cos_sin(longitudes // LANES, LANES), cos_sin(LANES, 1)
+    cos_c, sin_c = cos_c * weight, sin_c * weight
     for at in range(longitudes // LANES):
         cos_a, sin_a = cos_c[:, at : at + 1], sin_c[:, at : at + 1]
         columns = slice(at * LANES, (at + 1) * LANES)
@@ -353,66 +368,118 @@
     )(offsets, low, *in_hbm(own), high, *tokens)
 
 
-def finish_kernel(first, block, waves, received, noise, even, odd, *rest):
-    spectra_out, fourier_out = rest[-2:]
+def last_kernel(first, block, waves, received, noise, even, odd, *rest):
+    spectra_out, fourier_out, noise_here, spectra_here, fourier_here, order, sems, out_sems = rest[-8:]
     truncation = even.shape[0]
-    mem_local, parts, fields = noise.shape[1:4]
-    step = pl.program_id(0)
-    per_slot = received.shape[1] // block
-    rows = jnp.concatenate([received[g] for g in range(received.shape[0])], axis=-1)
-    contract = (((1,), (1,)), ((), ()))
-    by_even = lax.dot_general(rows, even[...], contract, preferred_element_type=jnp.float32)
-    by_odd = lax.dot_general(rows, odd[...], contract, preferred_element_type=jnp.float32)
-    degree = lax.broadcasted_iota(jnp.int32, (per_slot, truncation), 1)
-    even_rows, odd_rows = [], []
-    for slot in range(block):
-        wave = waves[first + step * block + slot]
-        least = jnp.where(wave < truncation, wave, truncation)
-        is_odd = wave % 2 == 1
-        active = degree >= least
-        here = slice(slot * per_slot, (slot + 1) * per_slot)
-        spectra = jnp.where(is_odd, by_odd[here], by_even[here])
-        spectra = spectra.astype(jnp.bfloat16).astype(jnp.float32)
-        added = noise[slot].astype(jnp.float32).reshape(per_slot, truncation)
-        child = jnp.where(active, spectra + added, 0.0)
-        spectra_out[slot] = child.reshape(noise.shape[1:]).astype(spectra_out.dtype)
-        even_rows.append(jnp.where(is_odd, 0.0, child).astype(jnp.bfloat16))
-        odd_rows.append(jnp.where(is_odd, child, 0.0).astype(jnp.bfloat16))
-    result = jnp.dot(
-        jnp.concatenate(even_rows, axis=0), even[...], preferred_element_type=jnp.float32
-    )
-    result += jnp.dot(
-        jnp.concatenate(odd_rows, axis=0), odd[...], preferred_element_type=jnp.float32
-    )
-    fourier_out[...] = result.reshape(fourier_out.shape).astype(fourier_out.dtype)
-
-
-def finish_transform(waves, first, block, received, noise, even, odd, outs):
+    slots, mem_local, parts, fields = noise_here.shape[:4]
+    per_slot = received.shape[1] // slots
+    fetch = pltpu.make_async_copy(noise.at[pl.ds(first, slots)], noise_here, sems.at[0])
+    fetch.start()
+
+    def place(slot, evens):
+        is_odd = waves[first + slot] % 2
+        order[jnp.where(is_odd == 1, slots - 1 - (slot - evens), evens)] = slot
+        return evens + 1 - is_odd
+
+    evens = lax.fori_loop(0, slots, place, jnp.int32(0))
+
+    def leave(slot):
+        return (
+            pltpu.make_async_copy(
+                spectra_here.at[slot], spectra_out.at[first + slot], out_sems.at[0, slot]
+            ),
+            pltpu.make_async_copy(
+                fourier_here.at[slot], fourier_out.at[first + slot], out_sems.at[1, slot]
+            ),
+        )
+
+    def transform(at, tables):
+        here = [order[at * block + slot] for slot in range(block)]
+        rows = []
+        for slot in here:
+            part = pl.ds(pl.multiple_of(slot * per_slot, per_slot), per_slot)
+            pieces = [received[g, part] for g in range(received.shape[0])]
+            rows.append(jnp.concatenate(pieces, axis=-1))
+        rows = jnp.concatenate(rows, axis=0)
+        contract = (((1,), (1,)), ((), ()))
+        results = [
+            lax.dot_general(rows, table[...], contract, preferred_element_type=jnp.float32)
+            for table in tables
+        ]
+
+        @pl.when(at == 0)
+        def _():
+            fetch.wait()
+
+        degree = lax.broadcasted_iota(jnp.int32, (per_slot, truncation), 1)
+        children = [[] for _ in tables]
+        for index, slot in enumerate(here):
+            wave = waves[first + slot]
+            least = jnp.where(wave < truncation, wave, truncation)
+            own = slice(index * per_slot, (index + 1) * per_slot)
+            spectra = results[0][own]
+            if len(tables) == 2:
+                spectra = jnp.where(wave % 2 == 1, results[1][own], spectra)
+            spectra = spectra.astype(jnp.bfloat16).astype(jnp.float32)
+            added = noise_here[slot].astype(jnp.float32).reshape(per_slot, truncation)
+            child = jnp.where(degree >= least, spectra + added, 0.0)
+            spectra_here[slot] = child.reshape(noise.shape[1:]).astype(spectra_out.dtype)
+            for parity, kept in enumerate(children):
+                if len(tables) == 2:
+                    kept.append(jnp.where(wave % 2 == parity, child, 0.0).astype(jnp.bfloat16))
+                else:
+                    kept.append(child.astype(jnp.bfloat16))
+        result = 0.0
+        for kept, table in zip(children, tables):
+            result += jnp.dot(
+                jnp.concatenate(kept, axis=0), table[...], preferred_element_type=jnp.float32
+            )
+        for index, slot in enumerate(here):
+            own = result[index * per_slot : (index + 1) * per_slot]
+            fourier_here[slot] = own.reshape(fourier_here.shape[1:]).astype(fourier_out.dtype)
+            for copy in leave(slot):
+                copy.start()
+
+    def body(at, carry):
+        all_even, all_odd = (at + 1) * block <= evens, at * block >= evens
+        pl.when(all_even)(lambda: transform(at, [even]))
+        pl.when(all_odd)(lambda: transform(at, [odd]))
+        pl.when(jnp.logical_not(all_even | all_odd))(lambda: transform(at, [even, odd]))
+        return carry
+
+    def end(slot, carry):
+        for copy in leave(slot):
+            copy.wait()
+        return carry
+
+    lax.fori_loop(0, slots // block, body, 0)
+    lax.fori_loop(0, slots, end, 0)
+
+
+def last_transform(waves, first, block, received, noise, even, odd, outs):
     slots_all, mem_local, parts, fields, truncation = noise.shape
     latitudes = even.shape[1]
-    groups, all_rows, lat_local = received.shape
-    per_slot = mem_local * parts * fields
-    at = first // block
-    far = lambda step, w: (at + step, 0, 0, 0, 0)
-    table = pl.BlockSpec(even.shape, lambda step, w: (0, 0))
-    noise_block = pl.BlockSpec((block,) + noise.shape[1:], far)
+    all_rows = received.shape[1]
+    slots = all_rows // (mem_local * parts * fields)
     fourier_shape = noise.shape[:4] + (latitudes,)
-    fourier_block = pl.BlockSpec((block,) + fourier_shape[1:], far)
-    received_block = pl.BlockSpec(
-        (groups, block * per_slot, lat_local), lambda step, w: (0, step, 0)
-    )
+    here = pl.BlockSpec(memory_space=pltpu.VMEM)
+    anywhere = pl.BlockSpec(memory_space=pl.ANY)
     return pl.pallas_call(
-        functools.partial(finish_kernel, first, block),
-        grid_spec=pltpu.PrefetchScalarGridSpec(
-            num_scalar_prefetch=1,
-            grid=(all_rows // (block * per_slot),),
-            in_specs=[received_block, noise_block, table, table]
-            + [pl.BlockSpec(memory_space=pl.ANY)] * 2,
-            out_specs=[noise_block, fourier_block],
-        ),
+        functools.partial(last_kernel, first, block),
+        in_specs=[pl.BlockSpec(memory_space=pltpu.SMEM), here, anywhere, here, here]
+        + [anywhere] * 2,
+        out_specs=[anywhere, anywhere],
         out_shape=[
             jax.ShapeDtypeStruct(noise.shape, jnp.bfloat16),
             jax.ShapeDtypeStruct(fourier_shape, jnp.bfloat16),
+        ],
+        scratch_shapes=[
+            pltpu.VMEM((slots,) + noise.shape[1:], jnp.bfloat16),
+            pltpu.VMEM((slots,) + noise.shape[1:], jnp.bfloat16),
+            pltpu.VMEM((slots,) + fourier_shape[1:], jnp.bfloat16),
+            pltpu.SMEM((slots,), jnp.int32),
+            pltpu.SemaphoreType.DMA((1,)),
+            pltpu.SemaphoreType.DMA((2, slots)),
         ],
         input_output_aliases={5: 0, 6: 1},
         compiler_params=pltpu.CompilerParams(vmem_limit_bytes=VMEM_BYTES),
@@ -421,15 +488,14 @@
             bytes_accessed=2 * all_rows * (2 * truncation + 2 * latitudes) + 4 * even.size,
             transcendentals=0,
         ),
-        name="finish",
-    )(waves, *in_hbm(received, noise), *in_vmem(even, odd), *in_hbm(*outs))
+        name="last",
+    )(waves, received, *in_hbm(noise), *in_vmem(even, odd), *in_hbm(*outs))
 
 
 def chunk_bounds(slots_here, block):
     blocks = slots_here // block
-    edges = [0, (blocks * 5 + 10) // 11, (blocks * 10 + 10) // 11, blocks]
-    edges = [edge * block for edge in edges]
-    return [(start, stop) for start, stop in zip(edges[:-1], edges[1:]) if stop > start]
+    edge = (blocks * 6 + 10) // 11 * block
+    return [(0, edge)] + ([(edge, slots_here)] if edge < slots_here else [])
 
 
 def per_device(velocity, tracer, wave_slots, parents, noise):
@@ -471,21 +537,20 @@
             moved = jnp.swapaxes(moved, 0, 1).reshape(1, -1, latitudes)
         return moved
 
-    def copied(at, tokens):
-        return copy_parents(offsets, *neighbours(zonal(at), per_member), tokens)
-
     received = exchanged(zonal(0))
     even, odd = meridional_tables(truncation, latitudes, starts, inner)
-    later = [exchanged(copied(1, []))] if len(bounds) > 1 else []
+    later = [
+        exchanged(copy_parents(offsets, *neighbours(zonal(at), per_member), []))
+        for at in range(1, len(bounds))
+    ]
     spectra, _ = forward_transform(
         (own_waves, per_member), 0, block, received, even, odd, mem_local, []
     )
-    *outs, token = inverse_transform(
+    *outs, _ = inverse_transform(
         own_waves, offsets, 0, block, *neighbours(spectra, 1), noise, even, odd, None
     )
-    later += [exchanged(copied(at, [token])) for at in range(2, len(bounds))]
     for (start, _), received in zip(bounds[1:], later):
-        outs = finish_transform(own_waves, start, block, received, noise, even, odd, outs)
+        outs = last_transform(own_waves, start, block, received, noise, even, odd, outs)
     return tuple(outs)
 
 

time: 168 us -> 171 us (1.018)
  waiting for transfers between devices: 48.3 us -> 75.3 us
  Pallas kernels: 76 us -> 62.1 us
  starting transfers between devices: 34.3 us -> 22.8 us
  local copies, waits for them, and re-layouts: 2.91 us -> 4.69 us
    ppermute x3 -> x2, waiting for transfers between devices: 8.8 us -> 52.7 us  [neighbours(): high = lax.ppermute(rows[:, :SPREAD * per_member], 'member', downward)]
    ppermute x3 -> x2, waiting for transfers between devices: 33.4 us -> 2.17 us  [neighbours(): lax.ppermute(rows[:, rows.shape[1] - SPREAD * per_member:], 'member', upw...]
    all_to_all x3 -> x2, waiting for transfers between devices: 6.1 us -> 20.4 us  [exchanged(): lax.all_to_all(outgoing, 'lat', split_axis=0, concat_axis=0, tiled=True)]
    pallas_call x3 -> x2, Pallas kernels: 30.9 us -> 23.7 us  [zonal_transform(): pl.pallas_call(functools.partial(zonal_kernel, truncation, len(tokens)),...]
    ppermute x3 -> x2, starting transfers between devices: 12.3 us -> 6.05 us  [neighbours(): lax.ppermute(rows[:, rows.shape[1] - SPREAD * per_member:], 'member', upw...]
    all_to_all x3 -> x2, starting transfers between devices: 16.2 us -> 11.1 us  [exchanged(): lax.all_to_all(outgoing, 'lat', split_axis=0, concat_axis=0, tiled=True)]
    pallas_call x2 -> x1, Pallas kernels: 16.6 us -> 11.7 us  [last_transform(): pl.pallas_call(functools.partial(last_kernel, first, block), in_specs=[pl...]
    pallas_call x2 -> x1, Pallas kernels: 9.59 us -> 6.02 us  [copy_parents(): pl.pallas_call(copy_kernel, grid_spec=pltpu.PrefetchScalarGridSpec(num_sc...]
  transfers between devices with their start and end apart: 9 -> 6, of which waited for: 7 -> 6; matrix products, arithmetic and copies ran while one was open for 2% -> 2% of each run, Pallas kernels for 36% -> 22%
where the time goes in v11:
time: 171 us; the launch traced here: 169 us
  waiting for transfers between devices  75.3 us (44%)
  Pallas kernels  62.1 us (36%)
  starting transfers between devices  22.8 us (13%)
  local copies, waits for them, and re-layouts  4.69 us (3%)
  other arithmetic  2.88 us (2%)
    ppermute x2, waiting for transfers between devices, neighbours(): high = lax.ppermute(rows[:, :SPREAD * per_member], 'member', downward)  52.7 us
    pallas_call x2, Pallas kernels, zonal_transform(): pl.pallas_call(functools.partial(zonal_kernel, truncation, len(tokens)),...  23.7 us
    all_to_all x2, waiting for transfers between devices, exchanged(): lax.all_to_all(outgoing, 'lat', split_axis=0, concat_axis=0, tiled=True)  20.4 us
    pallas_call x1, Pallas kernels, last_transform(): pl.pallas_call(functools.partial(last_kernel, first, block), in_specs=[pl...  11.7 us
    all_to_all x2, starting transfers between devices, exchanged(): lax.all_to_all(outgoing, 'lat', split_axis=0, concat_axis=0, tiled=True)  11.1 us
    pallas_call x1, Pallas kernels, inverse_transform(): pl.pallas_call(functools.partial(inverse_kernel, first, block), grid_spec...  9.6 us
    pallas_call x1, Pallas kernels, forward_transform(): pl.pallas_call(functools.partial(forward_kernel, first, block), grid_spec...  9.3 us
    ppermute x2, starting transfers between devices, neighbours(): lax.ppermute(rows[:, rows.shape[1] - SPREAD * per_member:], 'member', upw...  6.05 us
  transfers between devices with their start and end apart: 6, of which 6 were waited for; matrix products, arithmetic and copies ran while one was open for 2% of the time, Pallas kernels for 22%

profile of v11, /device:TPU:1, one launch (start us, length us, event | category | flops | bytes accessed | tf_op | source)
XLA Modules:
  0.0 168.8 jit_solution(9063970157228182625)
XLA Ops:
  0.6 0.8 reshape.28
  1.4 0.1 reshape.34.waves
  1.5 12.8 %zonal.3 = bf16[384,32,128]{2,1,0:T(8,128)(2,1)} custom-call(s32[384,1]{1,0:T(8,128)S(1)} %reshape.34.waves, bf16[2,8,128,2048]{3,2,1,0:T(8,128)(2,1)} %velocity.3, bf16[2,8,128,2048]{3,2,1,0:T(8,128)(2,1)} %tracer.3), custom_call_target="tpu_custom_call" | custom-call | flops 6442450944 | bytes 19922944 | tf_op jit(solution)/shard_map/zonal/pallas_call | solution.py:171
  14.3 6.4 %all-to-all-start.1 = ((bf16[8,1536,128]{2,1,0:T(8,128)(2,1)}), bf16[8,1536,128]{2,1,0:T(8,128)(2,1)}, u32[]{:S(2)}, u32[]{:S(2)}) async-start(bf16[8,1536,128]{2,1,0:T(8,128)(2,1)} %bitcast.4), calls=%async_computation.1 | async-start | bytes 6291456 | tf_op jit(solution)/shard_map/all_to_all | solution.py:535
  20.7 0.1 slice.6
  20.8 0.1 reshape.33.waves
  20.9 0.0 copy-start.4
  20.9 11.0 %zonal.2.own = bf16[320,32,128]{2,1,0:T(8,128)(2,1)} custom-call(s32[320,1]{1,0:T(8,128)S(1)} %reshape.33.waves, bf16[2,8,128,2048]{3,2,1,0:T(8,128)(2,1)} %velocity.3, bf16[2,8,128,2048]{3,2,1,0:T(8,128)(2,1)} %tracer.3), custom_call_target="tpu_custom_call" | custom-call | flops 5368709120 | bytes 19398656 | tf_op jit(solution)/shard_map/zonal/pallas_call | solution.py:171
  31.9 2.9 %collective-permute-start.1 = (bf16[320,32,128]{2,1,0:T(8,128)(2,1)}, bf16[320,32,128]{2,1,0:T(8,128)(2,1)S(1)}, u32[]{:S(2)}, u32[]{:S(2)}) collective-permute-start(bf16[320,32,128]{2,1,0:T(8,128)(2,1)} %zonal.2.own), channel_id=1, source_target_pairs={{8,0},{16,8},{24,16},{9,1},{17,9},{25,17},{10,2},{18,10},{26,18},{... | collective-permute-start | bytes 7864328 | tf_op jit(solution)/shard_map/ppermute | solution.py:530
  34.7 3.0 %collective-permute-start = (bf16[320,32,128]{2,1,0:T(8,128)(2,1)}, bf16[320,32,128]{2,1,0:T(8,128)(2,1)}, u32[]{:S(2)}, u32[]{:S(2)}) collective-permute-start(bf16[320,32,128]{2,1,0:T(8,128)(2,1)} %zonal.2.own), channel_id=1, source_target_pairs={{0,8},{8,16},{16,24},{1,9},{9,17},{17,25},{2,10},{10,18},{18,26},{... | collective-permute-start | bytes 7864328 | tf_op jit(solution)/shard_map/ppermute | solution.py:529
  37.8 0.0 copy-done.4
  37.8 0.1 subtract_add_fusion.offsets
  37.9 27.9 %collective-permute-done.1.high = bf16[320,32,128]{2,1,0:T(8,128)(2,1)S(1)} collective-permute-done((bf16[320,32,128]{2,1,0:T(8,128)(2,1)}, bf16[320,32,128]{2,1,0:T(8,128)(2,1)S(1)}, u32[]{:S(2)}, u32[]{:S(2)}) %collective-permute-start.1) | collective-permute-done | bytes 2621472 | tf_op jit(solution)/shard_map/ppermute | solution.py:530
  65.8 0.9 collective-permute-done.low
  66.7 6.0 %parents.1 = bf16[320,32,128]{2,1,0:T(8,128)(2,1)} custom-call(s32[2]{0:T(128)S(1)} %subtract_add_fusion.offsets, bf16[320,32,128]{2,1,0:T(8,128)(2,1)} %collective-permute-done.low, bf16[320,32,128]{2,1,0:T(8,128)(2,1)} %zonal.2.own, bf16[320,32,128]{2,1,0:T(8,128)(2,1)S(1)} %collective-permute-done.1.high), custom_call_target="tpu_custom_call" | custom-call | bytes 10485760 | tf_op jit(solution)/shard_map/parents/pallas_call | solution.py:355
  72.7 18.0 %all-to-all-done.1.received = bf16[8,1536,128]{2,1,0:T(8,128)(2,1)} async-done(((bf16[8,1536,128]{2,1,0:T(8,128)(2,1)}), bf16[8,1536,128]{2,1,0:T(8,128)(2,1)}, u32[]{:S(2)}, u32[]{:S(2)}) %all-to-all-start.1) | async-done | bytes 3145760 | tf_op jit(solution)/shard_map/all_to_all | solution.py:535
  90.6 4.7 %all-to-all-start = ((bf16[8,1280,128]{2,1,0:T(8,128)(2,1)}), bf16[8,1280,128]{2,1,0:T(8,128)(2,1)S(1)}, u32[]{:S(2)}, u32[]{:S(2)}) async-start(bf16[8,1280,128]{2,1,0:T(8,128)(2,1)} %bitcast.3), calls=%async_computation | async-start | bytes 5242880 | tf_op jit(solution)/shard_map/all_to_all | solution.py:535
  95.3 0.8 dynamic_slice.6.waves
  96.1 0.1 fusion.9
  96.2 0.2 copy.12
  96.4 1.4 fusion.6
  97.8 1.3 sine_multiply_fusion
  99.1 1.8 %tables.1 = (bf16[683,1024]{1,0:T(8,128)(2,1)S(1)}, bf16[683,1024]{1,0:T(8,128)(2,1)S(1)}) custom-call(f32[683,8]{1,0:T(8,128)S(1)} %get-tuple-element.13.cos_c, f32[683,8]{1,0:T(8,128)S(1)} %get-tuple-element.12.sin_c, f32[683,128]{1,0:T(8,128)S(1)} %get-tuple-element.15.cos_f, f32[683,128]{1,0:T(8,128)S(1)} %get-tuple-element.14.sin_f), custom_call_target="tpu_custom_call" | custom-call | flops 4196352 | bytes 2797568 | tf_op jit(solution)/shard_map/tables/pallas_call | solution.py:53
  100.9 0.0 copy-start
  100.9 0.0 copy-start.2
  100.9 9.3 %forward.1 = (bf16[48,2,16,683]{3,2,1,0:T(8,128)(2,1)}, f32[8,128]{1,0:T(8,128)}) custom-call(s32[88]{0:T(128)S(1)} %dynamic_slice.6.waves, bf16[8,1536,128]{2,1,0:T(8,128)(2,1)} %all-to-all-done.1.received, bf16[683,1024]{1,0:T(8,128)(2,1)S(1)} %get-tuple-element.7.even, bf16[683,1024]{1,0:T(8,128)(2,1)S(1)} %get-tuple-element.8.odd), custom_call_target="tpu_custom_call" | custom-call | flops 4297064448 | bytes 8041472 | tf_op jit(solution)/shard_map/forward/pallas_call | solution.py:219
  110.2 2.9 %collective-permute-start.3 = (bf16[48,2,16,683]{3,2,1,0:T(8,128)(2,1)}, bf16[48,2,16,683]{3,2,1,0:T(8,128)(2,1)S(1)}, u32[]{:S(2)}, u32[]{:S(2)}) collective-permute-start(bf16[48,2,16,683]{3,2,1,0:T(8,128)(2,1)} %get-tuple-element.9.own), channel_id=1, source_target_pairs={{8,0},{16,8},{24,16},{9,1},{17,9},{25,17},{10,2},{18,10},{26,18},{... | collective-permute-start | bytes 6294536 | tf_op jit(solution)/shard_map/ppermute | solution.py:530
  113.0 3.0 %collective-permute-start.2 = (bf16[48,2,16,683]{3,2,1,0:T(8,128)(2,1)}, bf16[48,2,16,683]{3,2,1,0:T(8,128)(2,1)S(1)}, u32[]{:S(2)}, u32[]{:S(2)}) collective-permute-start(bf16[48,2,16,683]{3,2,1,0:T(8,128)(2,1)} %get-tuple-element.9.own), channel_id=1, source_target_pairs={{0,8},{8,16},{16,24},{1,9},{9,17},{17,25},{2,10},{10,18},{18,26},{... | collective-permute-start | bytes 6294536 | tf_op jit(solution)/shard_map/ppermute | solution.py:529
  116.1 24.8 %collective-permute-done.3.high = bf16[48,2,16,683]{3,2,1,0:T(8,128)(2,1)S(1)} collective-permute-done((bf16[48,2,16,683]{3,2,1,0:T(8,128)(2,1)}, bf16[48,2,16,683]{3,2,1,0:T(8,128)(2,1)S(1)}, u32[]{:S(2)}, u32[]{:S(2)}) %collective-permute-start.3) | collective-permute-done | bytes 2098208 | tf_op jit(solution)/shard_map/ppermute | solution.py:530
  140.9 1.3 collective-permute-done.2.low
  142.2 0.0 copy-done
  142.2 0.0 copy-done.2
  142.2 9.6 %inverse.1 = (bf16[88,2,2,8,683]{4,3,2,1,0:T(8,128)(2,1)}, bf16[88,2,2,8,1024]{4,3,2,1,0:T(8,128)(2,1)}, f32[8,128]{1,0:T(8,128)}) custom-call(s32[88]{0:T(128)S(1)} %dynamic_slice.6.waves, s32[2]{0:T(128)S(1)} %subtract_add_fusion.offsets, bf16[48,2,16,683]{3,2,1,0:T(8,128)(2,1)S(1)} %collective-permute-done.2.low, ...), custom_call_target="tpu_custom_call" | custom-call | flops 4297064448 | bytes 16434176 | tf_op jit(solution)/shard_map/inverse/pallas_call | solution.py:309
  151.8 2.4 %all-to-all-done.received = bf16[8,1280,128]{2,1,0:T(8,128)(2,1)S(1)} async-done(((bf16[8,1280,128]{2,1,0:T(8,128)(2,1)}), bf16[8,1280,128]{2,1,0:T(8,128)(2,1)S(1)}, u32[]{:S(2)}, u32[]{:S(2)}) %all-to-all-start) | async-done | bytes 2621472 | tf_op jit(solution)/shard_map/all_to_all | solution.py:535
  154.2 0.0 copy-start.1
  154.2 1.3 copy-done.1
  155.5 0.0 copy-start.3
  155.5 1.3 copy-done.3
  156.9 11.7 %last.1 = (bf16[88,2,2,8,683]{4,3,2,1,0:T(8,128)(2,1)}, bf16[88,2,2,8,1024]{4,3,2,1,0:T(8,128)(2,1)}) custom-call(s32[88]{0:T(128)S(1)} %dynamic_slice.6.waves, bf16[8,1280,128]{2,1,0:T(8,128)(2,1)S(1)} %all-to-all-done.received, bf16[88,2,2,8,683]{4,3,2,1,0:T(8,128)(2,1)} %noise.3, ...), custom_call_target="tpu_custom_call", output_to_operand_aliasing={{0}: (5, {}), {1}: (6, {})} | custom-call | flops 7161774080 | bytes 11537408 | tf_op jit(solution)/shard_map/last/pallas_call | solution.py:467
  (2 shorter events, 0.0 us)
Async XLA Ops:
  14.3 76.3 %all-to-all-start.1 = ((bf16[8,1536,128]{2,1,0:T(8,128)(2,1)}), bf16[8,1536,128]{2,1,0:T(8,128)(2,1)}, u32[]{:S(2)}, u32[]{:S(2)}) async-start(bf16[8,1536,128]{2,1,0:T(8,128)(2,1)} %bitcast.4), calls=%async_computation.1 | async-start | bytes 6291456 | tf_op jit(solution)/shard_map/all_to_all | solution.py:535
  20.9 16.9 %copy-start.4 = (s32[8]{0:T(128)S(1)}, s32[8]{0:T(128)}, u32[]{:S(2)}) copy-start(s32[8]{0:T(128)} %param.8) | copy-start | bytes 100
  31.9 33.9 %collective-permute-start.1 = (bf16[320,32,128]{2,1,0:T(8,128)(2,1)}, bf16[320,32,128]{2,1,0:T(8,128)(2,1)S(1)}, u32[]{:S(2)}, u32[]{:S(2)}) collective-permute-start(bf16[320,32,128]{2,1,0:T(8,128)(2,1)} %zonal.2.own), channel_id=1, source_target_pairs={{8,0},{16,8},{24,16},{9,1},{17,9},{25,17},{10,2},{18,10},{26,18},{... | collective-permute-start | bytes 7864328 | tf_op jit(solution)/shard_map/ppermute | solution.py:530
  34.7 31.9 %collective-permute-start = (bf16[320,32,128]{2,1,0:T(8,128)(2,1)}, bf16[320,32,128]{2,1,0:T(8,128)(2,1)}, u32[]{:S(2)}, u32[]{:S(2)}) collective-permute-start(bf16[320,32,128]{2,1,0:T(8,128)(2,1)} %zonal.2.own), channel_id=1, source_target_pairs={{0,8},{8,16},{16,24},{1,9},{9,17},{17,25},{2,10},{10,18},{18,26},{... | collective-permute-start | bytes 7864328 | tf_op jit(solution)/shard_map/ppermute | solution.py:529
  90.6 63.5 %all-to-all-start = ((bf16[8,1280,128]{2,1,0:T(8,128)(2,1)}), bf16[8,1280,128]{2,1,0:T(8,128)(2,1)S(1)}, u32[]{:S(2)}, u32[]{:S(2)}) async-start(bf16[8,1280,128]{2,1,0:T(8,128)(2,1)} %bitcast.3), calls=%async_computation | async-start | bytes 5242880 | tf_op jit(solution)/shard_map/all_to_all | solution.py:535
  100.9 41.3 %copy-start = (bf16[683,1024]{1,0:T(8,128)(2,1)}, bf16[683,1024]{1,0:T(8,128)(2,1)S(1)}, u32[]{:S(2)}) copy-start(bf16[683,1024]{1,0:T(8,128)(2,1)S(1)} %get-tuple-element.7.even) | copy-start | bytes 4196356
  100.9 41.3 %copy-start.2 = (bf16[683,1024]{1,0:T(8,128)(2,1)}, bf16[683,1024]{1,0:T(8,128)(2,1)S(1)}, u32[]{:S(2)}) copy-start(bf16[683,1024]{1,0:T(8,128)(2,1)S(1)} %get-tuple-element.8.odd) | copy-start | bytes 4196356
  110.2 30.7 %collective-permute-start.3 = (bf16[48,2,16,683]{3,2,1,0:T(8,128)(2,1)}, bf16[48,2,16,683]{3,2,1,0:T(8,128)(2,1)S(1)}, u32[]{:S(2)}, u32[]{:S(2)}) collective-permute-start(bf16[48,2,16,683]{3,2,1,0:T(8,128)(2,1)} %get-tuple-element.9.own), channel_id=1, source_target_pairs={{8,0},{16,8},{24,16},{9,1},{17,9},{25,17},{10,2},{18,10},{26,18},{... | collective-permute-start | bytes 6294536 | tf_op jit(solution)/shard_map/ppermute | solution.py:530
  113.0 29.1 %collective-permute-start.2 = (bf16[48,2,16,683]{3,2,1,0:T(8,128)(2,1)}, bf16[48,2,16,683]{3,2,1,0:T(8,128)(2,1)S(1)}, u32[]{:S(2)}, u32[]{:S(2)}) collective-permute-start(bf16[48,2,16,683]{3,2,1,0:T(8,128)(2,1)} %get-tuple-element.9.own), channel_id=1, source_target_pairs={{0,8},{8,16},{16,24},{1,9},{9,17},{17,25},{2,10},{10,18},{18,26},{... | collective-permute-start | bytes 6294536 | tf_op jit(solution)/shard_map/ppermute | solution.py:529
  154.2 1.4 copy-start.1
  155.5 1.4 copy-start.3

commit v12 on v9

--- a/solution.py
+++ b/solution.py
@@ -63,7 +63,8 @@
 
 
 def zonal_kernel(truncation, tokens, waves, velocity, tracer, *rest):
-    out, table, total, turned, velocity_here, tracer_here, sems, out_sems = rest[tokens:]
+    outs, rest = rest[tokens:-7], rest[-7:]
+    table, total, turned, velocity_here, tracer_here, sems, out_sems = rest
     members, fields, lat_local, longitudes = velocity.shape
     rows = waves.shape[0]
     groups = velocity_here.shape[0]
@@ -86,14 +87,29 @@
     wave = waves[...]
     weight = jnp.where(wave < truncation, 1.0 / math.sqrt(longitudes), 0.0)
 
-    def angles(count, stride):
+    def cos_sin(count, stride):
         points = lax.broadcasted_iota(jnp.int32, (rows, count), 1) * stride
         phase = lax.rem(wave * points, jnp.full((), longitudes, jnp.int32))
-        return phase.astype(jnp.float32) * (2.0 * math.pi / longitudes)
-
-    coarse, fine = angles(longitudes // LANES, LANES), angles(LANES, 1)
-    cos_c, sin_c = jnp.cos(coarse) * weight, jnp.sin(coarse) * weight
-    cos_f, sin_f = jnp.cos(fine), jnp.sin(fine)
+        quarter = longitudes // 4
+        turns = lax.div(phase + quarter // 2, jnp.full((), quarter, jnp.int32))
+        angle = (phase - turns * quarter).astype(jnp.float32) * (2.0 * math.pi / longitudes)
+        square = angle * angle
+        cos, sin = 1.0 / 40320, -1.0 / 5040
+        for power in (6, 4, 2, 0):
+            sign = -1.0 if power % 4 else 1.0
+            cos = cos * square + sign / math.factorial(power)
+        for power in (5, 3, 1):
+            sign = -1.0 if power % 4 == 3 else 1.0
+            sin = sin * square + sign / math.factorial(power)
+        sin = sin * angle
+        swap = turns % 2 == 1
+        cos, sin = jnp.where(swap, sin, cos), jnp.where(swap, cos, sin)
+        cos = jnp.where((turns == 1) | (turns == 2), -cos, cos)
+        sin = jnp.where((turns == 2) | (turns == 3), -sin, sin)
+        return cos, sin
+
+    (cos_c, sin_c), (cos_f, sin_f) = cos_sin(longitudes // LANES, LANES), cos_sin(LANES, 1)
+    cos_c, sin_c = cos_c * weight, sin_c * weight
     for at in range(longitudes // LANES):
         cos_a, sin_a = cos_c[:, at : at + 1], sin_c[:, at : at + 1]
         columns = slice(at * LANES, (at + 1) * LANES)
@@ -121,30 +137,37 @@
 
     lax.fori_loop(0, groups, body, 0)
 
-    tiles = rows // SUBLANES
+    tiles = rows // SUBLANES // len(outs)
     batch = math.gcd(tiles, 4)
 
-    def leave(at):
-        part = pl.ds(pl.multiple_of(at * batch * SUBLANES, SUBLANES), batch * SUBLANES)
-        return pltpu.make_async_copy(turned.at[part], out.at[part], out_sems.at[at])
-
-    def turn(at, carry):
-        for tile in range(batch):
-            first = pl.multiple_of((at * batch + tile) * SUBLANES, SUBLANES)
-            tiles_here = jnp.swapaxes(total[at * batch + tile], 0, 1)
-            turned[pl.ds(first, SUBLANES)] = tiles_here.astype(out.dtype)
-        leave(at).start()
-        return carry
-
-    def end(at, carry):
-        leave(at).wait()
-        return carry
-
-    lax.fori_loop(0, tiles // batch, turn, 0)
-    lax.fori_loop(0, tiles // batch, end, 0)
-
-
-def zonal_transform(waves, truncation, velocity, tracer, tokens):
+    def leave(piece, at):
+        size = batch * SUBLANES
+        part = pl.ds(pl.multiple_of(at * size, SUBLANES), size)
+        source = turned.at[pl.ds(pl.multiple_of((piece * tiles + at * batch) * SUBLANES, SUBLANES), size)]
+        return pltpu.make_async_copy(source, outs[piece].at[part], out_sems.at[piece, at])
+
+    for piece in range(len(outs)):
+
+        def turn(at, carry):
+            for tile in range(batch):
+                index = piece * tiles + at * batch + tile
+                first = pl.multiple_of(index * SUBLANES, SUBLANES)
+                turned[pl.ds(first, SUBLANES)] = jnp.swapaxes(total[index], 0, 1).astype(turned.dtype)
+            leave(piece, at).start()
+            return carry
+
+        lax.fori_loop(0, tiles // batch, turn, 0)
+
+    for piece in range(len(outs)):
+
+        def end(at, carry):
+            leave(piece, at).wait()
+            return carry
+
+        lax.fori_loop(0, tiles // batch, end, 0)
+
+
+def zonal_transform(waves, truncation, velocity, tracer, pieces, tokens):
     mem_local, fields, lat_local, longitudes = velocity.shape
     rows = waves.shape[0]
     fields_step = min(fields, max(1, 512 // lat_local))
@@ -157,8 +180,8 @@
         functools.partial(zonal_kernel, truncation, len(tokens)),
         in_specs=[pl.BlockSpec(memory_space=pltpu.VMEM)]
         + [pl.BlockSpec(memory_space=pl.ANY)] * (2 + len(tokens)),
-        out_specs=pl.BlockSpec(memory_space=pl.ANY),
-        out_shape=pltpu.HBM((rows, out_rows, lat_local), jnp.bfloat16),
+        out_specs=[pl.BlockSpec(memory_space=pl.ANY)] * pieces,
+        out_shape=[pltpu.HBM((rows // pieces, out_rows, lat_local), jnp.bfloat16)] * pieces,
         scratch_shapes=[
             pltpu.VMEM((2 * rows, longitudes), jnp.bfloat16),
             pltpu.VMEM((rows // SUBLANES, out_rows, SUBLANES, lat_local), jnp.float32),
@@ -166,7 +189,7 @@
             grid_part,
             grid_part,
             pltpu.SemaphoreType.DMA((groups, 2)),
-            pltpu.SemaphoreType.DMA((rows // SUBLANES,)),
+            pltpu.SemaphoreType.DMA((pieces, rows // SUBLANES // pieces)),
         ],
         compiler_params=pltpu.CompilerParams(vmem_limit_bytes=ZONAL_BYTES),
         cost_estimate=pl.CostEstimate(flops=flops, bytes_accessed=moved, transcendentals=0),
@@ -229,6 +252,53 @@
         ),
         name="forward",
     )(waves[0], *in_hbm(received), *in_vmem(even, odd), *tokens)
+
+
+def paired_kernel(first, waves, place, *refs):
+    received, (even, odd, out, rows) = refs[:-4], refs[-4:]
+    truncation = even.shape[0]
+    block = out.shape[0]
+    lat_local = received[0].shape[2]
+    per_slot = rows.shape[0] // block
+    me = place[0]
+    for k, piece in enumerate(received):
+        columns = pl.ds(pl.multiple_of((me ^ k) * lat_local, LANES), lat_local)
+        rows[:, columns] = piece[place[k]] if k > 0 else piece[0]
+    contract = (((1,), (1,)), ((), ()))
+    lines = rows[...]
+    by_even = lax.dot_general(lines, even[...], contract, preferred_element_type=jnp.float32)
+    by_odd = lax.dot_general(lines, odd[...], contract, preferred_element_type=jnp.float32)
+    degree = lax.broadcasted_iota(jnp.int32, (per_slot, truncation), 1)
+    for slot in range(block):
+        wave = waves[first + slot]
+        least = jnp.where(wave < truncation, wave, truncation)
+        here = slice(slot * per_slot, (slot + 1) * per_slot)
+        chosen = jnp.where(wave % 2 == 1, by_odd[here], by_even[here])
+        chosen = jnp.where(degree >= least, chosen, 0.0)
+        out[slot] = chosen.astype(out.dtype).reshape(out.shape[1:])
+
+
+def paired_transform(waves, first, place, received, even, odd, mem_local, per_member):
+    truncation, latitudes = even.shape
+    all_rows = received[0].shape[1]
+    slots = all_rows // (mem_local * per_member)
+    here = pl.BlockSpec(memory_space=pltpu.VMEM)
+    scalars = pl.BlockSpec(memory_space=pltpu.SMEM)
+    out_shape = (slots, mem_local, per_member, truncation)
+    return pl.pallas_call(
+        functools.partial(paired_kernel, first),
+        in_specs=[scalars, scalars] + [here] * (len(received) + 2),
+        out_specs=here,
+        out_shape=jax.ShapeDtypeStruct(out_shape, jnp.bfloat16),
+        scratch_shapes=[pltpu.VMEM((all_rows, latitudes), jnp.bfloat16)],
+        compiler_params=pltpu.CompilerParams(vmem_limit_bytes=VMEM_BYTES),
+        cost_estimate=pl.CostEstimate(
+            flops=4 * all_rows * truncation * latitudes,
+            bytes_accessed=2 * (all_rows * latitudes + 2 * even.size + all_rows * truncation),
+            transcendentals=0,
+        ),
+        name="paired",
+    )(waves, place, *received, *in_vmem(even, odd))
 
 
 def inverse_kernel(first, block, waves, offsets, low, own, high, noise, even, odd, *rest):
@@ -353,11 +423,9 @@
     )(offsets, low, *in_hbm(own), high, *tokens)
 
 
-def finish_kernel(first, block, waves, received, noise, even, odd, *rest):
-    spectra_out, fourier_out = rest[-2:]
+def finish_block(first, waves, received, noise, even, odd, spectra_out, fourier_out, ready, store):
     truncation = even.shape[0]
-    mem_local, parts, fields = noise.shape[1:4]
-    step = pl.program_id(0)
+    block, mem_local, parts, fields = noise.shape[:4]
     per_slot = received.shape[1] // block
     rows = jnp.concatenate([received[g] for g in range(received.shape[0])], axis=-1)
     contract = (((1,), (1,)), ((), ()))
@@ -365,8 +433,9 @@
     by_odd = lax.dot_general(rows, odd[...], contract, preferred_element_type=jnp.float32)
     degree = lax.broadcasted_iota(jnp.int32, (per_slot, truncation), 1)
     even_rows, odd_rows = [], []
+    ready()
     for slot in range(block):
-        wave = waves[first + step * block + slot]
+        wave = waves[first + slot]
         least = jnp.where(wave < truncation, wave, truncation)
         is_odd = wave % 2 == 1
         active = degree >= least
@@ -378,6 +447,7 @@
         spectra_out[slot] = child.reshape(noise.shape[1:]).astype(spectra_out.dtype)
         even_rows.append(jnp.where(is_odd, 0.0, child).astype(jnp.bfloat16))
         odd_rows.append(jnp.where(is_odd, child, 0.0).astype(jnp.bfloat16))
+    store()
     result = jnp.dot(
         jnp.concatenate(even_rows, axis=0), even[...], preferred_element_type=jnp.float32
     )
@@ -385,6 +455,12 @@
         jnp.concatenate(odd_rows, axis=0), odd[...], preferred_element_type=jnp.float32
     )
     fourier_out[...] = result.reshape(fourier_out.shape).astype(fourier_out.dtype)
+
+
+def finish_kernel(first, block, waves, received, noise, even, odd, *rest):
+    start = first + pl.program_id(0) * block
+    nothing = lambda: None
+    finish_block(start, waves, received, noise, even, odd, *rest[-2:], nothing, nothing)
 
 
 def finish_transform(waves, first, block, received, noise, even, odd, outs):
@@ -427,7 +503,7 @@
 
 def chunk_bounds(slots_here, block):
     blocks = slots_here // block
-    edges = [0, (blocks * 5 + 10) // 11, (blocks * 10 + 10) // 11, blocks]
+    edges = [0, (blocks * 6 + 10) // 11, (blocks * 10 + 10) // 11, blocks]
     edges = [edge * block for edge in edges]
     return [(start, stop) for start, stop in zip(edges[:-1], edges[1:]) if stop > start]
 
@@ -454,10 +530,10 @@
     inner = min(lat_local, LANES)
     starts = jnp.arange(latitudes // inner, dtype=jnp.int32) * inner
 
-    def zonal(at):
+    def zonal(at, grid, pieces):
         start, stop = bounds[at]
-        waves = slot_grid[:, start:stop].reshape(-1, 1)
-        return zonal_transform(waves, truncation, velocity, tracer, [])
+        waves = grid[:, start:stop].reshape(-1, 1)
+        return zonal_transform(waves, truncation, velocity, tracer, pieces, [])
 
     def neighbours(rows, per_member):
         low = lax.ppermute(rows[:, rows.shape[1] - SPREAD * per_member :], "member", upward)
@@ -471,21 +547,55 @@
             moved = jnp.swapaxes(moved, 0, 1).reshape(1, -1, latitudes)
         return moved
 
-    def copied(at, tokens):
-        return copy_parents(offsets, *neighbours(zonal(at), per_member), tokens)
-
-    received = exchanged(zonal(0))
+    def inverse(start, spectra, outs):
+        *outs, _ = inverse_transform(
+            own_waves, offsets, start, block, *neighbours(spectra, 1), noise, even, odd, outs
+        )
+        return outs
+
+    received = exchanged(zonal(0, slot_grid, 1)[0])
     even, odd = meridional_tables(truncation, latitudes, starts, inner)
-    later = [exchanged(copied(1, []))] if len(bounds) > 1 else []
+    in_pairs = len(bounds) > 2 and lat_local % LANES == 0 and lat_count & (lat_count - 1) == 0
+    tokens = []
+    if in_pairs:
+        ranks = jnp.arange(lat_count, dtype=jnp.int32)
+        pieces = zonal(2, slot_grid[ranks ^ lat_index], lat_count)
+        tokens = [pieces[0]]
+        highest = jnp.array([1 << max(k.bit_length() - 1, 0) for k in range(lat_count)], jnp.int32)
+        place = jnp.where(ranks == 0, lat_index, (lat_index & highest == 0).astype(jnp.int32))
+        moved = [pieces[0].reshape(1, -1, lat_local)]
+        for k in range(1, lat_count):
+            pairs = [[i, i ^ k] for i in range(lat_count) if i < i ^ k]
+            piece = pieces[k].reshape(-1, lat_local)
+            moved.append(lax.all_gather(piece, "lat", axis_index_groups=pairs))
+    second = None
+    if len(bounds) > 1:
+        outgoing = neighbours(zonal(1, slot_grid, 1)[0], per_member)
+        second = exchanged(copy_parents(offsets, *outgoing, tokens))
     spectra, _ = forward_transform(
         (own_waves, per_member), 0, block, received, even, odd, mem_local, []
     )
-    *outs, token = inverse_transform(
-        own_waves, offsets, 0, block, *neighbours(spectra, 1), noise, even, odd, None
-    )
-    later += [exchanged(copied(at, [token])) for at in range(2, len(bounds))]
-    for (start, _), received in zip(bounds[1:], later):
-        outs = finish_transform(own_waves, start, block, received, noise, even, odd, outs)
+    outs = inverse(0, spectra, None)
+    if len(bounds) > 2:
+        start = bounds[2][0]
+        if in_pairs:
+            spectra = paired_transform(
+                own_waves, start, place, moved, even, odd, mem_local, per_member
+            )
+        else:
+            spectra, _ = forward_transform(
+                (own_waves, per_member),
+                start,
+                block,
+                exchanged(zonal(2, slot_grid, 1)[0]),
+                even,
+                odd,
+                mem_local,
+                [],
+            )
+        outs = inverse(start, spectra, outs)
+    if second is not None:
+        outs = finish_transform(own_waves, bounds[1][0], block, second, noise, even, odd, outs)
     return tuple(outs)
 
 

time: 168 us -> 204 us (1.21)
  blocking collectives: 0 us -> 51.1 us
  waiting for transfers between devices: 48.3 us -> 39.9 us
  Pallas kernels: 76 us -> 71 us
    all_gather x0 -> x7, blocking collectives: none -> 51.1 us  [per_device(): moved.append(lax.all_gather(piece, 'lat', axis_index_groups=pairs))]
    ppermute x3, waiting for transfers between devices: 33.4 us -> 12.8 us  [neighbours(): lax.ppermute(rows[:, rows.shape[1] - SPREAD * per_member:], 'member', upw...]
    all_to_all x3 -> x2, waiting for transfers between devices: 6.1 us -> 22.4 us  [exchanged(): lax.all_to_all(outgoing, 'lat', split_axis=0, concat_axis=0, tiled=True)]
    pallas_call x2 -> x1, Pallas kernels: 16.6 us -> 10.3 us  [finish_transform(): pl.pallas_call(functools.partial(finish_kernel, first, block), grid_spec=...]
    all_to_all x3 -> x2, starting transfers between devices: 16.2 us -> 11.1 us  [exchanged(): lax.all_to_all(outgoing, 'lat', split_axis=0, concat_axis=0, tiled=True)]
    ppermute x3, starting transfers between devices: 12.3 us -> 16.7 us  [neighbours(): lax.ppermute(rows[:, rows.shape[1] - SPREAD * per_member:], 'member', upw...]
    pallas_call x2 -> x1, Pallas kernels: 9.59 us -> 5.42 us  [copy_parents(): pl.pallas_call(copy_kernel, grid_spec=pltpu.PrefetchScalarGridSpec(num_sc...]
    ppermute x3, waiting for transfers between devices: 8.8 us -> 4.7 us  [neighbours(): high = lax.ppermute(rows[:, :SPREAD * per_member], 'member', downward)]
  transfers between devices with their start and end apart: 9 -> 8, of which waited for: 7 -> 3; matrix products, arithmetic and copies ran while one was open for 2% -> 2% of each run, Pallas kernels for 36% -> 24%
where the time goes in v12:
time: 204 us; the launch traced here: 203 us
  Pallas kernels  71 us (35%)
  blocking collectives  51.1 us (25%)
  waiting for transfers between devices  39.9 us (20%)
  starting transfers between devices  33.6 us (16%)
  local copies, waits for them, and re-layouts  3.6 us (2%)
  other arithmetic  2.89 us (1%)
    all_gather x7, blocking collectives, per_device(): moved.append(lax.all_gather(piece, 'lat', axis_index_groups=pairs))  51.1 us
    pallas_call x3, Pallas kernels, zonal_transform(): pl.pallas_call(functools.partial(zonal_kernel, truncation, len(tokens)),...  29.6 us
    all_to_all x2, waiting for transfers between devices, exchanged(): lax.all_to_all(outgoing, 'lat', split_axis=0, concat_axis=0, tiled=True)  22.4 us
    ppermute x3, starting transfers between devices, neighbours(): lax.ppermute(rows[:, rows.shape[1] - SPREAD * per_member:], 'member', upw...  16.7 us
    pallas_call x2, Pallas kernels, inverse_transform(): pl.pallas_call(functools.partial(inverse_kernel, first, block), grid_spec...  13.3 us
    ppermute x3, waiting for transfers between devices, neighbours(): lax.ppermute(rows[:, rows.shape[1] - SPREAD * per_member:], 'member', upw...  12.8 us
    all_to_all x2, starting transfers between devices, exchanged(): lax.all_to_all(outgoing, 'lat', split_axis=0, concat_axis=0, tiled=True)  11.1 us
    pallas_call x1, Pallas kernels, finish_transform(): pl.pallas_call(functools.partial(finish_kernel, first, block), grid_spec=...  10.3 us
  transfers between devices with their start and end apart: 8, of which 3 were waited for; matrix products, arithmetic and copies ran while one was open for 2% of the time, Pallas kernels for 24%

profile of v12, /device:TPU:1, one launch (start us, length us, event | category | flops | bytes accessed | tf_op | source)
XLA Modules:
  0.0 203.0 jit_solution(8493221400765377827)
XLA Ops:
  0.6 0.8 reshape.50
  1.4 0.1 reshape.67.waves
  1.5 12.8 %zonal.5 = bf16[384,32,128]{2,1,0:T(8,128)(2,1)} custom-call(s32[384,1]{1,0:T(8,128)S(1)} %reshape.67.waves, bf16[2,8,128,2048]{3,2,1,0:T(8,128)(2,1)} %velocity.5, bf16[2,8,128,2048]{3,2,1,0:T(8,128)(2,1)} %tracer.5), custom_call_target="tpu_custom_call" | custom-call | flops 6442450944 | bytes 19922944 | tf_op jit(solution)/shard_map/zonal/pallas_call | solution.py:179
  14.3 6.4 %all-to-all-start.1 = ((bf16[8,1536,128]{2,1,0:T(8,128)(2,1)}), bf16[8,1536,128]{2,1,0:T(8,128)(2,1)}, u32[]{:S(2)}, u32[]{:S(2)}) async-start(bf16[8,1536,128]{2,1,0:T(8,128)(2,1)} %bitcast.15), calls=%async_computation.1 | async-start | bytes 6291456 | tf_op jit(solution)/shard_map/all_to_all | solution.py:545
  20.7 0.1 slice.9
  20.8 0.1 reshape.65.waves
  20.9 9.2 %zonal.3.own = bf16[256,32,128]{2,1,0:T(8,128)(2,1)} custom-call(s32[256,1]{1,0:T(8,128)S(1)} %reshape.65.waves, bf16[2,8,128,2048]{3,2,1,0:T(8,128)(2,1)} %velocity.5, bf16[2,8,128,2048]{3,2,1,0:T(8,128)(2,1)} %tracer.5), custom_call_target="tpu_custom_call" | custom-call | flops 4294967296 | bytes 18874368 | tf_op jit(solution)/shard_map/zonal/pallas_call | solution.py:179
  30.1 4.0 %collective-permute-start = (bf16[256,32,128]{2,1,0:T(8,128)(2,1)}, bf16[256,32,128]{2,1,0:T(8,128)(2,1)S(1)}, u32[]{:S(2)}, u32[]{:S(2)}) collective-permute-start(bf16[256,32,128]{2,1,0:T(8,128)(2,1)} %zonal.3.own), channel_id=1, source_target_pairs={{0,8},{8,16},{16,24},{1,9},{9,17},{17,25},{2,10},{10,18},{18,26},{... | collective-permute-start | bytes 6291464 | tf_op jit(solution)/shard_map/ppermute | solution.py:539
  34.1 1.9 collective-permute-start.1
  36.0 0.6 gather_fusion
  36.6 0.1 slice.10
  36.7 0.1 reshape.66.waves
  36.7 7.7 %zonal.4 = (bf16[8,32,128]{2,1,0:T(8,128)(2,1)}, bf16[8,32,128]{2,1,0:T(8,128)(2,1)}, bf16[8,32,128]{2,1,0:T(8,128)(2,1)}, bf16[8,32,128]{2,1,0:T(8,128)(2,1)}, ...) custom-call(s32[64,1]{1,0:T(8,128)S(1)} %reshape.66.waves, ...), custom_call_target="tpu_custom_call" | custom-call | flops 1073741824 | bytes 17301504 | tf_op jit(solution)/shard_map/zonal/pallas_call | solution.py:179
  44.4 0.1 subtract_add_fusion.offsets
  44.5 12.8 %collective-permute-done.low = bf16[256,32,128]{2,1,0:T(8,128)(2,1)S(1)} collective-permute-done((bf16[256,32,128]{2,1,0:T(8,128)(2,1)}, bf16[256,32,128]{2,1,0:T(8,128)(2,1)S(1)}, u32[]{:S(2)}, u32[]{:S(2)}) %collective-permute-start) | collective-permute-done | bytes 2097184 | tf_op jit(solution)/shard_map/ppermute | solution.py:539
  57.3 4.7 %collective-permute-done.1.high = bf16[256,32,128]{2,1,0:T(8,128)(2,1)} collective-permute-done((bf16[256,32,128]{2,1,0:T(8,128)(2,1)}, bf16[256,32,128]{2,1,0:T(8,128)(2,1)}, u32[]{:S(2)}, u32[]{:S(2)}) %collective-permute-start.1) | collective-permute-done | bytes 2097184 | tf_op jit(solution)/shard_map/ppermute | solution.py:540
  62.0 0.8 copy-done.1
  62.9 5.4 %parents.1 = bf16[256,32,128]{2,1,0:T(8,128)(2,1)} custom-call(s32[2]{0:T(128)S(1)} %subtract_add_fusion.offsets, bf16[256,32,128]{2,1,0:T(8,128)(2,1)S(1)} %collective-permute-done.low, bf16[256,32,128]{2,1,0:T(8,128)(2,1)} %zonal.3.own, bf16[256,32,128]{2,1,0:T(8,128)(2,1)} %collective-permute-done.1.high, bf16[8,32,128]{2,1,0:T(8,128)(2,1)S(1)} %copy-done.1), custom_call_target="tpu_custom_call" | custom-call | bytes 8388608 | tf_op jit(solution)/shard_map/parents/pallas_call | solution.py:410
  68.3 22.4 %all-to-all-done.1.received = bf16[8,1536,128]{2,1,0:T(8,128)(2,1)} async-done(((bf16[8,1536,128]{2,1,0:T(8,128)(2,1)}), bf16[8,1536,128]{2,1,0:T(8,128)(2,1)}, u32[]{:S(2)}, u32[]{:S(2)}) %all-to-all-start.1) | async-done | bytes 3145760 | tf_op jit(solution)/shard_map/all_to_all | solution.py:545
  90.7 4.7 %all-to-all-start = ((bf16[8,1024,128]{2,1,0:T(8,128)(2,1)}), bf16[8,1024,128]{2,1,0:T(8,128)(2,1)}, u32[]{:S(2)}, u32[]{:S(2)}) async-start(bf16[8,1024,128]{2,1,0:T(8,128)(2,1)} %bitcast.14), calls=%async_computation | async-start | bytes 4194304 | tf_op jit(solution)/shard_map/all_to_all | solution.py:545
  95.3 0.1 fusion.9
  95.4 0.8 dynamic_slice.6.waves
  96.2 0.2 copy.21
  96.4 1.4 fusion.6
  97.8 1.3 sine_multiply_fusion
  99.1 1.8 tables.1
  101.0 0.0 copy-start.11
  101.0 8.9 %forward.1 = (bf16[48,2,16,683]{3,2,1,0:T(8,128)(2,1)}, f32[8,128]{1,0:T(8,128)}) custom-call(s32[88]{0:T(128)S(1)} %dynamic_slice.6.waves, bf16[8,1536,128]{2,1,0:T(8,128)(2,1)} %all-to-all-done.1.received, bf16[683,1024]{1,0:T(8,128)(2,1)S(1)} %get-tuple-element.18.refs_8_.even, bf16[683,1024]{1,0:T(8,128)(2,1)S(1)} %get-tuple-element.19.refs_9_.odd), custom_call_target="tpu_custom_call" | custom-call | flops 4297064448 | bytes 8041472 | tf_op jit(solution)/shard_map/forward/pallas_call | solution.py:227
  109.9 4.7 %collective-permute-start.4 = (bf16[48,2,16,683]{3,2,1,0:T(8,128)(2,1)}, bf16[48,2,16,683]{3,2,1,0:T(8,128)(2,1)S(1)}, u32[]{:S(2)}, u32[]{:S(2)}) collective-permute-start(bf16[48,2,16,683]{3,2,1,0:T(8,128)(2,1)} %get-tuple-element.27.own), channel_id=1, source_target_pairs={{0,8},{8,16},{16,24},{1,9},{9,17},{17,25},{2,10},{10,18},{18,26},{... | collective-permute-start | bytes 6294536 | tf_op jit(solution)/shard_map/ppermute | solution.py:539
  114.6 1.9 collective-permute-start.5
  116.6 6.6 %all_gather.21.refs_1_ = bf16[2,256,128]{2,1,0:T(8,128)(2,1)S(1)} all-gather(bf16[1,256,128]{2,1,0:T(8,128)(2,1)S(1)} %bitcast.23), channel_id=1, replica_groups={{0,1},{2,3},{4,5},{6,7},{8,9},{10,11},{12,13},{14,15},{16,17},{18,19},{..., dimensions={0}, use_global_device_ids=true | all-gather | bytes 196608 | tf_op jit(solution)/shard_map/all_gather | solution.py:570
  123.1 6.7 %all_gather.22.refs_2_ = bf16[2,256,128]{2,1,0:T(8,128)(2,1)S(1)} all-gather(bf16[1,256,128]{2,1,0:T(8,128)(2,1)S(1)} %bitcast.22), channel_id=1, replica_groups={{0,2},{1,3},{4,6},{5,7},{8,10},{9,11},{12,14},{13,15},{16,18},{17,19},{..., dimensions={0}, use_global_device_ids=true | all-gather | bytes 196608 | tf_op jit(solution)/shard_map/all_gather | solution.py:570
  129.9 5.5 %all_gather.23.refs_3_ = bf16[2,256,128]{2,1,0:T(8,128)(2,1)S(1)} all-gather(bf16[1,256,128]{2,1,0:T(8,128)(2,1)S(1)} %bitcast.21), channel_id=1, replica_groups={{0,3},{1,2},{4,7},{5,6},{8,11},{9,10},{12,15},{13,14},{16,19},{17,18},{..., dimensions={0}, use_global_device_ids=true | all-gather | bytes 196608 | tf_op jit(solution)/shard_map/all_gather | solution.py:570
  135.4 13.9 %all_gather.24.refs_4_ = bf16[2,256,128]{2,1,0:T(8,128)(2,1)S(1)} all-gather(bf16[1,256,128]{2,1,0:T(8,128)(2,1)S(1)} %bitcast.20), channel_id=1, replica_groups={{0,4},{1,5},{2,6},{3,7},{8,12},{9,13},{10,14},{11,15},{16,20},{17,21},{..., dimensions={0}, use_global_device_ids=true | all-gather | bytes 196608 | tf_op jit(solution)/shard_map/all_gather | solution.py:570
  149.3 5.6 %all_gather.25.refs_5_ = bf16[2,256,128]{2,1,0:T(8,128)(2,1)S(1)} all-gather(bf16[1,256,128]{2,1,0:T(8,128)(2,1)S(1)} %bitcast.19), channel_id=1, replica_groups={{0,5},{1,4},{2,7},{3,6},{8,13},{9,12},{10,15},{11,14},{16,21},{17,20},{..., dimensions={0}, use_global_device_ids=true | all-gather | bytes 196608 | tf_op jit(solution)/shard_map/all_gather | solution.py:570
  154.9 5.7 %all_gather.26.refs_6_ = bf16[2,256,128]{2,1,0:T(8,128)(2,1)S(1)} all-gather(bf16[1,256,128]{2,1,0:T(8,128)(2,1)S(1)} %bitcast.18), channel_id=1, replica_groups={{0,6},{1,7},{2,4},{3,5},{8,14},{9,15},{10,12},{11,13},{16,22},{17,23},{..., dimensions={0}, use_global_device_ids=true | all-gather | bytes 196608 | tf_op jit(solution)/shard_map/all_gather | solution.py:570
  160.6 7.1 %all_gather.27.refs_7_ = bf16[2,256,128]{2,1,0:T(8,128)(2,1)S(1)} all-gather(bf16[1,256,128]{2,1,0:T(8,128)(2,1)S(1)} %bitcast.17), channel_id=1, replica_groups={{0,7},{1,6},{2,5},{3,4},{8,15},{9,14},{10,13},{11,12},{16,23},{17,22},{..., dimensions={0}, use_global_device_ids=true | all-gather | bytes 196608 | tf_op jit(solution)/shard_map/all_gather | solution.py:570
  167.7 1.7 paired.1.own
  169.4 8.1 %collective-permute-start.2 = (bf16[8,2,16,683]{3,2,1,0:T(8,128)(2,1)S(1)}, bf16[8,2,16,683]{3,2,1,0:T(8,128)(2,1)S(1)}, u32[]{:S(2)}, u32[]{:S(2)}) collective-permute-start(bf16[8,2,16,683]{3,2,1,0:T(8,128)(2,1)S(1)} %paired.1.own), channel_id=1, source_target_pairs={{0,8},{8,16},{16,24},{1,9},{9,17},{17,25},{2,10},{10,18},{18,26},{... | collective-permute-start | bytes 1049096 | tf_op jit(solution)/shard_map/ppermute | solution.py:539
  177.5 1.9 collective-permute-start.3
  179.4 0.0 collective-permute-done.4.low
  179.4 0.0 collective-permute-done.5.high
  179.5 9.7 %inverse.2 = (bf16[88,2,2,8,683]{4,3,2,1,0:T(8,128)(2,1)}, bf16[88,2,2,8,1024]{4,3,2,1,0:T(8,128)(2,1)}, f32[8,128]{1,0:T(8,128)}) custom-call(s32[88]{0:T(128)S(1)} %dynamic_slice.6.waves, s32[2]{0:T(128)S(1)} %subtract_add_fusion.offsets, bf16[48,2,16,683]{3,2,1,0:T(8,128)(2,1)S(1)} %collective-permute-done.4.low, ...), custom_call_target="tpu_custom_call" | custom-call | flops 4297064448 | bytes 16434176 | tf_op jit(solution)/shard_map/inverse/pallas_call | solution.py:364
  189.2 0.0 collective-permute-done.2.low
  189.2 0.0 collective-permute-done.3.high
  189.2 3.5 %inverse.3 = (bf16[88,2,2,8,683]{4,3,2,1,0:T(8,128)(2,1)}, bf16[88,2,2,8,1024]{4,3,2,1,0:T(8,128)(2,1)}, f32[8,128]{1,0:T(8,128)}) custom-call(s32[88]{0:T(128)S(1)} %dynamic_slice.6.waves, s32[2]{0:T(128)S(1)} %subtract_add_fusion.offsets, bf16[8,2,16,683]{3,2,1,0:T(8,128)(2,1)S(1)} %collective-permute-done.2.low, ...), custom_call_target="tpu_custom_call", output_to_operand_aliasing={{0}: (8, {}), {1}: (9, {})} | custom-call | flops 716177408 | bytes 5070336 | tf_op jit(solution)/shard_map/inverse/pallas_call | solution.py:364
  192.7 0.0 all-to-all-done.received
  192.7 10.3 %finish.1 = (bf16[88,2,2,8,683]{4,3,2,1,0:T(8,128)(2,1)}, bf16[88,2,2,8,1024]{4,3,2,1,0:T(8,128)(2,1)}) custom-call(s32[88]{0:T(128)S(1)} %dynamic_slice.6.waves, bf16[8,1024,128]{2,1,0:T(8,128)(2,1)} %all-to-all-done.received, bf16[88,2,2,8,683]{4,3,2,1,0:T(8,128)(2,1)} %noise.5, ...), custom_call_target="tpu_custom_call", output_to_operand_aliasing={{0}: (5, {}), {1}: (6, {})} | custom-call | flops 5729419264 | bytes 9789440 | tf_op jit(solution)/shard_map/finish/pallas_call | solution.py:480
  (27 shorter events, 0.1 us)
Async XLA Ops:
  14.3 76.3 %all-to-all-start.1 = ((bf16[8,1536,128]{2,1,0:T(8,128)(2,1)}), bf16[8,1536,128]{2,1,0:T(8,128)(2,1)}, u32[]{:S(2)}, u32[]{:S(2)}) async-start(bf16[8,1536,128]{2,1,0:T(8,128)(2,1)} %bitcast.15), calls=%async_computation.1 | async-start | bytes 6291456 | tf_op jit(solution)/shard_map/all_to_all | solution.py:545
  30.1 27.2 %collective-permute-start = (bf16[256,32,128]{2,1,0:T(8,128)(2,1)}, bf16[256,32,128]{2,1,0:T(8,128)(2,1)S(1)}, u32[]{:S(2)}, u32[]{:S(2)}) collective-permute-start(bf16[256,32,128]{2,1,0:T(8,128)(2,1)} %zonal.3.own), channel_id=1, source_target_pairs={{0,8},{8,16},{16,24},{1,9},{9,17},{17,25},{2,10},{10,18},{18,26},{... | collective-permute-start | bytes 6291464 | tf_op jit(solution)/shard_map/ppermute | solution.py:539
  34.1 28.0 %collective-permute-start.1 = (bf16[256,32,128]{2,1,0:T(8,128)(2,1)}, bf16[256,32,128]{2,1,0:T(8,128)(2,1)}, u32[]{:S(2)}, u32[]{:S(2)}) collective-permute-start(bf16[256,32,128]{2,1,0:T(8,128)(2,1)} %zonal.3.own), channel_id=1, source_target_pairs={{8,0},{16,8},{24,16},{9,1},{17,9},{25,17},{10,2},{18,10},{26,18},{... | collective-permute-start | bytes 6291464 | tf_op jit(solution)/shard_map/ppermute | solution.py:540
  36.7 7.7 %copy-start.10 = (s32[8]{0:T(128)S(1)}, s32[8]{0:T(128)}, u32[]{:S(2)}) copy-start(s32[8]{0:T(128)} %param.9) | copy-start | bytes 100
  62.0 0.8 copy-start.1
  90.7 102.1 %all-to-all-start = ((bf16[8,1024,128]{2,1,0:T(8,128)(2,1)}), bf16[8,1024,128]{2,1,0:T(8,128)(2,1)}, u32[]{:S(2)}, u32[]{:S(2)}) async-start(bf16[8,1024,128]{2,1,0:T(8,128)(2,1)} %bitcast.14), calls=%async_computation | async-start | bytes 4194304 | tf_op jit(solution)/shard_map/all_to_all | solution.py:545
  100.9 15.7 %copy-start.9 = (bf16[8,32,128]{2,1,0:T(8,128)(2,1)S(1)}, bf16[8,32,128]{2,1,0:T(8,128)(2,1)}, u32[]{:S(2)}) copy-start(bf16[8,32,128]{2,1,0:T(8,128)(2,1)} %get-tuple-element.20) | copy-start | bytes 196612
  100.9 22.2 %copy-start.8 = (bf16[8,32,128]{2,1,0:T(8,128)(2,1)S(1)}, bf16[8,32,128]{2,1,0:T(8,128)(2,1)}, u32[]{:S(2)}) copy-start(bf16[8,32,128]{2,1,0:T(8,128)(2,1)} %get-tuple-element.21) | copy-start | bytes 196612
  100.9 28.9 %copy-start.7 = (bf16[8,32,128]{2,1,0:T(8,128)(2,1)S(1)}, bf16[8,32,128]{2,1,0:T(8,128)(2,1)}, u32[]{:S(2)}) copy-start(bf16[8,32,128]{2,1,0:T(8,128)(2,1)} %get-tuple-element.22) | copy-start | bytes 196612
  100.9 34.5 %copy-start.6 = (bf16[8,32,128]{2,1,0:T(8,128)(2,1)S(1)}, bf16[8,32,128]{2,1,0:T(8,128)(2,1)}, u32[]{:S(2)}) copy-start(bf16[8,32,128]{2,1,0:T(8,128)(2,1)} %get-tuple-element.23) | copy-start | bytes 196612
  100.9 48.4 %copy-start.5 = (bf16[8,32,128]{2,1,0:T(8,128)(2,1)S(1)}, bf16[8,32,128]{2,1,0:T(8,128)(2,1)}, u32[]{:S(2)}) copy-start(bf16[8,32,128]{2,1,0:T(8,128)(2,1)} %get-tuple-element.24) | copy-start | bytes 196612
  100.9 53.9 %copy-start.4 = (bf16[8,32,128]{2,1,0:T(8,128)(2,1)S(1)}, bf16[8,32,128]{2,1,0:T(8,128)(2,1)}, u32[]{:S(2)}) copy-start(bf16[8,32,128]{2,1,0:T(8,128)(2,1)} %get-tuple-element.25) | copy-start | bytes 196612
  101.0 59.6 %copy-start.3 = (bf16[8,32,128]{2,1,0:T(8,128)(2,1)S(1)}, bf16[8,32,128]{2,1,0:T(8,128)(2,1)}, u32[]{:S(2)}) copy-start(bf16[8,32,128]{2,1,0:T(8,128)(2,1)} %get-tuple-element.26) | copy-start | bytes 196612
  101.0 66.7 %copy-start.11 = (s32[8]{0:T(128)S(1)}, s32[8]{0:T(128)}, u32[]{:S(2)}) copy-start(s32[8]{0:T(128)} %constant.57.clone) | copy-start | bytes 100
  101.0 66.7 %copy-start.2 = (bf16[8,32,128]{2,1,0:T(8,128)(2,1)S(1)}, bf16[8,32,128]{2,1,0:T(8,128)(2,1)}, u32[]{:S(2)}) copy-start(bf16[8,32,128]{2,1,0:T(8,128)(2,1)} %get-tuple-element.17.rest_0_) | copy-start | bytes 196612
  109.9 69.5 %collective-permute-start.4 = (bf16[48,2,16,683]{3,2,1,0:T(8,128)(2,1)}, bf16[48,2,16,683]{3,2,1,0:T(8,128)(2,1)S(1)}, u32[]{:S(2)}, u32[]{:S(2)}) collective-permute-start(bf16[48,2,16,683]{3,2,1,0:T(8,128)(2,1)} %get-tuple-element.27.own), channel_id=1, source_target_pairs={{0,8},{8,16},{16,24},{1,9},{9,17},{17,25},{2,10},{10,18},{18,26},{... | collective-permute-start | bytes 6294536 | tf_op jit(solution)/shard_map/ppermute | solution.py:539
  114.6 64.8 %collective-permute-start.5 = (bf16[48,2,16,683]{3,2,1,0:T(8,128)(2,1)}, bf16[48,2,16,683]{3,2,1,0:T(8,128)(2,1)S(1)}, u32[]{:S(2)}, u32[]{:S(2)}) collective-permute-start(bf16[48,2,16,683]{3,2,1,0:T(8,128)(2,1)} %get-tuple-element.27.own), channel_id=1, source_target_pairs={{8,0},{16,8},{24,16},{9,1},{17,9},{25,17},{10,2},{18,10},{26,18},{... | collective-permute-start | bytes 6294536 | tf_op jit(solution)/shard_map/ppermute | solution.py:540
  169.4 19.8 %copy-start = (bf16[8,2,16,683]{3,2,1,0:T(8,128)(2,1)}, bf16[8,2,16,683]{3,2,1,0:T(8,128)(2,1)S(1)}, u32[]{:S(2)}) copy-start(bf16[8,2,16,683]{3,2,1,0:T(8,128)(2,1)S(1)} %paired.1.own) | copy-start | bytes 1049092
  169.4 19.8 %collective-permute-start.2 = (bf16[8,2,16,683]{3,2,1,0:T(8,128)(2,1)S(1)}, bf16[8,2,16,683]{3,2,1,0:T(8,128)(2,1)S(1)}, u32[]{:S(2)}, u32[]{:S(2)}) collective-permute-start(bf16[8,2,16,683]{3,2,1,0:T(8,128)(2,1)S(1)} %paired.1.own), channel_id=1, source_target_pairs={{0,8},{8,16},{16,24},{1,9},{9,17},{17,25},{2,10},{10,18},{18,26},{... | collective-permute-start | bytes 1049096 | tf_op jit(solution)/shard_map/ppermute | solution.py:539
  177.5 11.7 %collective-permute-start.3 = (bf16[8,2,16,683]{3,2,1,0:T(8,128)(2,1)S(1)}, bf16[8,2,16,683]{3,2,1,0:T(8,128)(2,1)S(1)}, u32[]{:S(2)}, u32[]{:S(2)}) collective-permute-start(bf16[8,2,16,683]{3,2,1,0:T(8,128)(2,1)S(1)} %paired.1.own), channel_id=1, source_target_pairs={{8,0},{16,8},{24,16},{9,1},{17,9},{25,17},{10,2},{18,10},{26,18},{... | collective-permute-start | bytes 1049096 | tf_op jit(solution)/shard_map/ppermute | solution.py:540

commit v13 on v10

--- a/solution.py
+++ b/solution.py
@@ -86,14 +86,29 @@
     wave = waves[...]
     weight = jnp.where(wave < truncation, 1.0 / math.sqrt(longitudes), 0.0)
 
-    def angles(count, stride):
+    def cos_sin(count, stride):
         points = lax.broadcasted_iota(jnp.int32, (rows, count), 1) * stride
         phase = lax.rem(wave * points, jnp.full((), longitudes, jnp.int32))
-        return phase.astype(jnp.float32) * (2.0 * math.pi / longitudes)
-
-    coarse, fine = angles(longitudes // LANES, LANES), angles(LANES, 1)
-    cos_c, sin_c = jnp.cos(coarse) * weight, jnp.sin(coarse) * weight
-    cos_f, sin_f = jnp.cos(fine), jnp.sin(fine)
+        quarter = longitudes // 4
+        turns = lax.div(phase + quarter // 2, jnp.full((), quarter, jnp.int32))
+        angle = (phase - turns * quarter).astype(jnp.float32) * (2.0 * math.pi / longitudes)
+        square = angle * angle
+        cos, sin = 1.0 / 40320, -1.0 / 5040
+        for power in (6, 4, 2, 0):
+            sign = -1.0 if power % 4 else 1.0
+            cos = cos * square + sign / math.factorial(power)
+        for power in (5, 3, 1):
+            sign = -1.0 if power % 4 == 3 else 1.0
+            sin = sin * square + sign / math.factorial(power)
+        sin = sin * angle
+        swap = turns % 2 == 1
+        cos, sin = jnp.where(swap, sin, cos), jnp.where(swap, cos, sin)
+        cos = jnp.where((turns == 1) | (turns == 2), -cos, cos)
+        sin = jnp.where((turns == 2) | (turns == 3), -sin, sin)
+        return cos, sin
+
+    (cos_c, sin_c), (cos_f, sin_f) = cos_sin(longitudes // LANES, LANES), cos_sin(LANES, 1)
+    cos_c, sin_c = cos_c * weight, sin_c * weight
     for at in range(longitudes // LANES):
         cos_a, sin_a = cos_c[:, at : at + 1], sin_c[:, at : at + 1]
         columns = slice(at * LANES, (at + 1) * LANES)

time: 166 us -> 166 us (level)
  transfers between devices with their start and end apart: 9 -> 9, of which waited for: 7 -> 7; matrix products, arithmetic and copies ran while one was open for 2% -> 2% of each run, Pallas kernels for 37% -> 36%
where the time goes in v13:
time: 166 us; the launch traced here: 163 us
  Pallas kernels  73.7 us (44%)
  waiting for transfers between devices  48.9 us (29%)
  starting transfers between devices  34.3 us (21%)
  other arithmetic  2.88 us (2%)
  local copies, waits for them, and re-layouts  2.12 us (1%)
    ppermute x3, waiting for transfers between devices, neighbours(): lax.ppermute(rows[:, rows.shape[1] - SPREAD * per_member:], 'member', upw...  33.4 us
    pallas_call x3, Pallas kernels, zonal_transform(): pl.pallas_call(functools.partial(zonal_kernel, truncation, len(tokens)),...  29.6 us
    all_to_all x3, starting transfers between devices, exchanged(): lax.all_to_all(outgoing, 'lat', split_axis=0, concat_axis=0, tiled=True)  16.2 us
    ppermute x3, starting transfers between devices, neighbours(): lax.ppermute(rows[:, rows.shape[1] - SPREAD * per_member:], 'member', upw...  12.3 us
    pallas_call x1, Pallas kernels, finish_transform(): pl.pallas_call(functools.partial(finish_kernel, first, block), grid_spec=...  12.2 us
    pallas_call x2, Pallas kernels, copy_parents(): pl.pallas_call(copy_kernel, grid_spec=pltpu.PrefetchScalarGridSpec(num_sc...  9.59 us
    pallas_call x1, Pallas kernels, inverse_transform(): pl.pallas_call(functools.partial(inverse_kernel, first, block), grid_spec...  9.27 us
    ppermute x3, waiting for transfers between devices, neighbours(): high = lax.ppermute(rows[:, :SPREAD * per_member], 'member', downward)  8.8 us
  transfers between devices with their start and end apart: 9, of which 7 were waited for; matrix products, arithmetic and copies ran while one was open for 2% of the time, Pallas kernels for 36%

profile of v13, /device:TPU:1, one launch (start us, length us, event | category | flops | bytes accessed | tf_op | source)
XLA Modules:
  0.0 162.8 jit_solution(2376374253598802078)
XLA Ops:
  0.6 0.8 reshape.34
  1.4 0.1 fusion.13
  1.5 0.1 reshape.42.waves
  1.6 11.0 %zonal.4 = bf16[320,32,128]{2,1,0:T(8,128)(2,1)} custom-call(s32[320,1]{1,0:T(8,128)S(1)} %reshape.42.waves, bf16[2,8,128,2048]{3,2,1,0:T(8,128)(2,1)} %velocity.5, bf16[2,8,128,2048]{3,2,1,0:T(8,128)(2,1)} %tracer.5), custom_call_target="tpu_custom_call" | custom-call | flops 5368709120 | bytes 19398656 | tf_op jit(solution)/shard_map/zonal/pallas_call | solution.py:171
  12.5 6.4 %all-to-all-start = ((bf16[8,1280,128]{2,1,0:T(8,128)(2,1)}), bf16[8,1280,128]{2,1,0:T(8,128)(2,1)}, u32[]{:S(2)}, u32[]{:S(2)}) async-start(bf16[8,1280,128]{2,1,0:T(8,128)(2,1)} %bitcast.4), calls=%async_computation | async-start | bytes 5242880 | tf_op jit(solution)/shard_map/all_to_all | solution.py:548
  18.9 0.1 reshape.43.waves
  19.0 0.0 copy-start
  19.1 11.0 %zonal.5.own = bf16[320,32,128]{2,1,0:T(8,128)(2,1)} custom-call(s32[320,1]{1,0:T(8,128)S(1)} %reshape.43.waves, bf16[2,8,128,2048]{3,2,1,0:T(8,128)(2,1)} %velocity.5, bf16[2,8,128,2048]{3,2,1,0:T(8,128)(2,1)} %tracer.5), custom_call_target="tpu_custom_call" | custom-call | flops 5368709120 | bytes 19398656 | tf_op jit(solution)/shard_map/zonal/pallas_call | solution.py:171
  30.0 4.0 %collective-permute-start.4 = (bf16[320,32,128]{2,1,0:T(8,128)(2,1)}, bf16[320,32,128]{2,1,0:T(8,128)(2,1)S(1)}, u32[]{:S(2)}, u32[]{:S(2)}) collective-permute-start(bf16[320,32,128]{2,1,0:T(8,128)(2,1)} %zonal.5.own), channel_id=1, source_target_pairs={{0,8},{8,16},{16,24},{1,9},{9,17},{17,25},{2,10},{10,18},{18,26},{... | collective-permute-start | bytes 7864328 | tf_op jit(solution)/shard_map/ppermute | solution.py:542
  34.0 1.9 %collective-permute-start.5 = (bf16[320,32,128]{2,1,0:T(8,128)(2,1)}, bf16[320,32,128]{2,1,0:T(8,128)(2,1)}, u32[]{:S(2)}, u32[]{:S(2)}) collective-permute-start(bf16[320,32,128]{2,1,0:T(8,128)(2,1)} %zonal.5.own), channel_id=1, source_target_pairs={{8,0},{16,8},{24,16},{9,1},{17,9},{25,17},{10,2},{18,10},{26,18},{... | collective-permute-start | bytes 7864328 | tf_op jit(solution)/shard_map/ppermute | solution.py:543
  35.9 0.0 copy-done
  35.9 0.1 subtract_add_fusion.offsets
  36.0 26.9 %collective-permute-done.4.low = bf16[320,32,128]{2,1,0:T(8,128)(2,1)S(1)} collective-permute-done((bf16[320,32,128]{2,1,0:T(8,128)(2,1)}, bf16[320,32,128]{2,1,0:T(8,128)(2,1)S(1)}, u32[]{:S(2)}, u32[]{:S(2)}) %collective-permute-start.4) | collective-permute-done | bytes 2621472 | tf_op jit(solution)/shard_map/ppermute | solution.py:542
  62.9 4.4 %collective-permute-done.5.high = bf16[320,32,128]{2,1,0:T(8,128)(2,1)} collective-permute-done((bf16[320,32,128]{2,1,0:T(8,128)(2,1)}, bf16[320,32,128]{2,1,0:T(8,128)(2,1)}, u32[]{:S(2)}, u32[]{:S(2)}) %collective-permute-start.5) | collective-permute-done | bytes 2621472 | tf_op jit(solution)/shard_map/ppermute | solution.py:543
  67.3 5.7 %parents.3 = bf16[320,32,128]{2,1,0:T(8,128)(2,1)} custom-call(s32[2]{0:T(128)S(1)} %subtract_add_fusion.offsets, bf16[320,32,128]{2,1,0:T(8,128)(2,1)S(1)} %collective-permute-done.4.low, bf16[320,32,128]{2,1,0:T(8,128)(2,1)} %zonal.5.own, bf16[320,32,128]{2,1,0:T(8,128)(2,1)} %collective-permute-done.5.high), custom_call_target="tpu_custom_call" | custom-call | bytes 10485760 | tf_op jit(solution)/shard_map/parents/pallas_call | solution.py:355
  73.0 4.6 %all-to-all-done.received = bf16[8,1280,128]{2,1,0:T(8,128)(2,1)} async-done(((bf16[8,1280,128]{2,1,0:T(8,128)(2,1)}), bf16[8,1280,128]{2,1,0:T(8,128)(2,1)}, u32[]{:S(2)}, u32[]{:S(2)}) %all-to-all-start) | async-done | bytes 2621472 | tf_op jit(solution)/shard_map/all_to_all | solution.py:548
  77.6 4.7 %all-to-all-start.2 = ((bf16[8,1280,128]{2,1,0:T(8,128)(2,1)}), bf16[8,1280,128]{2,1,0:T(8,128)(2,1)}, u32[]{:S(2)}, u32[]{:S(2)}) async-start(bf16[8,1280,128]{2,1,0:T(8,128)(2,1)} %bitcast.3), calls=%async_computation.2 | async-start | bytes 5242880 | tf_op jit(solution)/shard_map/all_to_all | solution.py:548
  82.3 0.8 dynamic_slice.6.waves
  83.1 0.1 fusion.9
  83.2 0.2 copy.17
  83.4 1.4 fusion.6
  84.8 1.3 sine_multiply_fusion
  86.1 1.8 %tables.1 = (bf16[683,1024]{1,0:T(8,128)(2,1)S(1)}, bf16[683,1024]{1,0:T(8,128)(2,1)S(1)}) custom-call(f32[683,8]{1,0:T(8,128)S(1)} %get-tuple-element.19.cos_c, f32[683,8]{1,0:T(8,128)S(1)} %get-tuple-element.18.sin_c, f32[683,128]{1,0:T(8,128)S(1)} %get-tuple-element.23.cos_f, f32[683,128]{1,0:T(8,128)S(1)} %get-tuple-element.22.sin_f), custom_call_target="tpu_custom_call" | custom-call | flops 4196352 | bytes 2797568 | tf_op jit(solution)/shard_map/tables/pallas_call | solution.py:53
  87.9 7.8 %forward.1 = (bf16[40,2,16,683]{3,2,1,0:T(8,128)(2,1)}, f32[8,128]{1,0:T(8,128)}) custom-call(s32[88]{0:T(128)S(1)} %dynamic_slice.6.waves, bf16[8,1280,128]{2,1,0:T(8,128)(2,1)} %all-to-all-done.received, bf16[683,1024]{1,0:T(8,128)(2,1)S(1)} %get-tuple-element.10.even, bf16[683,1024]{1,0:T(8,128)(2,1)S(1)} %get-tuple-element.11.odd), custom_call_target="tpu_custom_call" | custom-call | flops 3580887040 | bytes 7167488 | tf_op jit(solution)/shard_map/forward/pallas_call | solution.py:219
  95.7 4.7 %collective-permute-start.2 = (bf16[40,2,16,683]{3,2,1,0:T(8,128)(2,1)}, bf16[40,2,16,683]{3,2,1,0:T(8,128)(2,1)}, u32[]{:S(2)}, u32[]{:S(2)}) collective-permute-start(bf16[40,2,16,683]{3,2,1,0:T(8,128)(2,1)} %get-tuple-element.12.own), channel_id=1, source_target_pairs={{0,8},{8,16},{16,24},{1,9},{9,17},{17,25},{2,10},{10,18},{18,26},{... | collective-permute-start | bytes 5245448 | tf_op jit(solution)/shard_map/ppermute | solution.py:542
  100.4 1.9 %collective-permute-start.3 = (bf16[40,2,16,683]{3,2,1,0:T(8,128)(2,1)}, bf16[40,2,16,683]{3,2,1,0:T(8,128)(2,1)}, u32[]{:S(2)}, u32[]{:S(2)}) collective-permute-start(bf16[40,2,16,683]{3,2,1,0:T(8,128)(2,1)} %get-tuple-element.12.own), channel_id=1, source_target_pairs={{8,0},{16,8},{24,16},{9,1},{17,9},{25,17},{10,2},{18,10},{26,18},{... | collective-permute-start | bytes 5245448 | tf_op jit(solution)/shard_map/ppermute | solution.py:543
  102.4 0.1 slice.9
  102.4 0.1 reshape.41.waves
  102.5 7.7 %zonal.3.own = bf16[64,32,128]{2,1,0:T(8,128)(2,1)} custom-call(s32[64,1]{1,0:T(8,128)S(1)} %reshape.41.waves, bf16[2,8,128,2048]{3,2,1,0:T(8,128)(2,1)} %velocity.5, bf16[2,8,128,2048]{3,2,1,0:T(8,128)(2,1)} %tracer.5), custom_call_target="tpu_custom_call" | custom-call | flops 1073741824 | bytes 17301504 | tf_op jit(solution)/shard_map/zonal/pallas_call | solution.py:171
  110.2 3.6 %collective-permute-start = (bf16[64,32,128]{2,1,0:T(8,128)(2,1)}, bf16[64,32,128]{2,1,0:T(8,128)(2,1)S(1)}, u32[]{:S(2)}, u32[]{:S(2)}) collective-permute-start(bf16[64,32,128]{2,1,0:T(8,128)(2,1)} %zonal.3.own), channel_id=1, source_target_pairs={{0,8},{8,16},{16,24},{1,9},{9,17},{17,25},{2,10},{10,18},{18,26},{... | collective-permute-start | bytes 1572872 | tf_op jit(solution)/shard_map/ppermute | solution.py:542
  113.9 1.9 %collective-permute-start.1 = (bf16[64,32,128]{2,1,0:T(8,128)(2,1)}, bf16[64,32,128]{2,1,0:T(8,128)(2,1)S(1)}, u32[]{:S(2)}, u32[]{:S(2)}) collective-permute-start(bf16[64,32,128]{2,1,0:T(8,128)(2,1)} %zonal.3.own), channel_id=1, source_target_pairs={{8,0},{16,8},{24,16},{9,1},{17,9},{25,17},{10,2},{18,10},{26,18},{... | collective-permute-start | bytes 1572872 | tf_op jit(solution)/shard_map/ppermute | solution.py:543
  115.8 6.5 %collective-permute-done.2.low = bf16[40,2,16,683]{3,2,1,0:T(8,128)(2,1)} collective-permute-done((bf16[40,2,16,683]{3,2,1,0:T(8,128)(2,1)}, bf16[40,2,16,683]{3,2,1,0:T(8,128)(2,1)}, u32[]{:S(2)}, u32[]{:S(2)}) %collective-permute-start.2) | collective-permute-done | bytes 1748512 | tf_op jit(solution)/shard_map/ppermute | solution.py:542
  122.3 4.4 %collective-permute-done.3.high = bf16[40,2,16,683]{3,2,1,0:T(8,128)(2,1)} collective-permute-done((bf16[40,2,16,683]{3,2,1,0:T(8,128)(2,1)}, bf16[40,2,16,683]{3,2,1,0:T(8,128)(2,1)}, u32[]{:S(2)}, u32[]{:S(2)}) %collective-permute-start.3) | collective-permute-done | bytes 1748512 | tf_op jit(solution)/shard_map/ppermute | solution.py:543
  126.7 9.3 %inverse.1 = (bf16[88,2,2,8,683]{4,3,2,1,0:T(8,128)(2,1)}, bf16[88,2,2,8,1024]{4,3,2,1,0:T(8,128)(2,1)}, f32[8,128]{1,0:T(8,128)S(1)}) custom-call(s32[88]{0:T(128)S(1)} %dynamic_slice.6.waves, s32[2]{0:T(128)S(1)} %subtract_add_fusion.offsets, bf16[40,2,16,683]{3,2,1,0:T(8,128)(2,1)} %collective-permute-done.2.low, ...), custom_call_target="tpu_custom_call" | custom-call | flops 3580887040 | bytes 14161408 | tf_op jit(solution)/shard_map/inverse/pallas_call | solution.py:309
  136.0 0.0 collective-permute-done.low
  136.0 0.0 collective-permute-done.1.high
  136.0 3.9 %parents.2 = bf16[64,32,128]{2,1,0:T(8,128)(2,1)} custom-call(s32[2]{0:T(128)S(1)} %subtract_add_fusion.offsets, bf16[64,32,128]{2,1,0:T(8,128)(2,1)S(1)} %collective-permute-done.low, bf16[64,32,128]{2,1,0:T(8,128)(2,1)} %zonal.3.own, bf16[64,32,128]{2,1,0:T(8,128)(2,1)S(1)} %collective-permute-done.1.high, f32[8,128]{1,0:T(8,128)S(1)} %get-tuple-element.13.rest_0_), custom_call_target="tpu_custom_call" | custom-call | bytes 2097152 | tf_op jit(solution)/shard_map/parents/pallas_call | solution.py:355
  139.8 0.8 all-to-all-done.2.received
  140.6 5.1 %all-to-all-start.1 = ((bf16[8,256,128]{2,1,0:T(8,128)(2,1)}), bf16[8,256,128]{2,1,0:T(8,128)(2,1)S(1)}, u32[]{:S(2)}, u32[]{:S(2)}) async-start(bf16[8,256,128]{2,1,0:T(8,128)(2,1)} %bitcast.5), calls=%async_computation.1 | async-start | bytes 1048576 | tf_op jit(solution)/shard_map/all_to_all | solution.py:548
  145.7 12.2 %finish.1 = (bf16[88,2,2,8,683]{4,3,2,1,0:T(8,128)(2,1)}, bf16[88,2,2,8,1024]{4,3,2,1,0:T(8,128)(2,1)}) custom-call(s32[88]{0:T(128)S(1)} %dynamic_slice.6.waves, bf16[8,1280,128]{2,1,0:T(8,128)(2,1)} %all-to-all-done.2.received, bf16[88,2,2,8,683]{4,3,2,1,0:T(8,128)(2,1)} %noise.5, ...), custom_call_target="tpu_custom_call", output_to_operand_aliasing={{0}: (5, {}), {1}: (6, {})} | custom-call | flops 7161774080 | bytes 11537408 | tf_op jit(solution)/shard_map/finish/pallas_call | solution.py:483
  157.9 1.3 all-to-all-done.1.received
  159.2 3.4 %last.1 = (bf16[88,2,2,8,683]{4,3,2,1,0:T(8,128)(2,1)}, bf16[88,2,2,8,1024]{4,3,2,1,0:T(8,128)(2,1)}) custom-call(s32[88]{0:T(128)S(1)} %dynamic_slice.6.waves, bf16[8,256,128]{2,1,0:T(8,128)(2,1)S(1)} %all-to-all-done.1.received, bf16[88,2,2,8,683]{4,3,2,1,0:T(8,128)(2,1)} %noise.5, ...), custom_call_target="tpu_custom_call", output_to_operand_aliasing={{0}: (5, {}), {1}: (6, {})} | custom-call | flops 1432354816 | bytes 4545536 | tf_op jit(solution)/shard_map/last/pallas_call | solution.py:443
  (2 shorter events, 0.0 us)
Async XLA Ops:
  12.5 65.1 %all-to-all-start = ((bf16[8,1280,128]{2,1,0:T(8,128)(2,1)}), bf16[8,1280,128]{2,1,0:T(8,128)(2,1)}, u32[]{:S(2)}, u32[]{:S(2)}) async-start(bf16[8,1280,128]{2,1,0:T(8,128)(2,1)} %bitcast.4), calls=%async_computation | async-start | bytes 5242880 | tf_op jit(solution)/shard_map/all_to_all | solution.py:548
  19.0 16.9 %copy-start = (s32[8]{0:T(128)S(1)}, s32[8]{0:T(128)}, u32[]{:S(2)}) copy-start(s32[8]{0:T(128)} %param.8) | copy-start | bytes 100
  30.0 32.9 %collective-permute-start.4 = (bf16[320,32,128]{2,1,0:T(8,128)(2,1)}, bf16[320,32,128]{2,1,0:T(8,128)(2,1)S(1)}, u32[]{:S(2)}, u32[]{:S(2)}) collective-permute-start(bf16[320,32,128]{2,1,0:T(8,128)(2,1)} %zonal.5.own), channel_id=1, source_target_pairs={{0,8},{8,16},{16,24},{1,9},{9,17},{17,25},{2,10},{10,18},{18,26},{... | collective-permute-start | bytes 7864328 | tf_op jit(solution)/shard_map/ppermute | solution.py:542
  34.0 33.3 %collective-permute-start.5 = (bf16[320,32,128]{2,1,0:T(8,128)(2,1)}, bf16[320,32,128]{2,1,0:T(8,128)(2,1)}, u32[]{:S(2)}, u32[]{:S(2)}) collective-permute-start(bf16[320,32,128]{2,1,0:T(8,128)(2,1)} %zonal.5.own), channel_id=1, source_target_pairs={{8,0},{16,8},{24,16},{9,1},{17,9},{25,17},{10,2},{18,10},{26,18},{... | collective-permute-start | bytes 7864328 | tf_op jit(solution)/shard_map/ppermute | solution.py:543
  77.6 63.0 %all-to-all-start.2 = ((bf16[8,1280,128]{2,1,0:T(8,128)(2,1)}), bf16[8,1280,128]{2,1,0:T(8,128)(2,1)}, u32[]{:S(2)}, u32[]{:S(2)}) async-start(bf16[8,1280,128]{2,1,0:T(8,128)(2,1)} %bitcast.3), calls=%async_computation.2 | async-start | bytes 5242880 | tf_op jit(solution)/shard_map/all_to_all | solution.py:548
  95.7 26.6 %collective-permute-start.2 = (bf16[40,2,16,683]{3,2,1,0:T(8,128)(2,1)}, bf16[40,2,16,683]{3,2,1,0:T(8,128)(2,1)}, u32[]{:S(2)}, u32[]{:S(2)}) collective-permute-start(bf16[40,2,16,683]{3,2,1,0:T(8,128)(2,1)} %get-tuple-element.12.own), channel_id=1, source_target_pairs={{0,8},{8,16},{16,24},{1,9},{9,17},{17,25},{2,10},{10,18},{18,26},{... | collective-permute-start | bytes 5245448 | tf_op jit(solution)/shard_map/ppermute | solution.py:542
  100.4 26.3 %collective-permute-start.3 = (bf16[40,2,16,683]{3,2,1,0:T(8,128)(2,1)}, bf16[40,2,16,683]{3,2,1,0:T(8,128)(2,1)}, u32[]{:S(2)}, u32[]{:S(2)}) collective-permute-start(bf16[40,2,16,683]{3,2,1,0:T(8,128)(2,1)} %get-tuple-element.12.own), channel_id=1, source_target_pairs={{8,0},{16,8},{24,16},{9,1},{17,9},{25,17},{10,2},{18,10},{26,18},{... | collective-permute-start | bytes 5245448 | tf_op jit(solution)/shard_map/ppermute | solution.py:543
  110.2 25.7 %collective-permute-start = (bf16[64,32,128]{2,1,0:T(8,128)(2,1)}, bf16[64,32,128]{2,1,0:T(8,128)(2,1)S(1)}, u32[]{:S(2)}, u32[]{:S(2)}) collective-permute-start(bf16[64,32,128]{2,1,0:T(8,128)(2,1)} %zonal.3.own), channel_id=1, source_target_pairs={{0,8},{8,16},{16,24},{1,9},{9,17},{17,25},{2,10},{10,18},{18,26},{... | collective-permute-start | bytes 1572872 | tf_op jit(solution)/shard_map/ppermute | solution.py:542
  113.9 22.1 %collective-permute-start.1 = (bf16[64,32,128]{2,1,0:T(8,128)(2,1)}, bf16[64,32,128]{2,1,0:T(8,128)(2,1)S(1)}, u32[]{:S(2)}, u32[]{:S(2)}) collective-permute-start(bf16[64,32,128]{2,1,0:T(8,128)(2,1)} %zonal.3.own), channel_id=1, source_target_pairs={{8,0},{16,8},{24,16},{9,1},{17,9},{25,17},{10,2},{18,10},{26,18},{... | collective-permute-start | bytes 1572872 | tf_op jit(solution)/shard_map/ppermute | solution.py:543
  140.6 18.6 %all-to-all-start.1 = ((bf16[8,256,128]{2,1,0:T(8,128)(2,1)}), bf16[8,256,128]{2,1,0:T(8,128)(2,1)S(1)}, u32[]{:S(2)}, u32[]{:S(2)}) async-start(bf16[8,256,128]{2,1,0:T(8,128)(2,1)} %bitcast.5), calls=%async_computation.1 | async-start | bytes 1048576 | tf_op jit(solution)/shard_map/all_to_all | solution.py:548

commit v14 on v13

--- a/solution.py
+++ b/solution.py
@@ -37,7 +37,8 @@
     return jnp.cos(coarse) * factor, jnp.sin(coarse) * factor, jnp.cos(fine), jnp.sin(fine)
 
 
-def tables_kernel(cos_c, sin_c, cos_f, sin_f, even, odd):
+def tables_kernel(cos_c, sin_c, cos_f, sin_f, even, odd, token):
+    token[...] = jnp.zeros_like(token)
     width = cos_f.shape[1]
     cos_b, sin_b = cos_f[...], sin_f[...]
     for at in range(cos_c.shape[1]):
@@ -52,7 +53,7 @@
     shape = pltpu.VMEM((truncation, starts.shape[0] * width), jnp.bfloat16)
     return pl.pallas_call(
         tables_kernel,
-        out_shape=[shape, shape],
+        out_shape=[shape, shape, jax.ShapeDtypeStruct(TOKEN, jnp.float32)],
         compiler_params=pltpu.CompilerParams(vmem_limit_bytes=VMEM_BYTES),
         cost_estimate=pl.CostEstimate(
             flops=6 * truncation * latitudes, bytes_accessed=4 * truncation * latitudes,
@@ -550,19 +551,37 @@
             moved = jnp.swapaxes(moved, 0, 1).reshape(1, -1, latitudes)
         return moved
 
-    def copied(at, tokens):
-        return copy_parents(offsets, *neighbours(zonal(at), per_member), tokens)
+    def exchanged_in_two(outgoing, token):
+        outgoing = outgoing.reshape(lat_count // 2, 2, -1, lat_local)
+        side = lat_index % 2
+        kept = lax.dynamic_index_in_dim(outgoing, side, 1, keepdims=False)
+        sent = lax.dynamic_index_in_dim(outgoing, 1 - side, 1, keepdims=False)
+        swapped = lax.ppermute(sent, "lat", [(i, i ^ 1) for i in range(lat_count)])
+        side = side + token[0, 0].astype(jnp.int32)
+        pair = jnp.where(side == 0, jnp.stack([kept, swapped], 1), jnp.stack([swapped, kept], 1))
+        groups = [list(range(first, lat_count, 2)) for first in range(2)]
+        moved = lax.all_to_all(
+            pair, "lat", split_axis=0, concat_axis=0, axis_index_groups=groups, tiled=True
+        )
+        return moved.reshape(lat_count, -1, lat_local)
 
     received = exchanged(zonal(0))
-    even, odd = meridional_tables(truncation, latitudes, starts, inner)
-    later = [exchanged(copied(1, []))] if len(bounds) > 1 else []
+    even, odd, made = meridional_tables(truncation, latitudes, starts, inner)
+    sides = [neighbours(zonal(at), per_member) for at in range(1, len(bounds))]
+    tokens = [made] + [part for low, _, high in sides[1:] for part in (low, high)]
+    later = [exchanged(copy_parents(offsets, *side, tokens)) for side in sides[:1]]
+    picked = [copy_parents(offsets, *side, []) for side in sides[1:]]
     spectra, _ = forward_transform(
         (own_waves, per_member), 0, block, received, even, odd, mem_local, []
     )
     *outs, token = inverse_transform(
         own_waves, offsets, 0, block, *neighbours(spectra, 1), noise, even, odd, None
     )
-    later += [exchanged(copied(at, [token])) for at in range(2, len(bounds))]
+    for outgoing in picked:
+        if lat_count % 2 == 0 and lat_local % LANES == 0:
+            later.append(exchanged_in_two(outgoing, token))
+        else:
+            later.append(exchanged(outgoing))
     for (start, stop), received in zip(bounds[1:], later):
         if stop - start == block:
             outs = last_transform(own_waves, start, received, noise, even, odd, outs)

time: 166 us -> 166 us (level)
  waiting for transfers between devices: 48.9 us -> 38.5 us
  local copies, waits for them, and re-layouts: 2.12 us -> 8.74 us
  other arithmetic: 2.88 us -> 4.77 us
  starting transfers between devices: 34.3 us -> 36.1 us
    ppermute x3, waiting for transfers between devices: 33.4 us -> 2.18 us  [neighbours(): lax.ppermute(rows[:, rows.shape[1] - SPREAD * per_member:], 'member', upw...]
    ppermute x3, waiting for transfers between devices: 8.8 us -> 26.6 us  [neighbours(): high = lax.ppermute(rows[:, :SPREAD * per_member], 'member', downward)]
    all_to_all x0 -> x1, starting transfers between devices: none -> 5.07 us  [exchanged_in_two(): lax.all_to_all(pair, 'lat', split_axis=0, concat_axis=0, axis_index_group...]
    unnamed x2 -> x14, local copies, waits for them, and re-layouts: 0.01 us -> 5.04 us
    all_to_all x3 -> x2, starting transfers between devices: 16.2 us -> 11.2 us  [exchanged(): lax.all_to_all(outgoing, 'lat', split_axis=0, concat_axis=0, tiled=True)]
    ppermute x3, starting transfers between devices: 5.76 us -> 9.14 us  [neighbours(): high = lax.ppermute(rows[:, :SPREAD * per_member], 'member', downward)]
    ppermute x3, starting transfers between devices: 12.3 us -> 8.96 us  [neighbours(): lax.ppermute(rows[:, rows.shape[1] - SPREAD * per_member:], 'member', upw...]
    all_to_all x0 -> x1, waiting for transfers between devices: none -> 1.95 us  [exchanged_in_two(): lax.all_to_all(pair, 'lat', split_axis=0, concat_axis=0, axis_index_group...]
  transfers between devices with their start and end apart: 9 -> 10, of which waited for: 7 -> 7; matrix products, arithmetic and copies ran while one was open for 2% -> 5% of each run, Pallas kernels for 36% -> 36%
where the time goes in v14:
time: 166 us; the launch traced here: 163 us
  Pallas kernels  73.6 us (44%)
  waiting for transfers between devices  38.5 us (23%)
  starting transfers between devices  36.1 us (22%)
  local copies, waits for them, and re-layouts  8.74 us (5%)
  other arithmetic  4.77 us (3%)
    pallas_call x3, Pallas kernels, zonal_transform(): pl.pallas_call(functools.partial(zonal_kernel, truncation, len(tokens)),...  29.6 us
    ppermute x3, waiting for transfers between devices, neighbours(): high = lax.ppermute(rows[:, :SPREAD * per_member], 'member', downward)  26.6 us
    pallas_call x1, Pallas kernels, finish_transform(): pl.pallas_call(functools.partial(finish_kernel, first, block), grid_spec=...  12.1 us
    all_to_all x2, starting transfers between devices, exchanged(): lax.all_to_all(outgoing, 'lat', split_axis=0, concat_axis=0, tiled=True)  11.2 us
    pallas_call x2, Pallas kernels, copy_parents(): pl.pallas_call(copy_kernel, grid_spec=pltpu.PrefetchScalarGridSpec(num_sc...  9.74 us
    pallas_call x1, Pallas kernels, inverse_transform(): pl.pallas_call(functools.partial(inverse_kernel, first, block), grid_spec...  9.25 us
    ppermute x3, starting transfers between devices, neighbours(): high = lax.ppermute(rows[:, :SPREAD * per_member], 'member', downward)  9.14 us
    ppermute x3, starting transfers between devices, neighbours(): lax.ppermute(rows[:, rows.shape[1] - SPREAD * per_member:], 'member', upw...  8.96 us
  transfers between devices with their start and end apart: 10, of which 7 were waited for; matrix products, arithmetic and copies ran while one was open for 5% of the time, Pallas kernels for 36%

profile of v14, /device:TPU:1, one launch (start us, length us, event | category | flops | bytes accessed | tf_op | source)
XLA Modules:
  0.0 163.3 jit_solution(5430051043119811031)
XLA Ops:
  0.6 0.8 reshape.38
  1.4 0.1 fusion.13
  1.5 0.1 reshape.46.waves
  1.6 11.0 %zonal.3 = bf16[320,32,128]{2,1,0:T(8,128)(2,1)} custom-call(s32[320,1]{1,0:T(8,128)S(1)} %reshape.46.waves, bf16[2,8,128,2048]{3,2,1,0:T(8,128)(2,1)} %velocity.5, bf16[2,8,128,2048]{3,2,1,0:T(8,128)(2,1)} %tracer.5), custom_call_target="tpu_custom_call" | custom-call | flops 5368709120 | bytes 19398656 | tf_op jit(solution)/shard_map/zonal/pallas_call | solution.py:172
  12.5 6.4 %all-to-all-start = ((bf16[8,1280,128]{2,1,0:T(8,128)(2,1)}), bf16[8,1280,128]{2,1,0:T(8,128)(2,1)}, u32[]{:S(2)}, u32[]{:S(2)}) async-start(bf16[8,1280,128]{2,1,0:T(8,128)(2,1)} %bitcast.10), calls=%async_computation | async-start | bytes 5242880 | tf_op jit(solution)/shard_map/all_to_all | solution.py:549
  18.9 0.1 reshape.48.waves
  19.0 11.0 %zonal.5.own = bf16[320,32,128]{2,1,0:T(8,128)(2,1)} custom-call(s32[320,1]{1,0:T(8,128)S(1)} %reshape.48.waves, bf16[2,8,128,2048]{3,2,1,0:T(8,128)(2,1)} %velocity.5, bf16[2,8,128,2048]{3,2,1,0:T(8,128)(2,1)} %tracer.5), custom_call_target="tpu_custom_call" | custom-call | flops 5368709120 | bytes 19398656 | tf_op jit(solution)/shard_map/zonal/pallas_call | solution.py:172
  30.0 2.9 %collective-permute-start.6 = (bf16[320,32,128]{2,1,0:T(8,128)(2,1)}, bf16[320,32,128]{2,1,0:T(8,128)(2,1)S(1)}, u32[]{:S(2)}, u32[]{:S(2)}) collective-permute-start(bf16[320,32,128]{2,1,0:T(8,128)(2,1)} %zonal.5.own), channel_id=1, source_target_pairs={{8,0},{16,8},{24,16},{9,1},{17,9},{25,17},{10,2},{18,10},{26,18},{... | collective-permute-start | bytes 7864328 | tf_op jit(solution)/shard_map/ppermute | solution.py:544
  32.9 3.0 %collective-permute-start.5 = (bf16[320,32,128]{2,1,0:T(8,128)(2,1)}, bf16[320,32,128]{2,1,0:T(8,128)(2,1)}, u32[]{:S(2)}, u32[]{:S(2)}) collective-permute-start(bf16[320,32,128]{2,1,0:T(8,128)(2,1)} %zonal.5.own), channel_id=1, source_target_pairs={{0,8},{8,16},{16,24},{1,9},{9,17},{17,25},{2,10},{10,18},{18,26},{... | collective-permute-start | bytes 7864328 | tf_op jit(solution)/shard_map/ppermute | solution.py:543
  35.9 0.1 slice.14
  36.0 0.1 reshape.47.waves
  36.1 7.7 %zonal.4.own = bf16[64,32,128]{2,1,0:T(8,128)(2,1)} custom-call(s32[64,1]{1,0:T(8,128)S(1)} %reshape.47.waves, bf16[2,8,128,2048]{3,2,1,0:T(8,128)(2,1)} %velocity.5, bf16[2,8,128,2048]{3,2,1,0:T(8,128)(2,1)} %tracer.5), custom_call_target="tpu_custom_call" | custom-call | flops 1073741824 | bytes 17301504 | tf_op jit(solution)/shard_map/zonal/pallas_call | solution.py:172
  43.8 0.0 copy-start.6
  43.8 2.8 %collective-permute-start.3 = (bf16[64,32,128]{2,1,0:T(8,128)(2,1)}, bf16[64,32,128]{2,1,0:T(8,128)(2,1)S(1)}, u32[]{:S(2)}, u32[]{:S(2)}) collective-permute-start(bf16[64,32,128]{2,1,0:T(8,128)(2,1)} %zonal.4.own), channel_id=1, source_target_pairs={{8,0},{16,8},{24,16},{9,1},{17,9},{25,17},{10,2},{18,10},{26,18},{... | collective-permute-start | bytes 1572872 | tf_op jit(solution)/shard_map/ppermute | solution.py:544
  46.6 2.9 %collective-permute-start.2 = (bf16[64,32,128]{2,1,0:T(8,128)(2,1)}, bf16[64,32,128]{2,1,0:T(8,128)(2,1)}, u32[]{:S(2)}, u32[]{:S(2)}) collective-permute-start(bf16[64,32,128]{2,1,0:T(8,128)(2,1)} %zonal.4.own), channel_id=1, source_target_pairs={{0,8},{8,16},{16,24},{1,9},{9,17},{17,25},{2,10},{10,18},{18,26},{... | collective-permute-start | bytes 1572872 | tf_op jit(solution)/shard_map/ppermute | solution.py:543
  49.6 0.1 fusion.9
  49.6 0.2 copy.16
  49.8 1.4 fusion.6
  51.2 1.3 sine_multiply_fusion
  52.5 1.8 %tables.1 = (bf16[683,1024]{1,0:T(8,128)(2,1)S(1)}, bf16[683,1024]{1,0:T(8,128)(2,1)S(1)}, f32[8,128]{1,0:T(8,128)S(1)}) custom-call(f32[683,8]{1,0:T(8,128)S(1)} %get-tuple-element.23.cos_c, f32[683,8]{1,0:T(8,128)S(1)} %get-tuple-element.22.sin_c, f32[683,128]{1,0:T(8,128)S(1)} %get-tuple-element.27.cos_f, f32[683,128]{1,0:T(8,128)S(1)} %get-tuple-element.26.sin_f), custom_call_target="tpu_custom_call" | custom-call | flops 4196352 | bytes 2797568 | tf_op jit(solution)/shard_map/tables/pallas_call | solution.py:54
  54.3 1.2 copy-done
  55.5 1.2 copy-done.2
  56.7 0.1 subtract_add_fusion.offsets
  56.7 12.4 %collective-permute-done.3.high.rest_2_ = bf16[64,32,128]{2,1,0:T(8,128)(2,1)S(1)} collective-permute-done((bf16[64,32,128]{2,1,0:T(8,128)(2,1)}, bf16[64,32,128]{2,1,0:T(8,128)(2,1)S(1)}, u32[]{:S(2)}, u32[]{:S(2)}) %collective-permute-start.3) | collective-permute-done | bytes 524320 | tf_op jit(solution)/shard_map/ppermute | solution.py:544
  69.1 1.3 collective-permute-done.2.low.rest_1_
  70.4 0.0 collective-permute-done.6.high
  70.4 5.7 %parents.3 = bf16[320,32,128]{2,1,0:T(8,128)(2,1)} custom-call(s32[2]{0:T(128)S(1)} %subtract_add_fusion.offsets, bf16[320,32,128]{2,1,0:T(8,128)(2,1)} %collective-permute-done.5.low, bf16[320,32,128]{2,1,0:T(8,128)(2,1)} %zonal.5.own, bf16[320,32,128]{2,1,0:T(8,128)(2,1)S(1)} %collective-permute-done.6.high, f32[8,128]{1,0:T(8,128)S(1)} %get-tuple-element.15.rest_0_, ...), custom_call_target="tpu_custom_call" | custom-call | bytes 10485760 | tf_op jit(solution)/shard_map/parents/pallas_call | solution.py:356
  76.2 1.5 all-to-all-done.received
  77.6 4.8 %all-to-all-start.2 = ((bf16[8,1280,128]{2,1,0:T(8,128)(2,1)}), bf16[8,1280,128]{2,1,0:T(8,128)(2,1)}, u32[]{:S(2)}, u32[]{:S(2)}) async-start(bf16[8,1280,128]{2,1,0:T(8,128)(2,1)} %bitcast.9), calls=%async_computation.2 | async-start | bytes 5242880 | tf_op jit(solution)/shard_map/all_to_all | solution.py:549
  82.5 0.8 dynamic_slice.13.waves
  83.2 1.3 copy-done.3
  84.6 7.8 %forward.1 = (bf16[40,2,16,683]{3,2,1,0:T(8,128)(2,1)}, f32[8,128]{1,0:T(8,128)}) custom-call(s32[88]{0:T(128)S(1)} %dynamic_slice.13.waves, bf16[8,1280,128]{2,1,0:T(8,128)(2,1)} %all-to-all-done.received, bf16[683,1024]{1,0:T(8,128)(2,1)S(1)} %copy-done.1, bf16[683,1024]{1,0:T(8,128)(2,1)S(1)} %copy-done.3), custom_call_target="tpu_custom_call" | custom-call | flops 3580887040 | bytes 7167488 | tf_op jit(solution)/shard_map/forward/pallas_call | solution.py:220
  92.4 3.4 %collective-permute-start.1 = (bf16[40,2,16,683]{3,2,1,0:T(8,128)(2,1)}, bf16[40,2,16,683]{3,2,1,0:T(8,128)(2,1)}, u32[]{:S(2)}, u32[]{:S(2)}) collective-permute-start(bf16[40,2,16,683]{3,2,1,0:T(8,128)(2,1)} %get-tuple-element.13.own), channel_id=1, source_target_pairs={{8,0},{16,8},{24,16},{9,1},{17,9},{25,17},{10,2},{18,10},{26,18},{... | collective-permute-start | bytes 5245448 | tf_op jit(solution)/shard_map/ppermute | solution.py:544
  95.8 3.0 %collective-permute-start = (bf16[40,2,16,683]{3,2,1,0:T(8,128)(2,1)}, bf16[40,2,16,683]{3,2,1,0:T(8,128)(2,1)}, u32[]{:S(2)}, u32[]{:S(2)}) collective-permute-start(bf16[40,2,16,683]{3,2,1,0:T(8,128)(2,1)} %get-tuple-element.13.own), channel_id=1, source_target_pairs={{0,8},{8,16},{16,24},{1,9},{9,17},{17,25},{2,10},{10,18},{18,26},{... | collective-permute-start | bytes 5245448 | tf_op jit(solution)/shard_map/ppermute | solution.py:543
  98.9 4.0 %parents.2 = bf16[64,32,128]{2,1,0:T(8,128)(2,1)} custom-call(s32[2]{0:T(128)S(1)} %subtract_add_fusion.offsets, bf16[64,32,128]{2,1,0:T(8,128)(2,1)} %collective-permute-done.2.low.rest_1_, bf16[64,32,128]{2,1,0:T(8,128)(2,1)} %zonal.4.own, bf16[64,32,128]{2,1,0:T(8,128)(2,1)S(1)} %collective-permute-done.3.high.rest_2_), custom_call_target="tpu_custom_call" | custom-call | bytes 2097152 | tf_op jit(solution)/shard_map/parents/pallas_call | solution.py:356
  102.9 1.1 constant_dynamic-slice_fusion
  104.0 1.7 %collective-permute-start.4 = (bf16[4,256,128]{2,1,0:T(8,128)(2,1)S(1)}, bf16[4,256,128]{2,1,0:T(8,128)(2,1)}, u32[]{:S(2)}, u32[]{:S(2)}) collective-permute-start(bf16[4,256,128]{2,1,0:T(8,128)(2,1)S(1)} %get-tuple-element.21), channel_id=1, source_target_pairs={{0,1},{1,0},{2,3},{3,2},{4,5},{5,4},{6,7},{7,6},{8,9},{9,8},{10,11... | collective-permute-start | bytes 786440 | tf_op jit(solution)/shard_map/ppermute | solution.py:559
  105.6 14.2 %collective-permute-done.1.high = bf16[40,2,16,683]{3,2,1,0:T(8,128)(2,1)} collective-permute-done((bf16[40,2,16,683]{3,2,1,0:T(8,128)(2,1)}, bf16[40,2,16,683]{3,2,1,0:T(8,128)(2,1)}, u32[]{:S(2)}, u32[]{:S(2)}) %collective-permute-start.1) | collective-permute-done | bytes 1748512 | tf_op jit(solution)/shard_map/ppermute | solution.py:544
  119.9 0.9 collective-permute-done.low
  120.8 1.3 copy-done.4
  122.1 9.3 %inverse.1 = (bf16[88,2,2,8,683]{4,3,2,1,0:T(8,128)(2,1)}, bf16[88,2,2,8,1024]{4,3,2,1,0:T(8,128)(2,1)}, f32[8,128]{1,0:T(8,128)S(1)}) custom-call(s32[88]{0:T(128)S(1)} %dynamic_slice.13.waves, s32[2]{0:T(128)S(1)} %subtract_add_fusion.offsets, bf16[40,2,16,683]{3,2,1,0:T(8,128)(2,1)} %collective-permute-done.low, ...), custom_call_target="tpu_custom_call" | custom-call | flops 3580887040 | bytes 14161408 | tf_op jit(solution)/shard_map/inverse/pallas_call | solution.py:310
  131.4 0.5 slice.13
  132.5 1.9 %maximum_select_fusion = bf16[4,2,256,128]{3,2,1,0:T(8,128)(2,1)} fusion(bf16[4,1,256,128]{3,2,1,0:T(8,128)(2,1)} %bitcast.4, bf16[4,1,256,128]{3,2,1,0:T(8,128)(2,1)S(1)} %get-tuple-element.20, pred[]{:T(512)S(6)} %eq.9), kind=kLoop, calls=%fused_computation.3 | loop fusion | flops 786432 | bytes 1048577 | tf_op jit(solution)/shard_map/jit(_where)/select_n | solution.py:561
  134.4 6.3 %all-to-all-done.2.received = bf16[8,1280,128]{2,1,0:T(8,128)(2,1)} async-done(((bf16[8,1280,128]{2,1,0:T(8,128)(2,1)}), bf16[8,1280,128]{2,1,0:T(8,128)(2,1)}, u32[]{:S(2)}, u32[]{:S(2)}) %all-to-all-start.2) | async-done | bytes 2621472 | tf_op jit(solution)/shard_map/all_to_all | solution.py:549
  140.7 5.1 %all-to-all-start.1 = ((bf16[4,2,256,128]{3,2,1,0:T(8,128)(2,1)}), bf16[4,2,256,128]{3,2,1,0:T(8,128)(2,1)S(1)}, u32[]{:S(2)}, u32[]{:S(2)}) async-start(bf16[4,2,256,128]{3,2,1,0:T(8,128)(2,1)} %maximum_select_fusion), calls=%async_computation.1 | async-start | bytes 1048576 | tf_op jit(solution)/shard_map/all_to_all | solution.py:563
  145.8 12.1 %finish.1 = (bf16[88,2,2,8,683]{4,3,2,1,0:T(8,128)(2,1)}, bf16[88,2,2,8,1024]{4,3,2,1,0:T(8,128)(2,1)}) custom-call(s32[88]{0:T(128)S(1)} %dynamic_slice.13.waves, bf16[8,1280,128]{2,1,0:T(8,128)(2,1)} %all-to-all-done.2.received, bf16[88,2,2,8,683]{4,3,2,1,0:T(8,128)(2,1)} %noise.5, ...), custom_call_target="tpu_custom_call", output_to_operand_aliasing={{0}: (5, {}), {1}: (6, {})} | custom-call | flops 7161774080 | bytes 11537408 | tf_op jit(solution)/shard_map/finish/pallas_call | solution.py:484
  157.8 2.0 %all-to-all-done.1 = bf16[4,2,256,128]{3,2,1,0:T(8,128)(2,1)S(1)} async-done(((bf16[4,2,256,128]{3,2,1,0:T(8,128)(2,1)}), bf16[4,2,256,128]{3,2,1,0:T(8,128)(2,1)S(1)}, u32[]{:S(2)}, u32[]{:S(2)}) %all-to-all-start.1) | async-done | bytes 524320 | tf_op jit(solution)/shard_map/all_to_all | solution.py:563
  159.8 3.4 %last.1 = (bf16[88,2,2,8,683]{4,3,2,1,0:T(8,128)(2,1)}, bf16[88,2,2,8,1024]{4,3,2,1,0:T(8,128)(2,1)}) custom-call(s32[88]{0:T(128)S(1)} %dynamic_slice.13.waves, bf16[8,256,128]{2,1,0:T(8,128)(2,1)S(1)} %bitcast.8, bf16[88,2,2,8,683]{4,3,2,1,0:T(8,128)(2,1)} %noise.5, bf16[683,1024]{1,0:T(8,128)(2,1)S(1)} %copy-done.1, ...), custom_call_target="tpu_custom_call", output_to_operand_aliasing={{0}: (5, {}), {1}: (6, {})} | custom-call | flops 1432354816 | bytes 4545536 | tf_op jit(solution)/shard_map/last/pallas_call | solution.py:444
  (13 shorter events, 0.0 us)
Async XLA Ops:
  12.5 65.1 %all-to-all-start = ((bf16[8,1280,128]{2,1,0:T(8,128)(2,1)}), bf16[8,1280,128]{2,1,0:T(8,128)(2,1)}, u32[]{:S(2)}, u32[]{:S(2)}) async-start(bf16[8,1280,128]{2,1,0:T(8,128)(2,1)} %bitcast.10), calls=%async_computation | async-start | bytes 5242880 | tf_op jit(solution)/shard_map/all_to_all | solution.py:549
  30.0 40.4 %collective-permute-start.6 = (bf16[320,32,128]{2,1,0:T(8,128)(2,1)}, bf16[320,32,128]{2,1,0:T(8,128)(2,1)S(1)}, u32[]{:S(2)}, u32[]{:S(2)}) collective-permute-start(bf16[320,32,128]{2,1,0:T(8,128)(2,1)} %zonal.5.own), channel_id=1, source_target_pairs={{8,0},{16,8},{24,16},{9,1},{17,9},{25,17},{10,2},{18,10},{26,18},{... | collective-permute-start | bytes 7864328 | tf_op jit(solution)/shard_map/ppermute | solution.py:544
  32.9 37.5 %collective-permute-start.5 = (bf16[320,32,128]{2,1,0:T(8,128)(2,1)}, bf16[320,32,128]{2,1,0:T(8,128)(2,1)}, u32[]{:S(2)}, u32[]{:S(2)}) collective-permute-start(bf16[320,32,128]{2,1,0:T(8,128)(2,1)} %zonal.5.own), channel_id=1, source_target_pairs={{0,8},{8,16},{16,24},{1,9},{9,17},{17,25},{2,10},{10,18},{18,26},{... | collective-permute-start | bytes 7864328 | tf_op jit(solution)/shard_map/ppermute | solution.py:543
  43.8 12.9 %copy-start.6 = (s32[8]{0:T(128)S(1)}, s32[8]{0:T(128)}, u32[]{:S(2)}) copy-start(s32[8]{0:T(128)} %param.8) | copy-start | bytes 100
  43.8 25.4 %collective-permute-start.3 = (bf16[64,32,128]{2,1,0:T(8,128)(2,1)}, bf16[64,32,128]{2,1,0:T(8,128)(2,1)S(1)}, u32[]{:S(2)}, u32[]{:S(2)}) collective-permute-start(bf16[64,32,128]{2,1,0:T(8,128)(2,1)} %zonal.4.own), channel_id=1, source_target_pairs={{8,0},{16,8},{24,16},{9,1},{17,9},{25,17},{10,2},{18,10},{26,18},{... | collective-permute-start | bytes 1572872 | tf_op jit(solution)/shard_map/ppermute | solution.py:544
  46.6 23.8 %collective-permute-start.2 = (bf16[64,32,128]{2,1,0:T(8,128)(2,1)}, bf16[64,32,128]{2,1,0:T(8,128)(2,1)}, u32[]{:S(2)}, u32[]{:S(2)}) collective-permute-start(bf16[64,32,128]{2,1,0:T(8,128)(2,1)} %zonal.4.own), channel_id=1, source_target_pairs={{0,8},{8,16},{16,24},{1,9},{9,17},{17,25},{2,10},{10,18},{18,26},{... | collective-permute-start | bytes 1572872 | tf_op jit(solution)/shard_map/ppermute | solution.py:543
  54.3 1.2 copy-start
  55.5 1.2 copy-start.2
  77.6 5.6 %copy-start.1 = (bf16[683,1024]{1,0:T(8,128)(2,1)S(1)}, bf16[683,1024]{1,0:T(8,128)(2,1)}, u32[]{:S(2)}) copy-start(bf16[683,1024]{1,0:T(8,128)(2,1)} %copy-done) | copy-start | bytes 4196356
  77.6 63.1 %all-to-all-start.2 = ((bf16[8,1280,128]{2,1,0:T(8,128)(2,1)}), bf16[8,1280,128]{2,1,0:T(8,128)(2,1)}, u32[]{:S(2)}, u32[]{:S(2)}) async-start(bf16[8,1280,128]{2,1,0:T(8,128)(2,1)} %bitcast.9), calls=%async_computation.2 | async-start | bytes 5242880 | tf_op jit(solution)/shard_map/all_to_all | solution.py:549
  83.2 1.4 copy-start.3
  92.4 27.5 %collective-permute-start.1 = (bf16[40,2,16,683]{3,2,1,0:T(8,128)(2,1)}, bf16[40,2,16,683]{3,2,1,0:T(8,128)(2,1)}, u32[]{:S(2)}, u32[]{:S(2)}) collective-permute-start(bf16[40,2,16,683]{3,2,1,0:T(8,128)(2,1)} %get-tuple-element.13.own), channel_id=1, source_target_pairs={{8,0},{16,8},{24,16},{9,1},{17,9},{25,17},{10,2},{18,10},{26,18},{... | collective-permute-start | bytes 5245448 | tf_op jit(solution)/shard_map/ppermute | solution.py:544
  95.8 24.9 %collective-permute-start = (bf16[40,2,16,683]{3,2,1,0:T(8,128)(2,1)}, bf16[40,2,16,683]{3,2,1,0:T(8,128)(2,1)}, u32[]{:S(2)}, u32[]{:S(2)}) collective-permute-start(bf16[40,2,16,683]{3,2,1,0:T(8,128)(2,1)} %get-tuple-element.13.own), channel_id=1, source_target_pairs={{0,8},{8,16},{16,24},{1,9},{9,17},{17,25},{2,10},{10,18},{18,26},{... | collective-permute-start | bytes 5245448 | tf_op jit(solution)/shard_map/ppermute | solution.py:543
  104.0 28.5 %collective-permute-start.4 = (bf16[4,256,128]{2,1,0:T(8,128)(2,1)S(1)}, bf16[4,256,128]{2,1,0:T(8,128)(2,1)}, u32[]{:S(2)}, u32[]{:S(2)}) collective-permute-start(bf16[4,256,128]{2,1,0:T(8,128)(2,1)S(1)} %get-tuple-element.21), channel_id=1, source_target_pairs={{0,1},{1,0},{2,3},{3,2},{4,5},{5,4},{6,7},{7,6},{8,9},{9,8},{10,11... | collective-permute-start | bytes 786440 | tf_op jit(solution)/shard_map/ppermute | solution.py:559
  120.7 1.4 copy-start.4
  122.1 23.7 %copy-start.5 = (bf16[683,1024]{1,0:T(8,128)(2,1)S(1)}, bf16[683,1024]{1,0:T(8,128)(2,1)}, u32[]{:S(2)}) copy-start(bf16[683,1024]{1,0:T(8,128)(2,1)} %copy-done.2) | copy-start | bytes 4196356
  140.7 19.1 %all-to-all-start.1 = ((bf16[4,2,256,128]{3,2,1,0:T(8,128)(2,1)}), bf16[4,2,256,128]{3,2,1,0:T(8,128)(2,1)S(1)}, u32[]{:S(2)}, u32[]{:S(2)}) async-start(bf16[4,2,256,128]{3,2,1,0:T(8,128)(2,1)} %maximum_select_fusion), calls=%async_computation.1 | async-start | bytes 1048576 | tf_op jit(solution)/shard_map/all_to_all | solution.py:563

commit v15 on v13

--- a/solution.py
+++ b/solution.py
@@ -37,7 +37,8 @@
     return jnp.cos(coarse) * factor, jnp.sin(coarse) * factor, jnp.cos(fine), jnp.sin(fine)
 
 
-def tables_kernel(cos_c, sin_c, cos_f, sin_f, even, odd):
+def tables_kernel(cos_c, sin_c, cos_f, sin_f, even, odd, token):
+    token[...] = jnp.zeros_like(token)
     width = cos_f.shape[1]
     cos_b, sin_b = cos_f[...], sin_f[...]
     for at in range(cos_c.shape[1]):
@@ -52,7 +53,7 @@
     shape = pltpu.VMEM((truncation, starts.shape[0] * width), jnp.bfloat16)
     return pl.pallas_call(
         tables_kernel,
-        out_shape=[shape, shape],
+        out_shape=[shape, shape, jax.ShapeDtypeStruct(TOKEN, jnp.float32)],
         compiler_params=pltpu.CompilerParams(vmem_limit_bytes=VMEM_BYTES),
         cost_estimate=pl.CostEstimate(
             flops=6 * truncation * latitudes, bytes_accessed=4 * truncation * latitudes,
@@ -550,19 +551,18 @@
             moved = jnp.swapaxes(moved, 0, 1).reshape(1, -1, latitudes)
         return moved
 
-    def copied(at, tokens):
-        return copy_parents(offsets, *neighbours(zonal(at), per_member), tokens)
-
     received = exchanged(zonal(0))
-    even, odd = meridional_tables(truncation, latitudes, starts, inner)
-    later = [exchanged(copied(1, []))] if len(bounds) > 1 else []
+    even, odd, made = meridional_tables(truncation, latitudes, starts, inner)
+    sides = [neighbours(zonal(at), per_member) for at in range(1, len(bounds))]
+    tokens = [made] + [part for low, _, high in sides[1:] for part in (low, high)]
+    later = [exchanged(copy_parents(offsets, *side, tokens)) for side in sides[:1]]
     spectra, _ = forward_transform(
         (own_waves, per_member), 0, block, received, even, odd, mem_local, []
     )
     *outs, token = inverse_transform(
         own_waves, offsets, 0, block, *neighbours(spectra, 1), noise, even, odd, None
     )
-    later += [exchanged(copied(at, [token])) for at in range(2, len(bounds))]
+    later += [exchanged(copy_parents(offsets, *side, [token])) for side in sides[1:]]
     for (start, stop), received in zip(bounds[1:], later):
         if stop - start == block:
             outs = last_transform(own_waves, start, received, noise, even, odd, outs)

time: 166 us -> 166 us (level)
  local copies, waits for them, and re-layouts: 2.12 us -> 7.1 us
  waiting for transfers between devices: 48.9 us -> 44.5 us
    ppermute x3, waiting for transfers between devices: 33.4 us -> 2.18 us  [neighbours(): lax.ppermute(rows[:, rows.shape[1] - SPREAD * per_member:], 'member', upw...]
    ppermute x3, waiting for transfers between devices: 8.8 us -> 33.4 us  [neighbours(): high = lax.ppermute(rows[:, :SPREAD * per_member], 'member', downward)]
    unnamed x2 -> x14, local copies, waits for them, and re-layouts: 0.01 us -> 4.99 us
    ppermute x3, starting transfers between devices: 5.76 us -> 9.14 us  [neighbours(): high = lax.ppermute(rows[:, :SPREAD * per_member], 'member', downward)]
    ppermute x3, starting transfers between devices: 12.3 us -> 8.98 us  [neighbours(): lax.ppermute(rows[:, rows.shape[1] - SPREAD * per_member:], 'member', upw...]
    all_to_all x3, waiting for transfers between devices: 6.72 us -> 8.89 us  [exchanged(): lax.all_to_all(outgoing, 'lat', split_axis=0, concat_axis=0, tiled=True)]
where the time goes in v15:
time: 166 us; the launch traced here: 163 us
  Pallas kernels  73 us (44%)
  waiting for transfers between devices  44.5 us (27%)
  starting transfers between devices  34.5 us (21%)
  local copies, waits for them, and re-layouts  7.1 us (4%)
  other arithmetic  2.87 us (2%)
    ppermute x3, waiting for transfers between devices, neighbours(): high = lax.ppermute(rows[:, :SPREAD * per_member], 'member', downward)  33.4 us
    pallas_call x3, Pallas kernels, zonal_transform(): pl.pallas_call(functools.partial(zonal_kernel, truncation, len(tokens)),...  29.6 us
    all_to_all x3, starting transfers between devices, exchanged(): lax.all_to_all(outgoing, 'lat', split_axis=0, concat_axis=0, tiled=True)  16.4 us
    pallas_call x1, Pallas kernels, finish_transform(): pl.pallas_call(functools.partial(finish_kernel, first, block), grid_spec=...  12.1 us
    pallas_call x2, Pallas kernels, copy_parents(): pl.pallas_call(copy_kernel, grid_spec=pltpu.PrefetchScalarGridSpec(num_sc...  9.76 us
    ppermute x3, starting transfers between devices, neighbours(): high = lax.ppermute(rows[:, :SPREAD * per_member], 'member', downward)  9.14 us
    ppermute x3, starting transfers between devices, neighbours(): lax.ppermute(rows[:, rows.shape[1] - SPREAD * per_member:], 'member', upw...  8.98 us
    all_to_all x3, waiting for transfers between devices, exchanged(): lax.all_to_all(outgoing, 'lat', split_axis=0, concat_axis=0, tiled=True)  8.89 us
  transfers between devices with their start and end apart: 9, of which 7 were waited for; matrix products, arithmetic and copies ran while one was open for 2% of the time, Pallas kernels for 36%

profile of v15, /device:TPU:1, one launch (start us, length us, event | category | flops | bytes accessed | tf_op | source)
XLA Modules:
  0.0 162.9 jit_solution(14904809317805206252)
XLA Ops:
  0.6 0.8 reshape.34
  1.4 0.1 fusion.13
  1.5 0.1 reshape.42.waves
  1.6 11.0 %zonal.4 = bf16[320,32,128]{2,1,0:T(8,128)(2,1)} custom-call(s32[320,1]{1,0:T(8,128)S(1)} %reshape.42.waves, bf16[2,8,128,2048]{3,2,1,0:T(8,128)(2,1)} %velocity.5, bf16[2,8,128,2048]{3,2,1,0:T(8,128)(2,1)} %tracer.5), custom_call_target="tpu_custom_call" | custom-call | flops 5368709120 | bytes 19398656 | tf_op jit(solution)/shard_map/zonal/pallas_call | solution.py:172
  12.5 6.4 %all-to-all-start = ((bf16[8,1280,128]{2,1,0:T(8,128)(2,1)}), bf16[8,1280,128]{2,1,0:T(8,128)(2,1)}, u32[]{:S(2)}, u32[]{:S(2)}) async-start(bf16[8,1280,128]{2,1,0:T(8,128)(2,1)} %bitcast.4), calls=%async_computation | async-start | bytes 5242880 | tf_op jit(solution)/shard_map/all_to_all | solution.py:549
  18.9 0.1 reshape.43.waves
  19.0 11.0 %zonal.5.own = bf16[320,32,128]{2,1,0:T(8,128)(2,1)} custom-call(s32[320,1]{1,0:T(8,128)S(1)} %reshape.43.waves, bf16[2,8,128,2048]{3,2,1,0:T(8,128)(2,1)} %velocity.5, bf16[2,8,128,2048]{3,2,1,0:T(8,128)(2,1)} %tracer.5), custom_call_target="tpu_custom_call" | custom-call | flops 5368709120 | bytes 19398656 | tf_op jit(solution)/shard_map/zonal/pallas_call | solution.py:172
  30.0 2.9 %collective-permute-start.5 = (bf16[320,32,128]{2,1,0:T(8,128)(2,1)}, bf16[320,32,128]{2,1,0:T(8,128)(2,1)S(1)}, u32[]{:S(2)}, u32[]{:S(2)}) collective-permute-start(bf16[320,32,128]{2,1,0:T(8,128)(2,1)} %zonal.5.own), channel_id=1, source_target_pairs={{8,0},{16,8},{24,16},{9,1},{17,9},{25,17},{10,2},{18,10},{26,18},{... | collective-permute-start | bytes 7864328 | tf_op jit(solution)/shard_map/ppermute | solution.py:544
  32.9 3.0 %collective-permute-start.4 = (bf16[320,32,128]{2,1,0:T(8,128)(2,1)}, bf16[320,32,128]{2,1,0:T(8,128)(2,1)}, u32[]{:S(2)}, u32[]{:S(2)}) collective-permute-start(bf16[320,32,128]{2,1,0:T(8,128)(2,1)} %zonal.5.own), channel_id=1, source_target_pairs={{0,8},{8,16},{16,24},{1,9},{9,17},{17,25},{2,10},{10,18},{18,26},{... | collective-permute-start | bytes 7864328 | tf_op jit(solution)/shard_map/ppermute | solution.py:543
  35.9 0.1 slice.9
  36.0 0.1 reshape.41.waves
  36.1 7.7 %zonal.3.own = bf16[64,32,128]{2,1,0:T(8,128)(2,1)} custom-call(s32[64,1]{1,0:T(8,128)S(1)} %reshape.41.waves, bf16[2,8,128,2048]{3,2,1,0:T(8,128)(2,1)} %velocity.5, bf16[2,8,128,2048]{3,2,1,0:T(8,128)(2,1)} %tracer.5), custom_call_target="tpu_custom_call" | custom-call | flops 1073741824 | bytes 17301504 | tf_op jit(solution)/shard_map/zonal/pallas_call | solution.py:172
  43.8 0.0 copy-start.6
  43.8 2.8 %collective-permute-start.1 = (bf16[64,32,128]{2,1,0:T(8,128)(2,1)}, bf16[64,32,128]{2,1,0:T(8,128)(2,1)S(1)}, u32[]{:S(2)}, u32[]{:S(2)}) collective-permute-start(bf16[64,32,128]{2,1,0:T(8,128)(2,1)} %zonal.3.own), channel_id=1, source_target_pairs={{8,0},{16,8},{24,16},{9,1},{17,9},{25,17},{10,2},{18,10},{26,18},{... | collective-permute-start | bytes 1572872 | tf_op jit(solution)/shard_map/ppermute | solution.py:544
  46.6 2.9 %collective-permute-start = (bf16[64,32,128]{2,1,0:T(8,128)(2,1)}, bf16[64,32,128]{2,1,0:T(8,128)(2,1)}, u32[]{:S(2)}, u32[]{:S(2)}) collective-permute-start(bf16[64,32,128]{2,1,0:T(8,128)(2,1)} %zonal.3.own), channel_id=1, source_target_pairs={{0,8},{8,16},{16,24},{1,9},{9,17},{17,25},{2,10},{10,18},{18,26},{... | collective-permute-start | bytes 1572872 | tf_op jit(solution)/shard_map/ppermute | solution.py:543
  49.6 0.1 fusion.9
  49.6 0.2 copy.17
  49.8 1.4 fusion.6
  51.2 1.3 sine_multiply_fusion
  52.5 1.8 %tables.1 = (bf16[683,1024]{1,0:T(8,128)(2,1)S(1)}, bf16[683,1024]{1,0:T(8,128)(2,1)S(1)}, f32[8,128]{1,0:T(8,128)S(1)}) custom-call(f32[683,8]{1,0:T(8,128)S(1)} %get-tuple-element.21.cos_c, f32[683,8]{1,0:T(8,128)S(1)} %get-tuple-element.20.sin_c, f32[683,128]{1,0:T(8,128)S(1)} %get-tuple-element.25.cos_f, f32[683,128]{1,0:T(8,128)S(1)} %get-tuple-element.24.sin_f), custom_call_target="tpu_custom_call" | custom-call | flops 4196352 | bytes 2797568 | tf_op jit(solution)/shard_map/tables/pallas_call | solution.py:54
  54.3 0.0 copy-start
  54.4 1.2 copy-done
  55.5 1.1 copy-done.2
  56.6 0.0 copy-done.6
  56.6 0.1 subtract_add_fusion.offsets
  56.7 12.4 %collective-permute-done.1.high.rest_2_ = bf16[64,32,128]{2,1,0:T(8,128)(2,1)S(1)} collective-permute-done((bf16[64,32,128]{2,1,0:T(8,128)(2,1)}, bf16[64,32,128]{2,1,0:T(8,128)(2,1)S(1)}, u32[]{:S(2)}, u32[]{:S(2)}) %collective-permute-start.1) | collective-permute-done | bytes 524320 | tf_op jit(solution)/shard_map/ppermute | solution.py:544
  69.1 1.3 collective-permute-done.low.rest_1_
  70.4 0.0 collective-permute-done.5.high
  70.4 0.0 collective-permute-done.4.low
  70.4 5.8 %parents.3 = bf16[320,32,128]{2,1,0:T(8,128)(2,1)} custom-call(s32[2]{0:T(128)S(1)} %subtract_add_fusion.offsets, bf16[320,32,128]{2,1,0:T(8,128)(2,1)} %collective-permute-done.4.low, bf16[320,32,128]{2,1,0:T(8,128)(2,1)} %zonal.5.own, bf16[320,32,128]{2,1,0:T(8,128)(2,1)S(1)} %collective-permute-done.5.high, f32[8,128]{1,0:T(8,128)S(1)} %get-tuple-element.15.rest_0_, ...), custom_call_target="tpu_custom_call" | custom-call | bytes 10485760 | tf_op jit(solution)/shard_map/parents/pallas_call | solution.py:356
  76.2 1.5 all-to-all-done.received
  77.6 4.8 %all-to-all-start.2 = ((bf16[8,1280,128]{2,1,0:T(8,128)(2,1)}), bf16[8,1280,128]{2,1,0:T(8,128)(2,1)}, u32[]{:S(2)}, u32[]{:S(2)}) async-start(bf16[8,1280,128]{2,1,0:T(8,128)(2,1)} %bitcast.3), calls=%async_computation.2 | async-start | bytes 5242880 | tf_op jit(solution)/shard_map/all_to_all | solution.py:549
  82.5 0.8 dynamic_slice.6.waves
  83.2 0.0 copy-done.1
  83.2 1.3 copy-done.3
  84.6 7.8 %forward.1 = (bf16[40,2,16,683]{3,2,1,0:T(8,128)(2,1)}, f32[8,128]{1,0:T(8,128)}) custom-call(s32[88]{0:T(128)S(1)} %dynamic_slice.6.waves, bf16[8,1280,128]{2,1,0:T(8,128)(2,1)} %all-to-all-done.received, bf16[683,1024]{1,0:T(8,128)(2,1)S(1)} %copy-done.1, bf16[683,1024]{1,0:T(8,128)(2,1)S(1)} %copy-done.3), custom_call_target="tpu_custom_call" | custom-call | flops 3580887040 | bytes 7167488 | tf_op jit(solution)/shard_map/forward/pallas_call | solution.py:220
  92.4 3.5 %collective-permute-start.3 = (bf16[40,2,16,683]{3,2,1,0:T(8,128)(2,1)}, bf16[40,2,16,683]{3,2,1,0:T(8,128)(2,1)S(1)}, u32[]{:S(2)}, u32[]{:S(2)}) collective-permute-start(bf16[40,2,16,683]{3,2,1,0:T(8,128)(2,1)} %get-tuple-element.13.own), channel_id=1, source_target_pairs={{8,0},{16,8},{24,16},{9,1},{17,9},{25,17},{10,2},{18,10},{26,18},{... | collective-permute-start | bytes 5245448 | tf_op jit(solution)/shard_map/ppermute | solution.py:544
  95.9 3.0 %collective-permute-start.2 = (bf16[40,2,16,683]{3,2,1,0:T(8,128)(2,1)}, bf16[40,2,16,683]{3,2,1,0:T(8,128)(2,1)S(1)}, u32[]{:S(2)}, u32[]{:S(2)}) collective-permute-start(bf16[40,2,16,683]{3,2,1,0:T(8,128)(2,1)} %get-tuple-element.13.own), channel_id=1, source_target_pairs={{0,8},{8,16},{16,24},{1,9},{9,17},{17,25},{2,10},{10,18},{18,26},{... | collective-permute-start | bytes 5245448 | tf_op jit(solution)/shard_map/ppermute | solution.py:543
  98.9 21.0 %collective-permute-done.3.high = bf16[40,2,16,683]{3,2,1,0:T(8,128)(2,1)S(1)} collective-permute-done((bf16[40,2,16,683]{3,2,1,0:T(8,128)(2,1)}, bf16[40,2,16,683]{3,2,1,0:T(8,128)(2,1)S(1)}, u32[]{:S(2)}, u32[]{:S(2)}) %collective-permute-start.3) | collective-permute-done | bytes 1748512 | tf_op jit(solution)/shard_map/ppermute | solution.py:544
  119.9 0.9 collective-permute-done.2.low
  120.8 8.5 %inverse.1 = (bf16[88,2,2,8,683]{4,3,2,1,0:T(8,128)(2,1)}, bf16[88,2,2,8,1024]{4,3,2,1,0:T(8,128)(2,1)}, f32[8,128]{1,0:T(8,128)S(1)}) custom-call(s32[88]{0:T(128)S(1)} %dynamic_slice.6.waves, s32[2]{0:T(128)S(1)} %subtract_add_fusion.offsets, bf16[40,2,16,683]{3,2,1,0:T(8,128)(2,1)S(1)} %collective-permute-done.2.low, ...), custom_call_target="tpu_custom_call" | custom-call | flops 3580887040 | bytes 14161408 | tf_op jit(solution)/shard_map/inverse/pallas_call | solution.py:310
  129.3 4.0 %parents.2 = bf16[64,32,128]{2,1,0:T(8,128)(2,1)} custom-call(s32[2]{0:T(128)S(1)} %subtract_add_fusion.offsets, bf16[64,32,128]{2,1,0:T(8,128)(2,1)} %collective-permute-done.low.rest_1_, bf16[64,32,128]{2,1,0:T(8,128)(2,1)} %zonal.3.own, bf16[64,32,128]{2,1,0:T(8,128)(2,1)S(1)} %collective-permute-done.1.high.rest_2_, f32[8,128]{1,0:T(8,128)S(1)} %get-tuple-element.14.rest_0_), custom_call_target="tpu_custom_call" | custom-call | bytes 2097152 | tf_op jit(solution)/shard_map/parents/pallas_call | solution.py:356
  133.3 7.4 %all-to-all-done.2.received = bf16[8,1280,128]{2,1,0:T(8,128)(2,1)} async-done(((bf16[8,1280,128]{2,1,0:T(8,128)(2,1)}), bf16[8,1280,128]{2,1,0:T(8,128)(2,1)}, u32[]{:S(2)}, u32[]{:S(2)}) %all-to-all-start.2) | async-done | bytes 2621472 | tf_op jit(solution)/shard_map/all_to_all | solution.py:549
  140.7 5.2 %all-to-all-start.1 = ((bf16[8,256,128]{2,1,0:T(8,128)(2,1)}), bf16[8,256,128]{2,1,0:T(8,128)(2,1)S(1)}, u32[]{:S(2)}, u32[]{:S(2)}) async-start(bf16[8,256,128]{2,1,0:T(8,128)(2,1)} %bitcast.5), calls=%async_computation.1 | async-start | bytes 1048576 | tf_op jit(solution)/shard_map/all_to_all | solution.py:549
  145.9 1.3 copy-done.4
  147.2 12.1 %finish.1 = (bf16[88,2,2,8,683]{4,3,2,1,0:T(8,128)(2,1)}, bf16[88,2,2,8,1024]{4,3,2,1,0:T(8,128)(2,1)}) custom-call(s32[88]{0:T(128)S(1)} %dynamic_slice.6.waves, bf16[8,1280,128]{2,1,0:T(8,128)(2,1)} %all-to-all-done.2.received, bf16[88,2,2,8,683]{4,3,2,1,0:T(8,128)(2,1)} %noise.5, ...), custom_call_target="tpu_custom_call", output_to_operand_aliasing={{0}: (5, {}), {1}: (6, {})} | custom-call | flops 7161774080 | bytes 11537408 | tf_op jit(solution)/shard_map/finish/pallas_call | solution.py:484
  159.3 0.1 all-to-all-done.1.received
  159.4 3.4 %last.1 = (bf16[88,2,2,8,683]{4,3,2,1,0:T(8,128)(2,1)}, bf16[88,2,2,8,1024]{4,3,2,1,0:T(8,128)(2,1)}) custom-call(s32[88]{0:T(128)S(1)} %dynamic_slice.6.waves, bf16[8,256,128]{2,1,0:T(8,128)(2,1)S(1)} %all-to-all-done.1.received, bf16[88,2,2,8,683]{4,3,2,1,0:T(8,128)(2,1)} %noise.5, ...), custom_call_target="tpu_custom_call", output_to_operand_aliasing={{0}: (5, {}), {1}: (6, {})} | custom-call | flops 1432354816 | bytes 4545536 | tf_op jit(solution)/shard_map/last/pallas_call | solution.py:444
  (8 shorter events, 0.0 us)
Async XLA Ops:
  12.5 65.1 %all-to-all-start = ((bf16[8,1280,128]{2,1,0:T(8,128)(2,1)}), bf16[8,1280,128]{2,1,0:T(8,128)(2,1)}, u32[]{:S(2)}, u32[]{:S(2)}) async-start(bf16[8,1280,128]{2,1,0:T(8,128)(2,1)} %bitcast.4), calls=%async_computation | async-start | bytes 5242880 | tf_op jit(solution)/shard_map/all_to_all | solution.py:549
  30.0 40.4 %collective-permute-start.5 = (bf16[320,32,128]{2,1,0:T(8,128)(2,1)}, bf16[320,32,128]{2,1,0:T(8,128)(2,1)S(1)}, u32[]{:S(2)}, u32[]{:S(2)}) collective-permute-start(bf16[320,32,128]{2,1,0:T(8,128)(2,1)} %zonal.5.own), channel_id=1, source_target_pairs={{8,0},{16,8},{24,16},{9,1},{17,9},{25,17},{10,2},{18,10},{26,18},{... | collective-permute-start | bytes 7864328 | tf_op jit(solution)/shard_map/ppermute | solution.py:544
  32.9 37.5 %collective-permute-start.4 = (bf16[320,32,128]{2,1,0:T(8,128)(2,1)}, bf16[320,32,128]{2,1,0:T(8,128)(2,1)}, u32[]{:S(2)}, u32[]{:S(2)}) collective-permute-start(bf16[320,32,128]{2,1,0:T(8,128)(2,1)} %zonal.5.own), channel_id=1, source_target_pairs={{0,8},{8,16},{16,24},{1,9},{9,17},{17,25},{2,10},{10,18},{18,26},{... | collective-permute-start | bytes 7864328 | tf_op jit(solution)/shard_map/ppermute | solution.py:543
  43.8 12.9 %copy-start.6 = (s32[8]{0:T(128)S(1)}, s32[8]{0:T(128)}, u32[]{:S(2)}) copy-start(s32[8]{0:T(128)} %param.8) | copy-start | bytes 100
  43.8 25.4 %collective-permute-start.1 = (bf16[64,32,128]{2,1,0:T(8,128)(2,1)}, bf16[64,32,128]{2,1,0:T(8,128)(2,1)S(1)}, u32[]{:S(2)}, u32[]{:S(2)}) collective-permute-start(bf16[64,32,128]{2,1,0:T(8,128)(2,1)} %zonal.3.own), channel_id=1, source_target_pairs={{8,0},{16,8},{24,16},{9,1},{17,9},{25,17},{10,2},{18,10},{26,18},{... | collective-permute-start | bytes 1572872 | tf_op jit(solution)/shard_map/ppermute | solution.py:544
  46.6 23.8 %collective-permute-start = (bf16[64,32,128]{2,1,0:T(8,128)(2,1)}, bf16[64,32,128]{2,1,0:T(8,128)(2,1)}, u32[]{:S(2)}, u32[]{:S(2)}) collective-permute-start(bf16[64,32,128]{2,1,0:T(8,128)(2,1)} %zonal.3.own), channel_id=1, source_target_pairs={{0,8},{8,16},{16,24},{1,9},{9,17},{17,25},{2,10},{10,18},{18,26},{... | collective-permute-start | bytes 1572872 | tf_op jit(solution)/shard_map/ppermute | solution.py:543
  54.3 1.2 copy-start
  55.5 1.1 copy-start.2
  77.6 5.6 %copy-start.1 = (bf16[683,1024]{1,0:T(8,128)(2,1)S(1)}, bf16[683,1024]{1,0:T(8,128)(2,1)}, u32[]{:S(2)}) copy-start(bf16[683,1024]{1,0:T(8,128)(2,1)} %copy-done) | copy-start | bytes 4196356
  77.6 63.0 %all-to-all-start.2 = ((bf16[8,1280,128]{2,1,0:T(8,128)(2,1)}), bf16[8,1280,128]{2,1,0:T(8,128)(2,1)}, u32[]{:S(2)}, u32[]{:S(2)}) async-start(bf16[8,1280,128]{2,1,0:T(8,128)(2,1)} %bitcast.3), calls=%async_computation.2 | async-start | bytes 5242880 | tf_op jit(solution)/shard_map/all_to_all | solution.py:549
  83.2 1.4 copy-start.3
  92.4 27.5 %collective-permute-start.3 = (bf16[40,2,16,683]{3,2,1,0:T(8,128)(2,1)}, bf16[40,2,16,683]{3,2,1,0:T(8,128)(2,1)S(1)}, u32[]{:S(2)}, u32[]{:S(2)}) collective-permute-start(bf16[40,2,16,683]{3,2,1,0:T(8,128)(2,1)} %get-tuple-element.13.own), channel_id=1, source_target_pairs={{8,0},{16,8},{24,16},{9,1},{17,9},{25,17},{10,2},{18,10},{26,18},{... | collective-permute-start | bytes 5245448 | tf_op jit(solution)/shard_map/ppermute | solution.py:544
  95.9 24.9 %collective-permute-start.2 = (bf16[40,2,16,683]{3,2,1,0:T(8,128)(2,1)}, bf16[40,2,16,683]{3,2,1,0:T(8,128)(2,1)S(1)}, u32[]{:S(2)}, u32[]{:S(2)}) collective-permute-start(bf16[40,2,16,683]{3,2,1,0:T(8,128)(2,1)} %get-tuple-element.13.own), channel_id=1, source_target_pairs={{0,8},{8,16},{16,24},{1,9},{9,17},{17,25},{2,10},{10,18},{18,26},{... | collective-permute-start | bytes 5245448 | tf_op jit(solution)/shard_map/ppermute | solution.py:543
  140.7 18.7 %all-to-all-start.1 = ((bf16[8,256,128]{2,1,0:T(8,128)(2,1)}), bf16[8,256,128]{2,1,0:T(8,128)(2,1)S(1)}, u32[]{:S(2)}, u32[]{:S(2)}) async-start(bf16[8,256,128]{2,1,0:T(8,128)(2,1)} %bitcast.5), calls=%async_computation.1 | async-start | bytes 1048576 | tf_op jit(solution)/shard_map/all_to_all | solution.py:549
  145.9 1.4 copy-start.4
  147.2 12.1 %copy-start.5 = (bf16[683,1024]{1,0:T(8,128)(2,1)S(1)}, bf16[683,1024]{1,0:T(8,128)(2,1)}, u32[]{:S(2)}) copy-start(bf16[683,1024]{1,0:T(8,128)(2,1)} %copy-done.2) | copy-start | bytes 4196356

commit v16 on v13

--- a/solution.py
+++ b/solution.py
@@ -368,7 +368,7 @@
     )(offsets, low, *in_hbm(own), high, *tokens)
 
 
-def finish_block(first, waves, received, noise, even, odd, spectra_out, fourier_out, ready, store):
+def finish_block(first, waves, received, noise, even, odd, spectra_out, fourier_out, ready, store, cuts):
     truncation = even.shape[0]
     block, mem_local, parts, fields = noise.shape[:4]
     per_slot = received.shape[1] // block
@@ -393,19 +393,20 @@
         even_rows.append(jnp.where(is_odd, 0.0, child).astype(jnp.bfloat16))
         odd_rows.append(jnp.where(is_odd, child, 0.0).astype(jnp.bfloat16))
     store()
-    result = jnp.dot(
-        jnp.concatenate(even_rows, axis=0), even[...], preferred_element_type=jnp.float32
-    )
-    result += jnp.dot(
-        jnp.concatenate(odd_rows, axis=0), odd[...], preferred_element_type=jnp.float32
-    )
-    fourier_out[...] = result.reshape(fourier_out.shape).astype(fourier_out.dtype)
+    even_rows, odd_rows = jnp.concatenate(even_rows, axis=0), jnp.concatenate(odd_rows, axis=0)
+    for columns, leave in cuts:
+        result = jnp.dot(even_rows, even[:, columns], preferred_element_type=jnp.float32)
+        result += jnp.dot(odd_rows, odd[:, columns], preferred_element_type=jnp.float32)
+        shape = fourier_out.shape[:-1] + (result.shape[1],)
+        fourier_out[..., columns] = result.reshape(shape).astype(fourier_out.dtype)
+        leave()
 
 
 def finish_kernel(first, block, waves, received, noise, even, odd, *rest):
     start = first + pl.program_id(0) * block
     nothing = lambda: None
-    finish_block(start, waves, received, noise, even, odd, *rest[-2:], nothing, nothing)
+    cuts = [(slice(0, even.shape[1]), nothing)]
+    finish_block(start, waves, received, noise, even, odd, *rest[-2:], nothing, nothing, cuts)
 
 
 def last_kernel(first, waves, received, noise, even, odd, *rest):
@@ -413,7 +414,16 @@
     part = pl.ds(first, noise_here.shape[0])
     fetch = pltpu.make_async_copy(noise.at[part], noise_here, sems.at[0])
     leave = pltpu.make_async_copy(spectra_here, spectra_out.at[part], sems.at[1])
-    leave_too = pltpu.make_async_copy(fourier_here, fourier_out.at[part], sems.at[2])
+    width = even.shape[1] // 2
+    cuts = [slice(0, width), slice(width, 2 * width)]
+    halves = [
+        pltpu.make_async_copy(
+            fourier_here.at[:, :, :, :, pl.ds(at * width, width)],
+            fourier_out.at[part, :, :, :, pl.ds(at * width, width)],
+            sems.at[2 + at],
+        )
+        for at in range(2)
+    ]
     fetch.start()
     finish_block(
         first,
@@ -426,10 +436,11 @@
         fourier_here,
         fetch.wait,
         leave.start,
-    )
-    leave_too.start()
+        [(columns, half.start) for columns, half in zip(cuts, halves)],
+    )
     leave.wait()
-    leave_too.wait()
+    for half in halves:
+        half.wait()
 
 
 def last_transform(waves, first, received, noise, even, odd, outs):
@@ -453,7 +464,7 @@
             pltpu.VMEM((block,) + noise.shape[1:], jnp.bfloat16),
             pltpu.VMEM((block,) + noise.shape[1:], jnp.bfloat16),
             pltpu.VMEM((block,) + fourier_shape[1:], jnp.bfloat16),
-            pltpu.SemaphoreType.DMA((3,)),
+            pltpu.SemaphoreType.DMA((4,)),
         ],
         input_output_aliases={5: 0, 6: 1},
         compiler_params=pltpu.CompilerParams(vmem_limit_bytes=VMEM_BYTES),

time: 166 us -> 166 us (level)
  no operation moved by 1% of the time
where the time goes in v16:
time: 166 us; the launch traced here: 163 us
  Pallas kernels  73.6 us (44%)
  waiting for transfers between devices  48.9 us (29%)
  starting transfers between devices  34.3 us (21%)
  other arithmetic  2.88 us (2%)
  local copies, waits for them, and re-layouts  2.12 us (1%)
    ppermute x3, waiting for transfers between devices, neighbours(): lax.ppermute(rows[:, rows.shape[1] - SPREAD * per_member:], 'member', upw...  33.4 us
    pallas_call x3, Pallas kernels, zonal_transform(): pl.pallas_call(functools.partial(zonal_kernel, truncation, len(tokens)),...  29.6 us
    all_to_all x3, starting transfers between devices, exchanged(): lax.all_to_all(outgoing, 'lat', split_axis=0, concat_axis=0, tiled=True)  16.2 us
    ppermute x3, starting transfers between devices, neighbours(): lax.ppermute(rows[:, rows.shape[1] - SPREAD * per_member:], 'member', upw...  12.3 us
    pallas_call x1, Pallas kernels, finish_transform(): pl.pallas_call(functools.partial(finish_kernel, first, block), grid_spec=...  12.2 us
    pallas_call x2, Pallas kernels, copy_parents(): pl.pallas_call(copy_kernel, grid_spec=pltpu.PrefetchScalarGridSpec(num_sc...  9.59 us
    pallas_call x1, Pallas kernels, inverse_transform(): pl.pallas_call(functools.partial(inverse_kernel, first, block), grid_spec...  9.27 us
    ppermute x3, waiting for transfers between devices, neighbours(): high = lax.ppermute(rows[:, :SPREAD * per_member], 'member', downward)  8.8 us
  transfers between devices with their start and end apart: 9, of which 7 were waited for; matrix products, arithmetic and copies ran while one was open for 2% of the time, Pallas kernels for 36%

profile of v16, /device:TPU:1, one launch (start us, length us, event | category | flops | bytes accessed | tf_op | source)
XLA Modules:
  0.0 162.7 jit_solution(674983270855967693)
XLA Ops:
  0.6 0.8 reshape.34
  1.4 0.1 fusion.13
  1.5 0.1 reshape.42.waves
  1.6 11.0 %zonal.4 = bf16[320,32,128]{2,1,0:T(8,128)(2,1)} custom-call(s32[320,1]{1,0:T(8,128)S(1)} %reshape.42.waves, bf16[2,8,128,2048]{3,2,1,0:T(8,128)(2,1)} %velocity.5, bf16[2,8,128,2048]{3,2,1,0:T(8,128)(2,1)} %tracer.5), custom_call_target="tpu_custom_call" | custom-call | flops 5368709120 | bytes 19398656 | tf_op jit(solution)/shard_map/zonal/pallas_call | solution.py:171
  12.5 6.4 %all-to-all-start = ((bf16[8,1280,128]{2,1,0:T(8,128)(2,1)}), bf16[8,1280,128]{2,1,0:T(8,128)(2,1)}, u32[]{:S(2)}, u32[]{:S(2)}) async-start(bf16[8,1280,128]{2,1,0:T(8,128)(2,1)} %bitcast.4), calls=%async_computation | async-start | bytes 5242880 | tf_op jit(solution)/shard_map/all_to_all | solution.py:559
  18.9 0.1 reshape.43.waves
  19.0 0.0 copy-start
  19.1 11.0 %zonal.5.own = bf16[320,32,128]{2,1,0:T(8,128)(2,1)} custom-call(s32[320,1]{1,0:T(8,128)S(1)} %reshape.43.waves, bf16[2,8,128,2048]{3,2,1,0:T(8,128)(2,1)} %velocity.5, bf16[2,8,128,2048]{3,2,1,0:T(8,128)(2,1)} %tracer.5), custom_call_target="tpu_custom_call" | custom-call | flops 5368709120 | bytes 19398656 | tf_op jit(solution)/shard_map/zonal/pallas_call | solution.py:171
  30.0 4.0 %collective-permute-start.4 = (bf16[320,32,128]{2,1,0:T(8,128)(2,1)}, bf16[320,32,128]{2,1,0:T(8,128)(2,1)S(1)}, u32[]{:S(2)}, u32[]{:S(2)}) collective-permute-start(bf16[320,32,128]{2,1,0:T(8,128)(2,1)} %zonal.5.own), channel_id=1, source_target_pairs={{0,8},{8,16},{16,24},{1,9},{9,17},{17,25},{2,10},{10,18},{18,26},{... | collective-permute-start | bytes 7864328 | tf_op jit(solution)/shard_map/ppermute | solution.py:553
  34.0 1.9 %collective-permute-start.5 = (bf16[320,32,128]{2,1,0:T(8,128)(2,1)}, bf16[320,32,128]{2,1,0:T(8,128)(2,1)}, u32[]{:S(2)}, u32[]{:S(2)}) collective-permute-start(bf16[320,32,128]{2,1,0:T(8,128)(2,1)} %zonal.5.own), channel_id=1, source_target_pairs={{8,0},{16,8},{24,16},{9,1},{17,9},{25,17},{10,2},{18,10},{26,18},{... | collective-permute-start | bytes 7864328 | tf_op jit(solution)/shard_map/ppermute | solution.py:554
  35.9 0.0 copy-done
  35.9 0.1 subtract_add_fusion.offsets
  36.0 26.9 %collective-permute-done.4.low = bf16[320,32,128]{2,1,0:T(8,128)(2,1)S(1)} collective-permute-done((bf16[320,32,128]{2,1,0:T(8,128)(2,1)}, bf16[320,32,128]{2,1,0:T(8,128)(2,1)S(1)}, u32[]{:S(2)}, u32[]{:S(2)}) %collective-permute-start.4) | collective-permute-done | bytes 2621472 | tf_op jit(solution)/shard_map/ppermute | solution.py:553
  62.9 4.4 %collective-permute-done.5.high = bf16[320,32,128]{2,1,0:T(8,128)(2,1)} collective-permute-done((bf16[320,32,128]{2,1,0:T(8,128)(2,1)}, bf16[320,32,128]{2,1,0:T(8,128)(2,1)}, u32[]{:S(2)}, u32[]{:S(2)}) %collective-permute-start.5) | collective-permute-done | bytes 2621472 | tf_op jit(solution)/shard_map/ppermute | solution.py:554
  67.3 5.7 %parents.3 = bf16[320,32,128]{2,1,0:T(8,128)(2,1)} custom-call(s32[2]{0:T(128)S(1)} %subtract_add_fusion.offsets, bf16[320,32,128]{2,1,0:T(8,128)(2,1)S(1)} %collective-permute-done.4.low, bf16[320,32,128]{2,1,0:T(8,128)(2,1)} %zonal.5.own, bf16[320,32,128]{2,1,0:T(8,128)(2,1)} %collective-permute-done.5.high), custom_call_target="tpu_custom_call" | custom-call | bytes 10485760 | tf_op jit(solution)/shard_map/parents/pallas_call | solution.py:355
  73.0 4.6 %all-to-all-done.received = bf16[8,1280,128]{2,1,0:T(8,128)(2,1)} async-done(((bf16[8,1280,128]{2,1,0:T(8,128)(2,1)}), bf16[8,1280,128]{2,1,0:T(8,128)(2,1)}, u32[]{:S(2)}, u32[]{:S(2)}) %all-to-all-start) | async-done | bytes 2621472 | tf_op jit(solution)/shard_map/all_to_all | solution.py:559
  77.6 4.7 %all-to-all-start.2 = ((bf16[8,1280,128]{2,1,0:T(8,128)(2,1)}), bf16[8,1280,128]{2,1,0:T(8,128)(2,1)}, u32[]{:S(2)}, u32[]{:S(2)}) async-start(bf16[8,1280,128]{2,1,0:T(8,128)(2,1)} %bitcast.3), calls=%async_computation.2 | async-start | bytes 5242880 | tf_op jit(solution)/shard_map/all_to_all | solution.py:559
  82.3 0.8 dynamic_slice.6.waves
  83.1 0.1 fusion.9
  83.2 0.2 copy.17
  83.4 1.4 fusion.6
  84.8 1.3 sine_multiply_fusion
  86.1 1.8 %tables.1 = (bf16[683,1024]{1,0:T(8,128)(2,1)S(1)}, bf16[683,1024]{1,0:T(8,128)(2,1)S(1)}) custom-call(f32[683,8]{1,0:T(8,128)S(1)} %get-tuple-element.19.cos_c, f32[683,8]{1,0:T(8,128)S(1)} %get-tuple-element.18.sin_c, f32[683,128]{1,0:T(8,128)S(1)} %get-tuple-element.23.cos_f, f32[683,128]{1,0:T(8,128)S(1)} %get-tuple-element.22.sin_f), custom_call_target="tpu_custom_call" | custom-call | flops 4196352 | bytes 2797568 | tf_op jit(solution)/shard_map/tables/pallas_call | solution.py:53
  87.9 7.8 %forward.1 = (bf16[40,2,16,683]{3,2,1,0:T(8,128)(2,1)}, f32[8,128]{1,0:T(8,128)}) custom-call(s32[88]{0:T(128)S(1)} %dynamic_slice.6.waves, bf16[8,1280,128]{2,1,0:T(8,128)(2,1)} %all-to-all-done.received, bf16[683,1024]{1,0:T(8,128)(2,1)S(1)} %get-tuple-element.10.even, bf16[683,1024]{1,0:T(8,128)(2,1)S(1)} %get-tuple-element.11.odd), custom_call_target="tpu_custom_call" | custom-call | flops 3580887040 | bytes 7167488 | tf_op jit(solution)/shard_map/forward/pallas_call | solution.py:219
  95.7 4.7 %collective-permute-start.2 = (bf16[40,2,16,683]{3,2,1,0:T(8,128)(2,1)}, bf16[40,2,16,683]{3,2,1,0:T(8,128)(2,1)}, u32[]{:S(2)}, u32[]{:S(2)}) collective-permute-start(bf16[40,2,16,683]{3,2,1,0:T(8,128)(2,1)} %get-tuple-element.12.own), channel_id=1, source_target_pairs={{0,8},{8,16},{16,24},{1,9},{9,17},{17,25},{2,10},{10,18},{18,26},{... | collective-permute-start | bytes 5245448 | tf_op jit(solution)/shard_map/ppermute | solution.py:553
  100.4 1.9 %collective-permute-start.3 = (bf16[40,2,16,683]{3,2,1,0:T(8,128)(2,1)}, bf16[40,2,16,683]{3,2,1,0:T(8,128)(2,1)}, u32[]{:S(2)}, u32[]{:S(2)}) collective-permute-start(bf16[40,2,16,683]{3,2,1,0:T(8,128)(2,1)} %get-tuple-element.12.own), channel_id=1, source_target_pairs={{8,0},{16,8},{24,16},{9,1},{17,9},{25,17},{10,2},{18,10},{26,18},{... | collective-permute-start | bytes 5245448 | tf_op jit(solution)/shard_map/ppermute | solution.py:554
  102.4 0.1 slice.9
  102.4 0.1 reshape.41.waves
  102.5 7.7 %zonal.3.own = bf16[64,32,128]{2,1,0:T(8,128)(2,1)} custom-call(s32[64,1]{1,0:T(8,128)S(1)} %reshape.41.waves, bf16[2,8,128,2048]{3,2,1,0:T(8,128)(2,1)} %velocity.5, bf16[2,8,128,2048]{3,2,1,0:T(8,128)(2,1)} %tracer.5), custom_call_target="tpu_custom_call" | custom-call | flops 1073741824 | bytes 17301504 | tf_op jit(solution)/shard_map/zonal/pallas_call | solution.py:171
  110.2 3.6 %collective-permute-start = (bf16[64,32,128]{2,1,0:T(8,128)(2,1)}, bf16[64,32,128]{2,1,0:T(8,128)(2,1)S(1)}, u32[]{:S(2)}, u32[]{:S(2)}) collective-permute-start(bf16[64,32,128]{2,1,0:T(8,128)(2,1)} %zonal.3.own), channel_id=1, source_target_pairs={{0,8},{8,16},{16,24},{1,9},{9,17},{17,25},{2,10},{10,18},{18,26},{... | collective-permute-start | bytes 1572872 | tf_op jit(solution)/shard_map/ppermute | solution.py:553
  113.9 1.9 %collective-permute-start.1 = (bf16[64,32,128]{2,1,0:T(8,128)(2,1)}, bf16[64,32,128]{2,1,0:T(8,128)(2,1)S(1)}, u32[]{:S(2)}, u32[]{:S(2)}) collective-permute-start(bf16[64,32,128]{2,1,0:T(8,128)(2,1)} %zonal.3.own), channel_id=1, source_target_pairs={{8,0},{16,8},{24,16},{9,1},{17,9},{25,17},{10,2},{18,10},{26,18},{... | collective-permute-start | bytes 1572872 | tf_op jit(solution)/shard_map/ppermute | solution.py:554
  115.8 6.5 %collective-permute-done.2.low = bf16[40,2,16,683]{3,2,1,0:T(8,128)(2,1)} collective-permute-done((bf16[40,2,16,683]{3,2,1,0:T(8,128)(2,1)}, bf16[40,2,16,683]{3,2,1,0:T(8,128)(2,1)}, u32[]{:S(2)}, u32[]{:S(2)}) %collective-permute-start.2) | collective-permute-done | bytes 1748512 | tf_op jit(solution)/shard_map/ppermute | solution.py:553
  122.3 4.4 %collective-permute-done.3.high = bf16[40,2,16,683]{3,2,1,0:T(8,128)(2,1)} collective-permute-done((bf16[40,2,16,683]{3,2,1,0:T(8,128)(2,1)}, bf16[40,2,16,683]{3,2,1,0:T(8,128)(2,1)}, u32[]{:S(2)}, u32[]{:S(2)}) %collective-permute-start.3) | collective-permute-done | bytes 1748512 | tf_op jit(solution)/shard_map/ppermute | solution.py:554
  126.7 9.3 %inverse.1 = (bf16[88,2,2,8,683]{4,3,2,1,0:T(8,128)(2,1)}, bf16[88,2,2,8,1024]{4,3,2,1,0:T(8,128)(2,1)}, f32[8,128]{1,0:T(8,128)S(1)}) custom-call(s32[88]{0:T(128)S(1)} %dynamic_slice.6.waves, s32[2]{0:T(128)S(1)} %subtract_add_fusion.offsets, bf16[40,2,16,683]{3,2,1,0:T(8,128)(2,1)} %collective-permute-done.2.low, ...), custom_call_target="tpu_custom_call" | custom-call | flops 3580887040 | bytes 14161408 | tf_op jit(solution)/shard_map/inverse/pallas_call | solution.py:309
  136.0 0.0 collective-permute-done.low
  136.0 0.0 collective-permute-done.1.high
  136.0 3.9 %parents.2 = bf16[64,32,128]{2,1,0:T(8,128)(2,1)} custom-call(s32[2]{0:T(128)S(1)} %subtract_add_fusion.offsets, bf16[64,32,128]{2,1,0:T(8,128)(2,1)S(1)} %collective-permute-done.low, bf16[64,32,128]{2,1,0:T(8,128)(2,1)} %zonal.3.own, bf16[64,32,128]{2,1,0:T(8,128)(2,1)S(1)} %collective-permute-done.1.high, f32[8,128]{1,0:T(8,128)S(1)} %get-tuple-element.13.rest_0_), custom_call_target="tpu_custom_call" | custom-call | bytes 2097152 | tf_op jit(solution)/shard_map/parents/pallas_call | solution.py:355
  139.8 0.8 all-to-all-done.2.received
  140.6 5.1 %all-to-all-start.1 = ((bf16[8,256,128]{2,1,0:T(8,128)(2,1)}), bf16[8,256,128]{2,1,0:T(8,128)(2,1)S(1)}, u32[]{:S(2)}, u32[]{:S(2)}) async-start(bf16[8,256,128]{2,1,0:T(8,128)(2,1)} %bitcast.5), calls=%async_computation.1 | async-start | bytes 1048576 | tf_op jit(solution)/shard_map/all_to_all | solution.py:559
  145.7 12.2 %finish.1 = (bf16[88,2,2,8,683]{4,3,2,1,0:T(8,128)(2,1)}, bf16[88,2,2,8,1024]{4,3,2,1,0:T(8,128)(2,1)}) custom-call(s32[88]{0:T(128)S(1)} %dynamic_slice.6.waves, bf16[8,1280,128]{2,1,0:T(8,128)(2,1)} %all-to-all-done.2.received, bf16[88,2,2,8,683]{4,3,2,1,0:T(8,128)(2,1)} %noise.5, ...), custom_call_target="tpu_custom_call", output_to_operand_aliasing={{0}: (5, {}), {1}: (6, {})} | custom-call | flops 7161774080 | bytes 11537408 | tf_op jit(solution)/shard_map/finish/pallas_call | solution.py:494
  157.9 1.3 all-to-all-done.1.received
  159.2 3.3 %last.1 = (bf16[88,2,2,8,683]{4,3,2,1,0:T(8,128)(2,1)}, bf16[88,2,2,8,1024]{4,3,2,1,0:T(8,128)(2,1)}) custom-call(s32[88]{0:T(128)S(1)} %dynamic_slice.6.waves, bf16[8,256,128]{2,1,0:T(8,128)(2,1)S(1)} %all-to-all-done.1.received, bf16[88,2,2,8,683]{4,3,2,1,0:T(8,128)(2,1)} %noise.5, ...), custom_call_target="tpu_custom_call", output_to_operand_aliasing={{0}: (5, {}), {1}: (6, {})} | custom-call | flops 1432354816 | bytes 4545536 | tf_op jit(solution)/shard_map/last/pallas_call | solution.py:454
  (2 shorter events, 0.0 us)
Async XLA Ops:
  12.5 65.1 %all-to-all-start = ((bf16[8,1280,128]{2,1,0:T(8,128)(2,1)}), bf16[8,1280,128]{2,1,0:T(8,128)(2,1)}, u32[]{:S(2)}, u32[]{:S(2)}) async-start(bf16[8,1280,128]{2,1,0:T(8,128)(2,1)} %bitcast.4), calls=%async_computation | async-start | bytes 5242880 | tf_op jit(solution)/shard_map/all_to_all | solution.py:559
  19.0 16.9 %copy-start = (s32[8]{0:T(128)S(1)}, s32[8]{0:T(128)}, u32[]{:S(2)}) copy-start(s32[8]{0:T(128)} %param.8) | copy-start | bytes 100
  30.0 32.9 %collective-permute-start.4 = (bf16[320,32,128]{2,1,0:T(8,128)(2,1)}, bf16[320,32,128]{2,1,0:T(8,128)(2,1)S(1)}, u32[]{:S(2)}, u32[]{:S(2)}) collective-permute-start(bf16[320,32,128]{2,1,0:T(8,128)(2,1)} %zonal.5.own), channel_id=1, source_target_pairs={{0,8},{8,16},{16,24},{1,9},{9,17},{17,25},{2,10},{10,18},{18,26},{... | collective-permute-start | bytes 7864328 | tf_op jit(solution)/shard_map/ppermute | solution.py:553
  34.0 33.3 %collective-permute-start.5 = (bf16[320,32,128]{2,1,0:T(8,128)(2,1)}, bf16[320,32,128]{2,1,0:T(8,128)(2,1)}, u32[]{:S(2)}, u32[]{:S(2)}) collective-permute-start(bf16[320,32,128]{2,1,0:T(8,128)(2,1)} %zonal.5.own), channel_id=1, source_target_pairs={{8,0},{16,8},{24,16},{9,1},{17,9},{25,17},{10,2},{18,10},{26,18},{... | collective-permute-start | bytes 7864328 | tf_op jit(solution)/shard_map/ppermute | solution.py:554
  77.6 63.0 %all-to-all-start.2 = ((bf16[8,1280,128]{2,1,0:T(8,128)(2,1)}), bf16[8,1280,128]{2,1,0:T(8,128)(2,1)}, u32[]{:S(2)}, u32[]{:S(2)}) async-start(bf16[8,1280,128]{2,1,0:T(8,128)(2,1)} %bitcast.3), calls=%async_computation.2 | async-start | bytes 5242880 | tf_op jit(solution)/shard_map/all_to_all | solution.py:559
  95.7 26.6 %collective-permute-start.2 = (bf16[40,2,16,683]{3,2,1,0:T(8,128)(2,1)}, bf16[40,2,16,683]{3,2,1,0:T(8,128)(2,1)}, u32[]{:S(2)}, u32[]{:S(2)}) collective-permute-start(bf16[40,2,16,683]{3,2,1,0:T(8,128)(2,1)} %get-tuple-element.12.own), channel_id=1, source_target_pairs={{0,8},{8,16},{16,24},{1,9},{9,17},{17,25},{2,10},{10,18},{18,26},{... | collective-permute-start | bytes 5245448 | tf_op jit(solution)/shard_map/ppermute | solution.py:553
  100.4 26.3 %collective-permute-start.3 = (bf16[40,2,16,683]{3,2,1,0:T(8,128)(2,1)}, bf16[40,2,16,683]{3,2,1,0:T(8,128)(2,1)}, u32[]{:S(2)}, u32[]{:S(2)}) collective-permute-start(bf16[40,2,16,683]{3,2,1,0:T(8,128)(2,1)} %get-tuple-element.12.own), channel_id=1, source_target_pairs={{8,0},{16,8},{24,16},{9,1},{17,9},{25,17},{10,2},{18,10},{26,18},{... | collective-permute-start | bytes 5245448 | tf_op jit(solution)/shard_map/ppermute | solution.py:554
  110.2 25.7 %collective-permute-start = (bf16[64,32,128]{2,1,0:T(8,128)(2,1)}, bf16[64,32,128]{2,1,0:T(8,128)(2,1)S(1)}, u32[]{:S(2)}, u32[]{:S(2)}) collective-permute-start(bf16[64,32,128]{2,1,0:T(8,128)(2,1)} %zonal.3.own), channel_id=1, source_target_pairs={{0,8},{8,16},{16,24},{1,9},{9,17},{17,25},{2,10},{10,18},{18,26},{... | collective-permute-start | bytes 1572872 | tf_op jit(solution)/shard_map/ppermute | solution.py:553
  113.9 22.1 %collective-permute-start.1 = (bf16[64,32,128]{2,1,0:T(8,128)(2,1)}, bf16[64,32,128]{2,1,0:T(8,128)(2,1)S(1)}, u32[]{:S(2)}, u32[]{:S(2)}) collective-permute-start(bf16[64,32,128]{2,1,0:T(8,128)(2,1)} %zonal.3.own), channel_id=1, source_target_pairs={{8,0},{16,8},{24,16},{9,1},{17,9},{25,17},{10,2},{18,10},{26,18},{... | collective-permute-start | bytes 1572872 | tf_op jit(solution)/shard_map/ppermute | solution.py:554
  140.6 18.6 %all-to-all-start.1 = ((bf16[8,256,128]{2,1,0:T(8,128)(2,1)}), bf16[8,256,128]{2,1,0:T(8,128)(2,1)S(1)}, u32[]{:S(2)}, u32[]{:S(2)}) async-start(bf16[8,256,128]{2,1,0:T(8,128)(2,1)} %bitcast.5), calls=%async_computation.1 | async-start | bytes 1048576 | tf_op jit(solution)/shard_map/all_to_all | solution.py:559

commit v17 on v13

--- a/solution.py
+++ b/solution.py
@@ -348,7 +348,7 @@
 
 
 def copy_parents(offsets, low, own, high, tokens):
-    steps = math.gcd(own.shape[0], 4)
+    steps = math.gcd(own.shape[0], 8)
     block = lambda array: pl.BlockSpec(
         (array.shape[0] // steps,) + array.shape[1:], lambda step, o: (step, 0, 0)
     )

time: 166 us -> 167 us (level); the launches traced: 163 us -> 166 us
  Pallas kernels: 73.7 us -> 77.1 us
    pallas_call x2, Pallas kernels: 9.59 us -> 13 us  [copy_parents(): pl.pallas_call(copy_kernel, grid_spec=pltpu.PrefetchScalarGridSpec(num_sc...]
  transfers between devices with their start and end apart: 9 -> 9, of which waited for: 7 -> 6; matrix products, arithmetic and copies ran while one was open for 2% -> 2% of each run, Pallas kernels for 36% -> 38%
where the time goes in v17:
time: 167 us; the launch traced here: 166 us
  Pallas kernels  77.1 us (46%)
  waiting for transfers between devices  47.9 us (29%)
  starting transfers between devices  34.6 us (21%)
  other arithmetic  2.88 us (2%)
  local copies, waits for them, and re-layouts  2.12 us (1%)
    ppermute x3, waiting for transfers between devices, neighbours(): lax.ppermute(rows[:, rows.shape[1] - SPREAD * per_member:], 'member', upw...  33.4 us
    pallas_call x3, Pallas kernels, zonal_transform(): pl.pallas_call(functools.partial(zonal_kernel, truncation, len(tokens)),...  29.6 us
    all_to_all x3, starting transfers between devices, exchanged(): lax.all_to_all(outgoing, 'lat', split_axis=0, concat_axis=0, tiled=True)  16.5 us
    pallas_call x2, Pallas kernels, copy_parents(): pl.pallas_call(copy_kernel, grid_spec=pltpu.PrefetchScalarGridSpec(num_sc...  13 us
    ppermute x3, starting transfers between devices, neighbours(): lax.ppermute(rows[:, rows.shape[1] - SPREAD * per_member:], 'member', upw...  12.3 us
    pallas_call x1, Pallas kernels, finish_transform(): pl.pallas_call(functools.partial(finish_kernel, first, block), grid_spec=...  12.2 us
    pallas_call x1, Pallas kernels, inverse_transform(): pl.pallas_call(functools.partial(inverse_kernel, first, block), grid_spec...  9.27 us
    ppermute x3, waiting for transfers between devices, neighbours(): high = lax.ppermute(rows[:, :SPREAD * per_member], 'member', downward)  8.8 us
  transfers between devices with their start and end apart: 9, of which 6 were waited for; matrix products, arithmetic and copies ran while one was open for 2% of the time, Pallas kernels for 38%

profile of v17, /device:TPU:1, one launch (start us, length us, event | category | flops | bytes accessed | tf_op | source)
XLA Modules:
  0.0 165.6 jit_solution(3484369225971894450)
XLA Ops:
  0.6 0.8 reshape.34
  1.4 0.1 fusion.13
  1.5 0.1 reshape.42.waves
  1.6 11.0 %zonal.4 = bf16[320,32,128]{2,1,0:T(8,128)(2,1)} custom-call(s32[320,1]{1,0:T(8,128)S(1)} %reshape.42.waves, bf16[2,8,128,2048]{3,2,1,0:T(8,128)(2,1)} %velocity.5, bf16[2,8,128,2048]{3,2,1,0:T(8,128)(2,1)} %tracer.5), custom_call_target="tpu_custom_call" | custom-call | flops 5368709120 | bytes 19398656 | tf_op jit(solution)/shard_map/zonal/pallas_call | solution.py:171
  12.5 6.4 %all-to-all-start = ((bf16[8,1280,128]{2,1,0:T(8,128)(2,1)}), bf16[8,1280,128]{2,1,0:T(8,128)(2,1)}, u32[]{:S(2)}, u32[]{:S(2)}) async-start(bf16[8,1280,128]{2,1,0:T(8,128)(2,1)} %bitcast.4), calls=%async_computation | async-start | bytes 5242880 | tf_op jit(solution)/shard_map/all_to_all | solution.py:548
  18.9 0.1 reshape.43.waves
  19.0 0.0 copy-start
  19.1 11.0 %zonal.5.own = bf16[320,32,128]{2,1,0:T(8,128)(2,1)} custom-call(s32[320,1]{1,0:T(8,128)S(1)} %reshape.43.waves, bf16[2,8,128,2048]{3,2,1,0:T(8,128)(2,1)} %velocity.5, bf16[2,8,128,2048]{3,2,1,0:T(8,128)(2,1)} %tracer.5), custom_call_target="tpu_custom_call" | custom-call | flops 5368709120 | bytes 19398656 | tf_op jit(solution)/shard_map/zonal/pallas_call | solution.py:171
  30.0 4.0 %collective-permute-start.4 = (bf16[320,32,128]{2,1,0:T(8,128)(2,1)}, bf16[320,32,128]{2,1,0:T(8,128)(2,1)S(1)}, u32[]{:S(2)}, u32[]{:S(2)}) collective-permute-start(bf16[320,32,128]{2,1,0:T(8,128)(2,1)} %zonal.5.own), channel_id=1, source_target_pairs={{0,8},{8,16},{16,24},{1,9},{9,17},{17,25},{2,10},{10,18},{18,26},{... | collective-permute-start | bytes 7864328 | tf_op jit(solution)/shard_map/ppermute | solution.py:542
  34.0 1.9 %collective-permute-start.5 = (bf16[320,32,128]{2,1,0:T(8,128)(2,1)}, bf16[320,32,128]{2,1,0:T(8,128)(2,1)}, u32[]{:S(2)}, u32[]{:S(2)}) collective-permute-start(bf16[320,32,128]{2,1,0:T(8,128)(2,1)} %zonal.5.own), channel_id=1, source_target_pairs={{8,0},{16,8},{24,16},{9,1},{17,9},{25,17},{10,2},{18,10},{26,18},{... | collective-permute-start | bytes 7864328 | tf_op jit(solution)/shard_map/ppermute | solution.py:543
  35.9 0.0 copy-done
  35.9 0.1 subtract_add_fusion.offsets
  36.0 26.9 %collective-permute-done.4.low = bf16[320,32,128]{2,1,0:T(8,128)(2,1)S(1)} collective-permute-done((bf16[320,32,128]{2,1,0:T(8,128)(2,1)}, bf16[320,32,128]{2,1,0:T(8,128)(2,1)S(1)}, u32[]{:S(2)}, u32[]{:S(2)}) %collective-permute-start.4) | collective-permute-done | bytes 2621472 | tf_op jit(solution)/shard_map/ppermute | solution.py:542
  62.9 4.4 %collective-permute-done.5.high = bf16[320,32,128]{2,1,0:T(8,128)(2,1)} collective-permute-done((bf16[320,32,128]{2,1,0:T(8,128)(2,1)}, bf16[320,32,128]{2,1,0:T(8,128)(2,1)}, u32[]{:S(2)}, u32[]{:S(2)}) %collective-permute-start.5) | collective-permute-done | bytes 2621472 | tf_op jit(solution)/shard_map/ppermute | solution.py:543
  67.3 7.6 %parents.3 = bf16[320,32,128]{2,1,0:T(8,128)(2,1)} custom-call(s32[2]{0:T(128)S(1)} %subtract_add_fusion.offsets, bf16[320,32,128]{2,1,0:T(8,128)(2,1)S(1)} %collective-permute-done.4.low, bf16[320,32,128]{2,1,0:T(8,128)(2,1)} %zonal.5.own, bf16[320,32,128]{2,1,0:T(8,128)(2,1)} %collective-permute-done.5.high), custom_call_target="tpu_custom_call" | custom-call | bytes 10485760 | tf_op jit(solution)/shard_map/parents/pallas_call | solution.py:355
  74.9 2.8 %all-to-all-done.received = bf16[8,1280,128]{2,1,0:T(8,128)(2,1)} async-done(((bf16[8,1280,128]{2,1,0:T(8,128)(2,1)}), bf16[8,1280,128]{2,1,0:T(8,128)(2,1)}, u32[]{:S(2)}, u32[]{:S(2)}) %all-to-all-start) | async-done | bytes 2621472 | tf_op jit(solution)/shard_map/all_to_all | solution.py:548
  77.6 4.7 %all-to-all-start.2 = ((bf16[8,1280,128]{2,1,0:T(8,128)(2,1)}), bf16[8,1280,128]{2,1,0:T(8,128)(2,1)}, u32[]{:S(2)}, u32[]{:S(2)}) async-start(bf16[8,1280,128]{2,1,0:T(8,128)(2,1)} %bitcast.3), calls=%async_computation.2 | async-start | bytes 5242880 | tf_op jit(solution)/shard_map/all_to_all | solution.py:548
  82.3 0.8 dynamic_slice.6.waves
  83.1 0.1 fusion.9
  83.2 0.2 copy.17
  83.4 1.4 fusion.6
  84.8 1.3 sine_multiply_fusion
  86.1 1.8 %tables.1 = (bf16[683,1024]{1,0:T(8,128)(2,1)S(1)}, bf16[683,1024]{1,0:T(8,128)(2,1)S(1)}) custom-call(f32[683,8]{1,0:T(8,128)S(1)} %get-tuple-element.19.cos_c, f32[683,8]{1,0:T(8,128)S(1)} %get-tuple-element.18.sin_c, f32[683,128]{1,0:T(8,128)S(1)} %get-tuple-element.23.cos_f, f32[683,128]{1,0:T(8,128)S(1)} %get-tuple-element.22.sin_f), custom_call_target="tpu_custom_call" | custom-call | flops 4196352 | bytes 2797568 | tf_op jit(solution)/shard_map/tables/pallas_call | solution.py:53
  87.9 7.8 %forward.1 = (bf16[40,2,16,683]{3,2,1,0:T(8,128)(2,1)}, f32[8,128]{1,0:T(8,128)}) custom-call(s32[88]{0:T(128)S(1)} %dynamic_slice.6.waves, bf16[8,1280,128]{2,1,0:T(8,128)(2,1)} %all-to-all-done.received, bf16[683,1024]{1,0:T(8,128)(2,1)S(1)} %get-tuple-element.10.even, bf16[683,1024]{1,0:T(8,128)(2,1)S(1)} %get-tuple-element.11.odd), custom_call_target="tpu_custom_call" | custom-call | flops 3580887040 | bytes 7167488 | tf_op jit(solution)/shard_map/forward/pallas_call | solution.py:219
  95.7 4.7 %collective-permute-start.2 = (bf16[40,2,16,683]{3,2,1,0:T(8,128)(2,1)}, bf16[40,2,16,683]{3,2,1,0:T(8,128)(2,1)}, u32[]{:S(2)}, u32[]{:S(2)}) collective-permute-start(bf16[40,2,16,683]{3,2,1,0:T(8,128)(2,1)} %get-tuple-element.12.own), channel_id=1, source_target_pairs={{0,8},{8,16},{16,24},{1,9},{9,17},{17,25},{2,10},{10,18},{18,26},{... | collective-permute-start | bytes 5245448 | tf_op jit(solution)/shard_map/ppermute | solution.py:542
  100.4 1.9 %collective-permute-start.3 = (bf16[40,2,16,683]{3,2,1,0:T(8,128)(2,1)}, bf16[40,2,16,683]{3,2,1,0:T(8,128)(2,1)}, u32[]{:S(2)}, u32[]{:S(2)}) collective-permute-start(bf16[40,2,16,683]{3,2,1,0:T(8,128)(2,1)} %get-tuple-element.12.own), channel_id=1, source_target_pairs={{8,0},{16,8},{24,16},{9,1},{17,9},{25,17},{10,2},{18,10},{26,18},{... | collective-permute-start | bytes 5245448 | tf_op jit(solution)/shard_map/ppermute | solution.py:543
  102.4 0.1 slice.9
  102.4 0.1 reshape.41.waves
  102.5 7.7 %zonal.3.own = bf16[64,32,128]{2,1,0:T(8,128)(2,1)} custom-call(s32[64,1]{1,0:T(8,128)S(1)} %reshape.41.waves, bf16[2,8,128,2048]{3,2,1,0:T(8,128)(2,1)} %velocity.5, bf16[2,8,128,2048]{3,2,1,0:T(8,128)(2,1)} %tracer.5), custom_call_target="tpu_custom_call" | custom-call | flops 1073741824 | bytes 17301504 | tf_op jit(solution)/shard_map/zonal/pallas_call | solution.py:171
  110.2 3.6 %collective-permute-start = (bf16[64,32,128]{2,1,0:T(8,128)(2,1)}, bf16[64,32,128]{2,1,0:T(8,128)(2,1)S(1)}, u32[]{:S(2)}, u32[]{:S(2)}) collective-permute-start(bf16[64,32,128]{2,1,0:T(8,128)(2,1)} %zonal.3.own), channel_id=1, source_target_pairs={{0,8},{8,16},{16,24},{1,9},{9,17},{17,25},{2,10},{10,18},{18,26},{... | collective-permute-start | bytes 1572872 | tf_op jit(solution)/shard_map/ppermute | solution.py:542
  113.9 1.9 %collective-permute-start.1 = (bf16[64,32,128]{2,1,0:T(8,128)(2,1)}, bf16[64,32,128]{2,1,0:T(8,128)(2,1)S(1)}, u32[]{:S(2)}, u32[]{:S(2)}) collective-permute-start(bf16[64,32,128]{2,1,0:T(8,128)(2,1)} %zonal.3.own), channel_id=1, source_target_pairs={{8,0},{16,8},{24,16},{9,1},{17,9},{25,17},{10,2},{18,10},{26,18},{... | collective-permute-start | bytes 1572872 | tf_op jit(solution)/shard_map/ppermute | solution.py:543
  115.8 6.5 %collective-permute-done.2.low = bf16[40,2,16,683]{3,2,1,0:T(8,128)(2,1)} collective-permute-done((bf16[40,2,16,683]{3,2,1,0:T(8,128)(2,1)}, bf16[40,2,16,683]{3,2,1,0:T(8,128)(2,1)}, u32[]{:S(2)}, u32[]{:S(2)}) %collective-permute-start.2) | collective-permute-done | bytes 1748512 | tf_op jit(solution)/shard_map/ppermute | solution.py:542
  122.3 4.4 %collective-permute-done.3.high = bf16[40,2,16,683]{3,2,1,0:T(8,128)(2,1)} collective-permute-done((bf16[40,2,16,683]{3,2,1,0:T(8,128)(2,1)}, bf16[40,2,16,683]{3,2,1,0:T(8,128)(2,1)}, u32[]{:S(2)}, u32[]{:S(2)}) %collective-permute-start.3) | collective-permute-done | bytes 1748512 | tf_op jit(solution)/shard_map/ppermute | solution.py:543
  126.7 9.3 %inverse.1 = (bf16[88,2,2,8,683]{4,3,2,1,0:T(8,128)(2,1)}, bf16[88,2,2,8,1024]{4,3,2,1,0:T(8,128)(2,1)}, f32[8,128]{1,0:T(8,128)S(1)}) custom-call(s32[88]{0:T(128)S(1)} %dynamic_slice.6.waves, s32[2]{0:T(128)S(1)} %subtract_add_fusion.offsets, bf16[40,2,16,683]{3,2,1,0:T(8,128)(2,1)} %collective-permute-done.2.low, ...), custom_call_target="tpu_custom_call" | custom-call | flops 3580887040 | bytes 14161408 | tf_op jit(solution)/shard_map/inverse/pallas_call | solution.py:309
  136.0 0.0 collective-permute-done.low
  136.0 0.0 collective-permute-done.1.high
  136.0 5.4 %parents.2 = bf16[64,32,128]{2,1,0:T(8,128)(2,1)} custom-call(s32[2]{0:T(128)S(1)} %subtract_add_fusion.offsets, bf16[64,32,128]{2,1,0:T(8,128)(2,1)S(1)} %collective-permute-done.low, bf16[64,32,128]{2,1,0:T(8,128)(2,1)} %zonal.3.own, bf16[64,32,128]{2,1,0:T(8,128)(2,1)S(1)} %collective-permute-done.1.high, f32[8,128]{1,0:T(8,128)S(1)} %get-tuple-element.13.rest_0_), custom_call_target="tpu_custom_call" | custom-call | bytes 2097152 | tf_op jit(solution)/shard_map/parents/pallas_call | solution.py:355
  141.4 0.0 all-to-all-done.2.received
  141.4 5.4 %all-to-all-start.1 = ((bf16[8,256,128]{2,1,0:T(8,128)(2,1)}), bf16[8,256,128]{2,1,0:T(8,128)(2,1)S(1)}, u32[]{:S(2)}, u32[]{:S(2)}) async-start(bf16[8,256,128]{2,1,0:T(8,128)(2,1)} %bitcast.5), calls=%async_computation.1 | async-start | bytes 1048576 | tf_op jit(solution)/shard_map/all_to_all | solution.py:548
  146.8 12.2 %finish.1 = (bf16[88,2,2,8,683]{4,3,2,1,0:T(8,128)(2,1)}, bf16[88,2,2,8,1024]{4,3,2,1,0:T(8,128)(2,1)}) custom-call(s32[88]{0:T(128)S(1)} %dynamic_slice.6.waves, bf16[8,1280,128]{2,1,0:T(8,128)(2,1)} %all-to-all-done.2.received, bf16[88,2,2,8,683]{4,3,2,1,0:T(8,128)(2,1)} %noise.5, ...), custom_call_target="tpu_custom_call", output_to_operand_aliasing={{0}: (5, {}), {1}: (6, {})} | custom-call | flops 7161774080 | bytes 11537408 | tf_op jit(solution)/shard_map/finish/pallas_call | solution.py:483
  159.0 3.0 %all-to-all-done.1.received = bf16[8,256,128]{2,1,0:T(8,128)(2,1)S(1)} async-done(((bf16[8,256,128]{2,1,0:T(8,128)(2,1)}), bf16[8,256,128]{2,1,0:T(8,128)(2,1)S(1)}, u32[]{:S(2)}, u32[]{:S(2)}) %all-to-all-start.1) | async-done | bytes 524320 | tf_op jit(solution)/shard_map/all_to_all | solution.py:548
  162.0 3.4 %last.1 = (bf16[88,2,2,8,683]{4,3,2,1,0:T(8,128)(2,1)}, bf16[88,2,2,8,1024]{4,3,2,1,0:T(8,128)(2,1)}) custom-call(s32[88]{0:T(128)S(1)} %dynamic_slice.6.waves, bf16[8,256,128]{2,1,0:T(8,128)(2,1)S(1)} %all-to-all-done.1.received, bf16[88,2,2,8,683]{4,3,2,1,0:T(8,128)(2,1)} %noise.5, ...), custom_call_target="tpu_custom_call", output_to_operand_aliasing={{0}: (5, {}), {1}: (6, {})} | custom-call | flops 1432354816 | bytes 4545536 | tf_op jit(solution)/shard_map/last/pallas_call | solution.py:443
  (2 shorter events, 0.0 us)
Async XLA Ops:
  12.5 65.1 %all-to-all-start = ((bf16[8,1280,128]{2,1,0:T(8,128)(2,1)}), bf16[8,1280,128]{2,1,0:T(8,128)(2,1)}, u32[]{:S(2)}, u32[]{:S(2)}) async-start(bf16[8,1280,128]{2,1,0:T(8,128)(2,1)} %bitcast.4), calls=%async_computation | async-start | bytes 5242880 | tf_op jit(solution)/shard_map/all_to_all | solution.py:548
  19.0 16.9 %copy-start = (s32[8]{0:T(128)S(1)}, s32[8]{0:T(128)}, u32[]{:S(2)}) copy-start(s32[8]{0:T(128)} %param.8) | copy-start | bytes 100
  30.0 32.9 %collective-permute-start.4 = (bf16[320,32,128]{2,1,0:T(8,128)(2,1)}, bf16[320,32,128]{2,1,0:T(8,128)(2,1)S(1)}, u32[]{:S(2)}, u32[]{:S(2)}) collective-permute-start(bf16[320,32,128]{2,1,0:T(8,128)(2,1)} %zonal.5.own), channel_id=1, source_target_pairs={{0,8},{8,16},{16,24},{1,9},{9,17},{17,25},{2,10},{10,18},{18,26},{... | collective-permute-start | bytes 7864328 | tf_op jit(solution)/shard_map/ppermute | solution.py:542
  34.0 33.3 %collective-permute-start.5 = (bf16[320,32,128]{2,1,0:T(8,128)(2,1)}, bf16[320,32,128]{2,1,0:T(8,128)(2,1)}, u32[]{:S(2)}, u32[]{:S(2)}) collective-permute-start(bf16[320,32,128]{2,1,0:T(8,128)(2,1)} %zonal.5.own), channel_id=1, source_target_pairs={{8,0},{16,8},{24,16},{9,1},{17,9},{25,17},{10,2},{18,10},{26,18},{... | collective-permute-start | bytes 7864328 | tf_op jit(solution)/shard_map/ppermute | solution.py:543
  77.6 63.8 %all-to-all-start.2 = ((bf16[8,1280,128]{2,1,0:T(8,128)(2,1)}), bf16[8,1280,128]{2,1,0:T(8,128)(2,1)}, u32[]{:S(2)}, u32[]{:S(2)}) async-start(bf16[8,1280,128]{2,1,0:T(8,128)(2,1)} %bitcast.3), calls=%async_computation.2 | async-start | bytes 5242880 | tf_op jit(solution)/shard_map/all_to_all | solution.py:548
  95.7 26.6 %collective-permute-start.2 = (bf16[40,2,16,683]{3,2,1,0:T(8,128)(2,1)}, bf16[40,2,16,683]{3,2,1,0:T(8,128)(2,1)}, u32[]{:S(2)}, u32[]{:S(2)}) collective-permute-start(bf16[40,2,16,683]{3,2,1,0:T(8,128)(2,1)} %get-tuple-element.12.own), channel_id=1, source_target_pairs={{0,8},{8,16},{16,24},{1,9},{9,17},{17,25},{2,10},{10,18},{18,26},{... | collective-permute-start | bytes 5245448 | tf_op jit(solution)/shard_map/ppermute | solution.py:542
  100.4 26.3 %collective-permute-start.3 = (bf16[40,2,16,683]{3,2,1,0:T(8,128)(2,1)}, bf16[40,2,16,683]{3,2,1,0:T(8,128)(2,1)}, u32[]{:S(2)}, u32[]{:S(2)}) collective-permute-start(bf16[40,2,16,683]{3,2,1,0:T(8,128)(2,1)} %get-tuple-element.12.own), channel_id=1, source_target_pairs={{8,0},{16,8},{24,16},{9,1},{17,9},{25,17},{10,2},{18,10},{26,18},{... | collective-permute-start | bytes 5245448 | tf_op jit(solution)/shard_map/ppermute | solution.py:543
  110.2 25.7 %collective-permute-start = (bf16[64,32,128]{2,1,0:T(8,128)(2,1)}, bf16[64,32,128]{2,1,0:T(8,128)(2,1)S(1)}, u32[]{:S(2)}, u32[]{:S(2)}) collective-permute-start(bf16[64,32,128]{2,1,0:T(8,128)(2,1)} %zonal.3.own), channel_id=1, source_target_pairs={{0,8},{8,16},{16,24},{1,9},{9,17},{17,25},{2,10},{10,18},{18,26},{... | collective-permute-start | bytes 1572872 | tf_op jit(solution)/shard_map/ppermute | solution.py:542
  113.9 22.1 %collective-permute-start.1 = (bf16[64,32,128]{2,1,0:T(8,128)(2,1)}, bf16[64,32,128]{2,1,0:T(8,128)(2,1)S(1)}, u32[]{:S(2)}, u32[]{:S(2)}) collective-permute-start(bf16[64,32,128]{2,1,0:T(8,128)(2,1)} %zonal.3.own), channel_id=1, source_target_pairs={{8,0},{16,8},{24,16},{9,1},{17,9},{25,17},{10,2},{18,10},{26,18},{... | collective-permute-start | bytes 1572872 | tf_op jit(solution)/shard_map/ppermute | solution.py:543
  141.4 20.6 %all-to-all-start.1 = ((bf16[8,256,128]{2,1,0:T(8,128)(2,1)}), bf16[8,256,128]{2,1,0:T(8,128)(2,1)S(1)}, u32[]{:S(2)}, u32[]{:S(2)}) async-start(bf16[8,256,128]{2,1,0:T(8,128)(2,1)} %bitcast.5), calls=%async_computation.1 | async-start | bytes 1048576 | tf_op jit(solution)/shard_map/all_to_all | solution.py:548
